TPU v7x, 32 devices: a whole 2x2x4 slice. The times are simulated.
32 devices in a mesh: pair: 8 (over y, x, core), sec: 4 (over z).
Axes of the slice: x: 2, y: 2, z: 4, core: 2. Of those that a mesh axis runs over, the one named last changes fastest.
Arguments:
- normal_ops: float32 [2, 16, 128, 512], P(None, 'pair', None, 'sec'), may hold values from -6 to 6
- integrals: float32 [2, 8, 16], P(None, 'pair'), may hold values from -2 to 2
- site_terms: float32 [2, 8, 4, 4], P(None, 'pair'), may hold values from -8 to 8
- basis: float32 [2, 4, 512, 512], P(None, None, None, 'sec'), may hold values from -0.25 to 0.25
Outputs:
- new_normal: float32 [2, 16, 4, 128, 512], P(None, 'pair', None, None, 'sec')
- new_comp: float32 [2, 8, 4, 128, 512], P(None, 'pair', None, None, 'sec')
All inputs are finite; a program needn't handle non-finite values.
Results may differ from a plain program's by a relative error of at most 0.00007.
Values sent between devices are 32-bit elements; how exact they have to be, the bound alone decides.
No kernel may reach another device: no remote copies, remote signals or barrier semaphores. Data moves between devices by JAX's collectives and lax.ppermute only.
A program may use at most 64 MiB of HBM per device.

v0:
```python
from functools import partial

import jax
import jax.numpy as jnp
from jax import lax
from jax.sharding import PartitionSpec as P

highest = lax.Precision.HIGHEST


def complex_einsum(form, left, right):
    real_part = jnp.einsum(form, left[0], right[0], precision=highest) - jnp.einsum(
        form, left[1], right[1], precision=highest
    )
    imag_part = jnp.einsum(form, left[0], right[1], precision=highest) + jnp.einsum(
        form, left[1], right[0], precision=highest
    )
    return jnp.stack([real_part, imag_part])


def renorm_add(carry, piece, start, basis):
    return complex_einsum("xij,ajn->xain", piece, basis)


def on_device(normal_ops, integrals, site_terms, basis):
    norm_local = normal_ops.shape[1]
    row_count = normal_ops.shape[2]
    col_local = normal_ops.shape[3]
    comp_local = integrals.shape[1]
    site_count = basis.shape[1]
    comp_ops = complex_einsum(
        "pr,rxc->pxc", integrals, lax.all_gather(normal_ops, "pair", axis=1, tiled=True)
    )
    zeros_normal = jnp.zeros((2, norm_local, site_count, row_count, col_local), jnp.float32)
    zeros_comp = jnp.zeros((2, comp_local, site_count, row_count, col_local), jnp.float32)
    renorm_step = partial(renorm_add, basis=basis)
    new_normal = renorm_step(
        zeros_normal, lax.all_gather(normal_ops, "sec", axis=3, tiled=True), jnp.int32(0)
    )
    new_comp = renorm_step(
        zeros_comp, lax.all_gather(comp_ops, "sec", axis=3, tiled=True), jnp.int32(0)
    )
    site_part = complex_einsum("pab,bin->pain", site_terms, basis[:, :, :row_count, :])
    return (new_normal, new_comp + site_part)


def solution(mesh):
    placed = (
        P(None, "pair", None, "sec"),
        P(None, "pair", None),
        P(None, "pair", None, None),
        P(None, None, None, "sec"),
    )
    return jax.shard_map(
        on_device,
        mesh=mesh,
        in_specs=placed,
        out_specs=(P(None, "pair", None, None, "sec"), P(None, "pair", None, None, "sec")),
        check_vma=False,
    )
```

profile of v0, /device:TPU:0, one launch (start us, length us, event | category | flops | bytes accessed | tf_op | source)
XLA Modules:
  0.0 104.0 jit_solution(3363027996315677026)
XLA Ops:
  7.2 0.0 copy-start.3
  7.2 0.0 all-gather.3.cloned.1.call-start
  7.2 0.7 all-gather.3.cloned.1.call-update
  7.9 0.0 all-gather.5.cloned.1.call-start
  8.0 0.7 all-gather.5.cloned.1.call-update
  8.7 1.1 %fusion.54 = (f32[1,4,128,128]{3,2,1,0:T(8,128)S(1)}, f32[1,4,128,128]{3,2,1,0:T(8,128)S(1)}) fusion(f32[2,4,512,128]{3,2,1,0:T(8,128)} %param.7), kind=kLoop, calls=%fused_computation.73 | loop fusion | bytes 1048576 | tf_op jit(solution)/shard_map/slice | solution.py:13
  9.7 0.0 copy-start
  9.7 1.5 %fusion.34 = f32[4,128,128]{2,0,1:T(4,128)S(1)} fusion(f32[1,4,128,128]{3,2,1,0:T(8,128)S(1)} %get-tuple-element.5, f32[2,1,4,4]{3,2,1,0:T(4,128)} %param.6), kind=kOutput, calls=%fused_computation.50 | convolution fusion | flops 3145728 | bytes 526336 | tf_op jit(solution)/shard_map/pab,bin->pain/dot_general | solution.py:15
  11.3 0.0 copy-done.3
  11.3 0.7 fusion.35
  12.0 0.7 fusion.36
  12.7 0.7 fusion.37
  13.3 0.8 fusion.32
  14.1 28.4 %all-gather.3.cloned.1.call-done = f32[2,2,128,512]{3,2,1,0:T(8,128)} async-done(((f32[2,2,128,128]{3,2,1,0:T(8,128)}), f32[2,2,128,512]{3,2,1,0:T(8,128)}) %all-gather.3.cloned.1.call-update) | async-done | bytes 1048592 | tf_op jit(solution)/shard_map/all_gather | solution.py:38
  42.5 0.0 copy-done
  42.5 0.0 copy-start.1
  42.5 2.9 %fusion.14 = f32[4,128,2,128]{3,1,2,0:T(8,128)S(1)} fusion(f32[2,4,512,128]{3,2,1,0:T(8,128)S(1)} %copy-done, f32[2,2,128,512]{3,2,1,0:T(8,128)} %all-gather.3.cloned.1.call-done), kind=kOutput, calls=%fused_computation.21 | convolution fusion | flops 805306368 | bytes 2097152 | tf_op jit(solution)/shard_map/xij,ajn->xain/dot_general | solution.py:12
  45.4 0.0 copy-done.1
  45.5 1.8 %fusion.1 = f32[1,2,4,128,128]{3,4,1,2,0:T(8,128)S(1)} fusion(f32[4,128,2,128]{3,1,2,0:T(8,128)S(1)} %fusion.14, f32[2,4,512,128]{3,2,1,0:T(8,128)S(1)} %copy-done, f32[2,2,128,512]{3,2,1,0:T(8,128)S(1)} %copy-done.1), kind=kOutput, calls=%fused_computation.3 | convolution fusion | flops 805437440 | bytes 2621440 | tf_op jit(solution)/shard_map/xij,ajn->xain/dot_general | solution.py:12
  47.3 1.8 %fusion.10 = f32[4,128,2,128]{3,1,2,0:T(8,128)S(1)} fusion(f32[2,4,512,128]{3,2,1,0:T(8,128)S(1)} %copy-done, f32[2,2,128,512]{3,2,1,0:T(8,128)S(1)} %copy-done.1), kind=kOutput, calls=%fused_computation.17 | convolution fusion | flops 805306368 | bytes 2097152 | tf_op jit(solution)/shard_map/xij,ajn->xain/dot_general | solution.py:15
  49.1 1.8 %fusion = f32[1,2,4,128,128]{3,4,1,2,0:T(8,128)S(1)} fusion(f32[4,128,2,128]{3,1,2,0:T(8,128)S(1)} %fusion.10, f32[2,4,512,128]{3,2,1,0:T(8,128)S(1)} %copy-done, f32[2,2,128,512]{3,2,1,0:T(8,128)S(1)} %copy-done.1), kind=kOutput, calls=%fused_computation.1 | convolution fusion | flops 805437440 | bytes 2621440 | tf_op jit(solution)/shard_map/xij,ajn->xain/dot_general | solution.py:15
  50.9 0.1 pad_maximum_fusion
  51.0 1.3 %copy.18 = f32[2,2,4,128,128]{4,3,2,1,0:T(8,128)} copy(f32[2,2,4,128,128]{3,4,1,2,0:T(8,128)S(1)} %pad_maximum_fusion) | data formatting | bytes 2097152
  52.3 0.0 copy-start.4
  52.3 18.4 %all-gather.5.cloned.1.call-done = f32[2,16,128,128]{3,2,1,0:T(8,128)} async-done(((f32[2,2,128,128]{3,2,1,0:T(8,128)}), f32[2,16,128,128]{3,2,1,0:T(8,128)}) %all-gather.5.cloned.1.call-update) | async-done | bytes 2097168 | tf_op jit(solution)/shard_map/all_gather | solution.py:32
  70.6 1.7 %slice_bitcast_fusion.1 = (f32[16,128,128]{2,1,0:T(8,128)S(1)}, f32[16,128,128]{2,1,0:T(8,128)S(1)}) fusion(f32[2,16,128,128]{3,2,1,0:T(8,128)} %all-gather.5.cloned.1.call-done), kind=kLoop, calls=%fused_computation.9 | loop fusion | bytes 4194304 | tf_op jit(solution)/shard_map/squeeze | solution.py:12
  72.3 0.0 copy-done.4
  72.3 1.2 %fusion.18 = f32[1,128,128]{2,0,1:T(1,128)S(1)} fusion(f32[16,128,128]{2,1,0:T(8,128)S(1)} %get-tuple-element.7, f32[2,1,16]{2,1,0:T(1,128)S(1)} %copy-done.4), kind=kOutput, calls=%fused_computation.25 | convolution fusion | flops 3145728 | bytes 1114624 | tf_op jit(solution)/shard_map/pr,rxc->pxc/dot_general | solution.py:12
  73.5 1.4 %fusion.16 = f32[1,128,128]{2,0,1:T(1,128)S(1)} fusion(f32[16,128,128]{2,1,0:T(8,128)S(1)} %get-tuple-element.7, f32[2,1,16]{2,1,0:T(1,128)S(1)} %copy-done.4), kind=kOutput, calls=%fused_computation.23 | convolution fusion | flops 3145728 | bytes 1114624 | tf_op jit(solution)/shard_map/pr,rxc->pxc/dot_general | solution.py:15
  74.9 1.2 %fusion.22 = f32[1,128,128]{2,0,1:T(1,128)S(1)} fusion(f32[16,128,128]{2,1,0:T(8,128)S(1)} %get-tuple-element.6, f32[2,1,16]{2,1,0:T(1,128)S(1)} %copy-done.4), kind=kOutput, calls=%fused_computation.29 | convolution fusion | flops 3145728 | bytes 1114624 | tf_op jit(solution)/shard_map/pr,rxc->pxc/dot_general | solution.py:12
  76.1 1.2 %fusion.20 = f32[1,128,128]{2,0,1:T(1,128)S(1)} fusion(f32[16,128,128]{2,1,0:T(8,128)S(1)} %get-tuple-element.6, f32[2,1,16]{2,1,0:T(1,128)S(1)} %copy-done.4), kind=kOutput, calls=%fused_computation.27 | convolution fusion | flops 3145728 | bytes 1114624 | tf_op jit(solution)/shard_map/pr,rxc->pxc/dot_general | solution.py:15
  77.3 16.1 %all_gather.11 = f32[2,1,128,512]{3,2,1,0:T(8,128)S(1)} all-gather(f32[2,1,128,128]{3,2,1,0:T(8,128)S(1)} %pad_maximum_fusion.1), channel_id=1, replica_groups=mesh['pair'=8,'sec'=4] {'sec'}, dimensions={3}, use_global_device_ids=true | all-gather | bytes 655360 | tf_op jit(solution)/shard_map/all_gather | solution.py:41
  93.4 0.7 fusion.8
  94.1 0.7 fusion.4
  94.8 0.0 copy-start.2
  94.8 0.7 fusion.3
  95.5 0.7 fusion.2
  96.3 0.0 copy-done.2
  96.3 0.9 maximum_add_fusion
  (2 shorter events, 0.0 us)
Async XLA Ops:
  7.2 4.1 %copy-start.3 = (f32[2,1,4,4]{3,2,1,0:T(4,128)S(1)}, f32[2,1,4,4]{3,2,1,0:T(4,128)}, u32[]{:S(2)}) copy-start(f32[2,1,4,4]{3,2,1,0:T(4,128)} %param.6) | copy-start | bytes 388
  7.2 35.3 %all-gather.3.cloned.1.call-start = ((), (), s32[]{:S(2)}) async-start(), calls=%async_computation | async-start | bytes 1310720 | tf_op jit(solution)/shard_map/all_gather | solution.py:38
  7.9 62.7 %all-gather.5.cloned.1.call-start = ((), (), s32[]{:S(2)}) async-start(), calls=%async_computation.1 | async-start | bytes 2359296 | tf_op jit(solution)/shard_map/all_gather | solution.py:32
  9.7 32.8 %copy-start = (f32[2,4,512,128]{3,2,1,0:T(8,128)S(1)}, f32[2,4,512,128]{3,2,1,0:T(8,128)}, u32[]{:S(2)}) copy-start(f32[2,4,512,128]{3,2,1,0:T(8,128)} %param.7) | copy-start | bytes 6291460
  42.5 2.9 %copy-start.1 = (f32[2,2,128,512]{3,2,1,0:T(8,128)S(1)}, f32[2,2,128,512]{3,2,1,0:T(8,128)}, u32[]{:S(2)}) copy-start(f32[2,2,128,512]{3,2,1,0:T(8,128)} %all-gather.3.cloned.1.call-done) | copy-start | bytes 3145732
  52.3 20.0 %copy-start.4 = (f32[2,1,16]{2,1,0:T(1,128)S(1)}, f32[2,1,16]{2,1,0:T(1,128)}, u32[]{:S(2)}) copy-start(f32[2,1,16]{2,1,0:T(1,128)} %param.5) | copy-start | bytes 388
  94.8 1.5 %copy-start.2 = (f32[1,1,4,128,128]{4,3,2,1,0:T(8,128)S(1)}, f32[1,1,4,128,128]{4,3,2,1,0:T(8,128)}, u32[]{:S(2)}) copy-start(f32[1,1,4,128,128]{4,3,2,1,0:T(8,128)} %get-tuple-element.11) | copy-start | bytes 786436
Sparse Core Ops, SparseCore 0:
  9.6 32.8 all-gather.2
  44.4 26.1 all-gather.4
where the time goes:
time: 104 us
  waiting for transfers between devices  48.1 us (46%)
  matrix products  19.7 us (19%)
  blocking collectives  16.1 us (15%)
  between operations  14.2 us (14%)
  local copies, waits for them, and re-layouts  4.09 us (4%)
  other arithmetic  1.73 us (2%)
    all_gather x1, waiting for transfers between devices, on_device(): lax.all_gather(normal_ops, 'sec', axis=3, tiled=True)  28.4 us
    all_gather x1, waiting for transfers between devices, on_device(): lax.all_gather(normal_ops, 'pair', axis=1, tiled=True)  18.4 us
    all_gather x1, blocking collectives, on_device(): lax.all_gather(comp_ops, 'sec', axis=3, tiled=True)  16.1 us
    dot_general x4, matrix products, complex_einsum(): jnp.einsum(form, left[0], right[0], precision=highest)  5.51 us
    dot_general x4, matrix products, complex_einsum(): jnp.einsum(form, left[1], right[0], precision=highest)  5.22 us
    dot_general x4, matrix products, complex_einsum(): jnp.einsum(form, left[0], right[1], precision=highest)  4.56 us
    dot_general x4, matrix products, complex_einsum(): jnp.einsum(form, left[1], right[1], precision=highest)  4.39 us
  transfers between devices with their start and end apart: 2, of which 2 were waited for; matrix products, arithmetic and copies ran while one was open for 15% of the time, Pallas kernels for 0%

commit v1 on v0

v1 whole, which is shorter than its diff:
```python
import functools

import jax
import jax.numpy as jnp
from jax import lax
from jax.experimental import pallas as pl
from jax.experimental.pallas import tpu as pltpu
from jax.sharding import PartitionSpec as P

VMEM_BYTES = 24 * 1024 * 1024
WIDE = 256
TILE = (8, 128)
VMEM = pl.BlockSpec(memory_space=pltpu.VMEM)
ANY = pl.BlockSpec(memory_space=pl.ANY)
HBM = pl.BlockSpec(memory_space=pltpu.HBM)


def call(kernel, out_shape, in_specs, flops, scratch_shapes=()):
    return pl.pallas_call(
        kernel,
        out_shape=out_shape,
        in_specs=in_specs,
        out_specs=jax.tree.map(lambda _: VMEM, out_shape),
        scratch_shapes=scratch_shapes,
        cost_estimate=pl.CostEstimate(flops=flops, bytes_accessed=4 << 20, transcendentals=0),
        compiler_params=pltpu.CompilerParams(vmem_limit_bytes=VMEM_BYTES),
    )


def split(x):
    high = x.astype(jnp.bfloat16)
    return high, (x - high.astype(jnp.float32)).astype(jnp.bfloat16)


def order(sec):
    return (1, 0) + tuple(range(2, sec))


def prepare_kernel(depth, basis_hbm, site_hbm, high_ref, low_ref, part_ref, *scratch):
    basis_ref, site_ref, basis_sem, site_sem = scratch
    _, sites, old, cols = basis_ref.shape
    rows = part_ref.shape[3]
    me = lax.axis_index("sec")
    site_copy = pltpu.make_async_copy(site_hbm, site_ref, site_sem)
    site_copy.start()
    copies = [
        (part, site, pltpu.make_async_copy(
            basis_hbm.at[part, site], basis_ref.at[part, site], basis_sem.at[part, site]
        ))
        for part in range(2)
        for site in range(sites)
    ]
    for _, _, copy in copies:
        copy.start()
    for part, site, copy in copies:
        copy.wait()
        for step, far in enumerate(order(old // depth)):
            start = pl.multiple_of((me ^ far) * depth, depth)
            at = pl.ds((step * 2 + part) * depth, depth)
            high, low = split(basis_ref[part, site, pl.ds(start, depth), :])
            high_ref[at, pl.ds(site * cols, cols)] = high
            low_ref[at, pl.ds(site * cols, cols)] = low
    site_copy.wait()
    for comp in range(part_ref.shape[1]):
        for site in range(sites):
            real = imag = None
            for other in range(sites):
                sr, si = site_ref[0, comp, site, other], site_ref[1, comp, site, other]
                br, bi = basis_ref[0, other, :rows, :], basis_ref[1, other, :rows, :]
                tr, ti = sr * br - si * bi, sr * bi + si * br
                real = tr if real is None else real + tr
                imag = ti if imag is None else imag + ti
            part_ref[0, comp, site] = real
            part_ref[1, comp, site] = imag


def prepare(basis, site_terms, rows, depth):
    _, sites, old, cols = basis.shape
    comps = site_terms.shape[1]
    half = jax.ShapeDtypeStruct((2 * old, sites * cols), jnp.bfloat16)
    part = jax.ShapeDtypeStruct((2, comps, sites, rows, cols), jnp.float32)
    return call(
        functools.partial(prepare_kernel, depth),
        (half, half, part),
        [HBM, HBM],
        8 * comps * sites * sites * rows * cols,
        [
            pltpu.VMEM(basis.shape, basis.dtype),
            pltpu.SMEM(site_terms.shape, site_terms.dtype),
            pltpu.SemaphoreType.DMA((2, sites)),
            pltpu.SemaphoreType.DMA,
        ],
    )(basis, site_terms)


def tile(integrals):
    _, comps, norms = integrals.shape

    def kernel(integrals_ref, out_ref):
        out_ref[...] = jnp.zeros(TILE, jnp.float32)
        for part in range(2):
            out_ref[part * comps : (part + 1) * comps, :norms] = integrals_ref[part]

    return call(kernel, jax.ShapeDtypeStruct(TILE, jnp.float32), [VMEM], 0)(integrals)


def pack(block, ops, tiles):
    _, _, rows, cols = block.shape

    def kernel(block_ref, *refs):
        out_ref = refs[-1]
        out_ref[:, :, :rows, :] = block_ref[:, ops.start : ops.stop]
        out_ref[:, :, rows:, :] = jnp.zeros((2, len(ops)) + TILE, jnp.float32)
        for part, ref in enumerate(refs[:-1]):
            out_ref[part, 0, rows:, :] = ref[...]

    out = jax.ShapeDtypeStruct((2, len(ops), rows + TILE[0], cols), block.dtype)
    return call(kernel, out, [VMEM] * (1 + len(tiles)), 0)(block, *tiles)


def after(x, *others):
    def kernel(x_ref, *refs):
        refs[-1][...] = x_ref[...]

    out = jax.ShapeDtypeStruct(x.shape, x.dtype)
    return call(kernel, out, [VMEM] + [ANY] * len(others), 0)(x, *others)


def renorm_kernel(steps, parts, carried, *refs):
    count = sum(parts)
    high_ref, low_ref = refs[count : count + 2]
    out_ref, token_ref, left_high, left_low = refs[-4:]
    token_ref[...] = jnp.zeros(TILE, jnp.float32)
    _, ops, sites, rows, cols = out_ref.shape
    depth = refs[0].shape[-1]
    tall = ops * rows
    for step in range(len(steps)):
        first = sum(parts[:step])
        value = sum(refs[at][:, :, :rows, :] for at in range(first + 1, first + parts[step]))
        value = (refs[first][:, :, :rows, :] + value).reshape(2, tall, depth)
        for scratch, real, imag in zip((left_high, left_low), split(value[0]), split(value[1])):
            at = 2 * step * depth
            scratch[:tall, at : at + depth] = real
            scratch[:tall, at + depth : at + 2 * depth] = -imag
            scratch[tall:, at : at + depth] = imag
            scratch[tall:, at + depth : at + 2 * depth] = real
    dot = functools.partial(jnp.dot, preferred_element_type=jnp.float32)
    deep = slice(2 * depth * steps[0], 2 * depth * (steps[-1] + 1))
    for first in range(0, sites * cols, WIDE):
        at = (deep, slice(first, first + WIDE))
        total = dot(left_high[...], high_ref[at])
        total = total + dot(left_high[...], low_ref[at])
        total = total + dot(left_low[...], high_ref[at])
        for site in range(first // cols, (first + WIDE) // cols):
            across = slice(site * cols - first, site * cols - first + cols)
            for part in range(2):
                for op in range(ops):
                    start = part * tall + op * rows
                    value = total[start : start + rows, across]
                    if carried:
                        value = value + refs[count + 2][part, op, site]
                    out_ref[part, op, site] = value


def renorm(blocks, steps, high, low, carry, shape):
    blocks = [block if isinstance(block, tuple) else (block,) for block in blocks]
    blocks = blocks[steps.start : steps.stop]
    parts = tuple(len(block) for block in blocks)
    args = sum(blocks, ()) + (high, low) + (() if carry is None else (carry,))
    _, ops, sites, rows, cols = shape
    depth = blocks[0][0].shape[-1]
    left = pltpu.VMEM((2 * ops * rows, 2 * depth * len(blocks)), jnp.bfloat16)
    return pl.pallas_call(
        functools.partial(renorm_kernel, steps, parts, carry is not None),
        out_shape=tuple(jax.ShapeDtypeStruct(dims, jnp.float32) for dims in (shape, TILE)),
        in_specs=[VMEM] * len(args),
        out_specs=(VMEM, VMEM),
        scratch_shapes=[left, left],
        cost_estimate=pl.CostEstimate(
            flops=24 * ops * rows * depth * len(blocks) * sites * cols,
            bytes_accessed=4 << 20,
            transcendentals=0,
        ),
        compiler_params=pltpu.CompilerParams(vmem_limit_bytes=VMEM_BYTES),
    )(*args)


def total(parts, awaited):
    def kernel(*refs):
        refs[-1][...] = sum((ref[...] for ref in refs[1 : len(parts)]), refs[0][...])

    out = jax.ShapeDtypeStruct(parts[0].shape, parts[0].dtype)
    specs = [VMEM] * len(parts) + [ANY] * len(awaited)
    return call(kernel, out, specs, out.size * len(parts))(*parts, *awaited)


def combine_kernel(operators, tables, per, *refs):
    outs = refs[len(refs) - len(tables) :]
    comps, rows, _ = outs[0].shape[1:]
    me = lax.axis_index("pair")
    lane = lax.broadcasted_iota(jnp.int32, (1, TILE[1]), 1)
    for (held, under), out_ref in zip(tables, outs):
        for comp in range(comps):
            real = imag = None
            for array, place, op, key in operators:
                coefficients = []
                for part in range(2):
                    at = part * comps + comp
                    if under is None:
                        row = refs[held][at : at + 1, :]
                    else:
                        row = refs[held][under, 0, rows + at : rows + at + 1, :]
                    here = jnp.where(lane == (me ^ key) * per + op, row, 0.0)
                    coefficients.append(jnp.sum(here, axis=1, keepdims=True))
                cr, ci = coefficients
                br, bi = (refs[array][part, place, :rows, :] for part in range(2))
                tr, ti = cr * br - ci * bi, cr * bi + ci * br
                real = tr if real is None else real + tr
                imag = ti if imag is None else imag + ti
            out_ref[0, comp] = real
            out_ref[1, comp] = imag


def combine(arrays, operators, tables, per, shape, awaited=()):
    rows, cols = shape[2:]
    return call(
        functools.partial(combine_kernel, operators, tables, per),
        (jax.ShapeDtypeStruct(shape, jnp.float32),) * len(tables),
        [VMEM] * len(arrays) + [ANY] * len(awaited),
        8 * len(tables) * len(operators) * rows * cols,
    )(*arrays, *awaited)


def swap(x, axis, size, key):
    return lax.ppermute(x, axis, [(at, at ^ key) for at in range(size)])


def chip_blocks(own, row, pairs):
    per = own.shape[1]
    arrays, tables = [own], []
    operators = [(0, op, op, 0) for op in range(per)]
    if pairs == 8 and per == 2:
        for key in (2, 4):
            operators += [(len(arrays), op, op, key) for op in range(per)]
            arrays.append(swap(own, "pair", pairs, key))
        beside = swap(row, "pair", pairs, 2)
        operators += [(3, 0, 0, 6), (4, 0, 1, 6)]
        arrays += [
            swap(pack(arrays[1], range(1), [row, beside]), "pair", pairs, 4),
            swap(pack(arrays[2], range(1, 2), []), "pair", pairs, 2),
            row,
            beside,
        ]
        tables = [(5, None), (6, None), (3, 0), (3, 1)]
    else:
        arrays[0] = pack(own, range(per), [row])
        tables = [(0, 0)]
        for key in range(2, pairs, 2):
            operators += [(len(arrays), op, op, key) for op in range(per)]
            tables.append((len(arrays), 0))
            arrays.append(swap(arrays[0], "pair", pairs, key))
    return arrays, operators, tables


def on_device(pairs, sec, normal_ops, integrals, site_terms, basis):
    _, norms, rows, depth = normal_ops.shape
    _, sites, _, cols = basis.shape
    comps = integrals.shape[1]
    shape = (2, comps, rows, depth)
    two = swap(normal_ops, "sec", sec, 2)
    one = swap(normal_ops, "sec", sec, 1)
    row = tile(integrals)
    arrays, operators, tables = chip_blocks(normal_ops, row, pairs)
    high, low, site_part = prepare(basis, site_terms, rows, depth)
    two = after(after(two, high), one)
    three = swap(two, "sec", sec, 1)
    normals = [one, normal_ops, two, three]
    held = arrays + [row, swap(row, "pair", pairs, 1)]
    here = [(len(arrays), None), (len(arrays) + 1, None)]
    mine, other = combine(held, operators, here, norms, shape)
    comp_ops = total([mine, swap(other, "pair", pairs, 1)], [two])
    far = swap(comp_ops, "sec", sec, 3)
    near = swap(comp_ops, "sec", sec, 1)
    held = [two, swap(two, "pair", pairs, 1)] + arrays
    operators = [(key, op, op, key) for key in range(2) for op in range(norms)]
    tables = [(2 + at, part) for at, part in tables]
    parts = combine(held, operators, tables, norms, shape, [comp_ops])
    summed = [parts[0]] + [
        swap(part, "pair", pairs, key) for part, key in zip(parts[1:], range(2, pairs, 2))
    ]
    shape = (2, norms, sites, rows, cols)
    early, _ = renorm(normals, range(sec - 1), high, low, None, shape)
    new_normal, _ = renorm(normals, range(sec - 1, sec), high, low, early, shape)
    shape = (2, comps, sites, rows, cols)
    arrived = [near, comp_ops, tuple(summed), far]
    early, _ = renorm(arrived, range(1, sec), high, low, site_part, shape)
    return new_normal, renorm(arrived, range(1), high, low, early, shape)[0]


def solution(mesh):
    placed = (
        P(None, "pair", None, "sec"),
        P(None, "pair", None),
        P(None, "pair", None, None),
        P(None, None, None, "sec"),
    )
    return jax.shard_map(
        functools.partial(on_device, mesh.shape["pair"], mesh.shape["sec"]),
        mesh=mesh,
        in_specs=placed,
        out_specs=(P(None, "pair", None, None, "sec"), P(None, "pair", None, None, "sec")),
        check_vma=False,
    )
```

time: 104 us -> 38.6 us (0.37)
  waiting for transfers between devices: 48.1 us -> 8.05 us
  matrix products: 19.7 us -> 0 us
  starting transfers between devices: 0.08 us -> 18.9 us
  blocking collectives: 16.1 us -> 0 us
  between operations: 14.2 us -> 0.71 us
  Pallas kernels: 0 us -> 7.77 us
  other arithmetic: 1.73 us -> 0 us
  local copies, waits for them, and re-layouts: 4.09 us -> 2.96 us
    all_gather x2 -> x0, waiting for transfers between devices: 46.7 us -> none  [the longest x1 28.4 us: on_device(): lax.all_gather(normal_ops, 'sec', axis=3, tiled=True)]
    dot_general x16 -> x0, matrix products: 19.7 us -> none  [the longest x4 5.51 us: complex_einsum(): jnp.einsum(form, left[0], right[0], precision=highest)]
    ppermute x0 -> x16, starting transfers between devices: none -> 18.9 us  [swap(): return lax.ppermute(x, axis, [(at, at ^ key) for at in range(size)])]
    all_gather x1 -> x0, blocking collectives: 16.1 us -> none  [on_device(): lax.all_gather(comp_ops, 'sec', axis=3, tiled=True)]
    ppermute x0 -> x16, waiting for transfers between devices: none -> 8.05 us  [swap(): return lax.ppermute(x, axis, [(at, at ^ key) for at in range(size)])]
    pallas_call x0 -> x13, Pallas kernels: none -> 7.77 us  [the longest x4 5.8 us: renorm(): pl.pallas_call(functools.partial(renorm_kernel, steps, parts, carry is no...]
    squeeze x1 -> x0, local copies, waits for them, and re-layouts: 1.68 us -> none  [complex_einsum(): right[0]]
    unnamed x11 -> x8, local copies, waits for them, and re-layouts: 1.33 us -> 2.96 us
  transfers between devices with their start and end apart: 2 -> 16, of which waited for: 2 -> 6; matrix products, arithmetic and copies ran while one was open for 15% -> 0% of each run, Pallas kernels for 0% -> 17%
where the time goes in v1:
time: 38.6 us; the launch traced here: 38.4 us
  starting transfers between devices  18.9 us (49%)
  waiting for transfers between devices  8.05 us (21%)
  Pallas kernels  7.77 us (20%)
  local copies, waits for them, and re-layouts  2.96 us (8%)
  between operations  0.71 us (2%)
    ppermute x16, starting transfers between devices, swap(): return lax.ppermute(x, axis, [(at, at ^ key) for at in range(size)])  18.9 us
    ppermute x16, waiting for transfers between devices, swap(): return lax.ppermute(x, axis, [(at, at ^ key) for at in range(size)])  8.05 us
    pallas_call x4, Pallas kernels, renorm(): pl.pallas_call(functools.partial(renorm_kernel, steps, parts, carry is no...  5.8 us
    unnamed x8, local copies, waits for them, and re-layouts  2.96 us
    pallas_call x1, Pallas kernels, prepare(): call(functools.partial(prepare_kernel, depth), (half, half, part), [HBM,...  0.97 us
    pallas_call x2, Pallas kernels, combine(): call(functools.partial(combine_kernel, operators, tables, per), (jax.Shap...  0.94 us
  transfers between devices with their start and end apart: 16, of which 6 were waited for; matrix products, arithmetic and copies ran while one was open for 0% of the time, Pallas kernels for 17%

profile of v1, /device:TPU:0, one launch (start us, length us, event | category | flops | bytes accessed | tf_op | source)
XLA Modules:
  0.0 38.4 jit_solution(5942249615559069239)
XLA Ops:
  0.6 3.0 %collective-permute-start.3 = (f32[2,2,128,128]{3,2,1,0:T(8,128)}, f32[2,2,128,128]{3,2,1,0:T(8,128)S(1)}, u32[]{:S(2)}, u32[]{:S(2)}) collective-permute-start(f32[2,2,128,128]{3,2,1,0:T(8,128)} %refs_2_.1), channel_id=1, source_target_pairs={{0,8},{4,12},{8,0},{12,4},{16,24},{20,28},{24,16},{28,20},{1,9},{5... | collective-permute-start | bytes 786440 | tf_op jit(solution)/shard_map/ppermute | solution.py:235
  3.6 1.5 %collective-permute-start.4 = (f32[2,2,128,128]{3,2,1,0:T(8,128)}, f32[2,2,128,128]{3,2,1,0:T(8,128)S(1)}, u32[]{:S(2)}, u32[]{:S(2)}) collective-permute-start(f32[2,2,128,128]{3,2,1,0:T(8,128)} %refs_2_.1), channel_id=1, source_target_pairs={{0,16},{4,20},{8,24},{12,28},{16,0},{20,4},{24,8},{28,12},{1,17},{... | collective-permute-start | bytes 786440 | tf_op jit(solution)/shard_map/ppermute | solution.py:235
  5.2 2.6 %collective-permute-start = (f32[2,2,128,128]{3,2,1,0:T(8,128)}, f32[2,2,128,128]{3,2,1,0:T(8,128)S(1)}, u32[]{:S(2)}, u32[]{:S(2)}) collective-permute-start(f32[2,2,128,128]{3,2,1,0:T(8,128)} %refs_2_.1), channel_id=1, source_target_pairs={{0,2},{1,3},{2,0},{3,1},{4,6},{5,7},{6,4},{7,5},{8,10},{9,11},{10,... | collective-permute-start | bytes 786440 | tf_op jit(solution)/shard_map/ppermute | solution.py:235
  7.7 1.6 %collective-permute-start.1 = (f32[2,2,128,128]{3,2,1,0:T(8,128)}, f32[2,2,128,128]{3,2,1,0:T(8,128)S(1)}, u32[]{:S(2)}, u32[]{:S(2)}) collective-permute-start(f32[2,2,128,128]{3,2,1,0:T(8,128)} %refs_2_.1), channel_id=1, source_target_pairs={{0,1},{1,0},{2,3},{3,2},{4,5},{5,4},{6,7},{7,6},{8,9},{9,8},{10,11... | collective-permute-start | bytes 786440 | tf_op jit(solution)/shard_map/ppermute | solution.py:235
  9.3 0.0 copy-start.3
  9.3 0.7 %copy-done.3 = f32[2,1,16]{2,1,0:T(1,128)S(1)} copy-done((f32[2,1,16]{2,1,0:T(1,128)S(1)}, f32[2,1,16]{2,1,0:T(1,128)}, u32[]{:S(2)}) %copy-start.3) | copy-done | bytes 152
  10.0 0.5 %collective-permute-start.5 = (f32[8,128]{1,0:T(8,128)S(1)}, f32[8,128]{1,0:T(8,128)S(1)}, u32[]{:S(2)}, u32[]{:S(2)}) collective-permute-start(f32[8,128]{1,0:T(8,128)S(1)} %shard_map.64.refs_0_.refs_5_.refs_7_), channel_id=1, source_target_pairs={{0,8},{4,12},{8,0},{12,4},{16,24},{20,28},{24,16},{28,20},{1,9},{5... | collective-permute-start | bytes 12296 | tf_op jit(solution)/shard_map/ppermute | solution.py:235
  10.5 3.1 %collective-permute-done.5.refs_1_.refs_6_.refs_8_ = f32[8,128]{1,0:T(8,128)S(1)} collective-permute-done((f32[8,128]{1,0:T(8,128)S(1)}, f32[8,128]{1,0:T(8,128)S(1)}, u32[]{:S(2)}, u32[]{:S(2)}) %collective-permute-start.5) | collective-permute-done | bytes 4128 | tf_op jit(solution)/shard_map/ppermute | solution.py:235
  13.6 0.0 collective-permute-done.3.block_ref.refs_1_.refs_3_
  13.6 0.6 %collective-permute-start.6 = (f32[2,1,136,128]{3,2,1,0:T(8,128)S(1)}, f32[2,1,136,128]{3,2,1,0:T(8,128)S(1)}, u32[]{:S(2)}, u32[]{:S(2)}) collective-permute-start(f32[2,1,136,128]{3,2,1,0:T(8,128)S(1)} %shard_map.65), channel_id=1, source_target_pairs={{0,16},{4,20},{8,24},{12,28},{16,0},{20,4},{24,8},{28,12},{1,17},{... | collective-permute-start | bytes 417800 | tf_op jit(solution)/shard_map/ppermute | solution.py:235
  14.2 0.0 collective-permute-done.4.block_ref.refs_2_.refs_4_
  14.2 0.6 %collective-permute-start.7 = (f32[2,1,136,128]{3,2,1,0:T(8,128)S(1)}, f32[2,1,136,128]{3,2,1,0:T(8,128)S(1)}, u32[]{:S(2)}, u32[]{:S(2)}) collective-permute-start(f32[2,1,136,128]{3,2,1,0:T(8,128)S(1)} %shard_map.66), channel_id=1, source_target_pairs={{0,8},{4,12},{8,0},{12,4},{16,24},{20,28},{24,16},{28,20},{1,9},{5... | collective-permute-start | bytes 417800 | tf_op jit(solution)/shard_map/ppermute | solution.py:235
  14.8 0.0 copy-start
  14.8 1.6 %copy-done = f32[2,4,512,128]{3,2,1,0:T(8,128)S(1)} copy-done((f32[2,4,512,128]{3,2,1,0:T(8,128)S(1)}, f32[2,4,512,128]{3,2,1,0:T(8,128)}, u32[]{:S(2)}) %copy-start) | copy-done | bytes 2097176
  16.4 0.0 copy-start.2
  16.4 0.7 %copy-done.2 = f32[2,1,4,4]{3,2,1,0:T(4,128)S(1)} copy-done((f32[2,1,4,4]{3,2,1,0:T(4,128)S(1)}, f32[2,1,4,4]{3,2,1,0:T(4,128)}, u32[]{:S(2)}) %copy-start.2) | copy-done | bytes 152
  17.1 0.0 copy-start.1
  17.1 1.0 %shard_map.59 = (bf16[1024,512]{1,0:T(8,128)(2,1)S(1)}, bf16[1024,512]{1,0:T(8,128)(2,1)S(1)}, f32[2,1,4,128,128]{4,3,2,1,0:T(8,128)S(1)}) custom-call(f32[2,4,512,128]{3,2,1,0:T(8,128)S(1)} %copy-done, f32[2,1,4,4]{3,2,1,0:T(4,128)S(1)} %copy-done.2), custom_call_target="tpu_custom_call" | custom-call | flops 2097152 | bytes 4194304 | tf_op jit(solution)/shard_map/pallas_call | solution.py:82
  18.1 1.4 %collective-permute-done.x_ref = f32[2,2,128,128]{3,2,1,0:T(8,128)S(1)} collective-permute-done((f32[2,2,128,128]{3,2,1,0:T(8,128)}, f32[2,2,128,128]{3,2,1,0:T(8,128)S(1)}, u32[]{:S(2)}, u32[]{:S(2)}) %collective-permute-start) | collective-permute-done | bytes 262176 | tf_op jit(solution)/shard_map/ppermute | solution.py:235
  19.5 0.1 collective-permute-done.1.refs_0_
  19.7 0.1 collective-permute-start.11
  19.8 1.5 %collective-permute-start.2 = (f32[2,2,128,128]{3,2,1,0:T(8,128)S(1)}, f32[2,2,128,128]{3,2,1,0:T(8,128)S(1)}, u32[]{:S(2)}, u32[]{:S(2)}) collective-permute-start(f32[2,2,128,128]{3,2,1,0:T(8,128)S(1)} %shard_map.61.refs_2_.refs_0_), channel_id=1, source_target_pairs={{0,1},{1,0},{2,3},{3,2},{4,5},{5,4},{6,7},{7,6},{8,9},{9,8},{10,11... | collective-permute-start | bytes 786440 | tf_op jit(solution)/shard_map/ppermute | solution.py:235
  21.3 0.2 collective-permute-start.8
  21.4 1.0 %collective-permute-done.8.refs_8_ = f32[8,128]{1,0:T(8,128)S(1)} collective-permute-done((f32[8,128]{1,0:T(8,128)S(1)}, f32[8,128]{1,0:T(8,128)S(1)}, u32[]{:S(2)}, u32[]{:S(2)}) %collective-permute-start.8) | collective-permute-done | bytes 4128 | tf_op jit(solution)/shard_map/ppermute | solution.py:235
  22.4 0.0 collective-permute-done.6.refs_3_.refs_5_
  22.4 0.0 collective-permute-done.7.refs_4_.refs_6_
  22.4 0.0 copy-done.1
  22.4 0.5 %shard_map.67 = (f32[2,1,128,128]{3,2,1,0:T(8,128)S(1)}, f32[2,1,128,128]{3,2,1,0:T(8,128)S(1)}) custom-call(f32[2,2,128,128]{3,2,1,0:T(8,128)S(1)} %copy-done.1, f32[2,2,128,128]{3,2,1,0:T(8,128)S(1)} %collective-permute-done.3.block_ref.refs_1_.refs_3_, f32[2,2,128,128]{3,2,1,0:T(8,128)S(1)} %collective-permute-done.4.block_ref.refs_2_.refs_4_, ...), custom_call_target="tpu_custom_call" | custom-call | flops 2097152 | bytes 4194304 | tf_op jit(solution)/shard_map/pallas_call | solution.py:226
  22.9 0.2 collective-permute-start.9
  23.2 1.2 %collective-permute-done.9.refs_1_ = f32[2,1,128,128]{3,2,1,0:T(8,128)S(1)} collective-permute-done((f32[2,1,128,128]{3,2,1,0:T(8,128)S(1)}, f32[2,1,128,128]{3,2,1,0:T(8,128)S(1)}, u32[]{:S(2)}, u32[]{:S(2)}) %collective-permute-start.9) | collective-permute-done | bytes 131104 | tf_op jit(solution)/shard_map/ppermute | solution.py:235
  24.4 2.2 %collective-permute-start.15 = (f32[2,1,128,128]{3,2,1,0:T(8,128)S(1)}, f32[2,1,128,128]{3,2,1,0:T(8,128)S(1)}, u32[]{:S(2)}, u32[]{:S(2)}) collective-permute-start(f32[2,1,128,128]{3,2,1,0:T(8,128)S(1)} %shard_map.68.refs_9_.refs_0_), channel_id=1, source_target_pairs={{0,3},{1,2},{2,1},{3,0},{4,7},{5,6},{6,5},{7,4},{8,11},{9,10},{10,... | collective-permute-start | bytes 393224 | tf_op jit(solution)/shard_map/ppermute | solution.py:235
  26.5 0.8 %collective-permute-start.10 = (f32[2,1,128,128]{3,2,1,0:T(8,128)S(1)}, f32[2,1,128,128]{3,2,1,0:T(8,128)S(1)}, u32[]{:S(2)}, u32[]{:S(2)}) collective-permute-start(f32[2,1,128,128]{3,2,1,0:T(8,128)S(1)} %shard_map.68.refs_9_.refs_0_), channel_id=1, source_target_pairs={{0,1},{1,0},{2,3},{3,2},{4,5},{5,4},{6,7},{7,6},{8,9},{9,8},{10,11... | collective-permute-start | bytes 393224 | tf_op jit(solution)/shard_map/ppermute | solution.py:235
  27.4 0.0 collective-permute-done.11.refs_1_
  27.4 0.5 %shard_map.69 = (f32[2,1,128,128]{3,2,1,0:T(8,128)S(1)}, f32[2,1,128,128]{3,2,1,0:T(8,128)S(1)}, f32[2,1,128,128]{3,2,1,0:T(8,128)S(1)}, f32[2,1,128,128]{3,2,1,0:T(8,128)S(1)}) custom-call(f32[2,2,128,128]{3,2,1,0:T(8,128)S(1)} %shard_map.61.refs_2_.refs_0_, f32[2,2,128,128]{3,2,1,0:T(8,128)S(1)} %collective-permute-done.11.refs_1_, ...), custom_call_target="tpu_custom_call" | custom-call | flops 2097152 | bytes 4194304 | tf_op jit(solution)/shard_map/pallas_call | solution.py:226
  27.8 0.6 %collective-permute-start.12 = (f32[2,1,128,128]{3,2,1,0:T(8,128)S(1)}, f32[2,1,128,128]{3,2,1,0:T(8,128)S(1)}, u32[]{:S(2)}, u32[]{:S(2)}) collective-permute-start(f32[2,1,128,128]{3,2,1,0:T(8,128)S(1)} %get-tuple-element.22), channel_id=1, source_target_pairs={{0,8},{4,12},{8,0},{12,4},{16,24},{20,28},{24,16},{28,20},{1,9},{5... | collective-permute-start | bytes 393224 | tf_op jit(solution)/shard_map/ppermute | solution.py:235
  28.4 0.5 %collective-permute-start.13 = (f32[2,1,128,128]{3,2,1,0:T(8,128)S(1)}, f32[2,1,128,128]{3,2,1,0:T(8,128)S(1)}, u32[]{:S(2)}, u32[]{:S(2)}) collective-permute-start(f32[2,1,128,128]{3,2,1,0:T(8,128)S(1)} %get-tuple-element.23), channel_id=1, source_target_pairs={{0,16},{4,20},{8,24},{12,28},{16,0},{20,4},{24,8},{28,12},{1,17},{... | collective-permute-start | bytes 393224 | tf_op jit(solution)/shard_map/ppermute | solution.py:235
  28.9 0.0 collective-permute-done.2.refs_0_
  28.9 2.4 %collective-permute-start.14 = (f32[2,1,128,128]{3,2,1,0:T(8,128)S(1)}, f32[2,1,128,128]{3,2,1,0:T(8,128)S(1)}, u32[]{:S(2)}, u32[]{:S(2)}) collective-permute-start(f32[2,1,128,128]{3,2,1,0:T(8,128)S(1)} %get-tuple-element.24), channel_id=1, source_target_pairs={{0,24},{4,28},{8,16},{12,20},{16,8},{20,12},{24,0},{28,4},{1,25},{... | collective-permute-start | bytes 393224 | tf_op jit(solution)/shard_map/ppermute | solution.py:235
  31.4 1.9 %shard_map.62 = (f32[2,2,4,128,128]{4,3,2,1,0:T(8,128)S(1)}, f32[8,128]{1,0:T(8,128)}) custom-call(f32[2,2,128,128]{3,2,1,0:T(8,128)S(1)} %collective-permute-done.1.refs_0_, f32[2,2,128,128]{3,2,1,0:T(8,128)S(1)} %copy-done.1, f32[2,2,128,128]{3,2,1,0:T(8,128)S(1)} %shard_map.61.refs_2_.refs_0_, ...), custom_call_target="tpu_custom_call" | custom-call | flops 1207959552 | bytes 4194304 | tf_op jit(solution)/shard_map/pallas_call | solution.py:173
  33.3 1.5 %shard_map.63 = (f32[2,2,4,128,128]{4,3,2,1,0:T(8,128)}, f32[8,128]{1,0:T(8,128)}) custom-call(f32[2,2,128,128]{3,2,1,0:T(8,128)S(1)} %collective-permute-done.2.refs_0_, bf16[1024,512]{1,0:T(8,128)(2,1)S(1)} %get-tuple-element.15.refs_0_.refs_3_.refs_1_.refs_6_, bf16[1024,512]{1,0:T(8,128)(2,1)S(1)} %get-tuple-element.16.refs_4_.refs_2_.refs_7_, ...), custom_call_target="tpu_custom_call" | custom-call | flops 402653184 | bytes 4194304 | tf_op jit(solution)/shard_map/pallas_call | solution.py:173
  34.8 0.0 collective-permute-done.12.refs_2_
  34.8 1.2 %collective-permute-done.13.refs_3_ = f32[2,1,128,128]{3,2,1,0:T(8,128)S(1)} collective-permute-done((f32[2,1,128,128]{3,2,1,0:T(8,128)S(1)}, f32[2,1,128,128]{3,2,1,0:T(8,128)S(1)}, u32[]{:S(2)}, u32[]{:S(2)}) %collective-permute-start.13) | collective-permute-done | bytes 131104 | tf_op jit(solution)/shard_map/ppermute | solution.py:235
  36.0 0.0 collective-permute-done.14.refs_4_
  36.0 0.0 collective-permute-done.15.refs_5_
  36.0 1.2 %shard_map.70 = (f32[2,1,4,128,128]{4,3,2,1,0:T(8,128)S(1)}, f32[8,128]{1,0:T(8,128)}) custom-call(f32[2,1,128,128]{3,2,1,0:T(8,128)S(1)} %shard_map.68.refs_9_.refs_0_, f32[2,1,128,128]{3,2,1,0:T(8,128)S(1)} %get-tuple-element.21.refs_1_, f32[2,1,128,128]{3,2,1,0:T(8,128)S(1)} %collective-permute-done.12.refs_2_, ...), custom_call_target="tpu_custom_call" | custom-call | flops 603979776 | bytes 4194304 | tf_op jit(solution)/shard_map/pallas_call | solution.py:173
  37.2 0.0 collective-permute-done.10.refs_0_
  37.2 1.2 %shard_map.71 = (f32[2,1,4,128,128]{4,3,2,1,0:T(8,128)}, f32[8,128]{1,0:T(8,128)}) custom-call(f32[2,1,128,128]{3,2,1,0:T(8,128)S(1)} %collective-permute-done.10.refs_0_, bf16[1024,512]{1,0:T(8,128)(2,1)S(1)} %get-tuple-element.15.refs_0_.refs_3_.refs_1_.refs_6_, bf16[1024,512]{1,0:T(8,128)(2,1)S(1)} %get-tuple-element.16.refs_4_.refs_2_.refs_7_, ...), custom_call_target="tpu_custom_call" | custom-call | flops 201326592 | bytes 4194304 | tf_op jit(solution)/shard_map/pallas_call | solution.py:173
  (6 shorter events, 0.1 us)
Async XLA Ops:
  0.6 13.0 %collective-permute-start.3 = (f32[2,2,128,128]{3,2,1,0:T(8,128)}, f32[2,2,128,128]{3,2,1,0:T(8,128)S(1)}, u32[]{:S(2)}, u32[]{:S(2)}) collective-permute-start(f32[2,2,128,128]{3,2,1,0:T(8,128)} %refs_2_.1), channel_id=1, source_target_pairs={{0,8},{4,12},{8,0},{12,4},{16,24},{20,28},{24,16},{28,20},{1,9},{5... | collective-permute-start | bytes 786440 | tf_op jit(solution)/shard_map/ppermute | solution.py:235
  3.6 10.6 %collective-permute-start.4 = (f32[2,2,128,128]{3,2,1,0:T(8,128)}, f32[2,2,128,128]{3,2,1,0:T(8,128)S(1)}, u32[]{:S(2)}, u32[]{:S(2)}) collective-permute-start(f32[2,2,128,128]{3,2,1,0:T(8,128)} %refs_2_.1), channel_id=1, source_target_pairs={{0,16},{4,20},{8,24},{12,28},{16,0},{20,4},{24,8},{28,12},{1,17},{... | collective-permute-start | bytes 786440 | tf_op jit(solution)/shard_map/ppermute | solution.py:235
  5.2 14.3 %collective-permute-start = (f32[2,2,128,128]{3,2,1,0:T(8,128)}, f32[2,2,128,128]{3,2,1,0:T(8,128)S(1)}, u32[]{:S(2)}, u32[]{:S(2)}) collective-permute-start(f32[2,2,128,128]{3,2,1,0:T(8,128)} %refs_2_.1), channel_id=1, source_target_pairs={{0,2},{1,3},{2,0},{3,1},{4,6},{5,7},{6,4},{7,5},{8,10},{9,11},{10,... | collective-permute-start | bytes 786440 | tf_op jit(solution)/shard_map/ppermute | solution.py:235
  7.7 11.9 %collective-permute-start.1 = (f32[2,2,128,128]{3,2,1,0:T(8,128)}, f32[2,2,128,128]{3,2,1,0:T(8,128)S(1)}, u32[]{:S(2)}, u32[]{:S(2)}) collective-permute-start(f32[2,2,128,128]{3,2,1,0:T(8,128)} %refs_2_.1), channel_id=1, source_target_pairs={{0,1},{1,0},{2,3},{3,2},{4,5},{5,4},{6,7},{7,6},{8,9},{9,8},{10,11... | collective-permute-start | bytes 786440 | tf_op jit(solution)/shard_map/ppermute | solution.py:235
  9.3 0.7 %copy-start.3 = (f32[2,1,16]{2,1,0:T(1,128)S(1)}, f32[2,1,16]{2,1,0:T(1,128)}, u32[]{:S(2)}) copy-start(f32[2,1,16]{2,1,0:T(1,128)} %integrals_ref.1) | copy-start | bytes 388
  10.0 3.6 %collective-permute-start.5 = (f32[8,128]{1,0:T(8,128)S(1)}, f32[8,128]{1,0:T(8,128)S(1)}, u32[]{:S(2)}, u32[]{:S(2)}) collective-permute-start(f32[8,128]{1,0:T(8,128)S(1)} %shard_map.64.refs_0_.refs_5_.refs_7_), channel_id=1, source_target_pairs={{0,8},{4,12},{8,0},{12,4},{16,24},{20,28},{24,16},{28,20},{1,9},{5... | collective-permute-start | bytes 12296 | tf_op jit(solution)/shard_map/ppermute | solution.py:235
  13.6 8.8 %collective-permute-start.6 = (f32[2,1,136,128]{3,2,1,0:T(8,128)S(1)}, f32[2,1,136,128]{3,2,1,0:T(8,128)S(1)}, u32[]{:S(2)}, u32[]{:S(2)}) collective-permute-start(f32[2,1,136,128]{3,2,1,0:T(8,128)S(1)} %shard_map.65), channel_id=1, source_target_pairs={{0,16},{4,20},{8,24},{12,28},{16,0},{20,4},{24,8},{28,12},{1,17},{... | collective-permute-start | bytes 417800 | tf_op jit(solution)/shard_map/ppermute | solution.py:235
  14.2 8.2 %collective-permute-start.7 = (f32[2,1,136,128]{3,2,1,0:T(8,128)S(1)}, f32[2,1,136,128]{3,2,1,0:T(8,128)S(1)}, u32[]{:S(2)}, u32[]{:S(2)}) collective-permute-start(f32[2,1,136,128]{3,2,1,0:T(8,128)S(1)} %shard_map.66), channel_id=1, source_target_pairs={{0,8},{4,12},{8,0},{12,4},{16,24},{20,28},{24,16},{28,20},{1,9},{5... | collective-permute-start | bytes 417800 | tf_op jit(solution)/shard_map/ppermute | solution.py:235
  14.8 1.6 %copy-start = (f32[2,4,512,128]{3,2,1,0:T(8,128)S(1)}, f32[2,4,512,128]{3,2,1,0:T(8,128)}, u32[]{:S(2)}) copy-start(f32[2,4,512,128]{3,2,1,0:T(8,128)} %basis_hbm.1) | copy-start | bytes 6291460
  16.4 0.7 %copy-start.2 = (f32[2,1,4,4]{3,2,1,0:T(4,128)S(1)}, f32[2,1,4,4]{3,2,1,0:T(4,128)}, u32[]{:S(2)}) copy-start(f32[2,1,4,4]{3,2,1,0:T(4,128)} %site_hbm.1) | copy-start | bytes 388
  17.1 5.3 %copy-start.1 = (f32[2,2,128,128]{3,2,1,0:T(8,128)S(1)}, f32[2,2,128,128]{3,2,1,0:T(8,128)}, u32[]{:S(2)}) copy-start(f32[2,2,128,128]{3,2,1,0:T(8,128)} %refs_2_.1) | copy-start | bytes 786436
  19.7 7.7 %collective-permute-start.11 = (f32[2,2,128,128]{3,2,1,0:T(8,128)S(1)}, f32[2,2,128,128]{3,2,1,0:T(8,128)S(1)}, u32[]{:S(2)}, u32[]{:S(2)}) collective-permute-start(f32[2,2,128,128]{3,2,1,0:T(8,128)S(1)} %shard_map.61.refs_2_.refs_0_), channel_id=1, source_target_pairs={{0,4},{4,0},{8,12},{12,8},{16,20},{20,16},{24,28},{28,24},{1,5},{5... | collective-permute-start | bytes 786440 | tf_op jit(solution)/shard_map/ppermute | solution.py:235
  19.8 9.2 %collective-permute-start.2 = (f32[2,2,128,128]{3,2,1,0:T(8,128)S(1)}, f32[2,2,128,128]{3,2,1,0:T(8,128)S(1)}, u32[]{:S(2)}, u32[]{:S(2)}) collective-permute-start(f32[2,2,128,128]{3,2,1,0:T(8,128)S(1)} %shard_map.61.refs_2_.refs_0_), channel_id=1, source_target_pairs={{0,1},{1,0},{2,3},{3,2},{4,5},{5,4},{6,7},{7,6},{8,9},{9,8},{10,11... | collective-permute-start | bytes 786440 | tf_op jit(solution)/shard_map/ppermute | solution.py:235
  21.3 1.2 %collective-permute-start.8 = (f32[8,128]{1,0:T(8,128)S(1)}, f32[8,128]{1,0:T(8,128)S(1)}, u32[]{:S(2)}, u32[]{:S(2)}) collective-permute-start(f32[8,128]{1,0:T(8,128)S(1)} %shard_map.64.refs_0_.refs_5_.refs_7_), channel_id=1, source_target_pairs={{0,4},{4,0},{8,12},{12,8},{16,20},{20,16},{24,28},{28,24},{1,5},{5... | collective-permute-start | bytes 12296 | tf_op jit(solution)/shard_map/ppermute | solution.py:235
  22.9 1.4 %collective-permute-start.9 = (f32[2,1,128,128]{3,2,1,0:T(8,128)S(1)}, f32[2,1,128,128]{3,2,1,0:T(8,128)S(1)}, u32[]{:S(2)}, u32[]{:S(2)}) collective-permute-start(f32[2,1,128,128]{3,2,1,0:T(8,128)S(1)} %get-tuple-element.20), channel_id=1, source_target_pairs={{0,4},{4,0},{8,12},{12,8},{16,20},{20,16},{24,28},{28,24},{1,5},{5... | collective-permute-start | bytes 393224 | tf_op jit(solution)/shard_map/ppermute | solution.py:235
  24.4 11.7 %collective-permute-start.15 = (f32[2,1,128,128]{3,2,1,0:T(8,128)S(1)}, f32[2,1,128,128]{3,2,1,0:T(8,128)S(1)}, u32[]{:S(2)}, u32[]{:S(2)}) collective-permute-start(f32[2,1,128,128]{3,2,1,0:T(8,128)S(1)} %shard_map.68.refs_9_.refs_0_), channel_id=1, source_target_pairs={{0,3},{1,2},{2,1},{3,0},{4,7},{5,6},{6,5},{7,4},{8,11},{9,10},{10,... | collective-permute-start | bytes 393224 | tf_op jit(solution)/shard_map/ppermute | solution.py:235
  26.5 10.7 %collective-permute-start.10 = (f32[2,1,128,128]{3,2,1,0:T(8,128)S(1)}, f32[2,1,128,128]{3,2,1,0:T(8,128)S(1)}, u32[]{:S(2)}, u32[]{:S(2)}) collective-permute-start(f32[2,1,128,128]{3,2,1,0:T(8,128)S(1)} %shard_map.68.refs_9_.refs_0_), channel_id=1, source_target_pairs={{0,1},{1,0},{2,3},{3,2},{4,5},{5,4},{6,7},{7,6},{8,9},{9,8},{10,11... | collective-permute-start | bytes 393224 | tf_op jit(solution)/shard_map/ppermute | solution.py:235
  27.8 7.0 %collective-permute-start.12 = (f32[2,1,128,128]{3,2,1,0:T(8,128)S(1)}, f32[2,1,128,128]{3,2,1,0:T(8,128)S(1)}, u32[]{:S(2)}, u32[]{:S(2)}) collective-permute-start(f32[2,1,128,128]{3,2,1,0:T(8,128)S(1)} %get-tuple-element.22), channel_id=1, source_target_pairs={{0,8},{4,12},{8,0},{12,4},{16,24},{20,28},{24,16},{28,20},{1,9},{5... | collective-permute-start | bytes 393224 | tf_op jit(solution)/shard_map/ppermute | solution.py:235
  28.4 7.6 %collective-permute-start.13 = (f32[2,1,128,128]{3,2,1,0:T(8,128)S(1)}, f32[2,1,128,128]{3,2,1,0:T(8,128)S(1)}, u32[]{:S(2)}, u32[]{:S(2)}) collective-permute-start(f32[2,1,128,128]{3,2,1,0:T(8,128)S(1)} %get-tuple-element.23), channel_id=1, source_target_pairs={{0,16},{4,20},{8,24},{12,28},{16,0},{20,4},{24,8},{28,12},{1,17},{... | collective-permute-start | bytes 393224 | tf_op jit(solution)/shard_map/ppermute | solution.py:235
  28.9 7.1 %collective-permute-start.14 = (f32[2,1,128,128]{3,2,1,0:T(8,128)S(1)}, f32[2,1,128,128]{3,2,1,0:T(8,128)S(1)}, u32[]{:S(2)}, u32[]{:S(2)}) collective-permute-start(f32[2,1,128,128]{3,2,1,0:T(8,128)S(1)} %get-tuple-element.24), channel_id=1, source_target_pairs={{0,24},{4,28},{8,16},{12,20},{16,8},{20,12},{24,0},{28,4},{1,25},{... | collective-permute-start | bytes 393224 | tf_op jit(solution)/shard_map/ppermute | solution.py:235

commit v2 on v1

--- a/solution.py
+++ b/solution.py
@@ -36,7 +36,7 @@
     return (1, 0) + tuple(range(2, sec))
 
 
-def prepare_kernel(depth, basis_hbm, site_hbm, high_ref, low_ref, part_ref, *scratch):
+def prepare_kernel(depth, basis_hbm, site_hbm, _, high_ref, low_ref, part_ref, *scratch):
     basis_ref, site_ref, basis_sem, site_sem = scratch
     _, sites, old, cols = basis_ref.shape
     rows = part_ref.shape[3]
@@ -74,7 +74,7 @@
             part_ref[1, comp, site] = imag
 
 
-def prepare(basis, site_terms, rows, depth):
+def prepare(basis, site_terms, rows, depth, awaited):
     _, sites, old, cols = basis.shape
     comps = site_terms.shape[1]
     half = jax.ShapeDtypeStruct((2 * old, sites * cols), jnp.bfloat16)
@@ -82,7 +82,7 @@
     return call(
         functools.partial(prepare_kernel, depth),
         (half, half, part),
-        [HBM, HBM],
+        [HBM, HBM, ANY],
         8 * comps * sites * sites * rows * cols,
         [
             pltpu.VMEM(basis.shape, basis.dtype),
@@ -90,7 +90,7 @@
             pltpu.SemaphoreType.DMA((2, sites)),
             pltpu.SemaphoreType.DMA,
         ],
-    )(basis, site_terms)
+    )(basis, site_terms, awaited)
 
 
 def tile(integrals):
@@ -126,11 +126,11 @@
     return call(kernel, out, [VMEM] + [ANY] * len(others), 0)(x, *others)
 
 
-def renorm_kernel(steps, parts, carried, *refs):
+def renorm_kernel(steps, parts, carried, streamed, *refs):
     count = sum(parts)
     high_ref, low_ref = refs[count : count + 2]
-    out_ref, token_ref, left_high, left_low = refs[-4:]
-    token_ref[...] = jnp.zeros(TILE, jnp.float32)
+    out_ref, left_high, left_low = refs[count + 2 + carried : count + 5 + carried]
+    out_hbm, out_ref, sems = (out_ref,) + refs[-2:] if streamed else (None, out_ref, None)
     _, ops, sites, rows, cols = out_ref.shape
     depth = refs[0].shape[-1]
     tall = ops * rows
@@ -146,23 +146,35 @@
             scratch[tall:, at + depth : at + 2 * depth] = real
     dot = functools.partial(jnp.dot, preferred_element_type=jnp.float32)
     deep = slice(2 * depth * steps[0], 2 * depth * (steps[-1] + 1))
+    copies = []
     for first in range(0, sites * cols, WIDE):
         at = (deep, slice(first, first + WIDE))
         total = dot(left_high[...], high_ref[at])
         total = total + dot(left_high[...], low_ref[at])
         total = total + dot(left_low[...], high_ref[at])
-        for site in range(first // cols, (first + WIDE) // cols):
-            across = slice(site * cols - first, site * cols - first + cols)
-            for part in range(2):
-                for op in range(ops):
+        some = range(first // cols, (first + WIDE) // cols)
+        for part in range(2):
+            for op in range(ops):
+                for site in some:
+                    across = slice(site * cols - first, site * cols - first + cols)
                     start = part * tall + op * rows
                     value = total[start : start + rows, across]
                     if carried:
                         value = value + refs[count + 2][part, op, site]
                     out_ref[part, op, site] = value
-
-
-def renorm(blocks, steps, high, low, carry, shape):
+                if streamed:
+                    piece = (part, op, pl.ds(some.start, len(some)))
+                    copies.append(
+                        pltpu.make_async_copy(
+                            out_ref.at[piece], out_hbm.at[piece], sems.at[len(copies)]
+                        )
+                    )
+                    copies[-1].start()
+    for copy in copies:
+        copy.wait()
+
+
+def renorm(blocks, steps, high, low, carry, shape, streamed=False):
     blocks = [block if isinstance(block, tuple) else (block,) for block in blocks]
     blocks = blocks[steps.start : steps.stop]
     parts = tuple(len(block) for block in blocks)
@@ -170,12 +182,14 @@
     _, ops, sites, rows, cols = shape
     depth = blocks[0][0].shape[-1]
     left = pltpu.VMEM((2 * ops * rows, 2 * depth * len(blocks)), jnp.bfloat16)
+    pieces = 2 * ops * sites * cols // WIDE
+    held = [pltpu.VMEM(shape, jnp.float32), pltpu.SemaphoreType.DMA((pieces,))]
     return pl.pallas_call(
-        functools.partial(renorm_kernel, steps, parts, carry is not None),
-        out_shape=tuple(jax.ShapeDtypeStruct(dims, jnp.float32) for dims in (shape, TILE)),
+        functools.partial(renorm_kernel, steps, parts, carry is not None, streamed),
+        out_shape=jax.ShapeDtypeStruct(shape, jnp.float32),
         in_specs=[VMEM] * len(args),
-        out_specs=(VMEM, VMEM),
-        scratch_shapes=[left, left],
+        out_specs=HBM if streamed else VMEM,
+        scratch_shapes=[left, left] + (held if streamed else []),
         cost_estimate=pl.CostEstimate(
             flops=24 * ops * rows * depth * len(blocks) * sites * cols,
             bytes_accessed=4 << 20,
@@ -239,19 +253,18 @@
     per = own.shape[1]
     arrays, tables = [own], []
     operators = [(0, op, op, 0) for op in range(per)]
-    if pairs == 8 and per == 2:
+    if pairs == 8:
         for key in (2, 4):
             operators += [(len(arrays), op, op, key) for op in range(per)]
             arrays.append(swap(own, "pair", pairs, key))
         beside = swap(row, "pair", pairs, 2)
-        operators += [(3, 0, 0, 6), (4, 0, 1, 6)]
+        operators += [(3, op, op, 6) for op in range(per)]
         arrays += [
-            swap(pack(arrays[1], range(1), [row, beside]), "pair", pairs, 4),
-            swap(pack(arrays[2], range(1, 2), []), "pair", pairs, 2),
+            swap(pack(arrays[1], range(per), [row, beside]), "pair", pairs, 4),
             row,
             beside,
         ]
-        tables = [(5, None), (6, None), (3, 0), (3, 1)]
+        tables = [(4, None), (5, None), (3, 0), (3, 1)]
     else:
         arrays[0] = pack(own, range(per), [row])
         tables = [(0, 0)]
@@ -271,30 +284,31 @@
     one = swap(normal_ops, "sec", sec, 1)
     row = tile(integrals)
     arrays, operators, tables = chip_blocks(normal_ops, row, pairs)
-    high, low, site_part = prepare(basis, site_terms, rows, depth)
-    two = after(after(two, high), one)
+    sibling = swap(row, "pair", pairs, 1)
+    high, low, site_part = prepare(basis, site_terms, rows, depth, sibling)
+    two = after(after(after(two, high), arrays[2]), one)
     three = swap(two, "sec", sec, 1)
     normals = [one, normal_ops, two, three]
-    held = arrays + [row, swap(row, "pair", pairs, 1)]
+    held = arrays + [row, sibling]
     here = [(len(arrays), None), (len(arrays) + 1, None)]
     mine, other = combine(held, operators, here, norms, shape)
-    comp_ops = total([mine, swap(other, "pair", pairs, 1)], [two])
-    far = swap(comp_ops, "sec", sec, 3)
-    near = swap(comp_ops, "sec", sec, 1)
     held = [two, swap(two, "pair", pairs, 1)] + arrays
     operators = [(key, op, op, key) for key in range(2) for op in range(norms)]
     tables = [(2 + at, part) for at, part in tables]
-    parts = combine(held, operators, tables, norms, shape, [comp_ops])
+    parts = combine(held, operators, tables, norms, shape)
+    comp_ops = total([mine, swap(other, "pair", pairs, 1)], [parts[0]])
+    far = swap(comp_ops, "sec", sec, 3)
+    near = swap(after(comp_ops, three), "sec", sec, 1)
     summed = [parts[0]] + [
         swap(part, "pair", pairs, key) for part, key in zip(parts[1:], range(2, pairs, 2))
     ]
     shape = (2, norms, sites, rows, cols)
-    early, _ = renorm(normals, range(sec - 1), high, low, None, shape)
-    new_normal, _ = renorm(normals, range(sec - 1, sec), high, low, early, shape)
+    early = renorm(normals, range(sec - 1), high, low, None, shape)
+    new_normal = renorm(normals, range(sec - 1, sec), high, low, early, shape, True)
     shape = (2, comps, sites, rows, cols)
     arrived = [near, comp_ops, tuple(summed), far]
-    early, _ = renorm(arrived, range(1, sec), high, low, site_part, shape)
-    return new_normal, renorm(arrived, range(1), high, low, early, shape)[0]
+    early = renorm(arrived, range(1, sec), high, low, site_part, shape)
+    return new_normal, renorm(arrived, range(1), high, low, early, shape, True)
 
 
 def solution(mesh):

time: 38.6 us -> 36.3 us (0.940)
  starting transfers between devices: 18.9 us -> 16.6 us
  Pallas kernels: 7.77 us -> 6.84 us
  waiting for transfers between devices: 8.05 us -> 8.96 us
    ppermute x16 -> x15, starting transfers between devices: 18.9 us -> 16.6 us  [swap(): return lax.ppermute(x, axis, [(at, at ^ key) for at in range(size)])]
    pallas_call x4, Pallas kernels: 5.8 us -> 4.84 us  [renorm(): pl.pallas_call(functools.partial(renorm_kernel, steps, parts, carry is no...]
    ppermute x16 -> x15, waiting for transfers between devices: 8.05 us -> 8.96 us  [swap(): return lax.ppermute(x, axis, [(at, at ^ key) for at in range(size)])]
  transfers between devices with their start and end apart: 16 -> 15, of which waited for: 6 -> 8; matrix products, arithmetic and copies ran while one was open for 0% -> 0% of each run, Pallas kernels for 17% -> 16%
where the time goes in v2:
time: 36.3 us; the launch traced here: 36.1 us
  starting transfers between devices  16.6 us (46%)
  waiting for transfers between devices  8.96 us (25%)
  Pallas kernels  6.84 us (19%)
  local copies, waits for them, and re-layouts  2.96 us (8%)
  between operations  0.77 us (2%)
    ppermute x15, starting transfers between devices, swap(): return lax.ppermute(x, axis, [(at, at ^ key) for at in range(size)])  16.6 us
    ppermute x15, waiting for transfers between devices, swap(): return lax.ppermute(x, axis, [(at, at ^ key) for at in range(size)])  8.96 us
    pallas_call x4, Pallas kernels, renorm(): pl.pallas_call(functools.partial(renorm_kernel, steps, parts, carry is no...  4.84 us
    unnamed x8, local copies, waits for them, and re-layouts  2.96 us
    pallas_call x1, Pallas kernels, prepare(): call(functools.partial(prepare_kernel, depth), (half, half, part), [HBM,...  0.97 us
    pallas_call x2, Pallas kernels, combine(): call(functools.partial(combine_kernel, operators, tables, per), (jax.Shap...  0.92 us
  transfers between devices with their start and end apart: 15, of which 8 were waited for; matrix products, arithmetic and copies ran while one was open for 0% of the time, Pallas kernels for 16%

profile of v2, /device:TPU:0, one launch (start us, length us, event | category | flops | bytes accessed | tf_op | source)
XLA Modules:
  0.0 36.1 jit_solution(3416027905953458159)
XLA Ops:
  0.6 3.0 %collective-permute-start.5 = (f32[2,2,128,128]{3,2,1,0:T(8,128)}, f32[2,2,128,128]{3,2,1,0:T(8,128)S(1)}, u32[]{:S(2)}, u32[]{:S(2)}) collective-permute-start(f32[2,2,128,128]{3,2,1,0:T(8,128)} %refs_2_.1), channel_id=1, source_target_pairs={{0,8},{4,12},{8,0},{12,4},{16,24},{20,28},{24,16},{28,20},{1,9},{5... | collective-permute-start | bytes 786440 | tf_op jit(solution)/shard_map/ppermute | solution.py:249
  3.6 2.6 %collective-permute-start = (f32[2,2,128,128]{3,2,1,0:T(8,128)}, f32[2,2,128,128]{3,2,1,0:T(8,128)S(1)}, u32[]{:S(2)}, u32[]{:S(2)}) collective-permute-start(f32[2,2,128,128]{3,2,1,0:T(8,128)} %refs_2_.1), channel_id=1, source_target_pairs={{0,2},{1,3},{2,0},{3,1},{4,6},{5,7},{6,4},{7,5},{8,10},{9,11},{10,... | collective-permute-start | bytes 786440 | tf_op jit(solution)/shard_map/ppermute | solution.py:249
  6.2 1.5 %collective-permute-start.2 = (f32[2,2,128,128]{3,2,1,0:T(8,128)}, f32[2,2,128,128]{3,2,1,0:T(8,128)S(1)}, u32[]{:S(2)}, u32[]{:S(2)}) collective-permute-start(f32[2,2,128,128]{3,2,1,0:T(8,128)} %refs_2_.1), channel_id=1, source_target_pairs={{0,16},{4,20},{8,24},{12,28},{16,0},{20,4},{24,8},{28,12},{1,17},{... | collective-permute-start | bytes 786440 | tf_op jit(solution)/shard_map/ppermute | solution.py:249
  7.7 1.6 %collective-permute-start.3 = (f32[2,2,128,128]{3,2,1,0:T(8,128)}, f32[2,2,128,128]{3,2,1,0:T(8,128)S(1)}, u32[]{:S(2)}, u32[]{:S(2)}) collective-permute-start(f32[2,2,128,128]{3,2,1,0:T(8,128)} %refs_2_.1), channel_id=1, source_target_pairs={{0,1},{1,0},{2,3},{3,2},{4,5},{5,4},{6,7},{7,6},{8,9},{9,8},{10,11... | collective-permute-start | bytes 786440 | tf_op jit(solution)/shard_map/ppermute | solution.py:249
  9.3 0.0 copy-start.3
  9.3 0.7 %copy-done.3 = f32[2,1,16]{2,1,0:T(1,128)S(1)} copy-done((f32[2,1,16]{2,1,0:T(1,128)S(1)}, f32[2,1,16]{2,1,0:T(1,128)}, u32[]{:S(2)}) %copy-start.3) | copy-done | bytes 152
  10.0 0.5 %collective-permute-start.6 = (f32[8,128]{1,0:T(8,128)S(1)}, f32[8,128]{1,0:T(8,128)S(1)}, u32[]{:S(2)}, u32[]{:S(2)}) collective-permute-start(f32[8,128]{1,0:T(8,128)S(1)} %shard_map.59.refs_0_.refs_4_.refs_6_), channel_id=1, source_target_pairs={{0,8},{4,12},{8,0},{12,4},{16,24},{20,28},{24,16},{28,20},{1,9},{5... | collective-permute-start | bytes 12296 | tf_op jit(solution)/shard_map/ppermute | solution.py:249
  10.5 3.1 %collective-permute-done.6.refs_1_.refs_5_.refs_7_ = f32[8,128]{1,0:T(8,128)S(1)} collective-permute-done((f32[8,128]{1,0:T(8,128)S(1)}, f32[8,128]{1,0:T(8,128)S(1)}, u32[]{:S(2)}, u32[]{:S(2)}) %collective-permute-start.6) | collective-permute-done | bytes 4128 | tf_op jit(solution)/shard_map/ppermute | solution.py:249
  13.6 0.0 collective-permute-done.5.block_ref.refs_1_.refs_3_
  13.6 0.6 %collective-permute-start.7 = (f32[2,2,136,128]{3,2,1,0:T(8,128)S(1)}, f32[2,2,136,128]{3,2,1,0:T(8,128)S(1)}, u32[]{:S(2)}, u32[]{:S(2)}) collective-permute-start(f32[2,2,136,128]{3,2,1,0:T(8,128)S(1)} %shard_map.66), channel_id=1, source_target_pairs={{0,16},{4,20},{8,24},{12,28},{16,0},{20,4},{24,8},{28,12},{1,17},{... | collective-permute-start | bytes 835592 | tf_op jit(solution)/shard_map/ppermute | solution.py:249
  14.2 0.0 collective-permute-start.1
  14.2 1.2 %collective-permute-done.1._.refs_7_ = f32[8,128]{1,0:T(8,128)S(1)} collective-permute-done((f32[8,128]{1,0:T(8,128)S(1)}, f32[8,128]{1,0:T(8,128)S(1)}, u32[]{:S(2)}, u32[]{:S(2)}) %collective-permute-start.1) | collective-permute-done | bytes 4128 | tf_op jit(solution)/shard_map/ppermute | solution.py:249
  15.4 0.0 copy-start
  15.4 1.6 %copy-done = f32[2,4,512,128]{3,2,1,0:T(8,128)S(1)} copy-done((f32[2,4,512,128]{3,2,1,0:T(8,128)S(1)}, f32[2,4,512,128]{3,2,1,0:T(8,128)}, u32[]{:S(2)}) %copy-start) | copy-done | bytes 2097176
  17.0 0.0 copy-start.2
  17.0 0.7 %copy-done.2 = f32[2,1,4,4]{3,2,1,0:T(4,128)S(1)} copy-done((f32[2,1,4,4]{3,2,1,0:T(4,128)S(1)}, f32[2,1,4,4]{3,2,1,0:T(4,128)}, u32[]{:S(2)}) %copy-start.2) | copy-done | bytes 152
  17.7 1.0 %shard_map.60 = (bf16[1024,512]{1,0:T(8,128)(2,1)S(1)}, bf16[1024,512]{1,0:T(8,128)(2,1)S(1)}, f32[2,1,4,128,128]{4,3,2,1,0:T(8,128)S(1)}) custom-call(f32[2,4,512,128]{3,2,1,0:T(8,128)S(1)} %copy-done, f32[2,1,4,4]{3,2,1,0:T(4,128)S(1)} %copy-done.2, f32[8,128]{1,0:T(8,128)S(1)} %collective-permute-done.1._.refs_7_), custom_call_target="tpu_custom_call" | custom-call | flops 2097152 | bytes 4194304 | tf_op jit(solution)/shard_map/pallas_call | solution.py:82
  18.6 0.0 copy-start.1
  18.6 0.0 collective-permute-done.x_ref
  18.7 0.0 collective-permute-done.2.refs_0_.refs_2_.refs_4_
  18.7 0.9 %collective-permute-done.3.refs_0_ = f32[2,2,128,128]{3,2,1,0:T(8,128)S(1)} collective-permute-done((f32[2,2,128,128]{3,2,1,0:T(8,128)}, f32[2,2,128,128]{3,2,1,0:T(8,128)S(1)}, u32[]{:S(2)}, u32[]{:S(2)}) %collective-permute-start.3) | collective-permute-done | bytes 262176 | tf_op jit(solution)/shard_map/ppermute | solution.py:249
  19.7 0.1 collective-permute-start.9
  19.8 0.3 collective-permute-start.4
  20.0 0.2 collective-permute-done.7.refs_3_.refs_5_
  20.3 0.0 copy-done.1
  20.3 0.5 %shard_map.67 = (f32[2,1,128,128]{3,2,1,0:T(8,128)S(1)}, f32[2,1,128,128]{3,2,1,0:T(8,128)S(1)}) custom-call(f32[2,2,128,128]{3,2,1,0:T(8,128)S(1)} %copy-done.1, f32[2,2,128,128]{3,2,1,0:T(8,128)S(1)} %collective-permute-done.5.block_ref.refs_1_.refs_3_, f32[2,2,128,128]{3,2,1,0:T(8,128)S(1)} %collective-permute-done.2.refs_0_.refs_2_.refs_4_, ...), custom_call_target="tpu_custom_call" | custom-call | flops 2097152 | bytes 4194304 | tf_op jit(solution)/shard_map/pallas_call | solution.py:240
  20.7 0.1 collective-permute-start.8
  20.8 0.5 %collective-permute-done.9.refs_1_ = f32[2,2,128,128]{3,2,1,0:T(8,128)S(1)} collective-permute-done((f32[2,2,128,128]{3,2,1,0:T(8,128)S(1)}, f32[2,2,128,128]{3,2,1,0:T(8,128)S(1)}, u32[]{:S(2)}, u32[]{:S(2)}) %collective-permute-start.9) | collective-permute-done | bytes 262176 | tf_op jit(solution)/shard_map/ppermute | solution.py:249
  21.3 0.4 %shard_map.68 = (f32[2,1,128,128]{3,2,1,0:T(8,128)S(1)}, f32[2,1,128,128]{3,2,1,0:T(8,128)S(1)}, f32[2,1,128,128]{3,2,1,0:T(8,128)S(1)}, f32[2,1,128,128]{3,2,1,0:T(8,128)S(1)}) custom-call(f32[2,2,128,128]{3,2,1,0:T(8,128)S(1)} %shard_map.63.refs_2_.refs_0_, f32[2,2,128,128]{3,2,1,0:T(8,128)S(1)} %collective-permute-done.9.refs_1_, ...), custom_call_target="tpu_custom_call" | custom-call | flops 2097152 | bytes 4194304 | tf_op jit(solution)/shard_map/pallas_call | solution.py:240
  21.7 0.6 %collective-permute-start.11 = (f32[2,1,128,128]{3,2,1,0:T(8,128)S(1)}, f32[2,1,128,128]{3,2,1,0:T(8,128)S(1)}, u32[]{:S(2)}, u32[]{:S(2)}) collective-permute-start(f32[2,1,128,128]{3,2,1,0:T(8,128)S(1)} %get-tuple-element.16), channel_id=1, source_target_pairs={{0,8},{4,12},{8,0},{12,4},{16,24},{20,28},{24,16},{28,20},{1,9},{5... | collective-permute-start | bytes 393224 | tf_op jit(solution)/shard_map/ppermute | solution.py:249
  22.3 1.0 %collective-permute-start.12 = (f32[2,1,128,128]{3,2,1,0:T(8,128)S(1)}, f32[2,1,128,128]{3,2,1,0:T(8,128)S(1)}, u32[]{:S(2)}, u32[]{:S(2)}) collective-permute-start(f32[2,1,128,128]{3,2,1,0:T(8,128)S(1)} %get-tuple-element.17), channel_id=1, source_target_pairs={{0,16},{4,20},{8,24},{12,28},{16,0},{20,4},{24,8},{28,12},{1,17},{... | collective-permute-start | bytes 393224 | tf_op jit(solution)/shard_map/ppermute | solution.py:249
  23.3 2.0 %collective-permute-start.13 = (f32[2,1,128,128]{3,2,1,0:T(8,128)S(1)}, f32[2,1,128,128]{3,2,1,0:T(8,128)S(1)}, u32[]{:S(2)}, u32[]{:S(2)}) collective-permute-start(f32[2,1,128,128]{3,2,1,0:T(8,128)S(1)} %get-tuple-element.18), channel_id=1, source_target_pairs={{0,24},{4,28},{8,16},{12,20},{16,8},{20,12},{24,0},{28,4},{1,25},{... | collective-permute-start | bytes 393224 | tf_op jit(solution)/shard_map/ppermute | solution.py:249
  25.3 0.0 collective-permute-done.8.refs_1_
  25.3 2.5 %collective-permute-start.14 = (f32[2,1,128,128]{3,2,1,0:T(8,128)S(1)}, f32[2,1,128,128]{3,2,1,0:T(8,128)S(1)}, u32[]{:S(2)}, u32[]{:S(2)}) collective-permute-start(f32[2,1,128,128]{3,2,1,0:T(8,128)S(1)} %shard_map.69.x_ref.refs_0_), channel_id=1, source_target_pairs={{0,3},{1,2},{2,1},{3,0},{4,7},{5,6},{6,5},{7,4},{8,11},{9,10},{10,... | collective-permute-start | bytes 393224 | tf_op jit(solution)/shard_map/ppermute | solution.py:249
  27.8 0.7 %collective-permute-done.4.refs_0_ = f32[2,2,128,128]{3,2,1,0:T(8,128)S(1)} collective-permute-done((f32[2,2,128,128]{3,2,1,0:T(8,128)S(1)}, f32[2,2,128,128]{3,2,1,0:T(8,128)S(1)}, u32[]{:S(2)}, u32[]{:S(2)}) %collective-permute-start.4) | collective-permute-done | bytes 262176 | tf_op jit(solution)/shard_map/ppermute | solution.py:249
  28.5 0.3 collective-permute-start.10
  28.8 1.4 %shard_map.64.refs_3_ = f32[2,2,4,128,128]{4,3,2,1,0:T(8,128)S(1)} custom-call(f32[2,2,128,128]{3,2,1,0:T(8,128)S(1)} %collective-permute-done.3.refs_0_, f32[2,2,128,128]{3,2,1,0:T(8,128)S(1)} %copy-done.1, f32[2,2,128,128]{3,2,1,0:T(8,128)S(1)} %shard_map.63.refs_2_.refs_0_, bf16[1024,512]{1,0:T(8,128)(2,1)S(1)} %get-tuple-element.11.refs_0_.refs_3_.refs_1_.refs_6_, ...), custom_call_target="tpu_custom_call" | custom-call | flops 1207959552 | bytes 4194304 | tf_op jit(solution)/shard_map/pallas_call | solution.py:187
  30.2 1.5 %shard_map.65 = f32[2,2,4,128,128]{4,3,2,1,0:T(8,128)} custom-call(f32[2,2,128,128]{3,2,1,0:T(8,128)S(1)} %collective-permute-done.4.refs_0_, bf16[1024,512]{1,0:T(8,128)(2,1)S(1)} %get-tuple-element.11.refs_0_.refs_3_.refs_1_.refs_6_, bf16[1024,512]{1,0:T(8,128)(2,1)S(1)} %get-tuple-element.12.refs_4_.refs_2_.refs_7_, ...), custom_call_target="tpu_custom_call" | custom-call | flops 402653184 | bytes 4194304 | tf_op jit(solution)/shard_map/pallas_call | solution.py:187
  31.7 0.0 collective-permute-done.11.refs_2_
  31.7 0.0 collective-permute-done.12.refs_3_
  31.8 0.0 collective-permute-done.13.refs_4_
  31.8 0.9 %collective-permute-done.14.refs_5_ = f32[2,1,128,128]{3,2,1,0:T(8,128)S(1)} collective-permute-done((f32[2,1,128,128]{3,2,1,0:T(8,128)S(1)}, f32[2,1,128,128]{3,2,1,0:T(8,128)S(1)}, u32[]{:S(2)}, u32[]{:S(2)}) %collective-permute-start.14) | collective-permute-done | bytes 131104 | tf_op jit(solution)/shard_map/ppermute | solution.py:249
  32.6 0.8 %shard_map.71.refs_3_ = f32[2,1,4,128,128]{4,3,2,1,0:T(8,128)S(1)} custom-call(f32[2,1,128,128]{3,2,1,0:T(8,128)S(1)} %shard_map.69.x_ref.refs_0_, f32[2,1,128,128]{3,2,1,0:T(8,128)S(1)} %get-tuple-element.15.refs_2_.refs_1_, f32[2,1,128,128]{3,2,1,0:T(8,128)S(1)} %collective-permute-done.11.refs_2_, f32[2,1,128,128]{3,2,1,0:T(8,128)S(1)} %collective-permute-done.12.refs_3_, ...), custom_call_target="tpu_custom_call" | custom-call | flops 603979776 | bytes 4194304 | tf_op jit(solution)/shard_map/pallas_call | solution.py:187
  33.4 1.5 %collective-permute-done.10.refs_0_ = f32[2,1,128,128]{3,2,1,0:T(8,128)S(1)} collective-permute-done((f32[2,1,128,128]{3,2,1,0:T(8,128)S(1)}, f32[2,1,128,128]{3,2,1,0:T(8,128)S(1)}, u32[]{:S(2)}, u32[]{:S(2)}) %collective-permute-start.10) | collective-permute-done | bytes 131104 | tf_op jit(solution)/shard_map/ppermute | solution.py:249
  35.0 1.2 %shard_map.72 = f32[2,1,4,128,128]{4,3,2,1,0:T(8,128)} custom-call(f32[2,1,128,128]{3,2,1,0:T(8,128)S(1)} %collective-permute-done.10.refs_0_, bf16[1024,512]{1,0:T(8,128)(2,1)S(1)} %get-tuple-element.11.refs_0_.refs_3_.refs_1_.refs_6_, bf16[1024,512]{1,0:T(8,128)(2,1)S(1)} %get-tuple-element.12.refs_4_.refs_2_.refs_7_, ...), custom_call_target="tpu_custom_call" | custom-call | flops 201326592 | bytes 4194304 | tf_op jit(solution)/shard_map/pallas_call | solution.py:187
  (7 shorter events, 0.1 us)
Async XLA Ops:
  0.6 13.0 %collective-permute-start.5 = (f32[2,2,128,128]{3,2,1,0:T(8,128)}, f32[2,2,128,128]{3,2,1,0:T(8,128)S(1)}, u32[]{:S(2)}, u32[]{:S(2)}) collective-permute-start(f32[2,2,128,128]{3,2,1,0:T(8,128)} %refs_2_.1), channel_id=1, source_target_pairs={{0,8},{4,12},{8,0},{12,4},{16,24},{20,28},{24,16},{28,20},{1,9},{5... | collective-permute-start | bytes 786440 | tf_op jit(solution)/shard_map/ppermute | solution.py:249
  3.6 15.0 %collective-permute-start = (f32[2,2,128,128]{3,2,1,0:T(8,128)}, f32[2,2,128,128]{3,2,1,0:T(8,128)S(1)}, u32[]{:S(2)}, u32[]{:S(2)}) collective-permute-start(f32[2,2,128,128]{3,2,1,0:T(8,128)} %refs_2_.1), channel_id=1, source_target_pairs={{0,2},{1,3},{2,0},{3,1},{4,6},{5,7},{6,4},{7,5},{8,10},{9,11},{10,... | collective-permute-start | bytes 786440 | tf_op jit(solution)/shard_map/ppermute | solution.py:249
  6.2 12.5 %collective-permute-start.2 = (f32[2,2,128,128]{3,2,1,0:T(8,128)}, f32[2,2,128,128]{3,2,1,0:T(8,128)S(1)}, u32[]{:S(2)}, u32[]{:S(2)}) collective-permute-start(f32[2,2,128,128]{3,2,1,0:T(8,128)} %refs_2_.1), channel_id=1, source_target_pairs={{0,16},{4,20},{8,24},{12,28},{16,0},{20,4},{24,8},{28,12},{1,17},{... | collective-permute-start | bytes 786440 | tf_op jit(solution)/shard_map/ppermute | solution.py:249
  7.7 11.9 %collective-permute-start.3 = (f32[2,2,128,128]{3,2,1,0:T(8,128)}, f32[2,2,128,128]{3,2,1,0:T(8,128)S(1)}, u32[]{:S(2)}, u32[]{:S(2)}) collective-permute-start(f32[2,2,128,128]{3,2,1,0:T(8,128)} %refs_2_.1), channel_id=1, source_target_pairs={{0,1},{1,0},{2,3},{3,2},{4,5},{5,4},{6,7},{7,6},{8,9},{9,8},{10,11... | collective-permute-start | bytes 786440 | tf_op jit(solution)/shard_map/ppermute | solution.py:249
  9.3 0.7 %copy-start.3 = (f32[2,1,16]{2,1,0:T(1,128)S(1)}, f32[2,1,16]{2,1,0:T(1,128)}, u32[]{:S(2)}) copy-start(f32[2,1,16]{2,1,0:T(1,128)} %integrals_ref.1) | copy-start | bytes 388
  10.0 3.6 %collective-permute-start.6 = (f32[8,128]{1,0:T(8,128)S(1)}, f32[8,128]{1,0:T(8,128)S(1)}, u32[]{:S(2)}, u32[]{:S(2)}) collective-permute-start(f32[8,128]{1,0:T(8,128)S(1)} %shard_map.59.refs_0_.refs_4_.refs_6_), channel_id=1, source_target_pairs={{0,8},{4,12},{8,0},{12,4},{16,24},{20,28},{24,16},{28,20},{1,9},{5... | collective-permute-start | bytes 12296 | tf_op jit(solution)/shard_map/ppermute | solution.py:249
  13.6 6.6 %collective-permute-start.7 = (f32[2,2,136,128]{3,2,1,0:T(8,128)S(1)}, f32[2,2,136,128]{3,2,1,0:T(8,128)S(1)}, u32[]{:S(2)}, u32[]{:S(2)}) collective-permute-start(f32[2,2,136,128]{3,2,1,0:T(8,128)S(1)} %shard_map.66), channel_id=1, source_target_pairs={{0,16},{4,20},{8,24},{12,28},{16,0},{20,4},{24,8},{28,12},{1,17},{... | collective-permute-start | bytes 835592 | tf_op jit(solution)/shard_map/ppermute | solution.py:249
  14.2 1.2 %collective-permute-start.1 = (f32[8,128]{1,0:T(8,128)S(1)}, f32[8,128]{1,0:T(8,128)S(1)}, u32[]{:S(2)}, u32[]{:S(2)}) collective-permute-start(f32[8,128]{1,0:T(8,128)S(1)} %shard_map.59.refs_0_.refs_4_.refs_6_), channel_id=1, source_target_pairs={{0,4},{4,0},{8,12},{12,8},{16,20},{20,16},{24,28},{28,24},{1,5},{5... | collective-permute-start | bytes 12296 | tf_op jit(solution)/shard_map/ppermute | solution.py:249
  15.4 1.6 %copy-start = (f32[2,4,512,128]{3,2,1,0:T(8,128)S(1)}, f32[2,4,512,128]{3,2,1,0:T(8,128)}, u32[]{:S(2)}) copy-start(f32[2,4,512,128]{3,2,1,0:T(8,128)} %basis_hbm.1) | copy-start | bytes 6291460
  17.0 0.7 %copy-start.2 = (f32[2,1,4,4]{3,2,1,0:T(4,128)S(1)}, f32[2,1,4,4]{3,2,1,0:T(4,128)}, u32[]{:S(2)}) copy-start(f32[2,1,4,4]{3,2,1,0:T(4,128)} %site_hbm.1) | copy-start | bytes 388
  18.6 1.6 %copy-start.1 = (f32[2,2,128,128]{3,2,1,0:T(8,128)S(1)}, f32[2,2,128,128]{3,2,1,0:T(8,128)}, u32[]{:S(2)}) copy-start(f32[2,2,128,128]{3,2,1,0:T(8,128)} %refs_2_.1) | copy-start | bytes 786436
  19.7 1.6 %collective-permute-start.9 = (f32[2,2,128,128]{3,2,1,0:T(8,128)S(1)}, f32[2,2,128,128]{3,2,1,0:T(8,128)S(1)}, u32[]{:S(2)}, u32[]{:S(2)}) collective-permute-start(f32[2,2,128,128]{3,2,1,0:T(8,128)S(1)} %shard_map.63.refs_2_.refs_0_), channel_id=1, source_target_pairs={{0,4},{4,0},{8,12},{12,8},{16,20},{20,16},{24,28},{28,24},{1,5},{5... | collective-permute-start | bytes 786440 | tf_op jit(solution)/shard_map/ppermute | solution.py:249
  19.8 8.7 %collective-permute-start.4 = (f32[2,2,128,128]{3,2,1,0:T(8,128)S(1)}, f32[2,2,128,128]{3,2,1,0:T(8,128)S(1)}, u32[]{:S(2)}, u32[]{:S(2)}) collective-permute-start(f32[2,2,128,128]{3,2,1,0:T(8,128)S(1)} %shard_map.63.refs_2_.refs_0_), channel_id=1, source_target_pairs={{0,1},{1,0},{2,3},{3,2},{4,5},{5,4},{6,7},{7,6},{8,9},{9,8},{10,11... | collective-permute-start | bytes 786440 | tf_op jit(solution)/shard_map/ppermute | solution.py:249
  20.7 4.6 %collective-permute-start.8 = (f32[2,1,128,128]{3,2,1,0:T(8,128)S(1)}, f32[2,1,128,128]{3,2,1,0:T(8,128)S(1)}, u32[]{:S(2)}, u32[]{:S(2)}) collective-permute-start(f32[2,1,128,128]{3,2,1,0:T(8,128)S(1)} %get-tuple-element.14), channel_id=1, source_target_pairs={{0,4},{4,0},{8,12},{12,8},{16,20},{20,16},{24,28},{28,24},{1,5},{5... | collective-permute-start | bytes 393224 | tf_op jit(solution)/shard_map/ppermute | solution.py:249
  21.7 10.0 %collective-permute-start.11 = (f32[2,1,128,128]{3,2,1,0:T(8,128)S(1)}, f32[2,1,128,128]{3,2,1,0:T(8,128)S(1)}, u32[]{:S(2)}, u32[]{:S(2)}) collective-permute-start(f32[2,1,128,128]{3,2,1,0:T(8,128)S(1)} %get-tuple-element.16), channel_id=1, source_target_pairs={{0,8},{4,12},{8,0},{12,4},{16,24},{20,28},{24,16},{28,20},{1,9},{5... | collective-permute-start | bytes 393224 | tf_op jit(solution)/shard_map/ppermute | solution.py:249
  22.3 9.4 %collective-permute-start.12 = (f32[2,1,128,128]{3,2,1,0:T(8,128)S(1)}, f32[2,1,128,128]{3,2,1,0:T(8,128)S(1)}, u32[]{:S(2)}, u32[]{:S(2)}) collective-permute-start(f32[2,1,128,128]{3,2,1,0:T(8,128)S(1)} %get-tuple-element.17), channel_id=1, source_target_pairs={{0,16},{4,20},{8,24},{12,28},{16,0},{20,4},{24,8},{28,12},{1,17},{... | collective-permute-start | bytes 393224 | tf_op jit(solution)/shard_map/ppermute | solution.py:249
  23.3 8.4 %collective-permute-start.13 = (f32[2,1,128,128]{3,2,1,0:T(8,128)S(1)}, f32[2,1,128,128]{3,2,1,0:T(8,128)S(1)}, u32[]{:S(2)}, u32[]{:S(2)}) collective-permute-start(f32[2,1,128,128]{3,2,1,0:T(8,128)S(1)} %get-tuple-element.18), channel_id=1, source_target_pairs={{0,24},{4,28},{8,16},{12,20},{16,8},{20,12},{24,0},{28,4},{1,25},{... | collective-permute-start | bytes 393224 | tf_op jit(solution)/shard_map/ppermute | solution.py:249
  25.3 7.3 %collective-permute-start.14 = (f32[2,1,128,128]{3,2,1,0:T(8,128)S(1)}, f32[2,1,128,128]{3,2,1,0:T(8,128)S(1)}, u32[]{:S(2)}, u32[]{:S(2)}) collective-permute-start(f32[2,1,128,128]{3,2,1,0:T(8,128)S(1)} %shard_map.69.x_ref.refs_0_), channel_id=1, source_target_pairs={{0,3},{1,2},{2,1},{3,0},{4,7},{5,6},{6,5},{7,4},{8,11},{9,10},{10,... | collective-permute-start | bytes 393224 | tf_op jit(solution)/shard_map/ppermute | solution.py:249
  28.5 6.5 %collective-permute-start.10 = (f32[2,1,128,128]{3,2,1,0:T(8,128)S(1)}, f32[2,1,128,128]{3,2,1,0:T(8,128)S(1)}, u32[]{:S(2)}, u32[]{:S(2)}) collective-permute-start(f32[2,1,128,128]{3,2,1,0:T(8,128)S(1)} %shard_map.70), channel_id=1, source_target_pairs={{0,1},{1,0},{2,3},{3,2},{4,5},{5,4},{6,7},{7,6},{8,9},{9,8},{10,11... | collective-permute-start | bytes 393224 | tf_op jit(solution)/shard_map/ppermute | solution.py:249

commit v3 on v2

--- a/solution.py
+++ b/solution.py
@@ -33,7 +33,7 @@
 
 
 def order(sec):
-    return (1, 0) + tuple(range(2, sec))
+    return (1, 2, 0) + tuple(range(3, sec))
 
 
 def prepare_kernel(depth, basis_hbm, site_hbm, _, high_ref, low_ref, part_ref, *scratch):
@@ -93,29 +93,21 @@
     )(basis, site_terms, awaited)
 
 
-def tile(integrals):
-    _, comps, norms = integrals.shape
-
-    def kernel(integrals_ref, out_ref):
-        out_ref[...] = jnp.zeros(TILE, jnp.float32)
-        for part in range(2):
-            out_ref[part * comps : (part + 1) * comps, :norms] = integrals_ref[part]
-
-    return call(kernel, jax.ShapeDtypeStruct(TILE, jnp.float32), [VMEM], 0)(integrals)
-
-
-def pack(block, ops, tiles):
-    _, _, rows, cols = block.shape
+def pack(block, tables):
+    _, per, rows, cols = block.shape
 
     def kernel(block_ref, *refs):
         out_ref = refs[-1]
-        out_ref[:, :, :rows, :] = block_ref[:, ops.start : ops.stop]
-        out_ref[:, :, rows:, :] = jnp.zeros((2, len(ops)) + TILE, jnp.float32)
-        for part, ref in enumerate(refs[:-1]):
-            out_ref[part, 0, rows:, :] = ref[...]
-
-    out = jax.ShapeDtypeStruct((2, len(ops), rows + TILE[0], cols), block.dtype)
-    return call(kernel, out, [VMEM] * (1 + len(tiles)), 0)(block, *tiles)
+        out_ref[:, :, :rows, :] = block_ref[...]
+        out_ref[:, :, rows:, :] = jnp.zeros((2, per) + TILE, jnp.float32)
+        for under, ref in enumerate(refs[:-1]):
+            _, comps, norms = ref.shape
+            for part in range(2):
+                first = rows + part * comps
+                out_ref[under, 0, first : first + comps, :norms] = ref[part]
+
+    out = jax.ShapeDtypeStruct((2, per, rows + TILE[0], cols), block.dtype)
+    return call(kernel, out, [VMEM] * (1 + len(tables)), 0)(block, *tables)
 
 
 def after(x, *others):
@@ -212,8 +204,8 @@
     outs = refs[len(refs) - len(tables) :]
     comps, rows, _ = outs[0].shape[1:]
     me = lax.axis_index("pair")
-    lane = lax.broadcasted_iota(jnp.int32, (1, TILE[1]), 1)
     for (held, under), out_ref in zip(tables, outs):
+        lane = lax.broadcasted_iota(jnp.int32, (1, refs[held].shape[-1]), 1)
         for comp in range(comps):
             real = imag = None
             for array, place, op, key in operators:
@@ -221,7 +213,7 @@
                 for part in range(2):
                     at = part * comps + comp
                     if under is None:
-                        row = refs[held][at : at + 1, :]
+                        row = refs[held][part, comp : comp + 1, :]
                     else:
                         row = refs[held][under, 0, rows + at : rows + at + 1, :]
                     here = jnp.where(lane == (me ^ key) * per + op, row, 0.0)
@@ -260,13 +252,13 @@
         beside = swap(row, "pair", pairs, 2)
         operators += [(3, op, op, 6) for op in range(per)]
         arrays += [
-            swap(pack(arrays[1], range(per), [row, beside]), "pair", pairs, 4),
+            swap(pack(arrays[1], [row, beside]), "pair", pairs, 4),
             row,
             beside,
         ]
         tables = [(4, None), (5, None), (3, 0), (3, 1)]
     else:
-        arrays[0] = pack(own, range(per), [row])
+        arrays[0] = pack(own, [row])
         tables = [(0, 0)]
         for key in range(2, pairs, 2):
             operators += [(len(arrays), op, op, key) for op in range(per)]
@@ -282,14 +274,14 @@
     shape = (2, comps, rows, depth)
     two = swap(normal_ops, "sec", sec, 2)
     one = swap(normal_ops, "sec", sec, 1)
-    row = tile(integrals)
-    arrays, operators, tables = chip_blocks(normal_ops, row, pairs)
-    sibling = swap(row, "pair", pairs, 1)
+    arrays, operators, tables = chip_blocks(normal_ops, integrals, pairs)
+    sibling = swap(integrals, "pair", pairs, 1)
     high, low, site_part = prepare(basis, site_terms, rows, depth, sibling)
-    two = after(after(after(two, high), arrays[2]), one)
+    two = after(two, high)
     three = swap(two, "sec", sec, 1)
-    normals = [one, normal_ops, two, three]
-    held = arrays + [row, sibling]
+    two = after(after(two, arrays[2]), one)
+    normals = [one, two, normal_ops, three]
+    held = arrays + [integrals, sibling]
     here = [(len(arrays), None), (len(arrays) + 1, None)]
     mine, other = combine(held, operators, here, norms, shape)
     held = [two, swap(two, "pair", pairs, 1)] + arrays
@@ -300,14 +292,16 @@
     far = swap(comp_ops, "sec", sec, 3)
     near = swap(after(comp_ops, three), "sec", sec, 1)
     summed = [parts[0]] + [
-        swap(part, "pair", pairs, key) for part, key in zip(parts[1:], range(2, pairs, 2))
+        swap(after(part, comp_ops), "pair", pairs, key)
+        for part, key in zip(parts[1:], range(2, pairs, 2))
     ]
     shape = (2, norms, sites, rows, cols)
     early = renorm(normals, range(sec - 1), high, low, None, shape)
     new_normal = renorm(normals, range(sec - 1, sec), high, low, early, shape, True)
     shape = (2, comps, sites, rows, cols)
-    arrived = [near, comp_ops, tuple(summed), far]
-    early = renorm(arrived, range(1, sec), high, low, site_part, shape)
+    arrived = [near, tuple(summed), comp_ops, far]
+    early = renorm(arrived, range(2, sec), high, low, site_part, shape)
+    early = renorm(arrived, range(1, 2), high, low, early, shape)
     return new_normal, renorm(arrived, range(1), high, low, early, shape, True)
 
 

time: 36.3 us -> 36.1 us (level)
  waiting for transfers between devices: 8.96 us -> 8.52 us
    ppermute x15, waiting for transfers between devices: 8.96 us -> 8.52 us  [swap(): return lax.ppermute(x, axis, [(at, at ^ key) for at in range(size)])]
    pallas_call x4 -> x5, Pallas kernels: 4.84 us -> 5.04 us  [renorm(): pl.pallas_call(functools.partial(renorm_kernel, steps, parts, carry is no...]
    unnamed x8 -> x10, local copies, waits for them, and re-layouts: 2.96 us -> 2.97 us
  transfers between devices with their start and end apart: 15 -> 15, of which waited for: 8 -> 9; matrix products, arithmetic and copies ran while one was open for 0% -> 0% of each run, Pallas kernels for 16% -> 16%
where the time goes in v3:
time: 36.1 us; the launch traced here: 35.9 us
  starting transfers between devices  16.6 us (46%)
  waiting for transfers between devices  8.52 us (24%)
  Pallas kernels  7.06 us (20%)
  local copies, waits for them, and re-layouts  2.97 us (8%)
  between operations  0.79 us (2%)
    ppermute x15, starting transfers between devices, swap(): return lax.ppermute(x, axis, [(at, at ^ key) for at in range(size)])  16.6 us
    ppermute x15, waiting for transfers between devices, swap(): return lax.ppermute(x, axis, [(at, at ^ key) for at in range(size)])  8.52 us
    pallas_call x5, Pallas kernels, renorm(): pl.pallas_call(functools.partial(renorm_kernel, steps, parts, carry is no...  5.04 us
    unnamed x10, local copies, waits for them, and re-layouts  2.97 us
    pallas_call x1, Pallas kernels, prepare(): call(functools.partial(prepare_kernel, depth), (half, half, part), [HBM,...  0.97 us
    pallas_call x2, Pallas kernels, combine(): call(functools.partial(combine_kernel, operators, tables, per), (jax.Shap...  0.92 us
  transfers between devices with their start and end apart: 15, of which 9 were waited for; matrix products, arithmetic and copies ran while one was open for 0% of the time, Pallas kernels for 16%

profile of v3, /device:TPU:0, one launch (start us, length us, event | category | flops | bytes accessed | tf_op | source)
XLA Modules:
  0.0 35.9 jit_solution(10816303640447289299)
XLA Ops:
  0.6 3.0 %collective-permute-start.5 = (f32[2,2,128,128]{3,2,1,0:T(8,128)}, f32[2,2,128,128]{3,2,1,0:T(8,128)S(1)}, u32[]{:S(2)}, u32[]{:S(2)}) collective-permute-start(f32[2,2,128,128]{3,2,1,0:T(8,128)} %refs_2_.3), channel_id=1, source_target_pairs={{0,8},{4,12},{8,0},{12,4},{16,24},{20,28},{24,16},{28,20},{1,9},{5... | collective-permute-start | bytes 786440 | tf_op jit(solution)/shard_map/ppermute | solution.py:241
  3.6 2.6 %collective-permute-start = (f32[2,2,128,128]{3,2,1,0:T(8,128)}, f32[2,2,128,128]{3,2,1,0:T(8,128)S(1)}, u32[]{:S(2)}, u32[]{:S(2)}) collective-permute-start(f32[2,2,128,128]{3,2,1,0:T(8,128)} %refs_2_.3), channel_id=1, source_target_pairs={{0,2},{1,3},{2,0},{3,1},{4,6},{5,7},{6,4},{7,5},{8,10},{9,11},{10,... | collective-permute-start | bytes 786440 | tf_op jit(solution)/shard_map/ppermute | solution.py:241
  6.2 1.5 %collective-permute-start.4 = (f32[2,2,128,128]{3,2,1,0:T(8,128)}, f32[2,2,128,128]{3,2,1,0:T(8,128)S(1)}, u32[]{:S(2)}, u32[]{:S(2)}) collective-permute-start(f32[2,2,128,128]{3,2,1,0:T(8,128)} %refs_2_.3), channel_id=1, source_target_pairs={{0,16},{4,20},{8,24},{12,28},{16,0},{20,4},{24,8},{28,12},{1,17},{... | collective-permute-start | bytes 786440 | tf_op jit(solution)/shard_map/ppermute | solution.py:241
  7.7 1.6 %collective-permute-start.3 = (f32[2,2,128,128]{3,2,1,0:T(8,128)}, f32[2,2,128,128]{3,2,1,0:T(8,128)S(1)}, u32[]{:S(2)}, u32[]{:S(2)}) collective-permute-start(f32[2,2,128,128]{3,2,1,0:T(8,128)} %refs_2_.3), channel_id=1, source_target_pairs={{0,1},{1,0},{2,3},{3,2},{4,5},{5,4},{6,7},{7,6},{8,9},{9,8},{10,11... | collective-permute-start | bytes 786440 | tf_op jit(solution)/shard_map/ppermute | solution.py:241
  9.3 0.5 %collective-permute-start.6 = (f32[2,1,16]{2,1,0:T(1,128)}, f32[2,1,16]{2,1,0:T(1,128)S(1)}, u32[]{:S(2)}, u32[]{:S(2)}) collective-permute-start(f32[2,1,16]{2,1,0:T(1,128)} %refs_6_.3), channel_id=1, source_target_pairs={{0,8},{4,12},{8,0},{12,4},{16,24},{20,28},{24,16},{28,20},{1,9},{5... | collective-permute-start | bytes 392 | tf_op jit(solution)/shard_map/ppermute | solution.py:241
  9.9 3.2 %collective-permute-done.6.refs_1_.refs_5_.refs_7_ = f32[2,1,16]{2,1,0:T(1,128)S(1)} collective-permute-done((f32[2,1,16]{2,1,0:T(1,128)}, f32[2,1,16]{2,1,0:T(1,128)S(1)}, u32[]{:S(2)}, u32[]{:S(2)}) %collective-permute-start.6) | collective-permute-done | bytes 160 | tf_op jit(solution)/shard_map/ppermute | solution.py:241
  13.1 0.0 collective-permute-done.5.block_ref.refs_1_.refs_3_
  13.1 0.0 copy-start.2
  13.1 0.7 %copy-done.2 = f32[2,1,16]{2,1,0:T(1,128)S(1)} copy-done((f32[2,1,16]{2,1,0:T(1,128)S(1)}, f32[2,1,16]{2,1,0:T(1,128)}, u32[]{:S(2)}) %copy-start.2) | copy-done | bytes 152
  13.8 0.6 %collective-permute-start.7 = (f32[2,2,136,128]{3,2,1,0:T(8,128)S(1)}, f32[2,2,136,128]{3,2,1,0:T(8,128)S(1)}, u32[]{:S(2)}, u32[]{:S(2)}) collective-permute-start(f32[2,2,136,128]{3,2,1,0:T(8,128)S(1)} %shard_map.65), channel_id=1, source_target_pairs={{0,16},{4,20},{8,24},{12,28},{16,0},{20,4},{24,8},{28,12},{1,17},{... | collective-permute-start | bytes 835592 | tf_op jit(solution)/shard_map/ppermute | solution.py:241
  14.4 0.0 collective-permute-start.1
  14.4 1.1 %collective-permute-done.1._.refs_7_ = f32[2,1,16]{2,1,0:T(1,128)S(1)} collective-permute-done((f32[2,1,16]{2,1,0:T(1,128)S(1)}, f32[2,1,16]{2,1,0:T(1,128)S(1)}, u32[]{:S(2)}, u32[]{:S(2)}) %collective-permute-start.1) | collective-permute-done | bytes 160 | tf_op jit(solution)/shard_map/ppermute | solution.py:241
  15.5 0.0 copy-start
  15.5 1.6 %copy-done = f32[2,4,512,128]{3,2,1,0:T(8,128)S(1)} copy-done((f32[2,4,512,128]{3,2,1,0:T(8,128)S(1)}, f32[2,4,512,128]{3,2,1,0:T(8,128)}, u32[]{:S(2)}) %copy-start) | copy-done | bytes 2097176
  17.1 0.0 copy-start.4
  17.1 0.7 %copy-done.4 = f32[2,1,4,4]{3,2,1,0:T(4,128)S(1)} copy-done((f32[2,1,4,4]{3,2,1,0:T(4,128)S(1)}, f32[2,1,4,4]{3,2,1,0:T(4,128)}, u32[]{:S(2)}) %copy-start.4) | copy-done | bytes 152
  17.8 1.0 %shard_map.59 = (bf16[1024,512]{1,0:T(8,128)(2,1)S(1)}, bf16[1024,512]{1,0:T(8,128)(2,1)S(1)}, f32[2,1,4,128,128]{4,3,2,1,0:T(8,128)S(1)}) custom-call(f32[2,4,512,128]{3,2,1,0:T(8,128)S(1)} %copy-done, f32[2,1,4,4]{3,2,1,0:T(4,128)S(1)} %copy-done.4, f32[2,1,16]{2,1,0:T(1,128)S(1)} %collective-permute-done.1._.refs_7_), custom_call_target="tpu_custom_call" | custom-call | flops 2097152 | bytes 4194304 | tf_op jit(solution)/shard_map/pallas_call | solution.py:82
  18.8 0.0 copy-start.1
  18.8 0.0 copy-start.3
  18.8 0.0 collective-permute-done.x_ref
  18.8 0.0 collective-permute-done.4.refs_0_.refs_2_.refs_4_
  18.9 0.8 %collective-permute-done.3.refs_0_ = f32[2,2,128,128]{3,2,1,0:T(8,128)S(1)} collective-permute-done((f32[2,2,128,128]{3,2,1,0:T(8,128)}, f32[2,2,128,128]{3,2,1,0:T(8,128)S(1)}, u32[]{:S(2)}, u32[]{:S(2)}) %collective-permute-start.3) | collective-permute-done | bytes 262176 | tf_op jit(solution)/shard_map/ppermute | solution.py:241
  19.7 0.1 collective-permute-start.9
  19.8 0.3 collective-permute-start.2
  20.0 0.4 %collective-permute-done.7.refs_3_.refs_5_ = f32[2,2,136,128]{3,2,1,0:T(8,128)S(1)} collective-permute-done((f32[2,2,136,128]{3,2,1,0:T(8,128)S(1)}, f32[2,2,136,128]{3,2,1,0:T(8,128)S(1)}, u32[]{:S(2)}, u32[]{:S(2)}) %collective-permute-start.7) | collective-permute-done | bytes 278560 | tf_op jit(solution)/shard_map/ppermute | solution.py:241
  20.4 0.0 copy-done.1
  20.4 0.0 copy-done.3
  20.4 0.5 %shard_map.66 = (f32[2,1,128,128]{3,2,1,0:T(8,128)S(1)}, f32[2,1,128,128]{3,2,1,0:T(8,128)S(1)}) custom-call(f32[2,2,128,128]{3,2,1,0:T(8,128)S(1)} %copy-done.1, f32[2,2,128,128]{3,2,1,0:T(8,128)S(1)} %collective-permute-done.5.block_ref.refs_1_.refs_3_, f32[2,2,128,128]{3,2,1,0:T(8,128)S(1)} %collective-permute-done.4.refs_0_.refs_2_.refs_4_, ...), custom_call_target="tpu_custom_call" | custom-call | flops 2097152 | bytes 4194304 | tf_op jit(solution)/shard_map/pallas_call | solution.py:232
  20.9 0.1 collective-permute-start.8
  21.0 0.3 collective-permute-done.9.refs_1_
  21.3 0.4 %shard_map.67 = (f32[2,1,128,128]{3,2,1,0:T(8,128)S(1)}, f32[2,1,128,128]{3,2,1,0:T(8,128)S(1)}, f32[2,1,128,128]{3,2,1,0:T(8,128)S(1)}, f32[2,1,128,128]{3,2,1,0:T(8,128)S(1)}) custom-call(f32[2,2,128,128]{3,2,1,0:T(8,128)S(1)} %shard_map.62.refs_1_.refs_0_, f32[2,2,128,128]{3,2,1,0:T(8,128)S(1)} %collective-permute-done.9.refs_1_, ...), custom_call_target="tpu_custom_call" | custom-call | flops 2097152 | bytes 4194304 | tf_op jit(solution)/shard_map/pallas_call | solution.py:232
  21.7 0.6 %collective-permute-done.8.refs_1_ = f32[2,1,128,128]{3,2,1,0:T(8,128)S(1)} collective-permute-done((f32[2,1,128,128]{3,2,1,0:T(8,128)S(1)}, f32[2,1,128,128]{3,2,1,0:T(8,128)S(1)}, u32[]{:S(2)}, u32[]{:S(2)}) %collective-permute-start.8) | collective-permute-done | bytes 131104 | tf_op jit(solution)/shard_map/ppermute | solution.py:241
  22.3 2.0 %collective-permute-start.14 = (f32[2,1,128,128]{3,2,1,0:T(8,128)S(1)}, f32[2,1,128,128]{3,2,1,0:T(8,128)S(1)}, u32[]{:S(2)}, u32[]{:S(2)}) collective-permute-start(f32[2,1,128,128]{3,2,1,0:T(8,128)S(1)} %shard_map.68.x_ref.refs_0_), channel_id=1, source_target_pairs={{0,3},{1,2},{2,1},{3,0},{4,7},{5,6},{6,5},{7,4},{8,11},{9,10},{10,... | collective-permute-start | bytes 393224 | tf_op jit(solution)/shard_map/ppermute | solution.py:241
  24.4 2.5 %collective-permute-start.13 = (f32[2,1,128,128]{3,2,1,0:T(8,128)S(1)}, f32[2,1,128,128]{3,2,1,0:T(8,128)S(1)}, u32[]{:S(2)}, u32[]{:S(2)}) collective-permute-start(f32[2,1,128,128]{3,2,1,0:T(8,128)S(1)} %shard_map.72), channel_id=1, source_target_pairs={{0,24},{4,28},{8,16},{12,20},{16,8},{20,12},{24,0},{28,4},{1,25},{... | collective-permute-start | bytes 393224 | tf_op jit(solution)/shard_map/ppermute | solution.py:241
  26.8 0.6 %collective-permute-start.12 = (f32[2,1,128,128]{3,2,1,0:T(8,128)S(1)}, f32[2,1,128,128]{3,2,1,0:T(8,128)S(1)}, u32[]{:S(2)}, u32[]{:S(2)}) collective-permute-start(f32[2,1,128,128]{3,2,1,0:T(8,128)S(1)} %shard_map.71), channel_id=1, source_target_pairs={{0,16},{4,20},{8,24},{12,28},{16,0},{20,4},{24,8},{28,12},{1,17},{... | collective-permute-start | bytes 393224 | tf_op jit(solution)/shard_map/ppermute | solution.py:241
  27.4 0.6 %collective-permute-start.11 = (f32[2,1,128,128]{3,2,1,0:T(8,128)S(1)}, f32[2,1,128,128]{3,2,1,0:T(8,128)S(1)}, u32[]{:S(2)}, u32[]{:S(2)}) collective-permute-start(f32[2,1,128,128]{3,2,1,0:T(8,128)S(1)} %shard_map.70), channel_id=1, source_target_pairs={{0,8},{4,12},{8,0},{12,4},{16,24},{20,28},{24,16},{28,20},{1,9},{5... | collective-permute-start | bytes 393224 | tf_op jit(solution)/shard_map/ppermute | solution.py:241
  28.1 0.4 %collective-permute-done.2.refs_0_ = f32[2,2,128,128]{3,2,1,0:T(8,128)S(1)} collective-permute-done((f32[2,2,128,128]{3,2,1,0:T(8,128)S(1)}, f32[2,2,128,128]{3,2,1,0:T(8,128)S(1)}, u32[]{:S(2)}, u32[]{:S(2)}) %collective-permute-start.2) | collective-permute-done | bytes 262176 | tf_op jit(solution)/shard_map/ppermute | solution.py:241
  28.5 0.7 %collective-permute-start.10 = (f32[2,1,128,128]{3,2,1,0:T(8,128)S(1)}, f32[2,1,128,128]{3,2,1,0:T(8,128)S(1)}, u32[]{:S(2)}, u32[]{:S(2)}) collective-permute-start(f32[2,1,128,128]{3,2,1,0:T(8,128)S(1)} %shard_map.69), channel_id=1, source_target_pairs={{0,1},{1,0},{2,3},{3,2},{4,5},{5,4},{6,7},{7,6},{8,9},{9,8},{10,11... | collective-permute-start | bytes 393224 | tf_op jit(solution)/shard_map/ppermute | solution.py:241
  29.2 1.4 %shard_map.63.refs_3_ = f32[2,2,4,128,128]{4,3,2,1,0:T(8,128)S(1)} custom-call(f32[2,2,128,128]{3,2,1,0:T(8,128)S(1)} %collective-permute-done.3.refs_0_, f32[2,2,128,128]{3,2,1,0:T(8,128)S(1)} %shard_map.62.refs_1_.refs_0_, f32[2,2,128,128]{3,2,1,0:T(8,128)S(1)} %copy-done.1, ...), custom_call_target="tpu_custom_call" | custom-call | flops 1207959552 | bytes 4194304 | tf_op jit(solution)/shard_map/pallas_call | solution.py:179
  30.6 1.5 %shard_map.64 = f32[2,2,4,128,128]{4,3,2,1,0:T(8,128)} custom-call(f32[2,2,128,128]{3,2,1,0:T(8,128)S(1)} %collective-permute-done.2.refs_0_, bf16[1024,512]{1,0:T(8,128)(2,1)S(1)} %get-tuple-element.11.refs_0_.refs_3_.refs_1_.refs_2_.refs_4_, bf16[1024,512]{1,0:T(8,128)(2,1)S(1)} %get-tuple-element.12.refs_4_.refs_2_.refs_3_.refs_5_, ...), custom_call_target="tpu_custom_call" | custom-call | flops 402653184 | bytes 4194304 | tf_op jit(solution)/shard_map/pallas_call | solution.py:179
  32.1 0.0 collective-permute-done.14.refs_1_
  32.1 0.6 %shard_map.73.refs_6_ = f32[2,1,4,128,128]{4,3,2,1,0:T(8,128)S(1)} custom-call(f32[2,1,128,128]{3,2,1,0:T(8,128)S(1)} %shard_map.68.x_ref.refs_0_, f32[2,1,128,128]{3,2,1,0:T(8,128)S(1)} %collective-permute-done.14.refs_1_, bf16[1024,512]{1,0:T(8,128)(2,1)S(1)} %get-tuple-element.11.refs_0_.refs_3_.refs_1_.refs_2_.refs_4_, ...), custom_call_target="tpu_custom_call" | custom-call | flops 402653184 | bytes 4194304 | tf_op jit(solution)/shard_map/pallas_call | solution.py:179
  32.7 0.0 collective-permute-done.13.refs_3_
  32.7 0.9 %collective-permute-done.12.refs_2_ = f32[2,1,128,128]{3,2,1,0:T(8,128)S(1)} collective-permute-done((f32[2,1,128,128]{3,2,1,0:T(8,128)S(1)}, f32[2,1,128,128]{3,2,1,0:T(8,128)S(1)}, u32[]{:S(2)}, u32[]{:S(2)}) %collective-permute-start.12) | collective-permute-done | bytes 131104 | tf_op jit(solution)/shard_map/ppermute | solution.py:241
  33.6 0.0 collective-permute-done.11.refs_1_
  33.6 0.4 %shard_map.74.refs_3_ = f32[2,1,4,128,128]{4,3,2,1,0:T(8,128)S(1)} custom-call(f32[2,1,128,128]{3,2,1,0:T(8,128)S(1)} %get-tuple-element.15.refs_2_.refs_0_, f32[2,1,128,128]{3,2,1,0:T(8,128)S(1)} %collective-permute-done.11.refs_1_, f32[2,1,128,128]{3,2,1,0:T(8,128)S(1)} %collective-permute-done.12.refs_2_, ...), custom_call_target="tpu_custom_call" | custom-call | flops 201326592 | bytes 4194304 | tf_op jit(solution)/shard_map/pallas_call | solution.py:179
  34.0 0.8 %collective-permute-done.10.refs_0_ = f32[2,1,128,128]{3,2,1,0:T(8,128)S(1)} collective-permute-done((f32[2,1,128,128]{3,2,1,0:T(8,128)S(1)}, f32[2,1,128,128]{3,2,1,0:T(8,128)S(1)}, u32[]{:S(2)}, u32[]{:S(2)}) %collective-permute-start.10) | collective-permute-done | bytes 131104 | tf_op jit(solution)/shard_map/ppermute | solution.py:241
  34.8 1.2 %shard_map.75 = f32[2,1,4,128,128]{4,3,2,1,0:T(8,128)} custom-call(f32[2,1,128,128]{3,2,1,0:T(8,128)S(1)} %collective-permute-done.10.refs_0_, bf16[1024,512]{1,0:T(8,128)(2,1)S(1)} %get-tuple-element.11.refs_0_.refs_3_.refs_1_.refs_2_.refs_4_, bf16[1024,512]{1,0:T(8,128)(2,1)S(1)} %get-tuple-element.12.refs_4_.refs_2_.refs_3_.refs_5_, ...), custom_call_target="tpu_custom_call" | custom-call | flops 201326592 | bytes 4194304 | tf_op jit(solution)/shard_map/pallas_call | solution.py:179
  (9 shorter events, 0.1 us)
Async XLA Ops:
  0.6 12.5 %collective-permute-start.5 = (f32[2,2,128,128]{3,2,1,0:T(8,128)}, f32[2,2,128,128]{3,2,1,0:T(8,128)S(1)}, u32[]{:S(2)}, u32[]{:S(2)}) collective-permute-start(f32[2,2,128,128]{3,2,1,0:T(8,128)} %refs_2_.3), channel_id=1, source_target_pairs={{0,8},{4,12},{8,0},{12,4},{16,24},{20,28},{24,16},{28,20},{1,9},{5... | collective-permute-start | bytes 786440 | tf_op jit(solution)/shard_map/ppermute | solution.py:241
  3.6 15.2 %collective-permute-start = (f32[2,2,128,128]{3,2,1,0:T(8,128)}, f32[2,2,128,128]{3,2,1,0:T(8,128)S(1)}, u32[]{:S(2)}, u32[]{:S(2)}) collective-permute-start(f32[2,2,128,128]{3,2,1,0:T(8,128)} %refs_2_.3), channel_id=1, source_target_pairs={{0,2},{1,3},{2,0},{3,1},{4,6},{5,7},{6,4},{7,5},{8,10},{9,11},{10,... | collective-permute-start | bytes 786440 | tf_op jit(solution)/shard_map/ppermute | solution.py:241
  6.2 12.6 %collective-permute-start.4 = (f32[2,2,128,128]{3,2,1,0:T(8,128)}, f32[2,2,128,128]{3,2,1,0:T(8,128)S(1)}, u32[]{:S(2)}, u32[]{:S(2)}) collective-permute-start(f32[2,2,128,128]{3,2,1,0:T(8,128)} %refs_2_.3), channel_id=1, source_target_pairs={{0,16},{4,20},{8,24},{12,28},{16,0},{20,4},{24,8},{28,12},{1,17},{... | collective-permute-start | bytes 786440 | tf_op jit(solution)/shard_map/ppermute | solution.py:241
  7.7 11.9 %collective-permute-start.3 = (f32[2,2,128,128]{3,2,1,0:T(8,128)}, f32[2,2,128,128]{3,2,1,0:T(8,128)S(1)}, u32[]{:S(2)}, u32[]{:S(2)}) collective-permute-start(f32[2,2,128,128]{3,2,1,0:T(8,128)} %refs_2_.3), channel_id=1, source_target_pairs={{0,1},{1,0},{2,3},{3,2},{4,5},{5,4},{6,7},{7,6},{8,9},{9,8},{10,11... | collective-permute-start | bytes 786440 | tf_op jit(solution)/shard_map/ppermute | solution.py:241
  9.3 3.8 %collective-permute-start.6 = (f32[2,1,16]{2,1,0:T(1,128)}, f32[2,1,16]{2,1,0:T(1,128)S(1)}, u32[]{:S(2)}, u32[]{:S(2)}) collective-permute-start(f32[2,1,16]{2,1,0:T(1,128)} %refs_6_.3), channel_id=1, source_target_pairs={{0,8},{4,12},{8,0},{12,4},{16,24},{20,28},{24,16},{28,20},{1,9},{5... | collective-permute-start | bytes 392 | tf_op jit(solution)/shard_map/ppermute | solution.py:241
  13.1 0.7 %copy-start.2 = (f32[2,1,16]{2,1,0:T(1,128)S(1)}, f32[2,1,16]{2,1,0:T(1,128)}, u32[]{:S(2)}) copy-start(f32[2,1,16]{2,1,0:T(1,128)} %refs_6_.3) | copy-start | bytes 388
  13.8 6.6 %collective-permute-start.7 = (f32[2,2,136,128]{3,2,1,0:T(8,128)S(1)}, f32[2,2,136,128]{3,2,1,0:T(8,128)S(1)}, u32[]{:S(2)}, u32[]{:S(2)}) collective-permute-start(f32[2,2,136,128]{3,2,1,0:T(8,128)S(1)} %shard_map.65), channel_id=1, source_target_pairs={{0,16},{4,20},{8,24},{12,28},{16,0},{20,4},{24,8},{28,12},{1,17},{... | collective-permute-start | bytes 835592 | tf_op jit(solution)/shard_map/ppermute | solution.py:241
  14.4 1.1 %collective-permute-start.1 = (f32[2,1,16]{2,1,0:T(1,128)S(1)}, f32[2,1,16]{2,1,0:T(1,128)S(1)}, u32[]{:S(2)}, u32[]{:S(2)}) collective-permute-start(f32[2,1,16]{2,1,0:T(1,128)S(1)} %copy-done.2), channel_id=1, source_target_pairs={{0,4},{4,0},{8,12},{12,8},{16,20},{20,16},{24,28},{28,24},{1,5},{5... | collective-permute-start | bytes 392 | tf_op jit(solution)/shard_map/ppermute | solution.py:241
  15.5 1.6 %copy-start = (f32[2,4,512,128]{3,2,1,0:T(8,128)S(1)}, f32[2,4,512,128]{3,2,1,0:T(8,128)}, u32[]{:S(2)}) copy-start(f32[2,4,512,128]{3,2,1,0:T(8,128)} %basis_hbm.1) | copy-start | bytes 6291460
  17.1 0.7 %copy-start.4 = (f32[2,1,4,4]{3,2,1,0:T(4,128)S(1)}, f32[2,1,4,4]{3,2,1,0:T(4,128)}, u32[]{:S(2)}) copy-start(f32[2,1,4,4]{3,2,1,0:T(4,128)} %site_hbm.1) | copy-start | bytes 388
  18.8 1.7 %copy-start.1 = (f32[2,2,128,128]{3,2,1,0:T(8,128)S(1)}, f32[2,2,128,128]{3,2,1,0:T(8,128)}, u32[]{:S(2)}) copy-start(f32[2,2,128,128]{3,2,1,0:T(8,128)} %refs_2_.3) | copy-start | bytes 786436
  18.8 1.6 %copy-start.3 = (f32[2,1,16]{2,1,0:T(1,128)S(1)}, f32[2,1,16]{2,1,0:T(1,128)}, u32[]{:S(2)}) copy-start(f32[2,1,16]{2,1,0:T(1,128)} %refs_6_.3) | copy-start | bytes 388
  19.7 1.6 %collective-permute-start.9 = (f32[2,2,128,128]{3,2,1,0:T(8,128)S(1)}, f32[2,2,128,128]{3,2,1,0:T(8,128)S(1)}, u32[]{:S(2)}, u32[]{:S(2)}) collective-permute-start(f32[2,2,128,128]{3,2,1,0:T(8,128)S(1)} %shard_map.62.refs_1_.refs_0_), channel_id=1, source_target_pairs={{0,4},{4,0},{8,12},{12,8},{16,20},{20,16},{24,28},{28,24},{1,5},{5... | collective-permute-start | bytes 786440 | tf_op jit(solution)/shard_map/ppermute | solution.py:241
  19.8 8.7 %collective-permute-start.2 = (f32[2,2,128,128]{3,2,1,0:T(8,128)S(1)}, f32[2,2,128,128]{3,2,1,0:T(8,128)S(1)}, u32[]{:S(2)}, u32[]{:S(2)}) collective-permute-start(f32[2,2,128,128]{3,2,1,0:T(8,128)S(1)} %shard_map.60.x_ref), channel_id=1, source_target_pairs={{0,1},{1,0},{2,3},{3,2},{4,5},{5,4},{6,7},{7,6},{8,9},{9,8},{10,11... | collective-permute-start | bytes 786440 | tf_op jit(solution)/shard_map/ppermute | solution.py:241
  20.9 1.4 %collective-permute-start.8 = (f32[2,1,128,128]{3,2,1,0:T(8,128)S(1)}, f32[2,1,128,128]{3,2,1,0:T(8,128)S(1)}, u32[]{:S(2)}, u32[]{:S(2)}) collective-permute-start(f32[2,1,128,128]{3,2,1,0:T(8,128)S(1)} %get-tuple-element.14), channel_id=1, source_target_pairs={{0,4},{4,0},{8,12},{12,8},{16,20},{20,16},{24,28},{28,24},{1,5},{5... | collective-permute-start | bytes 393224 | tf_op jit(solution)/shard_map/ppermute | solution.py:241
  22.3 9.8 %collective-permute-start.14 = (f32[2,1,128,128]{3,2,1,0:T(8,128)S(1)}, f32[2,1,128,128]{3,2,1,0:T(8,128)S(1)}, u32[]{:S(2)}, u32[]{:S(2)}) collective-permute-start(f32[2,1,128,128]{3,2,1,0:T(8,128)S(1)} %shard_map.68.x_ref.refs_0_), channel_id=1, source_target_pairs={{0,3},{1,2},{2,1},{3,0},{4,7},{5,6},{6,5},{7,4},{8,11},{9,10},{10,... | collective-permute-start | bytes 393224 | tf_op jit(solution)/shard_map/ppermute | solution.py:241
  24.4 8.4 %collective-permute-start.13 = (f32[2,1,128,128]{3,2,1,0:T(8,128)S(1)}, f32[2,1,128,128]{3,2,1,0:T(8,128)S(1)}, u32[]{:S(2)}, u32[]{:S(2)}) collective-permute-start(f32[2,1,128,128]{3,2,1,0:T(8,128)S(1)} %shard_map.72), channel_id=1, source_target_pairs={{0,24},{4,28},{8,16},{12,20},{16,8},{20,12},{24,0},{28,4},{1,25},{... | collective-permute-start | bytes 393224 | tf_op jit(solution)/shard_map/ppermute | solution.py:241
  26.8 6.8 %collective-permute-start.12 = (f32[2,1,128,128]{3,2,1,0:T(8,128)S(1)}, f32[2,1,128,128]{3,2,1,0:T(8,128)S(1)}, u32[]{:S(2)}, u32[]{:S(2)}) collective-permute-start(f32[2,1,128,128]{3,2,1,0:T(8,128)S(1)} %shard_map.71), channel_id=1, source_target_pairs={{0,16},{4,20},{8,24},{12,28},{16,0},{20,4},{24,8},{28,12},{1,17},{... | collective-permute-start | bytes 393224 | tf_op jit(solution)/shard_map/ppermute | solution.py:241
  27.4 6.2 %collective-permute-start.11 = (f32[2,1,128,128]{3,2,1,0:T(8,128)S(1)}, f32[2,1,128,128]{3,2,1,0:T(8,128)S(1)}, u32[]{:S(2)}, u32[]{:S(2)}) collective-permute-start(f32[2,1,128,128]{3,2,1,0:T(8,128)S(1)} %shard_map.70), channel_id=1, source_target_pairs={{0,8},{4,12},{8,0},{12,4},{16,24},{20,28},{24,16},{28,20},{1,9},{5... | collective-permute-start | bytes 393224 | tf_op jit(solution)/shard_map/ppermute | solution.py:241
  28.5 6.3 %collective-permute-start.10 = (f32[2,1,128,128]{3,2,1,0:T(8,128)S(1)}, f32[2,1,128,128]{3,2,1,0:T(8,128)S(1)}, u32[]{:S(2)}, u32[]{:S(2)}) collective-permute-start(f32[2,1,128,128]{3,2,1,0:T(8,128)S(1)} %shard_map.69), channel_id=1, source_target_pairs={{0,1},{1,0},{2,3},{3,2},{4,5},{5,4},{6,7},{7,6},{8,9},{9,8},{10,11... | collective-permute-start | bytes 393224 | tf_op jit(solution)/shard_map/ppermute | solution.py:241

commit v4 on v3

--- a/solution.py
+++ b/solution.py
@@ -33,10 +33,13 @@
 
 
 def order(sec):
-    return (1, 2, 0) + tuple(range(3, sec))
-
-
-def prepare_kernel(depth, basis_hbm, site_hbm, _, high_ref, low_ref, part_ref, *scratch):
+    return (3, 1, 0, 2) if sec == 4 else tuple(range(sec))
+
+
+def prepare_kernel(depth, basis_hbm, site_hbm, integrals_ref, *refs):
+    high_ref, low_ref, part_ref, row_ref = refs[:4]
+    scratch = refs[4:]
+    row_ref[...] = integrals_ref[...]
     basis_ref, site_ref, basis_sem, site_sem = scratch
     _, sites, old, cols = basis_ref.shape
     rows = part_ref.shape[3]
@@ -74,15 +77,15 @@
             part_ref[1, comp, site] = imag
 
 
-def prepare(basis, site_terms, rows, depth, awaited):
+def prepare(basis, site_terms, integrals, rows, depth):
     _, sites, old, cols = basis.shape
     comps = site_terms.shape[1]
     half = jax.ShapeDtypeStruct((2 * old, sites * cols), jnp.bfloat16)
     part = jax.ShapeDtypeStruct((2, comps, sites, rows, cols), jnp.float32)
     return call(
         functools.partial(prepare_kernel, depth),
-        (half, half, part),
-        [HBM, HBM, ANY],
+        (half, half, part, jax.ShapeDtypeStruct(integrals.shape, integrals.dtype)),
+        [HBM, HBM, VMEM],
         8 * comps * sites * sites * rows * cols,
         [
             pltpu.VMEM(basis.shape, basis.dtype),
@@ -90,7 +93,7 @@
             pltpu.SemaphoreType.DMA((2, sites)),
             pltpu.SemaphoreType.DMA,
         ],
-    )(basis, site_terms, awaited)
+    )(basis, site_terms, integrals)
 
 
 def pack(block, tables):
@@ -191,13 +194,50 @@
     )(*args)
 
 
-def total(parts, awaited):
-    def kernel(*refs):
-        refs[-1][...] = sum((ref[...] for ref in refs[1 : len(parts)]), refs[0][...])
-
-    out = jax.ShapeDtypeStruct(parts[0].shape, parts[0].dtype)
-    specs = [VMEM] * len(parts) + [ANY] * len(awaited)
-    return call(kernel, out, specs, out.size * len(parts))(*parts, *awaited)
+def first_rows(block, count):
+    _, norms, rows, cols = block.shape
+
+    def kernel(block_ref, out_ref):
+        for at in range(count):
+            out_ref[at] = block_ref[at // norms, at % norms]
+
+    return call(kernel, jax.ShapeDtypeStruct((count, rows, cols), block.dtype), [VMEM], 0)(block)
+
+
+def total(mine, other, block, count, awaited):
+    _, norms, rows, cols = block.shape
+    comps = mine.shape[1]
+    left = 2 * norms - count
+
+    def kernel(mine_ref, other_ref, block_ref, _, sum_ref, both_ref):
+        for at in range(left):
+            both_ref[at] = block_ref[(count + at) // norms, (count + at) % norms]
+        for part in range(2):
+            value = mine_ref[part] + other_ref[part]
+            sum_ref[part] = value
+            both_ref[left + part * comps : left + (part + 1) * comps] = value
+
+    out = (
+        jax.ShapeDtypeStruct(mine.shape, mine.dtype),
+        jax.ShapeDtypeStruct((left + 2 * comps, rows, cols), mine.dtype),
+    )
+    return call(kernel, out, [VMEM] * 3 + [ANY], mine.size)(mine, other, block, awaited)
+
+
+def unpack(first, both, norms):
+    count, rows, cols = first.shape
+    left = 2 * norms - count
+    comps = (both.shape[0] - left) // 2
+
+    def kernel(first_ref, both_ref, block_ref, sum_ref):
+        for at in range(2 * norms):
+            value = first_ref[at] if at < count else both_ref[at - count]
+            block_ref[at // norms, at % norms] = value
+        for part in range(2):
+            sum_ref[part] = both_ref[left + part * comps : left + (part + 1) * comps]
+
+    out = tuple(jax.ShapeDtypeStruct((2, n, rows, cols), first.dtype) for n in (norms, comps))
+    return call(kernel, out, [VMEM] * 2, 0)(first, both)
 
 
 def combine_kernel(operators, tables, per, *refs):
@@ -241,7 +281,7 @@
     return lax.ppermute(x, axis, [(at, at ^ key) for at in range(size)])
 
 
-def chip_blocks(own, row, pairs):
+def chip_blocks(own, row, beside, pairs):
     per = own.shape[1]
     arrays, tables = [own], []
     operators = [(0, op, op, 0) for op in range(per)]
@@ -249,7 +289,6 @@
         for key in (2, 4):
             operators += [(len(arrays), op, op, key) for op in range(per)]
             arrays.append(swap(own, "pair", pairs, key))
-        beside = swap(row, "pair", pairs, 2)
         operators += [(3, op, op, 6) for op in range(per)]
         arrays += [
             swap(pack(arrays[1], [row, beside]), "pair", pairs, 4),
@@ -274,32 +313,37 @@
     shape = (2, comps, rows, depth)
     two = swap(normal_ops, "sec", sec, 2)
     one = swap(normal_ops, "sec", sec, 1)
-    arrays, operators, tables = chip_blocks(normal_ops, integrals, pairs)
+    beside = swap(integrals, "pair", pairs, 2)
     sibling = swap(integrals, "pair", pairs, 1)
-    high, low, site_part = prepare(basis, site_terms, rows, depth, sibling)
-    two = after(two, high)
-    three = swap(two, "sec", sec, 1)
+    high, low, site_part, row = prepare(basis, site_terms, integrals, rows, depth)
+    arrays, operators, tables = chip_blocks(normal_ops, row, beside, pairs)
+    two = after(two, sibling)
+    count = 2 * norms - 1
+    three_first = swap(first_rows(two, count), "sec", sec, 1)
     two = after(after(two, arrays[2]), one)
-    normals = [one, two, normal_ops, three]
-    held = arrays + [integrals, sibling]
+    held = arrays + [row, sibling]
     here = [(len(arrays), None), (len(arrays) + 1, None)]
     mine, other = combine(held, operators, here, norms, shape)
     held = [two, swap(two, "pair", pairs, 1)] + arrays
     operators = [(key, op, op, key) for key in range(2) for op in range(norms)]
     tables = [(2 + at, part) for at, part in tables]
     parts = combine(held, operators, tables, norms, shape)
-    comp_ops = total([mine, swap(other, "pair", pairs, 1)], [parts[0]])
+    comp_ops, both = total(mine, swap(other, "pair", pairs, 1), two, count, parts[0])
+    both = swap(both, "sec", sec, 1)
+    at_two = [parts[0]]
+    for key in range(2, pairs, 2):
+        part = after(parts[key // 2], comp_ops)
+        if key < pairs - 2:
+            part = after(part, three_first)
+        at_two.append(swap(part, "pair", pairs, key))
     far = swap(comp_ops, "sec", sec, 3)
-    near = swap(after(comp_ops, three), "sec", sec, 1)
-    summed = [parts[0]] + [
-        swap(after(part, comp_ops), "pair", pairs, key)
-        for part, key in zip(parts[1:], range(2, pairs, 2))
-    ]
+    three, near = unpack(three_first, both, norms)
+    normals = [three, one, normal_ops, two]
     shape = (2, norms, sites, rows, cols)
-    early = renorm(normals, range(sec - 1), high, low, None, shape)
-    new_normal = renorm(normals, range(sec - 1, sec), high, low, early, shape, True)
+    early = renorm(normals, range(1, sec), high, low, None, shape)
+    new_normal = renorm(normals, range(1), high, low, early, shape, True)
     shape = (2, comps, sites, rows, cols)
-    arrived = [near, tuple(summed), comp_ops, far]
+    arrived = [far, near, comp_ops, tuple(at_two)]
     early = renorm(arrived, range(2, sec), high, low, site_part, shape)
     early = renorm(arrived, range(1, 2), high, low, early, shape)
     return new_normal, renorm(arrived, range(1), high, low, early, shape, True)

time: 36.1 us -> 37.2 us (1.030)
  waiting for transfers between devices: 8.52 us -> 9.43 us
    ppermute x15, waiting for transfers between devices: 8.52 us -> 9.43 us  [swap(): return lax.ppermute(x, axis, [(at, at ^ key) for at in range(size)])]
    pallas_call x2 -> x4, Pallas kernels: 0.98 us -> 1.03 us  [the longest x1 0.97 us: prepare(): call(functools.partial(prepare_kernel, depth), (half, half, part, jax.Sha...]
  transfers between devices with their start and end apart: 15 -> 15, of which waited for: 9 -> 6; matrix products, arithmetic and copies ran while one was open for 0% -> 0% of each run, Pallas kernels for 16% -> 16%
where the time goes in v4:
time: 37.2 us; the launch traced here: 37 us
  starting transfers between devices  16.6 us (45%)
  waiting for transfers between devices  9.43 us (25%)
  Pallas kernels  7.14 us (19%)
  local copies, waits for them, and re-layouts  2.96 us (8%)
  between operations  0.84 us (2%)
    ppermute x15, starting transfers between devices, swap(): return lax.ppermute(x, axis, [(at, at ^ key) for at in range(size)])  16.6 us
    ppermute x15, waiting for transfers between devices, swap(): return lax.ppermute(x, axis, [(at, at ^ key) for at in range(size)])  9.43 us
    pallas_call x5, Pallas kernels, renorm(): pl.pallas_call(functools.partial(renorm_kernel, steps, parts, carry is no...  5.05 us
    unnamed x10, local copies, waits for them, and re-layouts  2.96 us
    pallas_call x1, Pallas kernels, prepare(): call(functools.partial(prepare_kernel, depth), (half, half, part, jax.Sha...  0.97 us
    pallas_call x2, Pallas kernels, combine(): call(functools.partial(combine_kernel, operators, tables, per), (jax.Shap...  0.93 us
  transfers between devices with their start and end apart: 15, of which 6 were waited for; matrix products, arithmetic and copies ran while one was open for 0% of the time, Pallas kernels for 16%

profile of v4, /device:TPU:0, one launch (start us, length us, event | category | flops | bytes accessed | tf_op | source)
XLA Modules:
  0.0 37.0 jit_solution(15504201805437510954)
XLA Ops:
  0.6 3.0 %collective-permute-start.3 = (f32[2,2,128,128]{3,2,1,0:T(8,128)}, f32[2,2,128,128]{3,2,1,0:T(8,128)S(1)}, u32[]{:S(2)}, u32[]{:S(2)}) collective-permute-start(f32[2,2,128,128]{3,2,1,0:T(8,128)} %refs_1_.1), channel_id=1, source_target_pairs={{0,8},{4,12},{8,0},{12,4},{16,24},{20,28},{24,16},{28,20},{1,9},{5... | collective-permute-start | bytes 786440 | tf_op jit(solution)/shard_map/ppermute | solution.py:281
  3.6 2.6 %collective-permute-start = (f32[2,2,128,128]{3,2,1,0:T(8,128)}, f32[2,2,128,128]{3,2,1,0:T(8,128)S(1)}, u32[]{:S(2)}, u32[]{:S(2)}) collective-permute-start(f32[2,2,128,128]{3,2,1,0:T(8,128)} %refs_1_.1), channel_id=1, source_target_pairs={{0,2},{1,3},{2,0},{3,1},{4,6},{5,7},{6,4},{7,5},{8,10},{9,11},{10,... | collective-permute-start | bytes 786440 | tf_op jit(solution)/shard_map/ppermute | solution.py:281
  6.2 1.5 %collective-permute-start.4 = (f32[2,2,128,128]{3,2,1,0:T(8,128)}, f32[2,2,128,128]{3,2,1,0:T(8,128)S(1)}, u32[]{:S(2)}, u32[]{:S(2)}) collective-permute-start(f32[2,2,128,128]{3,2,1,0:T(8,128)} %refs_1_.1), channel_id=1, source_target_pairs={{0,16},{4,20},{8,24},{12,28},{16,0},{20,4},{24,8},{28,12},{1,17},{... | collective-permute-start | bytes 786440 | tf_op jit(solution)/shard_map/ppermute | solution.py:281
  7.7 1.6 %collective-permute-start.8 = (f32[2,2,128,128]{3,2,1,0:T(8,128)}, f32[2,2,128,128]{3,2,1,0:T(8,128)S(1)}, u32[]{:S(2)}, u32[]{:S(2)}) collective-permute-start(f32[2,2,128,128]{3,2,1,0:T(8,128)} %refs_1_.1), channel_id=1, source_target_pairs={{0,1},{1,0},{2,3},{3,2},{4,5},{5,4},{6,7},{7,6},{8,9},{9,8},{10,11... | collective-permute-start | bytes 786440 | tf_op jit(solution)/shard_map/ppermute | solution.py:281
  9.3 0.5 %collective-permute-start.5 = (f32[2,1,16]{2,1,0:T(1,128)}, f32[2,1,16]{2,1,0:T(1,128)S(1)}, u32[]{:S(2)}, u32[]{:S(2)}) collective-permute-start(f32[2,1,16]{2,1,0:T(1,128)} %integrals_ref.1), channel_id=1, source_target_pairs={{0,8},{4,12},{8,0},{12,4},{16,24},{20,28},{24,16},{28,20},{1,9},{5... | collective-permute-start | bytes 392 | tf_op jit(solution)/shard_map/ppermute | solution.py:281
  9.9 0.0 copy-start
  9.9 1.6 %copy-done = f32[2,4,512,128]{3,2,1,0:T(8,128)S(1)} copy-done((f32[2,4,512,128]{3,2,1,0:T(8,128)S(1)}, f32[2,4,512,128]{3,2,1,0:T(8,128)}, u32[]{:S(2)}) %copy-start) | copy-done | bytes 2097176
  11.4 0.0 copy-start.2
  11.4 0.7 %copy-done.2 = f32[2,1,4,4]{3,2,1,0:T(4,128)S(1)} copy-done((f32[2,1,4,4]{3,2,1,0:T(4,128)S(1)}, f32[2,1,4,4]{3,2,1,0:T(4,128)}, u32[]{:S(2)}) %copy-start.2) | copy-done | bytes 152
  12.1 0.0 copy-start.3
  12.1 0.7 %copy-done.3 = f32[2,1,16]{2,1,0:T(1,128)S(1)} copy-done((f32[2,1,16]{2,1,0:T(1,128)S(1)}, f32[2,1,16]{2,1,0:T(1,128)}, u32[]{:S(2)}) %copy-start.3) | copy-done | bytes 152
  12.8 0.0 copy-start.4
  12.8 0.0 copy-start.1
  12.8 1.0 %shard_map.61 = (bf16[1024,512]{1,0:T(8,128)(2,1)S(1)}, bf16[1024,512]{1,0:T(8,128)(2,1)S(1)}, f32[2,1,4,128,128]{4,3,2,1,0:T(8,128)S(1)}, f32[2,1,16]{2,1,0:T(1,128)S(1)}) custom-call(f32[2,4,512,128]{3,2,1,0:T(8,128)S(1)} %copy-done, f32[2,1,4,4]{3,2,1,0:T(4,128)S(1)} %copy-done.2, f32[2,1,16]{2,1,0:T(1,128)S(1)} %copy-done.3), custom_call_target="tpu_custom_call" | custom-call | flops 2097152 | bytes 4194304 | tf_op jit(solution)/shard_map/pallas_call | solution.py:85
  13.8 0.0 collective-permute-done.5.refs_1_.refs_5_.refs_7_
  13.8 0.0 collective-permute-done.3.block_ref.refs_1_.refs_3_
  13.8 0.6 %collective-permute-start.6 = (f32[2,2,136,128]{3,2,1,0:T(8,128)S(1)}, f32[2,2,136,128]{3,2,1,0:T(8,128)S(1)}, u32[]{:S(2)}, u32[]{:S(2)}) collective-permute-start(f32[2,2,136,128]{3,2,1,0:T(8,128)S(1)} %shard_map.62), channel_id=1, source_target_pairs={{0,16},{4,20},{8,24},{12,28},{16,0},{20,4},{24,8},{28,12},{1,17},{... | collective-permute-start | bytes 835592 | tf_op jit(solution)/shard_map/ppermute | solution.py:281
  14.4 0.0 copy-done.4
  14.4 0.0 collective-permute-start.1
  14.4 1.1 %collective-permute-done.1.refs_0_.refs_7_ = f32[2,1,16]{2,1,0:T(1,128)S(1)} collective-permute-done((f32[2,1,16]{2,1,0:T(1,128)S(1)}, f32[2,1,16]{2,1,0:T(1,128)S(1)}, u32[]{:S(2)}, u32[]{:S(2)}) %collective-permute-start.1) | collective-permute-done | bytes 160 | tf_op jit(solution)/shard_map/ppermute | solution.py:281
  15.6 2.7 %collective-permute-done.x_ref = f32[2,2,128,128]{3,2,1,0:T(8,128)S(1)} collective-permute-done((f32[2,2,128,128]{3,2,1,0:T(8,128)}, f32[2,2,128,128]{3,2,1,0:T(8,128)S(1)}, u32[]{:S(2)}, u32[]{:S(2)}) %collective-permute-start) | collective-permute-done | bytes 262176 | tf_op jit(solution)/shard_map/ppermute | solution.py:281
  18.3 0.0 collective-permute-done.4.refs_2_.refs_0_.refs_4_
  18.3 1.4 %collective-permute-done.8.refs_0_ = f32[2,2,128,128]{3,2,1,0:T(8,128)S(1)} collective-permute-done((f32[2,2,128,128]{3,2,1,0:T(8,128)}, f32[2,2,128,128]{3,2,1,0:T(8,128)S(1)}, u32[]{:S(2)}, u32[]{:S(2)}) %collective-permute-start.8) | collective-permute-done | bytes 262176 | tf_op jit(solution)/shard_map/ppermute | solution.py:281
  19.7 0.1 collective-permute-start.9
  19.8 0.3 collective-permute-start.2
  20.1 0.9 %collective-permute-done.6.refs_3_.refs_5_ = f32[2,2,136,128]{3,2,1,0:T(8,128)S(1)} collective-permute-done((f32[2,2,136,128]{3,2,1,0:T(8,128)S(1)}, f32[2,2,136,128]{3,2,1,0:T(8,128)S(1)}, u32[]{:S(2)}, u32[]{:S(2)}) %collective-permute-start.6) | collective-permute-done | bytes 278560 | tf_op jit(solution)/shard_map/ppermute | solution.py:281
  20.9 0.0 copy-done.1
  20.9 0.5 %shard_map.63 = (f32[2,1,128,128]{3,2,1,0:T(8,128)S(1)}, f32[2,1,128,128]{3,2,1,0:T(8,128)S(1)}) custom-call(f32[2,2,128,128]{3,2,1,0:T(8,128)S(1)} %copy-done.1, f32[2,2,128,128]{3,2,1,0:T(8,128)S(1)} %collective-permute-done.3.block_ref.refs_1_.refs_3_, f32[2,2,128,128]{3,2,1,0:T(8,128)S(1)} %collective-permute-done.4.refs_2_.refs_0_.refs_4_, ...), custom_call_target="tpu_custom_call" | custom-call | flops 2097152 | bytes 4194304 | tf_op jit(solution)/shard_map/pallas_call | solution.py:272
  21.4 0.1 collective-permute-start.7
  21.5 0.0 collective-permute-done.9.refs_1_
  21.5 0.5 %shard_map.66 = (f32[2,1,128,128]{3,2,1,0:T(8,128)S(1)}, f32[2,1,128,128]{3,2,1,0:T(8,128)S(1)}, f32[2,1,128,128]{3,2,1,0:T(8,128)S(1)}, f32[2,1,128,128]{3,2,1,0:T(8,128)S(1)}) custom-call(f32[2,2,128,128]{3,2,1,0:T(8,128)S(1)} %shard_map.65.refs_0_.block_ref.refs_2_, f32[2,2,128,128]{3,2,1,0:T(8,128)S(1)} %collective-permute-done.9.refs_1_, ...), custom_call_target="tpu_custom_call" | custom-call | flops 2097152 | bytes 4194304 | tf_op jit(solution)/shard_map/pallas_call | solution.py:272
  21.9 0.9 %collective-permute-done.7.other_ref = f32[2,1,128,128]{3,2,1,0:T(8,128)S(1)} collective-permute-done((f32[2,1,128,128]{3,2,1,0:T(8,128)S(1)}, f32[2,1,128,128]{3,2,1,0:T(8,128)S(1)}, u32[]{:S(2)}, u32[]{:S(2)}) %collective-permute-start.7) | collective-permute-done | bytes 131104 | tf_op jit(solution)/shard_map/ppermute | solution.py:281
  22.8 1.0 %collective-permute-start.10 = (f32[3,128,128]{2,1,0:T(8,128)S(1)}, f32[3,128,128]{2,1,0:T(8,128)S(1)}, u32[]{:S(2)}, u32[]{:S(2)}) collective-permute-start(f32[3,128,128]{2,1,0:T(8,128)S(1)} %get-tuple-element.20), channel_id=1, source_target_pairs={{0,1},{1,0},{2,3},{3,2},{4,5},{5,4},{6,7},{7,6},{8,9},{9,8},{10,11... | collective-permute-start | bytes 589832 | tf_op jit(solution)/shard_map/ppermute | solution.py:281
  23.9 1.1 %collective-permute-start.14 = (f32[2,1,128,128]{3,2,1,0:T(8,128)S(1)}, f32[2,1,128,128]{3,2,1,0:T(8,128)S(1)}, u32[]{:S(2)}, u32[]{:S(2)}) collective-permute-start(f32[2,1,128,128]{3,2,1,0:T(8,128)S(1)} %shard_map.75), channel_id=1, source_target_pairs={{0,24},{4,28},{8,16},{12,20},{16,8},{20,12},{24,0},{28,4},{1,25},{... | collective-permute-start | bytes 393224 | tf_op jit(solution)/shard_map/ppermute | solution.py:281
  25.0 2.5 %collective-permute-done.2.first_ref.refs_0_ = f32[3,128,128]{2,1,0:T(8,128)S(1)} collective-permute-done((f32[3,128,128]{2,1,0:T(8,128)S(1)}, f32[3,128,128]{2,1,0:T(8,128)S(1)}, u32[]{:S(2)}, u32[]{:S(2)}) %collective-permute-start.2) | collective-permute-done | bytes 196640 | tf_op jit(solution)/shard_map/ppermute | solution.py:281
  27.6 0.6 %collective-permute-start.13 = (f32[2,1,128,128]{3,2,1,0:T(8,128)S(1)}, f32[2,1,128,128]{3,2,1,0:T(8,128)S(1)}, u32[]{:S(2)}, u32[]{:S(2)}) collective-permute-start(f32[2,1,128,128]{3,2,1,0:T(8,128)S(1)} %shard_map.74), channel_id=1, source_target_pairs={{0,16},{4,20},{8,24},{12,28},{16,0},{20,4},{24,8},{28,12},{1,17},{... | collective-permute-start | bytes 393224 | tf_op jit(solution)/shard_map/ppermute | solution.py:281
  28.2 0.6 %collective-permute-start.12 = (f32[2,1,128,128]{3,2,1,0:T(8,128)S(1)}, f32[2,1,128,128]{3,2,1,0:T(8,128)S(1)}, u32[]{:S(2)}, u32[]{:S(2)}) collective-permute-start(f32[2,1,128,128]{3,2,1,0:T(8,128)S(1)} %shard_map.72), channel_id=1, source_target_pairs={{0,8},{4,12},{8,0},{12,4},{16,24},{20,28},{24,16},{28,20},{1,9},{5... | collective-permute-start | bytes 393224 | tf_op jit(solution)/shard_map/ppermute | solution.py:281
  28.8 3.0 %collective-permute-start.11 = (f32[2,1,128,128]{3,2,1,0:T(8,128)S(1)}, f32[2,1,128,128]{3,2,1,0:T(8,128)S(1)}, u32[]{:S(2)}, u32[]{:S(2)}) collective-permute-start(f32[2,1,128,128]{3,2,1,0:T(8,128)S(1)} %get-tuple-element.24.refs_0_), channel_id=1, source_target_pairs={{0,3},{1,2},{2,1},{3,0},{4,7},{5,6},{6,5},{7,4},{8,11},{9,10},{10,... | collective-permute-start | bytes 393224 | tf_op jit(solution)/shard_map/ppermute | solution.py:281
  31.8 1.4 %shard_map.69.refs_3_ = f32[2,2,4,128,128]{4,3,2,1,0:T(8,128)S(1)} custom-call(f32[2,2,128,128]{3,2,1,0:T(8,128)S(1)} %collective-permute-done.8.refs_0_, f32[2,2,128,128]{3,2,1,0:T(8,128)S(1)} %copy-done.1, f32[2,2,128,128]{3,2,1,0:T(8,128)S(1)} %shard_map.65.refs_0_.block_ref.refs_2_, bf16[1024,512]{1,0:T(8,128)(2,1)S(1)} %get-tuple-element.22.refs_3_.refs_1_.refs_5_, ...), custom_call_target="tpu_custom_call" | custom-call | flops 1207959552 | bytes 4194304 | tf_op jit(solution)/shard_map/pallas_call | solution.py:182
  33.2 0.0 collective-permute-done.14.refs_4_
  33.2 0.0 collective-permute-done.13.refs_3_
  33.2 0.0 collective-permute-done.12.refs_2_
  33.2 0.6 %shard_map.76.refs_3_ = f32[2,1,4,128,128]{4,3,2,1,0:T(8,128)S(1)} custom-call(f32[2,1,128,128]{3,2,1,0:T(8,128)S(1)} %get-tuple-element.24.refs_0_, f32[2,1,128,128]{3,2,1,0:T(8,128)S(1)} %get-tuple-element.19._.refs_1_, f32[2,1,128,128]{3,2,1,0:T(8,128)S(1)} %collective-permute-done.12.refs_2_, f32[2,1,128,128]{3,2,1,0:T(8,128)S(1)} %collective-permute-done.13.refs_3_, ...), custom_call_target="tpu_custom_call" | custom-call | flops 402653184 | bytes 4194304 | tf_op jit(solution)/shard_map/pallas_call | solution.py:182
  33.8 0.0 collective-permute-done.10.both_ref
  33.9 0.4 %shard_map.77.refs_3_ = f32[2,1,4,128,128]{4,3,2,1,0:T(8,128)S(1)} custom-call(f32[2,1,128,128]{3,2,1,0:T(8,128)S(1)} %get-tuple-element.25.refs_0_, bf16[1024,512]{1,0:T(8,128)(2,1)S(1)} %get-tuple-element.22.refs_3_.refs_1_.refs_5_, bf16[1024,512]{1,0:T(8,128)(2,1)S(1)} %get-tuple-element.23.refs_4_.refs_2_.refs_6_, ...), custom_call_target="tpu_custom_call" | custom-call | flops 201326592 | bytes 4194304 | tf_op jit(solution)/shard_map/pallas_call | solution.py:182
  34.3 1.5 %shard_map.70 = f32[2,2,4,128,128]{4,3,2,1,0:T(8,128)} custom-call(f32[2,2,128,128]{3,2,1,0:T(8,128)S(1)} %get-tuple-element.21.refs_0_, bf16[1024,512]{1,0:T(8,128)(2,1)S(1)} %get-tuple-element.22.refs_3_.refs_1_.refs_5_, bf16[1024,512]{1,0:T(8,128)(2,1)S(1)} %get-tuple-element.23.refs_4_.refs_2_.refs_6_, f32[2,2,4,128,128]{4,3,2,1,0:T(8,128)S(1)} %shard_map.69.refs_3_), custom_call_target="tpu_custom_call" | custom-call | flops 402653184 | bytes 4194304 | tf_op jit(solution)/shard_map/pallas_call | solution.py:182
  35.8 0.0 collective-permute-done.11.refs_0_
  35.8 1.2 %shard_map.78 = f32[2,1,4,128,128]{4,3,2,1,0:T(8,128)} custom-call(f32[2,1,128,128]{3,2,1,0:T(8,128)S(1)} %collective-permute-done.11.refs_0_, bf16[1024,512]{1,0:T(8,128)(2,1)S(1)} %get-tuple-element.22.refs_3_.refs_1_.refs_5_, bf16[1024,512]{1,0:T(8,128)(2,1)S(1)} %get-tuple-element.23.refs_4_.refs_2_.refs_6_, f32[2,1,4,128,128]{4,3,2,1,0:T(8,128)S(1)} %shard_map.77.refs_3_), custom_call_target="tpu_custom_call" | custom-call | flops 201326592 | bytes 4194304 | tf_op jit(solution)/shard_map/pallas_call | solution.py:182
  (12 shorter events, 0.2 us)
Async XLA Ops:
  0.6 13.2 %collective-permute-start.3 = (f32[2,2,128,128]{3,2,1,0:T(8,128)}, f32[2,2,128,128]{3,2,1,0:T(8,128)S(1)}, u32[]{:S(2)}, u32[]{:S(2)}) collective-permute-start(f32[2,2,128,128]{3,2,1,0:T(8,128)} %refs_1_.1), channel_id=1, source_target_pairs={{0,8},{4,12},{8,0},{12,4},{16,24},{20,28},{24,16},{28,20},{1,9},{5... | collective-permute-start | bytes 786440 | tf_op jit(solution)/shard_map/ppermute | solution.py:281
  3.6 14.6 %collective-permute-start = (f32[2,2,128,128]{3,2,1,0:T(8,128)}, f32[2,2,128,128]{3,2,1,0:T(8,128)S(1)}, u32[]{:S(2)}, u32[]{:S(2)}) collective-permute-start(f32[2,2,128,128]{3,2,1,0:T(8,128)} %refs_1_.1), channel_id=1, source_target_pairs={{0,2},{1,3},{2,0},{3,1},{4,6},{5,7},{6,4},{7,5},{8,10},{9,11},{10,... | collective-permute-start | bytes 786440 | tf_op jit(solution)/shard_map/ppermute | solution.py:281
  6.2 12.1 %collective-permute-start.4 = (f32[2,2,128,128]{3,2,1,0:T(8,128)}, f32[2,2,128,128]{3,2,1,0:T(8,128)S(1)}, u32[]{:S(2)}, u32[]{:S(2)}) collective-permute-start(f32[2,2,128,128]{3,2,1,0:T(8,128)} %refs_1_.1), channel_id=1, source_target_pairs={{0,16},{4,20},{8,24},{12,28},{16,0},{20,4},{24,8},{28,12},{1,17},{... | collective-permute-start | bytes 786440 | tf_op jit(solution)/shard_map/ppermute | solution.py:281
  7.7 11.9 %collective-permute-start.8 = (f32[2,2,128,128]{3,2,1,0:T(8,128)}, f32[2,2,128,128]{3,2,1,0:T(8,128)S(1)}, u32[]{:S(2)}, u32[]{:S(2)}) collective-permute-start(f32[2,2,128,128]{3,2,1,0:T(8,128)} %refs_1_.1), channel_id=1, source_target_pairs={{0,1},{1,0},{2,3},{3,2},{4,5},{5,4},{6,7},{7,6},{8,9},{9,8},{10,11... | collective-permute-start | bytes 786440 | tf_op jit(solution)/shard_map/ppermute | solution.py:281
  9.3 4.5 %collective-permute-start.5 = (f32[2,1,16]{2,1,0:T(1,128)}, f32[2,1,16]{2,1,0:T(1,128)S(1)}, u32[]{:S(2)}, u32[]{:S(2)}) collective-permute-start(f32[2,1,16]{2,1,0:T(1,128)} %integrals_ref.1), channel_id=1, source_target_pairs={{0,8},{4,12},{8,0},{12,4},{16,24},{20,28},{24,16},{28,20},{1,9},{5... | collective-permute-start | bytes 392 | tf_op jit(solution)/shard_map/ppermute | solution.py:281
  9.9 1.6 %copy-start = (f32[2,4,512,128]{3,2,1,0:T(8,128)S(1)}, f32[2,4,512,128]{3,2,1,0:T(8,128)}, u32[]{:S(2)}) copy-start(f32[2,4,512,128]{3,2,1,0:T(8,128)} %basis_hbm.1) | copy-start | bytes 6291460
  11.4 0.7 %copy-start.2 = (f32[2,1,4,4]{3,2,1,0:T(4,128)S(1)}, f32[2,1,4,4]{3,2,1,0:T(4,128)}, u32[]{:S(2)}) copy-start(f32[2,1,4,4]{3,2,1,0:T(4,128)} %site_hbm.1) | copy-start | bytes 388
  12.1 0.7 %copy-start.3 = (f32[2,1,16]{2,1,0:T(1,128)S(1)}, f32[2,1,16]{2,1,0:T(1,128)}, u32[]{:S(2)}) copy-start(f32[2,1,16]{2,1,0:T(1,128)} %integrals_ref.1) | copy-start | bytes 388
  12.8 1.6 %copy-start.4 = (f32[2,1,16]{2,1,0:T(1,128)S(1)}, f32[2,1,16]{2,1,0:T(1,128)}, u32[]{:S(2)}) copy-start(f32[2,1,16]{2,1,0:T(1,128)} %integrals_ref.1) | copy-start | bytes 388
  12.8 8.1 %copy-start.1 = (f32[2,2,128,128]{3,2,1,0:T(8,128)S(1)}, f32[2,2,128,128]{3,2,1,0:T(8,128)}, u32[]{:S(2)}) copy-start(f32[2,2,128,128]{3,2,1,0:T(8,128)} %refs_1_.1) | copy-start | bytes 786436
  13.8 7.1 %collective-permute-start.6 = (f32[2,2,136,128]{3,2,1,0:T(8,128)S(1)}, f32[2,2,136,128]{3,2,1,0:T(8,128)S(1)}, u32[]{:S(2)}, u32[]{:S(2)}) collective-permute-start(f32[2,2,136,128]{3,2,1,0:T(8,128)S(1)} %shard_map.62), channel_id=1, source_target_pairs={{0,16},{4,20},{8,24},{12,28},{16,0},{20,4},{24,8},{28,12},{1,17},{... | collective-permute-start | bytes 835592 | tf_op jit(solution)/shard_map/ppermute | solution.py:281
  14.4 1.1 %collective-permute-start.1 = (f32[2,1,16]{2,1,0:T(1,128)S(1)}, f32[2,1,16]{2,1,0:T(1,128)S(1)}, u32[]{:S(2)}, u32[]{:S(2)}) collective-permute-start(f32[2,1,16]{2,1,0:T(1,128)S(1)} %copy-done.4), channel_id=1, source_target_pairs={{0,4},{4,0},{8,12},{12,8},{16,20},{20,16},{24,28},{28,24},{1,5},{5... | collective-permute-start | bytes 392 | tf_op jit(solution)/shard_map/ppermute | solution.py:281
  19.7 1.8 %collective-permute-start.9 = (f32[2,2,128,128]{3,2,1,0:T(8,128)S(1)}, f32[2,2,128,128]{3,2,1,0:T(8,128)S(1)}, u32[]{:S(2)}, u32[]{:S(2)}) collective-permute-start(f32[2,2,128,128]{3,2,1,0:T(8,128)S(1)} %shard_map.65.refs_0_.block_ref.refs_2_), channel_id=1, source_target_pairs={{0,4},{4,0},{8,12},{12,8},{16,20},{20,16},{24,28},{28,24},{1,5},{5... | collective-permute-start | bytes 786440 | tf_op jit(solution)/shard_map/ppermute | solution.py:281
  19.8 7.8 %collective-permute-start.2 = (f32[3,128,128]{2,1,0:T(8,128)S(1)}, f32[3,128,128]{2,1,0:T(8,128)S(1)}, u32[]{:S(2)}, u32[]{:S(2)}) collective-permute-start(f32[3,128,128]{2,1,0:T(8,128)S(1)} %shard_map.60), channel_id=1, source_target_pairs={{0,1},{1,0},{2,3},{3,2},{4,5},{5,4},{6,7},{7,6},{8,9},{9,8},{10,11... | collective-permute-start | bytes 589832 | tf_op jit(solution)/shard_map/ppermute | solution.py:281
  21.4 1.4 %collective-permute-start.7 = (f32[2,1,128,128]{3,2,1,0:T(8,128)S(1)}, f32[2,1,128,128]{3,2,1,0:T(8,128)S(1)}, u32[]{:S(2)}, u32[]{:S(2)}) collective-permute-start(f32[2,1,128,128]{3,2,1,0:T(8,128)S(1)} %get-tuple-element.18), channel_id=1, source_target_pairs={{0,4},{4,0},{8,12},{12,8},{16,20},{20,16},{24,28},{28,24},{1,5},{5... | collective-permute-start | bytes 393224 | tf_op jit(solution)/shard_map/ppermute | solution.py:281
  22.8 11.0 %collective-permute-start.10 = (f32[3,128,128]{2,1,0:T(8,128)S(1)}, f32[3,128,128]{2,1,0:T(8,128)S(1)}, u32[]{:S(2)}, u32[]{:S(2)}) collective-permute-start(f32[3,128,128]{2,1,0:T(8,128)S(1)} %get-tuple-element.20), channel_id=1, source_target_pairs={{0,1},{1,0},{2,3},{3,2},{4,5},{5,4},{6,7},{7,6},{8,9},{9,8},{10,11... | collective-permute-start | bytes 589832 | tf_op jit(solution)/shard_map/ppermute | solution.py:281
  23.9 9.3 %collective-permute-start.14 = (f32[2,1,128,128]{3,2,1,0:T(8,128)S(1)}, f32[2,1,128,128]{3,2,1,0:T(8,128)S(1)}, u32[]{:S(2)}, u32[]{:S(2)}) collective-permute-start(f32[2,1,128,128]{3,2,1,0:T(8,128)S(1)} %shard_map.75), channel_id=1, source_target_pairs={{0,24},{4,28},{8,16},{12,20},{16,8},{20,12},{24,0},{28,4},{1,25},{... | collective-permute-start | bytes 393224 | tf_op jit(solution)/shard_map/ppermute | solution.py:281
  27.6 5.7 %collective-permute-start.13 = (f32[2,1,128,128]{3,2,1,0:T(8,128)S(1)}, f32[2,1,128,128]{3,2,1,0:T(8,128)S(1)}, u32[]{:S(2)}, u32[]{:S(2)}) collective-permute-start(f32[2,1,128,128]{3,2,1,0:T(8,128)S(1)} %shard_map.74), channel_id=1, source_target_pairs={{0,16},{4,20},{8,24},{12,28},{16,0},{20,4},{24,8},{28,12},{1,17},{... | collective-permute-start | bytes 393224 | tf_op jit(solution)/shard_map/ppermute | solution.py:281
  28.2 5.1 %collective-permute-start.12 = (f32[2,1,128,128]{3,2,1,0:T(8,128)S(1)}, f32[2,1,128,128]{3,2,1,0:T(8,128)S(1)}, u32[]{:S(2)}, u32[]{:S(2)}) collective-permute-start(f32[2,1,128,128]{3,2,1,0:T(8,128)S(1)} %shard_map.72), channel_id=1, source_target_pairs={{0,8},{4,12},{8,0},{12,4},{16,24},{20,28},{24,16},{28,20},{1,9},{5... | collective-permute-start | bytes 393224 | tf_op jit(solution)/shard_map/ppermute | solution.py:281
  28.8 7.0 %collective-permute-start.11 = (f32[2,1,128,128]{3,2,1,0:T(8,128)S(1)}, f32[2,1,128,128]{3,2,1,0:T(8,128)S(1)}, u32[]{:S(2)}, u32[]{:S(2)}) collective-permute-start(f32[2,1,128,128]{3,2,1,0:T(8,128)S(1)} %get-tuple-element.24.refs_0_), channel_id=1, source_target_pairs={{0,3},{1,2},{2,1},{3,0},{4,7},{5,6},{6,5},{7,4},{8,11},{9,10},{10,... | collective-permute-start | bytes 393224 | tf_op jit(solution)/shard_map/ppermute | solution.py:281

commit v5 on v3

--- a/solution.py
+++ b/solution.py
@@ -33,10 +33,13 @@
 
 
 def order(sec):
-    return (1, 2, 0) + tuple(range(3, sec))
-
-
-def prepare_kernel(depth, basis_hbm, site_hbm, _, high_ref, low_ref, part_ref, *scratch):
+    return (3, 1, 0, 2) if sec == 4 else tuple(range(sec))
+
+
+def prepare_kernel(depth, basis_hbm, site_hbm, integrals_ref, *refs):
+    high_ref, low_ref, part_ref, row_ref = refs[:4]
+    scratch = refs[4:]
+    row_ref[...] = integrals_ref[...]
     basis_ref, site_ref, basis_sem, site_sem = scratch
     _, sites, old, cols = basis_ref.shape
     rows = part_ref.shape[3]
@@ -74,15 +77,15 @@
             part_ref[1, comp, site] = imag
 
 
-def prepare(basis, site_terms, rows, depth, awaited):
+def prepare(basis, site_terms, integrals, rows, depth):
     _, sites, old, cols = basis.shape
     comps = site_terms.shape[1]
     half = jax.ShapeDtypeStruct((2 * old, sites * cols), jnp.bfloat16)
     part = jax.ShapeDtypeStruct((2, comps, sites, rows, cols), jnp.float32)
     return call(
         functools.partial(prepare_kernel, depth),
-        (half, half, part),
-        [HBM, HBM, ANY],
+        (half, half, part, jax.ShapeDtypeStruct(integrals.shape, integrals.dtype)),
+        [HBM, HBM, VMEM],
         8 * comps * sites * sites * rows * cols,
         [
             pltpu.VMEM(basis.shape, basis.dtype),
@@ -90,7 +93,7 @@
             pltpu.SemaphoreType.DMA((2, sites)),
             pltpu.SemaphoreType.DMA,
         ],
-    )(basis, site_terms, awaited)
+    )(basis, site_terms, integrals)
 
 
 def pack(block, tables):
@@ -118,10 +121,11 @@
     return call(kernel, out, [VMEM] + [ANY] * len(others), 0)(x, *others)
 
 
-def renorm_kernel(steps, parts, carried, streamed, *refs):
+def renorm_kernel(steps, parts, carried, awaited, streamed, *refs):
     count = sum(parts)
     high_ref, low_ref = refs[count : count + 2]
-    out_ref, left_high, left_low = refs[count + 2 + carried : count + 5 + carried]
+    first = count + 2 + carried + awaited
+    out_ref, left_high, left_low = refs[first : first + 3]
     out_hbm, out_ref, sems = (out_ref,) + refs[-2:] if streamed else (None, out_ref, None)
     _, ops, sites, rows, cols = out_ref.shape
     depth = refs[0].shape[-1]
@@ -166,7 +170,7 @@
         copy.wait()
 
 
-def renorm(blocks, steps, high, low, carry, shape, streamed=False):
+def renorm(blocks, steps, high, low, carry, shape, streamed=False, awaited=()):
     blocks = [block if isinstance(block, tuple) else (block,) for block in blocks]
     blocks = blocks[steps.start : steps.stop]
     parts = tuple(len(block) for block in blocks)
@@ -177,9 +181,11 @@
     pieces = 2 * ops * sites * cols // WIDE
     held = [pltpu.VMEM(shape, jnp.float32), pltpu.SemaphoreType.DMA((pieces,))]
     return pl.pallas_call(
-        functools.partial(renorm_kernel, steps, parts, carry is not None, streamed),
+        functools.partial(
+            renorm_kernel, steps, parts, carry is not None, len(awaited), streamed
+        ),
         out_shape=jax.ShapeDtypeStruct(shape, jnp.float32),
-        in_specs=[VMEM] * len(args),
+        in_specs=[VMEM] * len(args) + [ANY] * len(awaited),
         out_specs=HBM if streamed else VMEM,
         scratch_shapes=[left, left] + (held if streamed else []),
         cost_estimate=pl.CostEstimate(
@@ -188,7 +194,7 @@
             transcendentals=0,
         ),
         compiler_params=pltpu.CompilerParams(vmem_limit_bytes=VMEM_BYTES),
-    )(*args)
+    )(*args, *awaited)
 
 
 def total(parts, awaited):
@@ -241,7 +247,7 @@
     return lax.ppermute(x, axis, [(at, at ^ key) for at in range(size)])
 
 
-def chip_blocks(own, row, pairs):
+def chip_blocks(own, row, beside, pairs):
     per = own.shape[1]
     arrays, tables = [own], []
     operators = [(0, op, op, 0) for op in range(per)]
@@ -249,7 +255,6 @@
         for key in (2, 4):
             operators += [(len(arrays), op, op, key) for op in range(per)]
             arrays.append(swap(own, "pair", pairs, key))
-        beside = swap(row, "pair", pairs, 2)
         operators += [(3, op, op, 6) for op in range(per)]
         arrays += [
             swap(pack(arrays[1], [row, beside]), "pair", pairs, 4),
@@ -274,14 +279,15 @@
     shape = (2, comps, rows, depth)
     two = swap(normal_ops, "sec", sec, 2)
     one = swap(normal_ops, "sec", sec, 1)
-    arrays, operators, tables = chip_blocks(normal_ops, integrals, pairs)
+    beside = swap(integrals, "pair", pairs, 2)
     sibling = swap(integrals, "pair", pairs, 1)
-    high, low, site_part = prepare(basis, site_terms, rows, depth, sibling)
-    two = after(two, high)
+    high, low, site_part, row = prepare(basis, site_terms, integrals, rows, depth)
+    arrays, operators, tables = chip_blocks(normal_ops, row, beside, pairs)
+    two = after(two, sibling)
     three = swap(two, "sec", sec, 1)
     two = after(after(two, arrays[2]), one)
-    normals = [one, two, normal_ops, three]
-    held = arrays + [integrals, sibling]
+    normals = [three, one, normal_ops, two]
+    held = arrays + [row, sibling]
     here = [(len(arrays), None), (len(arrays) + 1, None)]
     mine, other = combine(held, operators, here, norms, shape)
     held = [two, swap(two, "pair", pairs, 1)] + arrays
@@ -290,19 +296,23 @@
     parts = combine(held, operators, tables, norms, shape)
     comp_ops = total([mine, swap(other, "pair", pairs, 1)], [parts[0]])
     far = swap(comp_ops, "sec", sec, 3)
-    near = swap(after(comp_ops, three), "sec", sec, 1)
-    summed = [parts[0]] + [
-        swap(after(part, comp_ops), "pair", pairs, key)
-        for part, key in zip(parts[1:], range(2, pairs, 2))
-    ]
+    near = swap(comp_ops, "sec", sec, 1)
+    last = pairs // 2
+    arrived = {
+        key: swap(parts[key // 2], "pair", pairs, key)
+        for key in range(2, pairs, 2)
+        if key != last
+    }
+    most = total([parts[0]] + list(arrived.values()), [])
+    rest = swap(after(parts[last // 2], comp_ops, arrived[2]), "pair", pairs, last)
     shape = (2, norms, sites, rows, cols)
-    early = renorm(normals, range(sec - 1), high, low, None, shape)
-    new_normal = renorm(normals, range(sec - 1, sec), high, low, early, shape, True)
+    early = renorm(normals, range(1, sec), high, low, None, shape)
+    new_normal = renorm(normals, range(1), high, low, early, shape, True)
     shape = (2, comps, sites, rows, cols)
-    arrived = [near, tuple(summed), comp_ops, far]
-    early = renorm(arrived, range(2, sec), high, low, site_part, shape)
-    early = renorm(arrived, range(1, 2), high, low, early, shape)
-    return new_normal, renorm(arrived, range(1), high, low, early, shape, True)
+    arrived = [far, near, comp_ops, (most, rest)]
+    early = renorm(arrived, range(2, 3), high, low, site_part, shape, awaited=[most])
+    early = renorm(arrived, range(2), high, low, early, shape)
+    return new_normal, renorm(arrived, range(3, sec), high, low, early, shape, True)
 
 
 def solution(mesh):

time: 36.1 us -> 36.4 us (level)
  waiting for transfers between devices: 8.52 us -> 8.96 us
    ppermute x15, waiting for transfers between devices: 8.52 us -> 8.96 us  [swap(): return lax.ppermute(x, axis, [(at, at ^ key) for at in range(size)])]
  transfers between devices with their start and end apart: 15 -> 15, of which waited for: 9 -> 7; matrix products, arithmetic and copies ran while one was open for 0% -> 0% of each run, Pallas kernels for 16% -> 16%
where the time goes in v5:
time: 36.4 us; the launch traced here: 36.2 us
  starting transfers between devices  16.4 us (45%)
  waiting for transfers between devices  8.96 us (25%)
  Pallas kernels  7.05 us (19%)
  local copies, waits for them, and re-layouts  2.96 us (8%)
  between operations  0.8 us (2%)
    ppermute x15, starting transfers between devices, swap(): return lax.ppermute(x, axis, [(at, at ^ key) for at in range(size)])  16.4 us
    ppermute x15, waiting for transfers between devices, swap(): return lax.ppermute(x, axis, [(at, at ^ key) for at in range(size)])  8.96 us
    pallas_call x5, Pallas kernels, renorm(): pl.pallas_call(functools.partial(renorm_kernel, steps, parts, carry is no...  5.03 us
    unnamed x10, local copies, waits for them, and re-layouts  2.96 us
    pallas_call x1, Pallas kernels, prepare(): call(functools.partial(prepare_kernel, depth), (half, half, part, jax.Sha...  0.97 us
    pallas_call x2, Pallas kernels, combine(): call(functools.partial(combine_kernel, operators, tables, per), (jax.Shap...  0.93 us
  transfers between devices with their start and end apart: 15, of which 7 were waited for; matrix products, arithmetic and copies ran while one was open for 0% of the time, Pallas kernels for 16%

profile of v5, /device:TPU:0, one launch (start us, length us, event | category | flops | bytes accessed | tf_op | source)
XLA Modules:
  0.0 36.2 jit_solution(6247861271424594517)
XLA Ops:
  0.6 3.0 %collective-permute-start.6 = (f32[2,2,128,128]{3,2,1,0:T(8,128)}, f32[2,2,128,128]{3,2,1,0:T(8,128)S(1)}, u32[]{:S(2)}, u32[]{:S(2)}) collective-permute-start(f32[2,2,128,128]{3,2,1,0:T(8,128)} %refs_0_.1), channel_id=1, source_target_pairs={{0,8},{4,12},{8,0},{12,4},{16,24},{20,28},{24,16},{28,20},{1,9},{5... | collective-permute-start | bytes 786440 | tf_op jit(solution)/shard_map/ppermute | solution.py:247
  3.6 2.6 %collective-permute-start = (f32[2,2,128,128]{3,2,1,0:T(8,128)}, f32[2,2,128,128]{3,2,1,0:T(8,128)S(1)}, u32[]{:S(2)}, u32[]{:S(2)}) collective-permute-start(f32[2,2,128,128]{3,2,1,0:T(8,128)} %refs_0_.1), channel_id=1, source_target_pairs={{0,2},{1,3},{2,0},{3,1},{4,6},{5,7},{6,4},{7,5},{8,10},{9,11},{10,... | collective-permute-start | bytes 786440 | tf_op jit(solution)/shard_map/ppermute | solution.py:247
  6.2 1.5 %collective-permute-start.4 = (f32[2,2,128,128]{3,2,1,0:T(8,128)}, f32[2,2,128,128]{3,2,1,0:T(8,128)S(1)}, u32[]{:S(2)}, u32[]{:S(2)}) collective-permute-start(f32[2,2,128,128]{3,2,1,0:T(8,128)} %refs_0_.1), channel_id=1, source_target_pairs={{0,16},{4,20},{8,24},{12,28},{16,0},{20,4},{24,8},{28,12},{1,17},{... | collective-permute-start | bytes 786440 | tf_op jit(solution)/shard_map/ppermute | solution.py:247
  7.7 1.6 %collective-permute-start.3 = (f32[2,2,128,128]{3,2,1,0:T(8,128)}, f32[2,2,128,128]{3,2,1,0:T(8,128)S(1)}, u32[]{:S(2)}, u32[]{:S(2)}) collective-permute-start(f32[2,2,128,128]{3,2,1,0:T(8,128)} %refs_0_.1), channel_id=1, source_target_pairs={{0,1},{1,0},{2,3},{3,2},{4,5},{5,4},{6,7},{7,6},{8,9},{9,8},{10,11... | collective-permute-start | bytes 786440 | tf_op jit(solution)/shard_map/ppermute | solution.py:247
  9.3 0.5 %collective-permute-start.7 = (f32[2,1,16]{2,1,0:T(1,128)}, f32[2,1,16]{2,1,0:T(1,128)S(1)}, u32[]{:S(2)}, u32[]{:S(2)}) collective-permute-start(f32[2,1,16]{2,1,0:T(1,128)} %integrals_ref.1), channel_id=1, source_target_pairs={{0,8},{4,12},{8,0},{12,4},{16,24},{20,28},{24,16},{28,20},{1,9},{5... | collective-permute-start | bytes 392 | tf_op jit(solution)/shard_map/ppermute | solution.py:247
  9.9 0.0 copy-start
  9.9 1.6 %copy-done = f32[2,4,512,128]{3,2,1,0:T(8,128)S(1)} copy-done((f32[2,4,512,128]{3,2,1,0:T(8,128)S(1)}, f32[2,4,512,128]{3,2,1,0:T(8,128)}, u32[]{:S(2)}) %copy-start) | copy-done | bytes 2097176
  11.4 0.0 copy-start.2
  11.4 0.7 %copy-done.2 = f32[2,1,4,4]{3,2,1,0:T(4,128)S(1)} copy-done((f32[2,1,4,4]{3,2,1,0:T(4,128)S(1)}, f32[2,1,4,4]{3,2,1,0:T(4,128)}, u32[]{:S(2)}) %copy-start.2) | copy-done | bytes 152
  12.1 0.0 copy-start.3
  12.1 0.7 %copy-done.3 = f32[2,1,16]{2,1,0:T(1,128)S(1)} copy-done((f32[2,1,16]{2,1,0:T(1,128)S(1)}, f32[2,1,16]{2,1,0:T(1,128)}, u32[]{:S(2)}) %copy-start.3) | copy-done | bytes 152
  12.8 0.0 copy-start.4
  12.8 0.0 copy-start.1
  12.8 1.0 %shard_map.60 = (bf16[1024,512]{1,0:T(8,128)(2,1)S(1)}, bf16[1024,512]{1,0:T(8,128)(2,1)S(1)}, f32[2,1,4,128,128]{4,3,2,1,0:T(8,128)S(1)}, f32[2,1,16]{2,1,0:T(1,128)S(1)}) custom-call(f32[2,4,512,128]{3,2,1,0:T(8,128)S(1)} %copy-done, f32[2,1,4,4]{3,2,1,0:T(4,128)S(1)} %copy-done.2, f32[2,1,16]{2,1,0:T(1,128)S(1)} %copy-done.3), custom_call_target="tpu_custom_call" | custom-call | flops 2097152 | bytes 4194304 | tf_op jit(solution)/shard_map/pallas_call | solution.py:85
  13.8 0.0 collective-permute-done.7.refs_1_.refs_7_.refs_5_
  13.8 0.0 collective-permute-done.6.block_ref.refs_3_.refs_1_
  13.8 0.6 %collective-permute-start.8 = (f32[2,2,136,128]{3,2,1,0:T(8,128)S(1)}, f32[2,2,136,128]{3,2,1,0:T(8,128)S(1)}, u32[]{:S(2)}, u32[]{:S(2)}) collective-permute-start(f32[2,2,136,128]{3,2,1,0:T(8,128)S(1)} %shard_map.65), channel_id=1, source_target_pairs={{0,16},{4,20},{8,24},{12,28},{16,0},{20,4},{24,8},{28,12},{1,17},{... | collective-permute-start | bytes 835592 | tf_op jit(solution)/shard_map/ppermute | solution.py:247
  14.4 0.0 copy-done.4
  14.4 0.0 collective-permute-start.1
  14.4 1.1 %collective-permute-done.1.refs_0_.refs_7_ = f32[2,1,16]{2,1,0:T(1,128)S(1)} collective-permute-done((f32[2,1,16]{2,1,0:T(1,128)S(1)}, f32[2,1,16]{2,1,0:T(1,128)S(1)}, u32[]{:S(2)}, u32[]{:S(2)}) %collective-permute-start.1) | collective-permute-done | bytes 160 | tf_op jit(solution)/shard_map/ppermute | solution.py:247
  15.6 2.7 %collective-permute-done.x_ref = f32[2,2,128,128]{3,2,1,0:T(8,128)S(1)} collective-permute-done((f32[2,2,128,128]{3,2,1,0:T(8,128)}, f32[2,2,128,128]{3,2,1,0:T(8,128)S(1)}, u32[]{:S(2)}, u32[]{:S(2)}) %collective-permute-start) | collective-permute-done | bytes 262176 | tf_op jit(solution)/shard_map/ppermute | solution.py:247
  18.3 0.0 collective-permute-done.4.refs_0_.refs_4_.refs_2_
  18.3 1.4 %collective-permute-done.3.refs_0_ = f32[2,2,128,128]{3,2,1,0:T(8,128)S(1)} collective-permute-done((f32[2,2,128,128]{3,2,1,0:T(8,128)}, f32[2,2,128,128]{3,2,1,0:T(8,128)S(1)}, u32[]{:S(2)}, u32[]{:S(2)}) %collective-permute-start.3) | collective-permute-done | bytes 262176 | tf_op jit(solution)/shard_map/ppermute | solution.py:247
  19.7 0.1 collective-permute-start.5
  19.8 0.3 collective-permute-start.2
  20.0 0.9 %collective-permute-done.8.refs_5_.refs_3_ = f32[2,2,136,128]{3,2,1,0:T(8,128)S(1)} collective-permute-done((f32[2,2,136,128]{3,2,1,0:T(8,128)S(1)}, f32[2,2,136,128]{3,2,1,0:T(8,128)S(1)}, u32[]{:S(2)}, u32[]{:S(2)}) %collective-permute-start.8) | collective-permute-done | bytes 278560 | tf_op jit(solution)/shard_map/ppermute | solution.py:247
  20.9 0.0 copy-done.1
  20.9 0.5 %shard_map.68 = (f32[2,1,128,128]{3,2,1,0:T(8,128)S(1)}, f32[2,1,128,128]{3,2,1,0:T(8,128)S(1)}) custom-call(f32[2,2,128,128]{3,2,1,0:T(8,128)S(1)} %copy-done.1, f32[2,2,128,128]{3,2,1,0:T(8,128)S(1)} %collective-permute-done.6.block_ref.refs_3_.refs_1_, f32[2,2,128,128]{3,2,1,0:T(8,128)S(1)} %collective-permute-done.4.refs_0_.refs_4_.refs_2_, ...), custom_call_target="tpu_custom_call" | custom-call | flops 2097152 | bytes 4194304 | tf_op jit(solution)/shard_map/pallas_call | solution.py:238
  21.4 0.1 collective-permute-start.11
  21.5 0.0 collective-permute-done.5.refs_1_
  21.5 0.5 %shard_map.66 = (f32[2,1,128,128]{3,2,1,0:T(8,128)S(1)}, f32[2,1,128,128]{3,2,1,0:T(8,128)S(1)}, f32[2,1,128,128]{3,2,1,0:T(8,128)S(1)}, f32[2,1,128,128]{3,2,1,0:T(8,128)S(1)}) custom-call(f32[2,2,128,128]{3,2,1,0:T(8,128)S(1)} %shard_map.62.refs_2_.refs_0_, f32[2,2,128,128]{3,2,1,0:T(8,128)S(1)} %collective-permute-done.5.refs_1_, ...), custom_call_target="tpu_custom_call" | custom-call | flops 2097152 | bytes 4194304 | tf_op jit(solution)/shard_map/pallas_call | solution.py:238
  21.9 1.6 %collective-permute-start.9 = (f32[2,1,128,128]{3,2,1,0:T(8,128)S(1)}, f32[2,1,128,128]{3,2,1,0:T(8,128)S(1)}, u32[]{:S(2)}, u32[]{:S(2)}) collective-permute-start(f32[2,1,128,128]{3,2,1,0:T(8,128)S(1)} %get-tuple-element.16), channel_id=1, source_target_pairs={{0,8},{4,12},{8,0},{12,4},{16,24},{20,28},{24,16},{28,20},{1,9},{5... | collective-permute-start | bytes 393224 | tf_op jit(solution)/shard_map/ppermute | solution.py:247
  23.5 0.8 %collective-permute-start.10 = (f32[2,1,128,128]{3,2,1,0:T(8,128)S(1)}, f32[2,1,128,128]{3,2,1,0:T(8,128)S(1)}, u32[]{:S(2)}, u32[]{:S(2)}) collective-permute-start(f32[2,1,128,128]{3,2,1,0:T(8,128)S(1)} %get-tuple-element.17), channel_id=1, source_target_pairs={{0,24},{4,28},{8,16},{12,20},{16,8},{20,12},{24,0},{28,4},{1,25},{... | collective-permute-start | bytes 393224 | tf_op jit(solution)/shard_map/ppermute | solution.py:247
  24.3 0.0 collective-permute-done.11.refs_1_
  24.3 2.6 %collective-permute-start.13 = (f32[2,1,128,128]{3,2,1,0:T(8,128)S(1)}, f32[2,1,128,128]{3,2,1,0:T(8,128)S(1)}, u32[]{:S(2)}, u32[]{:S(2)}) collective-permute-start(f32[2,1,128,128]{3,2,1,0:T(8,128)S(1)} %shard_map.69.refs_0_), channel_id=1, source_target_pairs={{0,3},{1,2},{2,1},{3,0},{4,7},{5,6},{6,5},{7,4},{8,11},{9,10},{10,... | collective-permute-start | bytes 393224 | tf_op jit(solution)/shard_map/ppermute | solution.py:247
  26.9 0.4 %collective-permute-start.14 = (f32[2,1,128,128]{3,2,1,0:T(8,128)S(1)}, f32[2,1,128,128]{3,2,1,0:T(8,128)S(1)}, u32[]{:S(2)}, u32[]{:S(2)}) collective-permute-start(f32[2,1,128,128]{3,2,1,0:T(8,128)S(1)} %shard_map.69.refs_0_), channel_id=1, source_target_pairs={{0,1},{1,0},{2,3},{3,2},{4,5},{5,4},{6,7},{7,6},{8,9},{9,8},{10,11... | collective-permute-start | bytes 393224 | tf_op jit(solution)/shard_map/ppermute | solution.py:247
  27.3 1.0 %collective-permute-done.9.refs_1_ = f32[2,1,128,128]{3,2,1,0:T(8,128)S(1)} collective-permute-done((f32[2,1,128,128]{3,2,1,0:T(8,128)S(1)}, f32[2,1,128,128]{3,2,1,0:T(8,128)S(1)}, u32[]{:S(2)}, u32[]{:S(2)}) %collective-permute-start.9) | collective-permute-done | bytes 131104 | tf_op jit(solution)/shard_map/ppermute | solution.py:247
  28.3 0.9 %collective-permute-start.12 = (f32[2,1,128,128]{3,2,1,0:T(8,128)S(1)}, f32[2,1,128,128]{3,2,1,0:T(8,128)S(1)}, u32[]{:S(2)}, u32[]{:S(2)}) collective-permute-start(f32[2,1,128,128]{3,2,1,0:T(8,128)S(1)} %shard_map.70), channel_id=1, source_target_pairs={{0,16},{4,20},{8,24},{12,28},{16,0},{20,4},{24,8},{28,12},{1,17},{... | collective-permute-start | bytes 393224 | tf_op jit(solution)/shard_map/ppermute | solution.py:247
  29.2 1.4 %shard_map.63.refs_3_ = f32[2,2,4,128,128]{4,3,2,1,0:T(8,128)S(1)} custom-call(f32[2,2,128,128]{3,2,1,0:T(8,128)S(1)} %collective-permute-done.3.refs_0_, f32[2,2,128,128]{3,2,1,0:T(8,128)S(1)} %copy-done.1, f32[2,2,128,128]{3,2,1,0:T(8,128)S(1)} %shard_map.62.refs_2_.refs_0_, bf16[1024,512]{1,0:T(8,128)(2,1)S(1)} %get-tuple-element.12.refs_3_.refs_1_.refs_2_, ...), custom_call_target="tpu_custom_call" | custom-call | flops 1207959552 | bytes 4194304 | tf_op jit(solution)/shard_map/pallas_call | solution.py:183
  30.6 0.0 collective-permute-done.2.refs_0_
  30.6 1.5 %shard_map.64 = f32[2,2,4,128,128]{4,3,2,1,0:T(8,128)} custom-call(f32[2,2,128,128]{3,2,1,0:T(8,128)S(1)} %collective-permute-done.2.refs_0_, bf16[1024,512]{1,0:T(8,128)(2,1)S(1)} %get-tuple-element.12.refs_3_.refs_1_.refs_2_, bf16[1024,512]{1,0:T(8,128)(2,1)S(1)} %get-tuple-element.13.refs_4_.refs_2_.refs_3_, f32[2,2,4,128,128]{4,3,2,1,0:T(8,128)S(1)} %shard_map.63.refs_3_), custom_call_target="tpu_custom_call" | custom-call | flops 402653184 | bytes 4194304 | tf_op jit(solution)/shard_map/pallas_call | solution.py:183
  32.1 0.0 collective-permute-done.10.refs_2_
  32.1 0.4 %shard_map.71.refs_4_ = f32[2,1,4,128,128]{4,3,2,1,0:T(8,128)S(1)} custom-call(f32[2,1,128,128]{3,2,1,0:T(8,128)S(1)} %shard_map.69.refs_0_, bf16[1024,512]{1,0:T(8,128)(2,1)S(1)} %get-tuple-element.12.refs_3_.refs_1_.refs_2_, bf16[1024,512]{1,0:T(8,128)(2,1)S(1)} %get-tuple-element.13.refs_4_.refs_2_.refs_3_, ...), custom_call_target="tpu_custom_call" | custom-call | flops 201326592 | bytes 4194304 | tf_op jit(solution)/shard_map/pallas_call | solution.py:183
  32.5 0.1 collective-permute-done.13.refs_0_
  32.6 1.8 %collective-permute-done.14.refs_1_ = f32[2,1,128,128]{3,2,1,0:T(8,128)S(1)} collective-permute-done((f32[2,1,128,128]{3,2,1,0:T(8,128)S(1)}, f32[2,1,128,128]{3,2,1,0:T(8,128)S(1)}, u32[]{:S(2)}, u32[]{:S(2)}) %collective-permute-start.14) | collective-permute-done | bytes 131104 | tf_op jit(solution)/shard_map/ppermute | solution.py:247
  34.4 0.6 %shard_map.72.refs_4_ = f32[2,1,4,128,128]{4,3,2,1,0:T(8,128)S(1)} custom-call(f32[2,1,128,128]{3,2,1,0:T(8,128)S(1)} %collective-permute-done.13.refs_0_, f32[2,1,128,128]{3,2,1,0:T(8,128)S(1)} %collective-permute-done.14.refs_1_, bf16[1024,512]{1,0:T(8,128)(2,1)S(1)} %get-tuple-element.12.refs_3_.refs_1_.refs_2_, ...), custom_call_target="tpu_custom_call" | custom-call | flops 402653184 | bytes 4194304 | tf_op jit(solution)/shard_map/pallas_call | solution.py:183
  35.0 0.0 collective-permute-done.12.refs_1_
  35.0 1.2 %shard_map.73 = f32[2,1,4,128,128]{4,3,2,1,0:T(8,128)} custom-call(f32[2,1,128,128]{3,2,1,0:T(8,128)S(1)} %shard_map.67.refs_4_.refs_0_, f32[2,1,128,128]{3,2,1,0:T(8,128)S(1)} %collective-permute-done.12.refs_1_, bf16[1024,512]{1,0:T(8,128)(2,1)S(1)} %get-tuple-element.12.refs_3_.refs_1_.refs_2_, ...), custom_call_target="tpu_custom_call" | custom-call | flops 201326592 | bytes 4194304 | tf_op jit(solution)/shard_map/pallas_call | solution.py:183
  (7 shorter events, 0.1 us)
Async XLA Ops:
  0.6 13.2 %collective-permute-start.6 = (f32[2,2,128,128]{3,2,1,0:T(8,128)}, f32[2,2,128,128]{3,2,1,0:T(8,128)S(1)}, u32[]{:S(2)}, u32[]{:S(2)}) collective-permute-start(f32[2,2,128,128]{3,2,1,0:T(8,128)} %refs_0_.1), channel_id=1, source_target_pairs={{0,8},{4,12},{8,0},{12,4},{16,24},{20,28},{24,16},{28,20},{1,9},{5... | collective-permute-start | bytes 786440 | tf_op jit(solution)/shard_map/ppermute | solution.py:247
  3.6 14.6 %collective-permute-start = (f32[2,2,128,128]{3,2,1,0:T(8,128)}, f32[2,2,128,128]{3,2,1,0:T(8,128)S(1)}, u32[]{:S(2)}, u32[]{:S(2)}) collective-permute-start(f32[2,2,128,128]{3,2,1,0:T(8,128)} %refs_0_.1), channel_id=1, source_target_pairs={{0,2},{1,3},{2,0},{3,1},{4,6},{5,7},{6,4},{7,5},{8,10},{9,11},{10,... | collective-permute-start | bytes 786440 | tf_op jit(solution)/shard_map/ppermute | solution.py:247
  6.2 12.1 %collective-permute-start.4 = (f32[2,2,128,128]{3,2,1,0:T(8,128)}, f32[2,2,128,128]{3,2,1,0:T(8,128)S(1)}, u32[]{:S(2)}, u32[]{:S(2)}) collective-permute-start(f32[2,2,128,128]{3,2,1,0:T(8,128)} %refs_0_.1), channel_id=1, source_target_pairs={{0,16},{4,20},{8,24},{12,28},{16,0},{20,4},{24,8},{28,12},{1,17},{... | collective-permute-start | bytes 786440 | tf_op jit(solution)/shard_map/ppermute | solution.py:247
  7.7 11.9 %collective-permute-start.3 = (f32[2,2,128,128]{3,2,1,0:T(8,128)}, f32[2,2,128,128]{3,2,1,0:T(8,128)S(1)}, u32[]{:S(2)}, u32[]{:S(2)}) collective-permute-start(f32[2,2,128,128]{3,2,1,0:T(8,128)} %refs_0_.1), channel_id=1, source_target_pairs={{0,1},{1,0},{2,3},{3,2},{4,5},{5,4},{6,7},{7,6},{8,9},{9,8},{10,11... | collective-permute-start | bytes 786440 | tf_op jit(solution)/shard_map/ppermute | solution.py:247
  9.3 4.5 %collective-permute-start.7 = (f32[2,1,16]{2,1,0:T(1,128)}, f32[2,1,16]{2,1,0:T(1,128)S(1)}, u32[]{:S(2)}, u32[]{:S(2)}) collective-permute-start(f32[2,1,16]{2,1,0:T(1,128)} %integrals_ref.1), channel_id=1, source_target_pairs={{0,8},{4,12},{8,0},{12,4},{16,24},{20,28},{24,16},{28,20},{1,9},{5... | collective-permute-start | bytes 392 | tf_op jit(solution)/shard_map/ppermute | solution.py:247
  9.9 1.6 %copy-start = (f32[2,4,512,128]{3,2,1,0:T(8,128)S(1)}, f32[2,4,512,128]{3,2,1,0:T(8,128)}, u32[]{:S(2)}) copy-start(f32[2,4,512,128]{3,2,1,0:T(8,128)} %basis_hbm.1) | copy-start | bytes 6291460
  11.4 0.7 %copy-start.2 = (f32[2,1,4,4]{3,2,1,0:T(4,128)S(1)}, f32[2,1,4,4]{3,2,1,0:T(4,128)}, u32[]{:S(2)}) copy-start(f32[2,1,4,4]{3,2,1,0:T(4,128)} %site_hbm.1) | copy-start | bytes 388
  12.1 0.7 %copy-start.3 = (f32[2,1,16]{2,1,0:T(1,128)S(1)}, f32[2,1,16]{2,1,0:T(1,128)}, u32[]{:S(2)}) copy-start(f32[2,1,16]{2,1,0:T(1,128)} %integrals_ref.1) | copy-start | bytes 388
  12.8 1.6 %copy-start.4 = (f32[2,1,16]{2,1,0:T(1,128)S(1)}, f32[2,1,16]{2,1,0:T(1,128)}, u32[]{:S(2)}) copy-start(f32[2,1,16]{2,1,0:T(1,128)} %integrals_ref.1) | copy-start | bytes 388
  12.8 8.1 %copy-start.1 = (f32[2,2,128,128]{3,2,1,0:T(8,128)S(1)}, f32[2,2,128,128]{3,2,1,0:T(8,128)}, u32[]{:S(2)}) copy-start(f32[2,2,128,128]{3,2,1,0:T(8,128)} %refs_0_.1) | copy-start | bytes 786436
  13.8 7.1 %collective-permute-start.8 = (f32[2,2,136,128]{3,2,1,0:T(8,128)S(1)}, f32[2,2,136,128]{3,2,1,0:T(8,128)S(1)}, u32[]{:S(2)}, u32[]{:S(2)}) collective-permute-start(f32[2,2,136,128]{3,2,1,0:T(8,128)S(1)} %shard_map.65), channel_id=1, source_target_pairs={{0,16},{4,20},{8,24},{12,28},{16,0},{20,4},{24,8},{28,12},{1,17},{... | collective-permute-start | bytes 835592 | tf_op jit(solution)/shard_map/ppermute | solution.py:247
  14.4 1.1 %collective-permute-start.1 = (f32[2,1,16]{2,1,0:T(1,128)S(1)}, f32[2,1,16]{2,1,0:T(1,128)S(1)}, u32[]{:S(2)}, u32[]{:S(2)}) collective-permute-start(f32[2,1,16]{2,1,0:T(1,128)S(1)} %copy-done.4), channel_id=1, source_target_pairs={{0,4},{4,0},{8,12},{12,8},{16,20},{20,16},{24,28},{28,24},{1,5},{5... | collective-permute-start | bytes 392 | tf_op jit(solution)/shard_map/ppermute | solution.py:247
  19.7 1.8 %collective-permute-start.5 = (f32[2,2,128,128]{3,2,1,0:T(8,128)S(1)}, f32[2,2,128,128]{3,2,1,0:T(8,128)S(1)}, u32[]{:S(2)}, u32[]{:S(2)}) collective-permute-start(f32[2,2,128,128]{3,2,1,0:T(8,128)S(1)} %shard_map.62.refs_2_.refs_0_), channel_id=1, source_target_pairs={{0,4},{4,0},{8,12},{12,8},{16,20},{20,16},{24,28},{28,24},{1,5},{5... | collective-permute-start | bytes 786440 | tf_op jit(solution)/shard_map/ppermute | solution.py:247
  19.8 10.8 %collective-permute-start.2 = (f32[2,2,128,128]{3,2,1,0:T(8,128)S(1)}, f32[2,2,128,128]{3,2,1,0:T(8,128)S(1)}, u32[]{:S(2)}, u32[]{:S(2)}) collective-permute-start(f32[2,2,128,128]{3,2,1,0:T(8,128)S(1)} %shard_map.59.x_ref), channel_id=1, source_target_pairs={{0,1},{1,0},{2,3},{3,2},{4,5},{5,4},{6,7},{7,6},{8,9},{9,8},{10,11... | collective-permute-start | bytes 786440 | tf_op jit(solution)/shard_map/ppermute | solution.py:247
  21.4 2.9 %collective-permute-start.11 = (f32[2,1,128,128]{3,2,1,0:T(8,128)S(1)}, f32[2,1,128,128]{3,2,1,0:T(8,128)S(1)}, u32[]{:S(2)}, u32[]{:S(2)}) collective-permute-start(f32[2,1,128,128]{3,2,1,0:T(8,128)S(1)} %get-tuple-element.20), channel_id=1, source_target_pairs={{0,4},{4,0},{8,12},{12,8},{16,20},{20,16},{24,28},{28,24},{1,5},{5... | collective-permute-start | bytes 393224 | tf_op jit(solution)/shard_map/ppermute | solution.py:247
  21.9 6.4 %collective-permute-start.9 = (f32[2,1,128,128]{3,2,1,0:T(8,128)S(1)}, f32[2,1,128,128]{3,2,1,0:T(8,128)S(1)}, u32[]{:S(2)}, u32[]{:S(2)}) collective-permute-start(f32[2,1,128,128]{3,2,1,0:T(8,128)S(1)} %get-tuple-element.16), channel_id=1, source_target_pairs={{0,8},{4,12},{8,0},{12,4},{16,24},{20,28},{24,16},{28,20},{1,9},{5... | collective-permute-start | bytes 393224 | tf_op jit(solution)/shard_map/ppermute | solution.py:247
  23.5 8.6 %collective-permute-start.10 = (f32[2,1,128,128]{3,2,1,0:T(8,128)S(1)}, f32[2,1,128,128]{3,2,1,0:T(8,128)S(1)}, u32[]{:S(2)}, u32[]{:S(2)}) collective-permute-start(f32[2,1,128,128]{3,2,1,0:T(8,128)S(1)} %get-tuple-element.17), channel_id=1, source_target_pairs={{0,24},{4,28},{8,16},{12,20},{16,8},{20,12},{24,0},{28,4},{1,25},{... | collective-permute-start | bytes 393224 | tf_op jit(solution)/shard_map/ppermute | solution.py:247
  24.3 8.4 %collective-permute-start.13 = (f32[2,1,128,128]{3,2,1,0:T(8,128)S(1)}, f32[2,1,128,128]{3,2,1,0:T(8,128)S(1)}, u32[]{:S(2)}, u32[]{:S(2)}) collective-permute-start(f32[2,1,128,128]{3,2,1,0:T(8,128)S(1)} %shard_map.69.refs_0_), channel_id=1, source_target_pairs={{0,3},{1,2},{2,1},{3,0},{4,7},{5,6},{6,5},{7,4},{8,11},{9,10},{10,... | collective-permute-start | bytes 393224 | tf_op jit(solution)/shard_map/ppermute | solution.py:247
  26.9 7.5 %collective-permute-start.14 = (f32[2,1,128,128]{3,2,1,0:T(8,128)S(1)}, f32[2,1,128,128]{3,2,1,0:T(8,128)S(1)}, u32[]{:S(2)}, u32[]{:S(2)}) collective-permute-start(f32[2,1,128,128]{3,2,1,0:T(8,128)S(1)} %shard_map.69.refs_0_), channel_id=1, source_target_pairs={{0,1},{1,0},{2,3},{3,2},{4,5},{5,4},{6,7},{7,6},{8,9},{9,8},{10,11... | collective-permute-start | bytes 393224 | tf_op jit(solution)/shard_map/ppermute | solution.py:247
  28.3 6.7 %collective-permute-start.12 = (f32[2,1,128,128]{3,2,1,0:T(8,128)S(1)}, f32[2,1,128,128]{3,2,1,0:T(8,128)S(1)}, u32[]{:S(2)}, u32[]{:S(2)}) collective-permute-start(f32[2,1,128,128]{3,2,1,0:T(8,128)S(1)} %shard_map.70), channel_id=1, source_target_pairs={{0,16},{4,20},{8,24},{12,28},{16,0},{20,4},{24,8},{28,12},{1,17},{... | collective-permute-start | bytes 393224 | tf_op jit(solution)/shard_map/ppermute | solution.py:247

commit v6 on v5

--- a/solution.py
+++ b/solution.py
@@ -15,14 +15,14 @@
 HBM = pl.BlockSpec(memory_space=pltpu.HBM)
 
 
-def call(kernel, out_shape, in_specs, flops, scratch_shapes=()):
+def call(kernel, out_shape, in_specs, flops, scratch_shapes=(), moved=4 << 20):
     return pl.pallas_call(
         kernel,
         out_shape=out_shape,
         in_specs=in_specs,
         out_specs=jax.tree.map(lambda _: VMEM, out_shape),
         scratch_shapes=scratch_shapes,
-        cost_estimate=pl.CostEstimate(flops=flops, bytes_accessed=4 << 20, transcendentals=0),
+        cost_estimate=pl.CostEstimate(flops=flops, bytes_accessed=moved, transcendentals=0),
         compiler_params=pltpu.CompilerParams(vmem_limit_bytes=VMEM_BYTES),
     )
 
@@ -33,7 +33,7 @@
 
 
 def order(sec):
-    return (3, 1, 0, 2) if sec == 4 else tuple(range(sec))
+    return (3, 0, 1, 2) if sec == 4 else tuple(range(sec))
 
 
 def prepare_kernel(depth, basis_hbm, site_hbm, integrals_ref, *refs):
@@ -93,6 +93,7 @@
             pltpu.SemaphoreType.DMA((2, sites)),
             pltpu.SemaphoreType.DMA,
         ],
+        4 << 20,
     )(basis, site_terms, integrals)
 
 
@@ -240,6 +241,7 @@
         (jax.ShapeDtypeStruct(shape, jnp.float32),) * len(tables),
         [VMEM] * len(arrays) + [ANY] * len(awaited),
         8 * len(tables) * len(operators) * rows * cols,
+        moved=4 << 20,
     )(*arrays, *awaited)
 
 
@@ -286,7 +288,7 @@
     two = after(two, sibling)
     three = swap(two, "sec", sec, 1)
     two = after(after(two, arrays[2]), one)
-    normals = [three, one, normal_ops, two]
+    normals = [three, normal_ops, one, two]
     held = arrays + [row, sibling]
     here = [(len(arrays), None), (len(arrays) + 1, None)]
     mine, other = combine(held, operators, here, norms, shape)
@@ -309,10 +311,9 @@
     early = renorm(normals, range(1, sec), high, low, None, shape)
     new_normal = renorm(normals, range(1), high, low, early, shape, True)
     shape = (2, comps, sites, rows, cols)
-    arrived = [far, near, comp_ops, (most, rest)]
-    early = renorm(arrived, range(2, 3), high, low, site_part, shape, awaited=[most])
-    early = renorm(arrived, range(2), high, low, early, shape)
-    return new_normal, renorm(arrived, range(3, sec), high, low, early, shape, True)
+    arrived = [far, comp_ops, near, (most, rest)]
+    early = renorm(arrived, range(2), high, low, site_part, shape, awaited=[most])
+    return new_normal, renorm(arrived, range(2, sec), high, low, early, shape, True)
 
 
 def solution(mesh):

time: 36.4 us -> 36 us (0.989)
    pallas_call x5 -> x4, Pallas kernels: 5.03 us -> 4.86 us  [renorm(): pl.pallas_call(functools.partial(renorm_kernel, steps, parts, carry is no...]
  transfers between devices with their start and end apart: 15 -> 15, of which waited for: 7 -> 8; matrix products, arithmetic and copies ran while one was open for 0% -> 0% of each run, Pallas kernels for 16% -> 15%
where the time goes in v6:
time: 36 us; the launch traced here: 35.8 us
  starting transfers between devices  16.4 us (46%)
  waiting for transfers between devices  8.75 us (24%)
  Pallas kernels  6.9 us (19%)
  local copies, waits for them, and re-layouts  2.96 us (8%)
  between operations  0.78 us (2%)
    ppermute x15, starting transfers between devices, swap(): return lax.ppermute(x, axis, [(at, at ^ key) for at in range(size)])  16.4 us
    ppermute x15, waiting for transfers between devices, swap(): return lax.ppermute(x, axis, [(at, at ^ key) for at in range(size)])  8.75 us
    pallas_call x4, Pallas kernels, renorm(): pl.pallas_call(functools.partial(renorm_kernel, steps, parts, carry is no...  4.86 us
    unnamed x10, local copies, waits for them, and re-layouts  2.96 us
    pallas_call x1, Pallas kernels, prepare(): call(functools.partial(prepare_kernel, depth), (half, half, part, jax.Sha...  0.97 us
    pallas_call x2, Pallas kernels, combine(): call(functools.partial(combine_kernel, operators, tables, per), (jax.Shap...  0.94 us
  transfers between devices with their start and end apart: 15, of which 8 were waited for; matrix products, arithmetic and copies ran while one was open for 0% of the time, Pallas kernels for 15%

profile of v6, /device:TPU:0, one launch (start us, length us, event | category | flops | bytes accessed | tf_op | source)
XLA Modules:
  0.0 35.8 jit_solution(457680813003620900)
XLA Ops:
  0.6 3.0 %collective-permute-start.5 = (f32[2,2,128,128]{3,2,1,0:T(8,128)}, f32[2,2,128,128]{3,2,1,0:T(8,128)S(1)}, u32[]{:S(2)}, u32[]{:S(2)}) collective-permute-start(f32[2,2,128,128]{3,2,1,0:T(8,128)} %refs_2_.1), channel_id=1, source_target_pairs={{0,8},{4,12},{8,0},{12,4},{16,24},{20,28},{24,16},{28,20},{1,9},{5... | collective-permute-start | bytes 786440 | tf_op jit(solution)/shard_map/ppermute | solution.py:249
  3.6 2.6 %collective-permute-start = (f32[2,2,128,128]{3,2,1,0:T(8,128)}, f32[2,2,128,128]{3,2,1,0:T(8,128)S(1)}, u32[]{:S(2)}, u32[]{:S(2)}) collective-permute-start(f32[2,2,128,128]{3,2,1,0:T(8,128)} %refs_2_.1), channel_id=1, source_target_pairs={{0,2},{1,3},{2,0},{3,1},{4,6},{5,7},{6,4},{7,5},{8,10},{9,11},{10,... | collective-permute-start | bytes 786440 | tf_op jit(solution)/shard_map/ppermute | solution.py:249
  6.2 1.5 %collective-permute-start.4 = (f32[2,2,128,128]{3,2,1,0:T(8,128)}, f32[2,2,128,128]{3,2,1,0:T(8,128)S(1)}, u32[]{:S(2)}, u32[]{:S(2)}) collective-permute-start(f32[2,2,128,128]{3,2,1,0:T(8,128)} %refs_2_.1), channel_id=1, source_target_pairs={{0,16},{4,20},{8,24},{12,28},{16,0},{20,4},{24,8},{28,12},{1,17},{... | collective-permute-start | bytes 786440 | tf_op jit(solution)/shard_map/ppermute | solution.py:249
  7.7 1.6 %collective-permute-start.3 = (f32[2,2,128,128]{3,2,1,0:T(8,128)}, f32[2,2,128,128]{3,2,1,0:T(8,128)S(1)}, u32[]{:S(2)}, u32[]{:S(2)}) collective-permute-start(f32[2,2,128,128]{3,2,1,0:T(8,128)} %refs_2_.1), channel_id=1, source_target_pairs={{0,1},{1,0},{2,3},{3,2},{4,5},{5,4},{6,7},{7,6},{8,9},{9,8},{10,11... | collective-permute-start | bytes 786440 | tf_op jit(solution)/shard_map/ppermute | solution.py:249
  9.3 0.5 %collective-permute-start.6 = (f32[2,1,16]{2,1,0:T(1,128)}, f32[2,1,16]{2,1,0:T(1,128)S(1)}, u32[]{:S(2)}, u32[]{:S(2)}) collective-permute-start(f32[2,1,16]{2,1,0:T(1,128)} %integrals_ref.1), channel_id=1, source_target_pairs={{0,8},{4,12},{8,0},{12,4},{16,24},{20,28},{24,16},{28,20},{1,9},{5... | collective-permute-start | bytes 392 | tf_op jit(solution)/shard_map/ppermute | solution.py:249
  9.9 0.0 copy-start
  9.9 1.6 %copy-done = f32[2,4,512,128]{3,2,1,0:T(8,128)S(1)} copy-done((f32[2,4,512,128]{3,2,1,0:T(8,128)S(1)}, f32[2,4,512,128]{3,2,1,0:T(8,128)}, u32[]{:S(2)}) %copy-start) | copy-done | bytes 2097176
  11.4 0.0 copy-start.2
  11.4 0.7 %copy-done.2 = f32[2,1,4,4]{3,2,1,0:T(4,128)S(1)} copy-done((f32[2,1,4,4]{3,2,1,0:T(4,128)S(1)}, f32[2,1,4,4]{3,2,1,0:T(4,128)}, u32[]{:S(2)}) %copy-start.2) | copy-done | bytes 152
  12.1 0.0 copy-start.3
  12.1 0.7 %copy-done.3 = f32[2,1,16]{2,1,0:T(1,128)S(1)} copy-done((f32[2,1,16]{2,1,0:T(1,128)S(1)}, f32[2,1,16]{2,1,0:T(1,128)}, u32[]{:S(2)}) %copy-start.3) | copy-done | bytes 152
  12.8 0.0 copy-start.4
  12.8 0.0 copy-start.1
  12.8 1.0 %shard_map.60 = (bf16[1024,512]{1,0:T(8,128)(2,1)S(1)}, bf16[1024,512]{1,0:T(8,128)(2,1)S(1)}, f32[2,1,4,128,128]{4,3,2,1,0:T(8,128)S(1)}, f32[2,1,16]{2,1,0:T(1,128)S(1)}) custom-call(f32[2,4,512,128]{3,2,1,0:T(8,128)S(1)} %copy-done, f32[2,1,4,4]{3,2,1,0:T(4,128)S(1)} %copy-done.2, f32[2,1,16]{2,1,0:T(1,128)S(1)} %copy-done.3), custom_call_target="tpu_custom_call" | custom-call | flops 2097152 | bytes 4194304 | tf_op jit(solution)/shard_map/pallas_call | solution.py:85
  13.8 0.0 collective-permute-done.6.refs_1_.refs_5_.refs_7_
  13.8 0.0 collective-permute-done.5.block_ref.refs_1_.refs_3_
  13.8 0.6 %collective-permute-start.7 = (f32[2,2,136,128]{3,2,1,0:T(8,128)S(1)}, f32[2,2,136,128]{3,2,1,0:T(8,128)S(1)}, u32[]{:S(2)}, u32[]{:S(2)}) collective-permute-start(f32[2,2,136,128]{3,2,1,0:T(8,128)S(1)} %shard_map.65), channel_id=1, source_target_pairs={{0,16},{4,20},{8,24},{12,28},{16,0},{20,4},{24,8},{28,12},{1,17},{... | collective-permute-start | bytes 835592 | tf_op jit(solution)/shard_map/ppermute | solution.py:249
  14.4 0.0 copy-done.4
  14.4 0.0 collective-permute-start.1
  14.4 1.1 %collective-permute-done.1.refs_0_.refs_7_ = f32[2,1,16]{2,1,0:T(1,128)S(1)} collective-permute-done((f32[2,1,16]{2,1,0:T(1,128)S(1)}, f32[2,1,16]{2,1,0:T(1,128)S(1)}, u32[]{:S(2)}, u32[]{:S(2)}) %collective-permute-start.1) | collective-permute-done | bytes 160 | tf_op jit(solution)/shard_map/ppermute | solution.py:249
  15.6 2.7 %collective-permute-done.x_ref = f32[2,2,128,128]{3,2,1,0:T(8,128)S(1)} collective-permute-done((f32[2,2,128,128]{3,2,1,0:T(8,128)}, f32[2,2,128,128]{3,2,1,0:T(8,128)S(1)}, u32[]{:S(2)}, u32[]{:S(2)}) %collective-permute-start) | collective-permute-done | bytes 262176 | tf_op jit(solution)/shard_map/ppermute | solution.py:249
  18.3 0.0 collective-permute-done.4.refs_0_.refs_2_.refs_4_
  18.3 1.4 %collective-permute-done.3.refs_0_.refs_1_ = f32[2,2,128,128]{3,2,1,0:T(8,128)S(1)} collective-permute-done((f32[2,2,128,128]{3,2,1,0:T(8,128)}, f32[2,2,128,128]{3,2,1,0:T(8,128)S(1)}, u32[]{:S(2)}, u32[]{:S(2)}) %collective-permute-start.3) | collective-permute-done | bytes 262176 | tf_op jit(solution)/shard_map/ppermute | solution.py:249
  19.7 0.1 collective-permute-start.9
  19.8 0.3 collective-permute-start.2
  20.0 0.9 %collective-permute-done.7.refs_3_.refs_5_ = f32[2,2,136,128]{3,2,1,0:T(8,128)S(1)} collective-permute-done((f32[2,2,136,128]{3,2,1,0:T(8,128)S(1)}, f32[2,2,136,128]{3,2,1,0:T(8,128)S(1)}, u32[]{:S(2)}, u32[]{:S(2)}) %collective-permute-start.7) | collective-permute-done | bytes 278560 | tf_op jit(solution)/shard_map/ppermute | solution.py:249
  20.9 0.0 copy-done.1
  20.9 0.5 %shard_map.66 = (f32[2,1,128,128]{3,2,1,0:T(8,128)S(1)}, f32[2,1,128,128]{3,2,1,0:T(8,128)S(1)}) custom-call(f32[2,2,128,128]{3,2,1,0:T(8,128)S(1)} %copy-done.1, f32[2,2,128,128]{3,2,1,0:T(8,128)S(1)} %collective-permute-done.5.block_ref.refs_1_.refs_3_, f32[2,2,128,128]{3,2,1,0:T(8,128)S(1)} %collective-permute-done.4.refs_0_.refs_2_.refs_4_, ...), custom_call_target="tpu_custom_call" | custom-call | flops 2097152 | bytes 4194304 | tf_op jit(solution)/shard_map/pallas_call | solution.py:239
  21.4 0.1 collective-permute-start.8
  21.5 0.0 collective-permute-done.9.refs_1_
  21.5 0.5 %shard_map.67 = (f32[2,1,128,128]{3,2,1,0:T(8,128)S(1)}, f32[2,1,128,128]{3,2,1,0:T(8,128)S(1)}, f32[2,1,128,128]{3,2,1,0:T(8,128)S(1)}, f32[2,1,128,128]{3,2,1,0:T(8,128)S(1)}) custom-call(f32[2,2,128,128]{3,2,1,0:T(8,128)S(1)} %shard_map.62.refs_2_.refs_0_, f32[2,2,128,128]{3,2,1,0:T(8,128)S(1)} %collective-permute-done.9.refs_1_, ...), custom_call_target="tpu_custom_call" | custom-call | flops 2097152 | bytes 4194304 | tf_op jit(solution)/shard_map/pallas_call | solution.py:239
  21.9 1.6 %collective-permute-start.11 = (f32[2,1,128,128]{3,2,1,0:T(8,128)S(1)}, f32[2,1,128,128]{3,2,1,0:T(8,128)S(1)}, u32[]{:S(2)}, u32[]{:S(2)}) collective-permute-start(f32[2,1,128,128]{3,2,1,0:T(8,128)S(1)} %get-tuple-element.18), channel_id=1, source_target_pairs={{0,8},{4,12},{8,0},{12,4},{16,24},{20,28},{24,16},{28,20},{1,9},{5... | collective-permute-start | bytes 393224 | tf_op jit(solution)/shard_map/ppermute | solution.py:249
  23.5 0.8 %collective-permute-start.12 = (f32[2,1,128,128]{3,2,1,0:T(8,128)S(1)}, f32[2,1,128,128]{3,2,1,0:T(8,128)S(1)}, u32[]{:S(2)}, u32[]{:S(2)}) collective-permute-start(f32[2,1,128,128]{3,2,1,0:T(8,128)S(1)} %get-tuple-element.19), channel_id=1, source_target_pairs={{0,24},{4,28},{8,16},{12,20},{16,8},{20,12},{24,0},{28,4},{1,25},{... | collective-permute-start | bytes 393224 | tf_op jit(solution)/shard_map/ppermute | solution.py:249
  24.3 0.0 collective-permute-done.8.refs_1_
  24.3 2.6 %collective-permute-start.14 = (f32[2,1,128,128]{3,2,1,0:T(8,128)S(1)}, f32[2,1,128,128]{3,2,1,0:T(8,128)S(1)}, u32[]{:S(2)}, u32[]{:S(2)}) collective-permute-start(f32[2,1,128,128]{3,2,1,0:T(8,128)S(1)} %shard_map.68.refs_0_.refs_1_), channel_id=1, source_target_pairs={{0,3},{1,2},{2,1},{3,0},{4,7},{5,6},{6,5},{7,4},{8,11},{9,10},{10,... | collective-permute-start | bytes 393224 | tf_op jit(solution)/shard_map/ppermute | solution.py:249
  26.9 0.4 %collective-permute-start.10 = (f32[2,1,128,128]{3,2,1,0:T(8,128)S(1)}, f32[2,1,128,128]{3,2,1,0:T(8,128)S(1)}, u32[]{:S(2)}, u32[]{:S(2)}) collective-permute-start(f32[2,1,128,128]{3,2,1,0:T(8,128)S(1)} %shard_map.68.refs_0_.refs_1_), channel_id=1, source_target_pairs={{0,1},{1,0},{2,3},{3,2},{4,5},{5,4},{6,7},{7,6},{8,9},{9,8},{10,11... | collective-permute-start | bytes 393224 | tf_op jit(solution)/shard_map/ppermute | solution.py:249
  27.3 1.0 %collective-permute-done.11.refs_1_ = f32[2,1,128,128]{3,2,1,0:T(8,128)S(1)} collective-permute-done((f32[2,1,128,128]{3,2,1,0:T(8,128)S(1)}, f32[2,1,128,128]{3,2,1,0:T(8,128)S(1)}, u32[]{:S(2)}, u32[]{:S(2)}) %collective-permute-start.11) | collective-permute-done | bytes 131104 | tf_op jit(solution)/shard_map/ppermute | solution.py:249
  28.3 0.9 %collective-permute-start.13 = (f32[2,1,128,128]{3,2,1,0:T(8,128)S(1)}, f32[2,1,128,128]{3,2,1,0:T(8,128)S(1)}, u32[]{:S(2)}, u32[]{:S(2)}) collective-permute-start(f32[2,1,128,128]{3,2,1,0:T(8,128)S(1)} %shard_map.70), channel_id=1, source_target_pairs={{0,16},{4,20},{8,24},{12,28},{16,0},{20,4},{24,8},{28,12},{1,17},{... | collective-permute-start | bytes 393224 | tf_op jit(solution)/shard_map/ppermute | solution.py:249
  29.2 1.4 %shard_map.63.refs_3_ = f32[2,2,4,128,128]{4,3,2,1,0:T(8,128)S(1)} custom-call(f32[2,2,128,128]{3,2,1,0:T(8,128)S(1)} %copy-done.1, f32[2,2,128,128]{3,2,1,0:T(8,128)S(1)} %collective-permute-done.3.refs_0_.refs_1_, f32[2,2,128,128]{3,2,1,0:T(8,128)S(1)} %shard_map.62.refs_2_.refs_0_, bf16[1024,512]{1,0:T(8,128)(2,1)S(1)} %get-tuple-element.12.refs_3_.refs_1_.refs_2_, ...), custom_call_target="tpu_custom_call" | custom-call | flops 1207959552 | bytes 4194304 | tf_op jit(solution)/shard_map/pallas_call | solution.py:184
  30.6 0.0 collective-permute-done.2.refs_0_
  30.6 1.5 %shard_map.64 = f32[2,2,4,128,128]{4,3,2,1,0:T(8,128)} custom-call(f32[2,2,128,128]{3,2,1,0:T(8,128)S(1)} %collective-permute-done.2.refs_0_, bf16[1024,512]{1,0:T(8,128)(2,1)S(1)} %get-tuple-element.12.refs_3_.refs_1_.refs_2_, bf16[1024,512]{1,0:T(8,128)(2,1)S(1)} %get-tuple-element.13.refs_4_.refs_2_.refs_3_, f32[2,2,4,128,128]{4,3,2,1,0:T(8,128)S(1)} %shard_map.63.refs_3_), custom_call_target="tpu_custom_call" | custom-call | flops 402653184 | bytes 4194304 | tf_op jit(solution)/shard_map/pallas_call | solution.py:184
  32.1 0.0 collective-permute-done.12.refs_2_
  32.2 0.5 %collective-permute-done.14.refs_0_ = f32[2,1,128,128]{3,2,1,0:T(8,128)S(1)} collective-permute-done((f32[2,1,128,128]{3,2,1,0:T(8,128)S(1)}, f32[2,1,128,128]{3,2,1,0:T(8,128)S(1)}, u32[]{:S(2)}, u32[]{:S(2)}) %collective-permute-start.14) | collective-permute-done | bytes 131104 | tf_op jit(solution)/shard_map/ppermute | solution.py:249
  32.6 0.6 %shard_map.71.refs_5_ = f32[2,1,4,128,128]{4,3,2,1,0:T(8,128)S(1)} custom-call(f32[2,1,128,128]{3,2,1,0:T(8,128)S(1)} %collective-permute-done.14.refs_0_, f32[2,1,128,128]{3,2,1,0:T(8,128)S(1)} %shard_map.68.refs_0_.refs_1_, bf16[1024,512]{1,0:T(8,128)(2,1)S(1)} %get-tuple-element.12.refs_3_.refs_1_.refs_2_, ...), custom_call_target="tpu_custom_call" | custom-call | flops 402653184 | bytes 4194304 | tf_op jit(solution)/shard_map/pallas_call | solution.py:184
  33.2 0.4 %collective-permute-done.13.refs_2_ = f32[2,1,128,128]{3,2,1,0:T(8,128)S(1)} collective-permute-done((f32[2,1,128,128]{3,2,1,0:T(8,128)S(1)}, f32[2,1,128,128]{3,2,1,0:T(8,128)S(1)}, u32[]{:S(2)}, u32[]{:S(2)}) %collective-permute-start.13) | collective-permute-done | bytes 131104 | tf_op jit(solution)/shard_map/ppermute | solution.py:249
  33.6 0.8 %collective-permute-done.10.refs_0_ = f32[2,1,128,128]{3,2,1,0:T(8,128)S(1)} collective-permute-done((f32[2,1,128,128]{3,2,1,0:T(8,128)S(1)}, f32[2,1,128,128]{3,2,1,0:T(8,128)S(1)}, u32[]{:S(2)}, u32[]{:S(2)}) %collective-permute-start.10) | collective-permute-done | bytes 131104 | tf_op jit(solution)/shard_map/ppermute | solution.py:249
  34.4 1.4 %shard_map.72 = f32[2,1,4,128,128]{4,3,2,1,0:T(8,128)} custom-call(f32[2,1,128,128]{3,2,1,0:T(8,128)S(1)} %collective-permute-done.10.refs_0_, f32[2,1,128,128]{3,2,1,0:T(8,128)S(1)} %shard_map.69.refs_5_.refs_1_, f32[2,1,128,128]{3,2,1,0:T(8,128)S(1)} %collective-permute-done.13.refs_2_, bf16[1024,512]{1,0:T(8,128)(2,1)S(1)} %get-tuple-element.12.refs_3_.refs_1_.refs_2_, ...), custom_call_target="tpu_custom_call" | custom-call | flops 402653184 | bytes 4194304 | tf_op jit(solution)/shard_map/pallas_call | solution.py:184
  (7 shorter events, 0.1 us)
Async XLA Ops:
  0.6 13.2 %collective-permute-start.5 = (f32[2,2,128,128]{3,2,1,0:T(8,128)}, f32[2,2,128,128]{3,2,1,0:T(8,128)S(1)}, u32[]{:S(2)}, u32[]{:S(2)}) collective-permute-start(f32[2,2,128,128]{3,2,1,0:T(8,128)} %refs_2_.1), channel_id=1, source_target_pairs={{0,8},{4,12},{8,0},{12,4},{16,24},{20,28},{24,16},{28,20},{1,9},{5... | collective-permute-start | bytes 786440 | tf_op jit(solution)/shard_map/ppermute | solution.py:249
  3.6 14.6 %collective-permute-start = (f32[2,2,128,128]{3,2,1,0:T(8,128)}, f32[2,2,128,128]{3,2,1,0:T(8,128)S(1)}, u32[]{:S(2)}, u32[]{:S(2)}) collective-permute-start(f32[2,2,128,128]{3,2,1,0:T(8,128)} %refs_2_.1), channel_id=1, source_target_pairs={{0,2},{1,3},{2,0},{3,1},{4,6},{5,7},{6,4},{7,5},{8,10},{9,11},{10,... | collective-permute-start | bytes 786440 | tf_op jit(solution)/shard_map/ppermute | solution.py:249
  6.2 12.1 %collective-permute-start.4 = (f32[2,2,128,128]{3,2,1,0:T(8,128)}, f32[2,2,128,128]{3,2,1,0:T(8,128)S(1)}, u32[]{:S(2)}, u32[]{:S(2)}) collective-permute-start(f32[2,2,128,128]{3,2,1,0:T(8,128)} %refs_2_.1), channel_id=1, source_target_pairs={{0,16},{4,20},{8,24},{12,28},{16,0},{20,4},{24,8},{28,12},{1,17},{... | collective-permute-start | bytes 786440 | tf_op jit(solution)/shard_map/ppermute | solution.py:249
  7.7 11.9 %collective-permute-start.3 = (f32[2,2,128,128]{3,2,1,0:T(8,128)}, f32[2,2,128,128]{3,2,1,0:T(8,128)S(1)}, u32[]{:S(2)}, u32[]{:S(2)}) collective-permute-start(f32[2,2,128,128]{3,2,1,0:T(8,128)} %refs_2_.1), channel_id=1, source_target_pairs={{0,1},{1,0},{2,3},{3,2},{4,5},{5,4},{6,7},{7,6},{8,9},{9,8},{10,11... | collective-permute-start | bytes 786440 | tf_op jit(solution)/shard_map/ppermute | solution.py:249
  9.3 4.5 %collective-permute-start.6 = (f32[2,1,16]{2,1,0:T(1,128)}, f32[2,1,16]{2,1,0:T(1,128)S(1)}, u32[]{:S(2)}, u32[]{:S(2)}) collective-permute-start(f32[2,1,16]{2,1,0:T(1,128)} %integrals_ref.1), channel_id=1, source_target_pairs={{0,8},{4,12},{8,0},{12,4},{16,24},{20,28},{24,16},{28,20},{1,9},{5... | collective-permute-start | bytes 392 | tf_op jit(solution)/shard_map/ppermute | solution.py:249
  9.9 1.6 %copy-start = (f32[2,4,512,128]{3,2,1,0:T(8,128)S(1)}, f32[2,4,512,128]{3,2,1,0:T(8,128)}, u32[]{:S(2)}) copy-start(f32[2,4,512,128]{3,2,1,0:T(8,128)} %basis_hbm.1) | copy-start | bytes 6291460
  11.4 0.7 %copy-start.2 = (f32[2,1,4,4]{3,2,1,0:T(4,128)S(1)}, f32[2,1,4,4]{3,2,1,0:T(4,128)}, u32[]{:S(2)}) copy-start(f32[2,1,4,4]{3,2,1,0:T(4,128)} %site_hbm.1) | copy-start | bytes 388
  12.1 0.7 %copy-start.3 = (f32[2,1,16]{2,1,0:T(1,128)S(1)}, f32[2,1,16]{2,1,0:T(1,128)}, u32[]{:S(2)}) copy-start(f32[2,1,16]{2,1,0:T(1,128)} %integrals_ref.1) | copy-start | bytes 388
  12.8 1.6 %copy-start.4 = (f32[2,1,16]{2,1,0:T(1,128)S(1)}, f32[2,1,16]{2,1,0:T(1,128)}, u32[]{:S(2)}) copy-start(f32[2,1,16]{2,1,0:T(1,128)} %integrals_ref.1) | copy-start | bytes 388
  12.8 8.1 %copy-start.1 = (f32[2,2,128,128]{3,2,1,0:T(8,128)S(1)}, f32[2,2,128,128]{3,2,1,0:T(8,128)}, u32[]{:S(2)}) copy-start(f32[2,2,128,128]{3,2,1,0:T(8,128)} %refs_2_.1) | copy-start | bytes 786436
  13.8 7.1 %collective-permute-start.7 = (f32[2,2,136,128]{3,2,1,0:T(8,128)S(1)}, f32[2,2,136,128]{3,2,1,0:T(8,128)S(1)}, u32[]{:S(2)}, u32[]{:S(2)}) collective-permute-start(f32[2,2,136,128]{3,2,1,0:T(8,128)S(1)} %shard_map.65), channel_id=1, source_target_pairs={{0,16},{4,20},{8,24},{12,28},{16,0},{20,4},{24,8},{28,12},{1,17},{... | collective-permute-start | bytes 835592 | tf_op jit(solution)/shard_map/ppermute | solution.py:249
  14.4 1.1 %collective-permute-start.1 = (f32[2,1,16]{2,1,0:T(1,128)S(1)}, f32[2,1,16]{2,1,0:T(1,128)S(1)}, u32[]{:S(2)}, u32[]{:S(2)}) collective-permute-start(f32[2,1,16]{2,1,0:T(1,128)S(1)} %copy-done.4), channel_id=1, source_target_pairs={{0,4},{4,0},{8,12},{12,8},{16,20},{20,16},{24,28},{28,24},{1,5},{5... | collective-permute-start | bytes 392 | tf_op jit(solution)/shard_map/ppermute | solution.py:249
  19.7 1.8 %collective-permute-start.9 = (f32[2,2,128,128]{3,2,1,0:T(8,128)S(1)}, f32[2,2,128,128]{3,2,1,0:T(8,128)S(1)}, u32[]{:S(2)}, u32[]{:S(2)}) collective-permute-start(f32[2,2,128,128]{3,2,1,0:T(8,128)S(1)} %shard_map.62.refs_2_.refs_0_), channel_id=1, source_target_pairs={{0,4},{4,0},{8,12},{12,8},{16,20},{20,16},{24,28},{28,24},{1,5},{5... | collective-permute-start | bytes 786440 | tf_op jit(solution)/shard_map/ppermute | solution.py:249
  19.8 10.8 %collective-permute-start.2 = (f32[2,2,128,128]{3,2,1,0:T(8,128)S(1)}, f32[2,2,128,128]{3,2,1,0:T(8,128)S(1)}, u32[]{:S(2)}, u32[]{:S(2)}) collective-permute-start(f32[2,2,128,128]{3,2,1,0:T(8,128)S(1)} %shard_map.59.x_ref), channel_id=1, source_target_pairs={{0,1},{1,0},{2,3},{3,2},{4,5},{5,4},{6,7},{7,6},{8,9},{9,8},{10,11... | collective-permute-start | bytes 786440 | tf_op jit(solution)/shard_map/ppermute | solution.py:249
  21.4 2.9 %collective-permute-start.8 = (f32[2,1,128,128]{3,2,1,0:T(8,128)S(1)}, f32[2,1,128,128]{3,2,1,0:T(8,128)S(1)}, u32[]{:S(2)}, u32[]{:S(2)}) collective-permute-start(f32[2,1,128,128]{3,2,1,0:T(8,128)S(1)} %get-tuple-element.16), channel_id=1, source_target_pairs={{0,4},{4,0},{8,12},{12,8},{16,20},{20,16},{24,28},{28,24},{1,5},{5... | collective-permute-start | bytes 393224 | tf_op jit(solution)/shard_map/ppermute | solution.py:249
  21.9 6.4 %collective-permute-start.11 = (f32[2,1,128,128]{3,2,1,0:T(8,128)S(1)}, f32[2,1,128,128]{3,2,1,0:T(8,128)S(1)}, u32[]{:S(2)}, u32[]{:S(2)}) collective-permute-start(f32[2,1,128,128]{3,2,1,0:T(8,128)S(1)} %get-tuple-element.18), channel_id=1, source_target_pairs={{0,8},{4,12},{8,0},{12,4},{16,24},{20,28},{24,16},{28,20},{1,9},{5... | collective-permute-start | bytes 393224 | tf_op jit(solution)/shard_map/ppermute | solution.py:249
  23.5 8.6 %collective-permute-start.12 = (f32[2,1,128,128]{3,2,1,0:T(8,128)S(1)}, f32[2,1,128,128]{3,2,1,0:T(8,128)S(1)}, u32[]{:S(2)}, u32[]{:S(2)}) collective-permute-start(f32[2,1,128,128]{3,2,1,0:T(8,128)S(1)} %get-tuple-element.19), channel_id=1, source_target_pairs={{0,24},{4,28},{8,16},{12,20},{16,8},{20,12},{24,0},{28,4},{1,25},{... | collective-permute-start | bytes 393224 | tf_op jit(solution)/shard_map/ppermute | solution.py:249
  24.3 8.4 %collective-permute-start.14 = (f32[2,1,128,128]{3,2,1,0:T(8,128)S(1)}, f32[2,1,128,128]{3,2,1,0:T(8,128)S(1)}, u32[]{:S(2)}, u32[]{:S(2)}) collective-permute-start(f32[2,1,128,128]{3,2,1,0:T(8,128)S(1)} %shard_map.68.refs_0_.refs_1_), channel_id=1, source_target_pairs={{0,3},{1,2},{2,1},{3,0},{4,7},{5,6},{6,5},{7,4},{8,11},{9,10},{10,... | collective-permute-start | bytes 393224 | tf_op jit(solution)/shard_map/ppermute | solution.py:249
  26.9 7.5 %collective-permute-start.10 = (f32[2,1,128,128]{3,2,1,0:T(8,128)S(1)}, f32[2,1,128,128]{3,2,1,0:T(8,128)S(1)}, u32[]{:S(2)}, u32[]{:S(2)}) collective-permute-start(f32[2,1,128,128]{3,2,1,0:T(8,128)S(1)} %shard_map.68.refs_0_.refs_1_), channel_id=1, source_target_pairs={{0,1},{1,0},{2,3},{3,2},{4,5},{5,4},{6,7},{7,6},{8,9},{9,8},{10,11... | collective-permute-start | bytes 393224 | tf_op jit(solution)/shard_map/ppermute | solution.py:249
  28.3 5.3 %collective-permute-start.13 = (f32[2,1,128,128]{3,2,1,0:T(8,128)S(1)}, f32[2,1,128,128]{3,2,1,0:T(8,128)S(1)}, u32[]{:S(2)}, u32[]{:S(2)}) collective-permute-start(f32[2,1,128,128]{3,2,1,0:T(8,128)S(1)} %shard_map.70), channel_id=1, source_target_pairs={{0,16},{4,20},{8,24},{12,28},{16,0},{20,4},{24,8},{28,12},{1,17},{... | collective-permute-start | bytes 393224 | tf_op jit(solution)/shard_map/ppermute | solution.py:249

commit v7 on v6

--- a/solution.py
+++ b/solution.py
@@ -37,8 +37,8 @@
 
 
 def prepare_kernel(depth, basis_hbm, site_hbm, integrals_ref, *refs):
-    high_ref, low_ref, part_ref, row_ref = refs[:4]
-    scratch = refs[4:]
+    split_ref, part_ref, row_ref = refs[:3]
+    scratch = refs[3:]
     row_ref[...] = integrals_ref[...]
     basis_ref, site_ref, basis_sem, site_sem = scratch
     _, sites, old, cols = basis_ref.shape
@@ -59,10 +59,10 @@
         copy.wait()
         for step, far in enumerate(order(old // depth)):
             start = pl.multiple_of((me ^ far) * depth, depth)
-            at = pl.ds((step * 2 + part) * depth, depth)
             high, low = split(basis_ref[part, site, pl.ds(start, depth), :])
-            high_ref[at, pl.ds(site * cols, cols)] = high
-            low_ref[at, pl.ds(site * cols, cols)] = low
+            for which, value in enumerate((high, low, high)):
+                at = pl.ds(((step * 3 + which) * 2 + part) * depth, depth)
+                split_ref[at, pl.ds(site * cols, cols)] = value
     site_copy.wait()
     for comp in range(part_ref.shape[1]):
         for site in range(sites):
@@ -80,11 +80,11 @@
 def prepare(basis, site_terms, integrals, rows, depth):
     _, sites, old, cols = basis.shape
     comps = site_terms.shape[1]
-    half = jax.ShapeDtypeStruct((2 * old, sites * cols), jnp.bfloat16)
+    halves = jax.ShapeDtypeStruct((6 * old, sites * cols), jnp.bfloat16)
     part = jax.ShapeDtypeStruct((2, comps, sites, rows, cols), jnp.float32)
     return call(
         functools.partial(prepare_kernel, depth),
-        (half, half, part, jax.ShapeDtypeStruct(integrals.shape, integrals.dtype)),
+        (halves, part, jax.ShapeDtypeStruct(integrals.shape, integrals.dtype)),
         [HBM, HBM, VMEM],
         8 * comps * sites * sites * rows * cols,
         [
@@ -124,9 +124,9 @@
 
 def renorm_kernel(steps, parts, carried, awaited, streamed, *refs):
     count = sum(parts)
-    high_ref, low_ref = refs[count : count + 2]
-    first = count + 2 + carried + awaited
-    out_ref, left_high, left_low = refs[first : first + 3]
+    split_ref = refs[count]
+    first = count + 1 + carried + awaited
+    out_ref, left = refs[first : first + 2]
     out_hbm, out_ref, sems = (out_ref,) + refs[-2:] if streamed else (None, out_ref, None)
     _, ops, sites, rows, cols = out_ref.shape
     depth = refs[0].shape[-1]
@@ -135,20 +135,18 @@
         first = sum(parts[:step])
         value = sum(refs[at][:, :, :rows, :] for at in range(first + 1, first + parts[step]))
         value = (refs[first][:, :, :rows, :] + value).reshape(2, tall, depth)
-        for scratch, real, imag in zip((left_high, left_low), split(value[0]), split(value[1])):
-            at = 2 * step * depth
-            scratch[:tall, at : at + depth] = real
-            scratch[:tall, at + depth : at + 2 * depth] = -imag
-            scratch[tall:, at : at + depth] = imag
-            scratch[tall:, at + depth : at + 2 * depth] = real
-    dot = functools.partial(jnp.dot, preferred_element_type=jnp.float32)
-    deep = slice(2 * depth * steps[0], 2 * depth * (steps[-1] + 1))
+        (rh, rl), (ih, il) = split(value[0]), split(value[1])
+        for which, (real, imag) in enumerate(((rh, ih), (rh, ih), (rl, il))):
+            at = 2 * (step * 3 + which) * depth
+            left[:tall, at : at + depth] = real
+            left[:tall, at + depth : at + 2 * depth] = -imag
+            left[tall:, at : at + depth] = imag
+            left[tall:, at + depth : at + 2 * depth] = real
+    deep = slice(6 * depth * steps[0], 6 * depth * (steps[-1] + 1))
     copies = []
     for first in range(0, sites * cols, WIDE):
         at = (deep, slice(first, first + WIDE))
-        total = dot(left_high[...], high_ref[at])
-        total = total + dot(left_high[...], low_ref[at])
-        total = total + dot(left_low[...], high_ref[at])
+        total = jnp.dot(left[...], split_ref[at], preferred_element_type=jnp.float32)
         some = range(first // cols, (first + WIDE) // cols)
         for part in range(2):
             for op in range(ops):
@@ -157,7 +155,7 @@
                     start = part * tall + op * rows
                     value = total[start : start + rows, across]
                     if carried:
-                        value = value + refs[count + 2][part, op, site]
+                        value = value + refs[count + 1][part, op, site]
                     out_ref[part, op, site] = value
                 if streamed:
                     piece = (part, op, pl.ds(some.start, len(some)))
@@ -171,14 +169,14 @@
         copy.wait()
 
 
-def renorm(blocks, steps, high, low, carry, shape, streamed=False, awaited=()):
+def renorm(blocks, steps, basis, carry, shape, streamed=False, awaited=()):
     blocks = [block if isinstance(block, tuple) else (block,) for block in blocks]
     blocks = blocks[steps.start : steps.stop]
     parts = tuple(len(block) for block in blocks)
-    args = sum(blocks, ()) + (high, low) + (() if carry is None else (carry,))
+    args = sum(blocks, ()) + (basis,) + (() if carry is None else (carry,))
     _, ops, sites, rows, cols = shape
     depth = blocks[0][0].shape[-1]
-    left = pltpu.VMEM((2 * ops * rows, 2 * depth * len(blocks)), jnp.bfloat16)
+    left = pltpu.VMEM((2 * ops * rows, 6 * depth * len(blocks)), jnp.bfloat16)
     pieces = 2 * ops * sites * cols // WIDE
     held = [pltpu.VMEM(shape, jnp.float32), pltpu.SemaphoreType.DMA((pieces,))]
     return pl.pallas_call(
@@ -188,7 +186,7 @@
         out_shape=jax.ShapeDtypeStruct(shape, jnp.float32),
         in_specs=[VMEM] * len(args) + [ANY] * len(awaited),
         out_specs=HBM if streamed else VMEM,
-        scratch_shapes=[left, left] + (held if streamed else []),
+        scratch_shapes=[left] + (held if streamed else []),
         cost_estimate=pl.CostEstimate(
             flops=24 * ops * rows * depth * len(blocks) * sites * cols,
             bytes_accessed=4 << 20,
@@ -283,7 +281,7 @@
     one = swap(normal_ops, "sec", sec, 1)
     beside = swap(integrals, "pair", pairs, 2)
     sibling = swap(integrals, "pair", pairs, 1)
-    high, low, site_part, row = prepare(basis, site_terms, integrals, rows, depth)
+    basis_split, site_part, row = prepare(basis, site_terms, integrals, rows, depth)
     arrays, operators, tables = chip_blocks(normal_ops, row, beside, pairs)
     two = after(two, sibling)
     three = swap(two, "sec", sec, 1)
@@ -308,12 +306,12 @@
     most = total([parts[0]] + list(arrived.values()), [])
     rest = swap(after(parts[last // 2], comp_ops, arrived[2]), "pair", pairs, last)
     shape = (2, norms, sites, rows, cols)
-    early = renorm(normals, range(1, sec), high, low, None, shape)
-    new_normal = renorm(normals, range(1), high, low, early, shape, True)
+    early = renorm(normals, range(1, sec), basis_split, None, shape)
+    new_normal = renorm(normals, range(1), basis_split, early, shape, True)
     shape = (2, comps, sites, rows, cols)
     arrived = [far, comp_ops, near, (most, rest)]
-    early = renorm(arrived, range(2), high, low, site_part, shape, awaited=[most])
-    return new_normal, renorm(arrived, range(2, sec), high, low, early, shape, True)
+    early = renorm(arrived, range(2), basis_split, site_part, shape, awaited=[most])
+    return new_normal, renorm(arrived, range(2, sec), basis_split, early, shape, True)
 
 
 def solution(mesh):

time: 36 us -> 36 us (level)
    unnamed x10 -> x8, local copies, waits for them, and re-layouts: 2.96 us -> 2.96 us
where the time goes in v7:
time: 36 us; the launch traced here: 35.8 us
  starting transfers between devices  16.4 us (46%)
  waiting for transfers between devices  8.79 us (24%)
  Pallas kernels  6.9 us (19%)
  local copies, waits for them, and re-layouts  2.96 us (8%)
  between operations  0.79 us (2%)
    ppermute x15, starting transfers between devices, swap(): return lax.ppermute(x, axis, [(at, at ^ key) for at in range(size)])  16.4 us
    ppermute x15, waiting for transfers between devices, swap(): return lax.ppermute(x, axis, [(at, at ^ key) for at in range(size)])  8.79 us
    pallas_call x4, Pallas kernels, renorm(): pl.pallas_call(functools.partial(renorm_kernel, steps, parts, carry is no...  4.85 us
    unnamed x8, local copies, waits for them, and re-layouts  2.96 us
    pallas_call x1, Pallas kernels, prepare(): call(functools.partial(prepare_kernel, depth), (halves, part, jax.ShapeDt...  0.99 us
    pallas_call x2, Pallas kernels, combine(): call(functools.partial(combine_kernel, operators, tables, per), (jax.Shap...  0.93 us
  transfers between devices with their start and end apart: 15, of which 8 were waited for; matrix products, arithmetic and copies ran while one was open for 0% of the time, Pallas kernels for 15%

profile of v7, /device:TPU:0, one launch (start us, length us, event | category | flops | bytes accessed | tf_op | source)
XLA Modules:
  0.0 35.8 jit_solution(9196183482402790464)
XLA Ops:
  0.6 0.0 copy-start
  0.6 3.0 %collective-permute-start.5 = (f32[2,2,128,128]{3,2,1,0:T(8,128)}, f32[2,2,128,128]{3,2,1,0:T(8,128)S(1)}, u32[]{:S(2)}, u32[]{:S(2)}) collective-permute-start(f32[2,2,128,128]{3,2,1,0:T(8,128)} %refs_2_.1), channel_id=1, source_target_pairs={{0,8},{4,12},{8,0},{12,4},{16,24},{20,28},{24,16},{28,20},{1,9},{5... | collective-permute-start | bytes 786440 | tf_op jit(solution)/shard_map/ppermute | solution.py:247
  3.6 2.6 %collective-permute-start = (f32[2,2,128,128]{3,2,1,0:T(8,128)}, f32[2,2,128,128]{3,2,1,0:T(8,128)S(1)}, u32[]{:S(2)}, u32[]{:S(2)}) collective-permute-start(f32[2,2,128,128]{3,2,1,0:T(8,128)} %refs_2_.1), channel_id=1, source_target_pairs={{0,2},{1,3},{2,0},{3,1},{4,6},{5,7},{6,4},{7,5},{8,10},{9,11},{10,... | collective-permute-start | bytes 786440 | tf_op jit(solution)/shard_map/ppermute | solution.py:247
  6.2 1.5 %collective-permute-start.4 = (f32[2,2,128,128]{3,2,1,0:T(8,128)}, f32[2,2,128,128]{3,2,1,0:T(8,128)S(1)}, u32[]{:S(2)}, u32[]{:S(2)}) collective-permute-start(f32[2,2,128,128]{3,2,1,0:T(8,128)} %refs_2_.1), channel_id=1, source_target_pairs={{0,16},{4,20},{8,24},{12,28},{16,0},{20,4},{24,8},{28,12},{1,17},{... | collective-permute-start | bytes 786440 | tf_op jit(solution)/shard_map/ppermute | solution.py:247
  7.8 1.6 %collective-permute-start.3 = (f32[2,2,128,128]{3,2,1,0:T(8,128)}, f32[2,2,128,128]{3,2,1,0:T(8,128)S(1)}, u32[]{:S(2)}, u32[]{:S(2)}) collective-permute-start(f32[2,2,128,128]{3,2,1,0:T(8,128)} %refs_2_.1), channel_id=1, source_target_pairs={{0,1},{1,0},{2,3},{3,2},{4,5},{5,4},{6,7},{7,6},{8,9},{9,8},{10,11... | collective-permute-start | bytes 786440 | tf_op jit(solution)/shard_map/ppermute | solution.py:247
  9.3 0.5 %collective-permute-start.6 = (f32[2,1,16]{2,1,0:T(1,128)}, f32[2,1,16]{2,1,0:T(1,128)S(1)}, u32[]{:S(2)}, u32[]{:S(2)}) collective-permute-start(f32[2,1,16]{2,1,0:T(1,128)} %integrals_ref.1), channel_id=1, source_target_pairs={{0,8},{4,12},{8,0},{12,4},{16,24},{20,28},{24,16},{28,20},{1,9},{5... | collective-permute-start | bytes 392 | tf_op jit(solution)/shard_map/ppermute | solution.py:247
  9.9 0.0 copy-start.1
  9.9 1.6 %copy-done.1 = f32[2,4,512,128]{3,2,1,0:T(8,128)S(1)} copy-done((f32[2,4,512,128]{3,2,1,0:T(8,128)S(1)}, f32[2,4,512,128]{3,2,1,0:T(8,128)}, u32[]{:S(2)}) %copy-start.1) | copy-done | bytes 2097176
  11.5 0.0 copy-start.2
  11.5 0.7 %copy-done.2 = f32[2,1,4,4]{3,2,1,0:T(4,128)S(1)} copy-done((f32[2,1,4,4]{3,2,1,0:T(4,128)S(1)}, f32[2,1,4,4]{3,2,1,0:T(4,128)}, u32[]{:S(2)}) %copy-start.2) | copy-done | bytes 152
  12.1 0.0 copy-start.3
  12.1 0.7 %copy-done.3 = f32[2,1,16]{2,1,0:T(1,128)S(1)} copy-done((f32[2,1,16]{2,1,0:T(1,128)S(1)}, f32[2,1,16]{2,1,0:T(1,128)}, u32[]{:S(2)}) %copy-start.3) | copy-done | bytes 152
  12.8 1.0 %shard_map.60 = (bf16[3072,512]{1,0:T(8,128)(2,1)S(1)}, f32[2,1,4,128,128]{4,3,2,1,0:T(8,128)S(1)}, f32[2,1,16]{2,1,0:T(1,128)S(1)}) custom-call(f32[2,4,512,128]{3,2,1,0:T(8,128)S(1)} %copy-done.1, f32[2,1,4,4]{3,2,1,0:T(4,128)S(1)} %copy-done.2, f32[2,1,16]{2,1,0:T(1,128)S(1)} %copy-done.3), custom_call_target="tpu_custom_call" | custom-call | flops 2097152 | bytes 4194304 | tf_op jit(solution)/shard_map/pallas_call | solution.py:85
  13.8 0.0 collective-permute-done.6.refs_1_.refs_5_.refs_7_
  13.8 0.0 collective-permute-done.5.block_ref.refs_1_.refs_3_
  13.9 0.6 %collective-permute-start.7 = (f32[2,2,136,128]{3,2,1,0:T(8,128)S(1)}, f32[2,2,136,128]{3,2,1,0:T(8,128)S(1)}, u32[]{:S(2)}, u32[]{:S(2)}) collective-permute-start(f32[2,2,136,128]{3,2,1,0:T(8,128)S(1)} %shard_map.65), channel_id=1, source_target_pairs={{0,16},{4,20},{8,24},{12,28},{16,0},{20,4},{24,8},{28,12},{1,17},{... | collective-permute-start | bytes 835592 | tf_op jit(solution)/shard_map/ppermute | solution.py:247
  14.4 0.0 collective-permute-start.1
  14.5 1.1 %collective-permute-done.1.refs_0_.refs_7_ = f32[2,1,16]{2,1,0:T(1,128)S(1)} collective-permute-done((f32[2,1,16]{2,1,0:T(1,128)S(1)}, f32[2,1,16]{2,1,0:T(1,128)S(1)}, u32[]{:S(2)}, u32[]{:S(2)}) %collective-permute-start.1) | collective-permute-done | bytes 160 | tf_op jit(solution)/shard_map/ppermute | solution.py:247
  15.6 2.7 %collective-permute-done.x_ref = f32[2,2,128,128]{3,2,1,0:T(8,128)S(1)} collective-permute-done((f32[2,2,128,128]{3,2,1,0:T(8,128)}, f32[2,2,128,128]{3,2,1,0:T(8,128)S(1)}, u32[]{:S(2)}, u32[]{:S(2)}) %collective-permute-start) | collective-permute-done | bytes 262176 | tf_op jit(solution)/shard_map/ppermute | solution.py:247
  18.3 0.0 collective-permute-done.4.refs_0_.refs_2_.refs_4_
  18.3 1.4 %collective-permute-done.3.refs_0_.refs_1_ = f32[2,2,128,128]{3,2,1,0:T(8,128)S(1)} collective-permute-done((f32[2,2,128,128]{3,2,1,0:T(8,128)}, f32[2,2,128,128]{3,2,1,0:T(8,128)S(1)}, u32[]{:S(2)}, u32[]{:S(2)}) %collective-permute-start.3) | collective-permute-done | bytes 262176 | tf_op jit(solution)/shard_map/ppermute | solution.py:247
  19.7 0.1 collective-permute-start.9
  19.8 0.3 collective-permute-start.2
  20.0 0.9 %collective-permute-done.7.refs_3_.refs_5_ = f32[2,2,136,128]{3,2,1,0:T(8,128)S(1)} collective-permute-done((f32[2,2,136,128]{3,2,1,0:T(8,128)S(1)}, f32[2,2,136,128]{3,2,1,0:T(8,128)S(1)}, u32[]{:S(2)}, u32[]{:S(2)}) %collective-permute-start.7) | collective-permute-done | bytes 278560 | tf_op jit(solution)/shard_map/ppermute | solution.py:247
  20.9 0.0 copy-done
  20.9 0.5 %shard_map.66 = (f32[2,1,128,128]{3,2,1,0:T(8,128)S(1)}, f32[2,1,128,128]{3,2,1,0:T(8,128)S(1)}) custom-call(f32[2,2,128,128]{3,2,1,0:T(8,128)S(1)} %copy-done, f32[2,2,128,128]{3,2,1,0:T(8,128)S(1)} %collective-permute-done.5.block_ref.refs_1_.refs_3_, f32[2,2,128,128]{3,2,1,0:T(8,128)S(1)} %collective-permute-done.4.refs_0_.refs_2_.refs_4_, ...), custom_call_target="tpu_custom_call" | custom-call | flops 2097152 | bytes 4194304 | tf_op jit(solution)/shard_map/pallas_call | solution.py:237
  21.4 0.1 collective-permute-start.8
  21.5 0.0 collective-permute-done.9.refs_1_
  21.5 0.5 %shard_map.67 = (f32[2,1,128,128]{3,2,1,0:T(8,128)S(1)}, f32[2,1,128,128]{3,2,1,0:T(8,128)S(1)}, f32[2,1,128,128]{3,2,1,0:T(8,128)S(1)}, f32[2,1,128,128]{3,2,1,0:T(8,128)S(1)}) custom-call(f32[2,2,128,128]{3,2,1,0:T(8,128)S(1)} %shard_map.62.refs_2_.refs_0_, f32[2,2,128,128]{3,2,1,0:T(8,128)S(1)} %collective-permute-done.9.refs_1_, ...), custom_call_target="tpu_custom_call" | custom-call | flops 2097152 | bytes 4194304 | tf_op jit(solution)/shard_map/pallas_call | solution.py:237
  22.0 1.6 %collective-permute-start.11 = (f32[2,1,128,128]{3,2,1,0:T(8,128)S(1)}, f32[2,1,128,128]{3,2,1,0:T(8,128)S(1)}, u32[]{:S(2)}, u32[]{:S(2)}) collective-permute-start(f32[2,1,128,128]{3,2,1,0:T(8,128)S(1)} %get-tuple-element.16), channel_id=1, source_target_pairs={{0,8},{4,12},{8,0},{12,4},{16,24},{20,28},{24,16},{28,20},{1,9},{5... | collective-permute-start | bytes 393224 | tf_op jit(solution)/shard_map/ppermute | solution.py:247
  23.5 0.7 %collective-permute-start.12 = (f32[2,1,128,128]{3,2,1,0:T(8,128)S(1)}, f32[2,1,128,128]{3,2,1,0:T(8,128)S(1)}, u32[]{:S(2)}, u32[]{:S(2)}) collective-permute-start(f32[2,1,128,128]{3,2,1,0:T(8,128)S(1)} %get-tuple-element.17), channel_id=1, source_target_pairs={{0,24},{4,28},{8,16},{12,20},{16,8},{20,12},{24,0},{28,4},{1,25},{... | collective-permute-start | bytes 393224 | tf_op jit(solution)/shard_map/ppermute | solution.py:247
  24.3 0.0 collective-permute-done.8.refs_1_
  24.3 2.6 %collective-permute-start.14 = (f32[2,1,128,128]{3,2,1,0:T(8,128)S(1)}, f32[2,1,128,128]{3,2,1,0:T(8,128)S(1)}, u32[]{:S(2)}, u32[]{:S(2)}) collective-permute-start(f32[2,1,128,128]{3,2,1,0:T(8,128)S(1)} %shard_map.68.refs_0_.refs_1_), channel_id=1, source_target_pairs={{0,3},{1,2},{2,1},{3,0},{4,7},{5,6},{6,5},{7,4},{8,11},{9,10},{10,... | collective-permute-start | bytes 393224 | tf_op jit(solution)/shard_map/ppermute | solution.py:247
  26.9 0.4 %collective-permute-start.10 = (f32[2,1,128,128]{3,2,1,0:T(8,128)S(1)}, f32[2,1,128,128]{3,2,1,0:T(8,128)S(1)}, u32[]{:S(2)}, u32[]{:S(2)}) collective-permute-start(f32[2,1,128,128]{3,2,1,0:T(8,128)S(1)} %shard_map.68.refs_0_.refs_1_), channel_id=1, source_target_pairs={{0,1},{1,0},{2,3},{3,2},{4,5},{5,4},{6,7},{7,6},{8,9},{9,8},{10,11... | collective-permute-start | bytes 393224 | tf_op jit(solution)/shard_map/ppermute | solution.py:247
  27.3 1.0 %collective-permute-done.11.refs_1_ = f32[2,1,128,128]{3,2,1,0:T(8,128)S(1)} collective-permute-done((f32[2,1,128,128]{3,2,1,0:T(8,128)S(1)}, f32[2,1,128,128]{3,2,1,0:T(8,128)S(1)}, u32[]{:S(2)}, u32[]{:S(2)}) %collective-permute-start.11) | collective-permute-done | bytes 131104 | tf_op jit(solution)/shard_map/ppermute | solution.py:247
  28.4 0.8 %collective-permute-start.13 = (f32[2,1,128,128]{3,2,1,0:T(8,128)S(1)}, f32[2,1,128,128]{3,2,1,0:T(8,128)S(1)}, u32[]{:S(2)}, u32[]{:S(2)}) collective-permute-start(f32[2,1,128,128]{3,2,1,0:T(8,128)S(1)} %shard_map.70), channel_id=1, source_target_pairs={{0,16},{4,20},{8,24},{12,28},{16,0},{20,4},{24,8},{28,12},{1,17},{... | collective-permute-start | bytes 393224 | tf_op jit(solution)/shard_map/ppermute | solution.py:247
  29.2 1.4 %shard_map.63.refs_2_ = f32[2,2,4,128,128]{4,3,2,1,0:T(8,128)S(1)} custom-call(f32[2,2,128,128]{3,2,1,0:T(8,128)S(1)} %copy-done, f32[2,2,128,128]{3,2,1,0:T(8,128)S(1)} %collective-permute-done.3.refs_0_.refs_1_, f32[2,2,128,128]{3,2,1,0:T(8,128)S(1)} %shard_map.62.refs_2_.refs_0_, bf16[3072,512]{1,0:T(8,128)(2,1)S(1)} %get-tuple-element.11.refs_3_.refs_1_.refs_2_), custom_call_target="tpu_custom_call" | custom-call | flops 1207959552 | bytes 4194304 | tf_op jit(solution)/shard_map/pallas_call | solution.py:182
  30.6 0.0 collective-permute-done.2.refs_0_
  30.6 1.5 %shard_map.64 = f32[2,2,4,128,128]{4,3,2,1,0:T(8,128)} custom-call(f32[2,2,128,128]{3,2,1,0:T(8,128)S(1)} %collective-permute-done.2.refs_0_, bf16[3072,512]{1,0:T(8,128)(2,1)S(1)} %get-tuple-element.11.refs_3_.refs_1_.refs_2_, f32[2,2,4,128,128]{4,3,2,1,0:T(8,128)S(1)} %shard_map.63.refs_2_), custom_call_target="tpu_custom_call" | custom-call | flops 402653184 | bytes 4194304 | tf_op jit(solution)/shard_map/pallas_call | solution.py:182
  32.1 0.0 collective-permute-done.12.refs_2_
  32.2 0.5 %collective-permute-done.14.refs_0_ = f32[2,1,128,128]{3,2,1,0:T(8,128)S(1)} collective-permute-done((f32[2,1,128,128]{3,2,1,0:T(8,128)S(1)}, f32[2,1,128,128]{3,2,1,0:T(8,128)S(1)}, u32[]{:S(2)}, u32[]{:S(2)}) %collective-permute-start.14) | collective-permute-done | bytes 131104 | tf_op jit(solution)/shard_map/ppermute | solution.py:247
  32.6 0.6 %shard_map.71.refs_4_ = f32[2,1,4,128,128]{4,3,2,1,0:T(8,128)S(1)} custom-call(f32[2,1,128,128]{3,2,1,0:T(8,128)S(1)} %collective-permute-done.14.refs_0_, f32[2,1,128,128]{3,2,1,0:T(8,128)S(1)} %shard_map.68.refs_0_.refs_1_, bf16[3072,512]{1,0:T(8,128)(2,1)S(1)} %get-tuple-element.11.refs_3_.refs_1_.refs_2_, ...), custom_call_target="tpu_custom_call" | custom-call | flops 402653184 | bytes 4194304 | tf_op jit(solution)/shard_map/pallas_call | solution.py:182
  33.2 0.4 %collective-permute-done.13.refs_2_ = f32[2,1,128,128]{3,2,1,0:T(8,128)S(1)} collective-permute-done((f32[2,1,128,128]{3,2,1,0:T(8,128)S(1)}, f32[2,1,128,128]{3,2,1,0:T(8,128)S(1)}, u32[]{:S(2)}, u32[]{:S(2)}) %collective-permute-start.13) | collective-permute-done | bytes 131104 | tf_op jit(solution)/shard_map/ppermute | solution.py:247
  33.6 0.8 %collective-permute-done.10.refs_0_ = f32[2,1,128,128]{3,2,1,0:T(8,128)S(1)} collective-permute-done((f32[2,1,128,128]{3,2,1,0:T(8,128)S(1)}, f32[2,1,128,128]{3,2,1,0:T(8,128)S(1)}, u32[]{:S(2)}, u32[]{:S(2)}) %collective-permute-start.10) | collective-permute-done | bytes 131104 | tf_op jit(solution)/shard_map/ppermute | solution.py:247
  34.4 1.4 %shard_map.72 = f32[2,1,4,128,128]{4,3,2,1,0:T(8,128)} custom-call(f32[2,1,128,128]{3,2,1,0:T(8,128)S(1)} %collective-permute-done.10.refs_0_, f32[2,1,128,128]{3,2,1,0:T(8,128)S(1)} %shard_map.69.refs_4_.refs_1_, f32[2,1,128,128]{3,2,1,0:T(8,128)S(1)} %collective-permute-done.13.refs_2_, bf16[3072,512]{1,0:T(8,128)(2,1)S(1)} %get-tuple-element.11.refs_3_.refs_1_.refs_2_, ...), custom_call_target="tpu_custom_call" | custom-call | flops 402653184 | bytes 4194304 | tf_op jit(solution)/shard_map/pallas_call | solution.py:182
  (7 shorter events, 0.1 us)
Async XLA Ops:
  0.6 20.3 %copy-start = (f32[2,2,128,128]{3,2,1,0:T(8,128)S(1)}, f32[2,2,128,128]{3,2,1,0:T(8,128)}, u32[]{:S(2)}) copy-start(f32[2,2,128,128]{3,2,1,0:T(8,128)} %refs_2_.1) | copy-start | bytes 786436
  0.6 13.2 %collective-permute-start.5 = (f32[2,2,128,128]{3,2,1,0:T(8,128)}, f32[2,2,128,128]{3,2,1,0:T(8,128)S(1)}, u32[]{:S(2)}, u32[]{:S(2)}) collective-permute-start(f32[2,2,128,128]{3,2,1,0:T(8,128)} %refs_2_.1), channel_id=1, source_target_pairs={{0,8},{4,12},{8,0},{12,4},{16,24},{20,28},{24,16},{28,20},{1,9},{5... | collective-permute-start | bytes 786440 | tf_op jit(solution)/shard_map/ppermute | solution.py:247
  3.6 14.6 %collective-permute-start = (f32[2,2,128,128]{3,2,1,0:T(8,128)}, f32[2,2,128,128]{3,2,1,0:T(8,128)S(1)}, u32[]{:S(2)}, u32[]{:S(2)}) collective-permute-start(f32[2,2,128,128]{3,2,1,0:T(8,128)} %refs_2_.1), channel_id=1, source_target_pairs={{0,2},{1,3},{2,0},{3,1},{4,6},{5,7},{6,4},{7,5},{8,10},{9,11},{10,... | collective-permute-start | bytes 786440 | tf_op jit(solution)/shard_map/ppermute | solution.py:247
  6.2 12.1 %collective-permute-start.4 = (f32[2,2,128,128]{3,2,1,0:T(8,128)}, f32[2,2,128,128]{3,2,1,0:T(8,128)S(1)}, u32[]{:S(2)}, u32[]{:S(2)}) collective-permute-start(f32[2,2,128,128]{3,2,1,0:T(8,128)} %refs_2_.1), channel_id=1, source_target_pairs={{0,16},{4,20},{8,24},{12,28},{16,0},{20,4},{24,8},{28,12},{1,17},{... | collective-permute-start | bytes 786440 | tf_op jit(solution)/shard_map/ppermute | solution.py:247
  7.8 11.9 %collective-permute-start.3 = (f32[2,2,128,128]{3,2,1,0:T(8,128)}, f32[2,2,128,128]{3,2,1,0:T(8,128)S(1)}, u32[]{:S(2)}, u32[]{:S(2)}) collective-permute-start(f32[2,2,128,128]{3,2,1,0:T(8,128)} %refs_2_.1), channel_id=1, source_target_pairs={{0,1},{1,0},{2,3},{3,2},{4,5},{5,4},{6,7},{7,6},{8,9},{9,8},{10,11... | collective-permute-start | bytes 786440 | tf_op jit(solution)/shard_map/ppermute | solution.py:247
  9.3 4.5 %collective-permute-start.6 = (f32[2,1,16]{2,1,0:T(1,128)}, f32[2,1,16]{2,1,0:T(1,128)S(1)}, u32[]{:S(2)}, u32[]{:S(2)}) collective-permute-start(f32[2,1,16]{2,1,0:T(1,128)} %integrals_ref.1), channel_id=1, source_target_pairs={{0,8},{4,12},{8,0},{12,4},{16,24},{20,28},{24,16},{28,20},{1,9},{5... | collective-permute-start | bytes 392 | tf_op jit(solution)/shard_map/ppermute | solution.py:247
  9.9 1.6 %copy-start.1 = (f32[2,4,512,128]{3,2,1,0:T(8,128)S(1)}, f32[2,4,512,128]{3,2,1,0:T(8,128)}, u32[]{:S(2)}) copy-start(f32[2,4,512,128]{3,2,1,0:T(8,128)} %basis_hbm.1) | copy-start | bytes 6291460
  11.5 0.7 %copy-start.2 = (f32[2,1,4,4]{3,2,1,0:T(4,128)S(1)}, f32[2,1,4,4]{3,2,1,0:T(4,128)}, u32[]{:S(2)}) copy-start(f32[2,1,4,4]{3,2,1,0:T(4,128)} %site_hbm.1) | copy-start | bytes 388
  12.1 0.7 %copy-start.3 = (f32[2,1,16]{2,1,0:T(1,128)S(1)}, f32[2,1,16]{2,1,0:T(1,128)}, u32[]{:S(2)}) copy-start(f32[2,1,16]{2,1,0:T(1,128)} %integrals_ref.1) | copy-start | bytes 388
  13.9 7.1 %collective-permute-start.7 = (f32[2,2,136,128]{3,2,1,0:T(8,128)S(1)}, f32[2,2,136,128]{3,2,1,0:T(8,128)S(1)}, u32[]{:S(2)}, u32[]{:S(2)}) collective-permute-start(f32[2,2,136,128]{3,2,1,0:T(8,128)S(1)} %shard_map.65), channel_id=1, source_target_pairs={{0,16},{4,20},{8,24},{12,28},{16,0},{20,4},{24,8},{28,12},{1,17},{... | collective-permute-start | bytes 835592 | tf_op jit(solution)/shard_map/ppermute | solution.py:247
  14.4 1.1 %collective-permute-start.1 = (f32[2,1,16]{2,1,0:T(1,128)S(1)}, f32[2,1,16]{2,1,0:T(1,128)S(1)}, u32[]{:S(2)}, u32[]{:S(2)}) collective-permute-start(f32[2,1,16]{2,1,0:T(1,128)S(1)} %copy-done.3), channel_id=1, source_target_pairs={{0,4},{4,0},{8,12},{12,8},{16,20},{20,16},{24,28},{28,24},{1,5},{5... | collective-permute-start | bytes 392 | tf_op jit(solution)/shard_map/ppermute | solution.py:247
  19.7 1.8 %collective-permute-start.9 = (f32[2,2,128,128]{3,2,1,0:T(8,128)S(1)}, f32[2,2,128,128]{3,2,1,0:T(8,128)S(1)}, u32[]{:S(2)}, u32[]{:S(2)}) collective-permute-start(f32[2,2,128,128]{3,2,1,0:T(8,128)S(1)} %shard_map.62.refs_2_.refs_0_), channel_id=1, source_target_pairs={{0,4},{4,0},{8,12},{12,8},{16,20},{20,16},{24,28},{28,24},{1,5},{5... | collective-permute-start | bytes 786440 | tf_op jit(solution)/shard_map/ppermute | solution.py:247
  19.8 10.8 %collective-permute-start.2 = (f32[2,2,128,128]{3,2,1,0:T(8,128)S(1)}, f32[2,2,128,128]{3,2,1,0:T(8,128)S(1)}, u32[]{:S(2)}, u32[]{:S(2)}) collective-permute-start(f32[2,2,128,128]{3,2,1,0:T(8,128)S(1)} %shard_map.59.x_ref), channel_id=1, source_target_pairs={{0,1},{1,0},{2,3},{3,2},{4,5},{5,4},{6,7},{7,6},{8,9},{9,8},{10,11... | collective-permute-start | bytes 786440 | tf_op jit(solution)/shard_map/ppermute | solution.py:247
  21.4 2.8 %collective-permute-start.8 = (f32[2,1,128,128]{3,2,1,0:T(8,128)S(1)}, f32[2,1,128,128]{3,2,1,0:T(8,128)S(1)}, u32[]{:S(2)}, u32[]{:S(2)}) collective-permute-start(f32[2,1,128,128]{3,2,1,0:T(8,128)S(1)} %get-tuple-element.14), channel_id=1, source_target_pairs={{0,4},{4,0},{8,12},{12,8},{16,20},{20,16},{24,28},{28,24},{1,5},{5... | collective-permute-start | bytes 393224 | tf_op jit(solution)/shard_map/ppermute | solution.py:247
  22.0 6.4 %collective-permute-start.11 = (f32[2,1,128,128]{3,2,1,0:T(8,128)S(1)}, f32[2,1,128,128]{3,2,1,0:T(8,128)S(1)}, u32[]{:S(2)}, u32[]{:S(2)}) collective-permute-start(f32[2,1,128,128]{3,2,1,0:T(8,128)S(1)} %get-tuple-element.16), channel_id=1, source_target_pairs={{0,8},{4,12},{8,0},{12,4},{16,24},{20,28},{24,16},{28,20},{1,9},{5... | collective-permute-start | bytes 393224 | tf_op jit(solution)/shard_map/ppermute | solution.py:247
  23.5 8.6 %collective-permute-start.12 = (f32[2,1,128,128]{3,2,1,0:T(8,128)S(1)}, f32[2,1,128,128]{3,2,1,0:T(8,128)S(1)}, u32[]{:S(2)}, u32[]{:S(2)}) collective-permute-start(f32[2,1,128,128]{3,2,1,0:T(8,128)S(1)} %get-tuple-element.17), channel_id=1, source_target_pairs={{0,24},{4,28},{8,16},{12,20},{16,8},{20,12},{24,0},{28,4},{1,25},{... | collective-permute-start | bytes 393224 | tf_op jit(solution)/shard_map/ppermute | solution.py:247
  24.3 8.3 %collective-permute-start.14 = (f32[2,1,128,128]{3,2,1,0:T(8,128)S(1)}, f32[2,1,128,128]{3,2,1,0:T(8,128)S(1)}, u32[]{:S(2)}, u32[]{:S(2)}) collective-permute-start(f32[2,1,128,128]{3,2,1,0:T(8,128)S(1)} %shard_map.68.refs_0_.refs_1_), channel_id=1, source_target_pairs={{0,3},{1,2},{2,1},{3,0},{4,7},{5,6},{6,5},{7,4},{8,11},{9,10},{10,... | collective-permute-start | bytes 393224 | tf_op jit(solution)/shard_map/ppermute | solution.py:247
  26.9 7.5 %collective-permute-start.10 = (f32[2,1,128,128]{3,2,1,0:T(8,128)S(1)}, f32[2,1,128,128]{3,2,1,0:T(8,128)S(1)}, u32[]{:S(2)}, u32[]{:S(2)}) collective-permute-start(f32[2,1,128,128]{3,2,1,0:T(8,128)S(1)} %shard_map.68.refs_0_.refs_1_), channel_id=1, source_target_pairs={{0,1},{1,0},{2,3},{3,2},{4,5},{5,4},{6,7},{7,6},{8,9},{9,8},{10,11... | collective-permute-start | bytes 393224 | tf_op jit(solution)/shard_map/ppermute | solution.py:247
  28.4 5.2 %collective-permute-start.13 = (f32[2,1,128,128]{3,2,1,0:T(8,128)S(1)}, f32[2,1,128,128]{3,2,1,0:T(8,128)S(1)}, u32[]{:S(2)}, u32[]{:S(2)}) collective-permute-start(f32[2,1,128,128]{3,2,1,0:T(8,128)S(1)} %shard_map.70), channel_id=1, source_target_pairs={{0,16},{4,20},{8,24},{12,28},{16,0},{20,4},{24,8},{28,12},{1,17},{... | collective-permute-start | bytes 393224 | tf_op jit(solution)/shard_map/ppermute | solution.py:247

commit v8 on v7

--- a/solution.py
+++ b/solution.py
@@ -285,7 +285,7 @@
     arrays, operators, tables = chip_blocks(normal_ops, row, beside, pairs)
     two = after(two, sibling)
     three = swap(two, "sec", sec, 1)
-    two = after(after(two, arrays[2]), one)
+    two = after(after(two, one), arrays[2])
     normals = [three, normal_ops, one, two]
     held = arrays + [row, sibling]
     here = [(len(arrays), None), (len(arrays) + 1, None)]

time: 36 us -> 36.3 us (level)
  starting transfers between devices: 16.4 us -> 18.1 us
  waiting for transfers between devices: 8.79 us -> 7.4 us
    ppermute x15, starting transfers between devices: 16.4 us -> 18.1 us  [swap(): return lax.ppermute(x, axis, [(at, at ^ key) for at in range(size)])]
    ppermute x15, waiting for transfers between devices: 8.79 us -> 7.4 us  [swap(): return lax.ppermute(x, axis, [(at, at ^ key) for at in range(size)])]
  transfers between devices with their start and end apart: 15 -> 15, of which waited for: 8 -> 7; matrix products, arithmetic and copies ran while one was open for 0% -> 0% of each run, Pallas kernels for 15% -> 15%
where the time goes in v8:
time: 36.3 us; the launch traced here: 36.1 us
  starting transfers between devices  18.1 us (50%)
  waiting for transfers between devices  7.4 us (20%)
  Pallas kernels  6.9 us (19%)
  local copies, waits for them, and re-layouts  2.96 us (8%)
  between operations  0.79 us (2%)
    ppermute x15, starting transfers between devices, swap(): return lax.ppermute(x, axis, [(at, at ^ key) for at in range(size)])  18.1 us
    ppermute x15, waiting for transfers between devices, swap(): return lax.ppermute(x, axis, [(at, at ^ key) for at in range(size)])  7.4 us
    pallas_call x4, Pallas kernels, renorm(): pl.pallas_call(functools.partial(renorm_kernel, steps, parts, carry is no...  4.85 us
    unnamed x8, local copies, waits for them, and re-layouts  2.96 us
    pallas_call x1, Pallas kernels, prepare(): call(functools.partial(prepare_kernel, depth), (halves, part, jax.ShapeDt...  0.99 us
    pallas_call x2, Pallas kernels, combine(): call(functools.partial(combine_kernel, operators, tables, per), (jax.Shap...  0.93 us
  transfers between devices with their start and end apart: 15, of which 7 were waited for; matrix products, arithmetic and copies ran while one was open for 0% of the time, Pallas kernels for 15%

profile of v8, /device:TPU:0, one launch (start us, length us, event | category | flops | bytes accessed | tf_op | source)
XLA Modules:
  0.0 36.1 jit_solution(10254062917050712263)
XLA Ops:
  0.6 0.0 copy-start
  0.6 3.0 %collective-permute-start.5 = (f32[2,2,128,128]{3,2,1,0:T(8,128)}, f32[2,2,128,128]{3,2,1,0:T(8,128)S(1)}, u32[]{:S(2)}, u32[]{:S(2)}) collective-permute-start(f32[2,2,128,128]{3,2,1,0:T(8,128)} %refs_2_.1), channel_id=1, source_target_pairs={{0,8},{4,12},{8,0},{12,4},{16,24},{20,28},{24,16},{28,20},{1,9},{5... | collective-permute-start | bytes 786440 | tf_op jit(solution)/shard_map/ppermute | solution.py:247
  3.6 2.6 %collective-permute-start = (f32[2,2,128,128]{3,2,1,0:T(8,128)}, f32[2,2,128,128]{3,2,1,0:T(8,128)S(1)}, u32[]{:S(2)}, u32[]{:S(2)}) collective-permute-start(f32[2,2,128,128]{3,2,1,0:T(8,128)} %refs_2_.1), channel_id=1, source_target_pairs={{0,2},{1,3},{2,0},{3,1},{4,6},{5,7},{6,4},{7,5},{8,10},{9,11},{10,... | collective-permute-start | bytes 786440 | tf_op jit(solution)/shard_map/ppermute | solution.py:247
  6.2 1.6 %collective-permute-start.3 = (f32[2,2,128,128]{3,2,1,0:T(8,128)}, f32[2,2,128,128]{3,2,1,0:T(8,128)S(1)}, u32[]{:S(2)}, u32[]{:S(2)}) collective-permute-start(f32[2,2,128,128]{3,2,1,0:T(8,128)} %refs_2_.1), channel_id=1, source_target_pairs={{0,1},{1,0},{2,3},{3,2},{4,5},{5,4},{6,7},{7,6},{8,9},{9,8},{10,11... | collective-permute-start | bytes 786440 | tf_op jit(solution)/shard_map/ppermute | solution.py:247
  7.8 1.5 %collective-permute-start.4 = (f32[2,2,128,128]{3,2,1,0:T(8,128)}, f32[2,2,128,128]{3,2,1,0:T(8,128)S(1)}, u32[]{:S(2)}, u32[]{:S(2)}) collective-permute-start(f32[2,2,128,128]{3,2,1,0:T(8,128)} %refs_2_.1), channel_id=1, source_target_pairs={{0,16},{4,20},{8,24},{12,28},{16,0},{20,4},{24,8},{28,12},{1,17},{... | collective-permute-start | bytes 786440 | tf_op jit(solution)/shard_map/ppermute | solution.py:247
  9.3 0.5 %collective-permute-start.6 = (f32[2,1,16]{2,1,0:T(1,128)}, f32[2,1,16]{2,1,0:T(1,128)S(1)}, u32[]{:S(2)}, u32[]{:S(2)}) collective-permute-start(f32[2,1,16]{2,1,0:T(1,128)} %integrals_ref.1), channel_id=1, source_target_pairs={{0,8},{4,12},{8,0},{12,4},{16,24},{20,28},{24,16},{28,20},{1,9},{5... | collective-permute-start | bytes 392 | tf_op jit(solution)/shard_map/ppermute | solution.py:247
  9.9 0.0 copy-start.1
  9.9 1.6 %copy-done.1 = f32[2,4,512,128]{3,2,1,0:T(8,128)S(1)} copy-done((f32[2,4,512,128]{3,2,1,0:T(8,128)S(1)}, f32[2,4,512,128]{3,2,1,0:T(8,128)}, u32[]{:S(2)}) %copy-start.1) | copy-done | bytes 2097176
  11.5 0.0 copy-start.2
  11.5 0.7 %copy-done.2 = f32[2,1,4,4]{3,2,1,0:T(4,128)S(1)} copy-done((f32[2,1,4,4]{3,2,1,0:T(4,128)S(1)}, f32[2,1,4,4]{3,2,1,0:T(4,128)}, u32[]{:S(2)}) %copy-start.2) | copy-done | bytes 152
  12.1 0.0 copy-start.3
  12.1 0.7 %copy-done.3 = f32[2,1,16]{2,1,0:T(1,128)S(1)} copy-done((f32[2,1,16]{2,1,0:T(1,128)S(1)}, f32[2,1,16]{2,1,0:T(1,128)}, u32[]{:S(2)}) %copy-start.3) | copy-done | bytes 152
  12.8 1.0 %shard_map.60 = (bf16[3072,512]{1,0:T(8,128)(2,1)S(1)}, f32[2,1,4,128,128]{4,3,2,1,0:T(8,128)S(1)}, f32[2,1,16]{2,1,0:T(1,128)S(1)}) custom-call(f32[2,4,512,128]{3,2,1,0:T(8,128)S(1)} %copy-done.1, f32[2,1,4,4]{3,2,1,0:T(4,128)S(1)} %copy-done.2, f32[2,1,16]{2,1,0:T(1,128)S(1)} %copy-done.3), custom_call_target="tpu_custom_call" | custom-call | flops 2097152 | bytes 4194304 | tf_op jit(solution)/shard_map/pallas_call | solution.py:85
  13.8 0.0 collective-permute-done.6.refs_1_.refs_5_.refs_7_
  13.8 0.0 collective-permute-done.5.block_ref.refs_1_.refs_3_
  13.9 0.6 %collective-permute-start.7 = (f32[2,2,136,128]{3,2,1,0:T(8,128)S(1)}, f32[2,2,136,128]{3,2,1,0:T(8,128)S(1)}, u32[]{:S(2)}, u32[]{:S(2)}) collective-permute-start(f32[2,2,136,128]{3,2,1,0:T(8,128)S(1)} %shard_map.65), channel_id=1, source_target_pairs={{0,16},{4,20},{8,24},{12,28},{16,0},{20,4},{24,8},{28,12},{1,17},{... | collective-permute-start | bytes 835592 | tf_op jit(solution)/shard_map/ppermute | solution.py:247
  14.4 0.0 collective-permute-start.1
  14.5 1.1 %collective-permute-done.1.refs_0_.refs_7_ = f32[2,1,16]{2,1,0:T(1,128)S(1)} collective-permute-done((f32[2,1,16]{2,1,0:T(1,128)S(1)}, f32[2,1,16]{2,1,0:T(1,128)S(1)}, u32[]{:S(2)}, u32[]{:S(2)}) %collective-permute-start.1) | collective-permute-done | bytes 160 | tf_op jit(solution)/shard_map/ppermute | solution.py:247
  15.6 2.7 %collective-permute-done.x_ref = f32[2,2,128,128]{3,2,1,0:T(8,128)S(1)} collective-permute-done((f32[2,2,128,128]{3,2,1,0:T(8,128)}, f32[2,2,128,128]{3,2,1,0:T(8,128)S(1)}, u32[]{:S(2)}, u32[]{:S(2)}) %collective-permute-start) | collective-permute-done | bytes 262176 | tf_op jit(solution)/shard_map/ppermute | solution.py:247
  18.3 0.1 collective-permute-done.3.refs_0_.refs_1_
  18.5 0.0 collective-permute-done.4.refs_0_.refs_2_.refs_4_
  18.5 0.1 collective-permute-start.9
  18.6 1.5 %collective-permute-start.2 = (f32[2,2,128,128]{3,2,1,0:T(8,128)S(1)}, f32[2,2,128,128]{3,2,1,0:T(8,128)S(1)}, u32[]{:S(2)}, u32[]{:S(2)}) collective-permute-start(f32[2,2,128,128]{3,2,1,0:T(8,128)S(1)} %shard_map.59.x_ref), channel_id=1, source_target_pairs={{0,1},{1,0},{2,3},{3,2},{4,5},{5,4},{6,7},{7,6},{8,9},{9,8},{10,11... | collective-permute-start | bytes 786440 | tf_op jit(solution)/shard_map/ppermute | solution.py:247
  20.1 1.1 %collective-permute-done.7.refs_3_.refs_5_ = f32[2,2,136,128]{3,2,1,0:T(8,128)S(1)} collective-permute-done((f32[2,2,136,128]{3,2,1,0:T(8,128)S(1)}, f32[2,2,136,128]{3,2,1,0:T(8,128)S(1)}, u32[]{:S(2)}, u32[]{:S(2)}) %collective-permute-start.7) | collective-permute-done | bytes 278560 | tf_op jit(solution)/shard_map/ppermute | solution.py:247
  21.2 0.0 copy-done
  21.2 0.5 %shard_map.66 = (f32[2,1,128,128]{3,2,1,0:T(8,128)S(1)}, f32[2,1,128,128]{3,2,1,0:T(8,128)S(1)}) custom-call(f32[2,2,128,128]{3,2,1,0:T(8,128)S(1)} %copy-done, f32[2,2,128,128]{3,2,1,0:T(8,128)S(1)} %collective-permute-done.5.block_ref.refs_1_.refs_3_, f32[2,2,128,128]{3,2,1,0:T(8,128)S(1)} %collective-permute-done.4.refs_0_.refs_2_.refs_4_, ...), custom_call_target="tpu_custom_call" | custom-call | flops 2097152 | bytes 4194304 | tf_op jit(solution)/shard_map/pallas_call | solution.py:237
  21.7 0.1 collective-permute-start.8
  21.8 0.0 collective-permute-done.9.refs_1_
  21.8 0.5 %shard_map.67 = (f32[2,1,128,128]{3,2,1,0:T(8,128)S(1)}, f32[2,1,128,128]{3,2,1,0:T(8,128)S(1)}, f32[2,1,128,128]{3,2,1,0:T(8,128)S(1)}, f32[2,1,128,128]{3,2,1,0:T(8,128)S(1)}) custom-call(f32[2,2,128,128]{3,2,1,0:T(8,128)S(1)} %shard_map.62.refs_2_.refs_0_, f32[2,2,128,128]{3,2,1,0:T(8,128)S(1)} %collective-permute-done.9.refs_1_, ...), custom_call_target="tpu_custom_call" | custom-call | flops 2097152 | bytes 4194304 | tf_op jit(solution)/shard_map/pallas_call | solution.py:237
  22.2 1.3 %collective-permute-start.11 = (f32[2,1,128,128]{3,2,1,0:T(8,128)S(1)}, f32[2,1,128,128]{3,2,1,0:T(8,128)S(1)}, u32[]{:S(2)}, u32[]{:S(2)}) collective-permute-start(f32[2,1,128,128]{3,2,1,0:T(8,128)S(1)} %get-tuple-element.16), channel_id=1, source_target_pairs={{0,8},{4,12},{8,0},{12,4},{16,24},{20,28},{24,16},{28,20},{1,9},{5... | collective-permute-start | bytes 393224 | tf_op jit(solution)/shard_map/ppermute | solution.py:247
  23.5 1.7 %collective-permute-start.12 = (f32[2,1,128,128]{3,2,1,0:T(8,128)S(1)}, f32[2,1,128,128]{3,2,1,0:T(8,128)S(1)}, u32[]{:S(2)}, u32[]{:S(2)}) collective-permute-start(f32[2,1,128,128]{3,2,1,0:T(8,128)S(1)} %get-tuple-element.17), channel_id=1, source_target_pairs={{0,24},{4,28},{8,16},{12,20},{16,8},{20,12},{24,0},{28,4},{1,25},{... | collective-permute-start | bytes 393224 | tf_op jit(solution)/shard_map/ppermute | solution.py:247
  25.3 0.0 collective-permute-done.8.refs_1_
  25.3 1.6 %collective-permute-start.14 = (f32[2,1,128,128]{3,2,1,0:T(8,128)S(1)}, f32[2,1,128,128]{3,2,1,0:T(8,128)S(1)}, u32[]{:S(2)}, u32[]{:S(2)}) collective-permute-start(f32[2,1,128,128]{3,2,1,0:T(8,128)S(1)} %shard_map.68.refs_0_.refs_1_), channel_id=1, source_target_pairs={{0,3},{1,2},{2,1},{3,0},{4,7},{5,6},{6,5},{7,4},{8,11},{9,10},{10,... | collective-permute-start | bytes 393224 | tf_op jit(solution)/shard_map/ppermute | solution.py:247
  26.9 0.4 %collective-permute-start.10 = (f32[2,1,128,128]{3,2,1,0:T(8,128)S(1)}, f32[2,1,128,128]{3,2,1,0:T(8,128)S(1)}, u32[]{:S(2)}, u32[]{:S(2)}) collective-permute-start(f32[2,1,128,128]{3,2,1,0:T(8,128)S(1)} %shard_map.68.refs_0_.refs_1_), channel_id=1, source_target_pairs={{0,1},{1,0},{2,3},{3,2},{4,5},{5,4},{6,7},{7,6},{8,9},{9,8},{10,11... | collective-permute-start | bytes 393224 | tf_op jit(solution)/shard_map/ppermute | solution.py:247
  27.3 1.3 %collective-permute-done.11.refs_1_ = f32[2,1,128,128]{3,2,1,0:T(8,128)S(1)} collective-permute-done((f32[2,1,128,128]{3,2,1,0:T(8,128)S(1)}, f32[2,1,128,128]{3,2,1,0:T(8,128)S(1)}, u32[]{:S(2)}, u32[]{:S(2)}) %collective-permute-start.11) | collective-permute-done | bytes 131104 | tf_op jit(solution)/shard_map/ppermute | solution.py:247
  28.6 1.6 %collective-permute-start.13 = (f32[2,1,128,128]{3,2,1,0:T(8,128)S(1)}, f32[2,1,128,128]{3,2,1,0:T(8,128)S(1)}, u32[]{:S(2)}, u32[]{:S(2)}) collective-permute-start(f32[2,1,128,128]{3,2,1,0:T(8,128)S(1)} %shard_map.70), channel_id=1, source_target_pairs={{0,16},{4,20},{8,24},{12,28},{16,0},{20,4},{24,8},{28,12},{1,17},{... | collective-permute-start | bytes 393224 | tf_op jit(solution)/shard_map/ppermute | solution.py:247
  30.2 1.4 %shard_map.63.refs_2_ = f32[2,2,4,128,128]{4,3,2,1,0:T(8,128)S(1)} custom-call(f32[2,2,128,128]{3,2,1,0:T(8,128)S(1)} %copy-done, f32[2,2,128,128]{3,2,1,0:T(8,128)S(1)} %collective-permute-done.3.refs_0_.refs_1_, f32[2,2,128,128]{3,2,1,0:T(8,128)S(1)} %shard_map.62.refs_2_.refs_0_, bf16[3072,512]{1,0:T(8,128)(2,1)S(1)} %get-tuple-element.11.refs_3_.refs_1_.refs_2_), custom_call_target="tpu_custom_call" | custom-call | flops 1207959552 | bytes 4194304 | tf_op jit(solution)/shard_map/pallas_call | solution.py:182
  31.6 0.0 collective-permute-done.2.refs_0_
  31.6 1.5 %shard_map.64 = f32[2,2,4,128,128]{4,3,2,1,0:T(8,128)} custom-call(f32[2,2,128,128]{3,2,1,0:T(8,128)S(1)} %collective-permute-done.2.refs_0_, bf16[3072,512]{1,0:T(8,128)(2,1)S(1)} %get-tuple-element.11.refs_3_.refs_1_.refs_2_, f32[2,2,4,128,128]{4,3,2,1,0:T(8,128)S(1)} %shard_map.63.refs_2_), custom_call_target="tpu_custom_call" | custom-call | flops 402653184 | bytes 4194304 | tf_op jit(solution)/shard_map/pallas_call | solution.py:182
  33.1 0.0 collective-permute-done.12.refs_2_
  33.2 0.4 %collective-permute-done.14.refs_0_ = f32[2,1,128,128]{3,2,1,0:T(8,128)S(1)} collective-permute-done((f32[2,1,128,128]{3,2,1,0:T(8,128)S(1)}, f32[2,1,128,128]{3,2,1,0:T(8,128)S(1)}, u32[]{:S(2)}, u32[]{:S(2)}) %collective-permute-start.14) | collective-permute-done | bytes 131104 | tf_op jit(solution)/shard_map/ppermute | solution.py:247
  33.5 0.6 %shard_map.71.refs_4_ = f32[2,1,4,128,128]{4,3,2,1,0:T(8,128)S(1)} custom-call(f32[2,1,128,128]{3,2,1,0:T(8,128)S(1)} %collective-permute-done.14.refs_0_, f32[2,1,128,128]{3,2,1,0:T(8,128)S(1)} %shard_map.68.refs_0_.refs_1_, bf16[3072,512]{1,0:T(8,128)(2,1)S(1)} %get-tuple-element.11.refs_3_.refs_1_.refs_2_, ...), custom_call_target="tpu_custom_call" | custom-call | flops 402653184 | bytes 4194304 | tf_op jit(solution)/shard_map/pallas_call | solution.py:182
  34.1 0.6 %collective-permute-done.13.refs_2_ = f32[2,1,128,128]{3,2,1,0:T(8,128)S(1)} collective-permute-done((f32[2,1,128,128]{3,2,1,0:T(8,128)S(1)}, f32[2,1,128,128]{3,2,1,0:T(8,128)S(1)}, u32[]{:S(2)}, u32[]{:S(2)}) %collective-permute-start.13) | collective-permute-done | bytes 131104 | tf_op jit(solution)/shard_map/ppermute | solution.py:247
  34.8 0.0 collective-permute-done.10.refs_0_
  34.8 1.4 %shard_map.72 = f32[2,1,4,128,128]{4,3,2,1,0:T(8,128)} custom-call(f32[2,1,128,128]{3,2,1,0:T(8,128)S(1)} %collective-permute-done.10.refs_0_, f32[2,1,128,128]{3,2,1,0:T(8,128)S(1)} %shard_map.69.refs_4_.refs_1_, f32[2,1,128,128]{3,2,1,0:T(8,128)S(1)} %collective-permute-done.13.refs_2_, bf16[3072,512]{1,0:T(8,128)(2,1)S(1)} %get-tuple-element.11.refs_3_.refs_1_.refs_2_, ...), custom_call_target="tpu_custom_call" | custom-call | flops 402653184 | bytes 4194304 | tf_op jit(solution)/shard_map/pallas_call | solution.py:182
  (7 shorter events, 0.1 us)
Async XLA Ops:
  0.6 20.6 %copy-start = (f32[2,2,128,128]{3,2,1,0:T(8,128)S(1)}, f32[2,2,128,128]{3,2,1,0:T(8,128)}, u32[]{:S(2)}) copy-start(f32[2,2,128,128]{3,2,1,0:T(8,128)} %refs_2_.1) | copy-start | bytes 786436
  0.6 13.2 %collective-permute-start.5 = (f32[2,2,128,128]{3,2,1,0:T(8,128)}, f32[2,2,128,128]{3,2,1,0:T(8,128)S(1)}, u32[]{:S(2)}, u32[]{:S(2)}) collective-permute-start(f32[2,2,128,128]{3,2,1,0:T(8,128)} %refs_2_.1), channel_id=1, source_target_pairs={{0,8},{4,12},{8,0},{12,4},{16,24},{20,28},{24,16},{28,20},{1,9},{5... | collective-permute-start | bytes 786440 | tf_op jit(solution)/shard_map/ppermute | solution.py:247
  3.6 14.6 %collective-permute-start = (f32[2,2,128,128]{3,2,1,0:T(8,128)}, f32[2,2,128,128]{3,2,1,0:T(8,128)S(1)}, u32[]{:S(2)}, u32[]{:S(2)}) collective-permute-start(f32[2,2,128,128]{3,2,1,0:T(8,128)} %refs_2_.1), channel_id=1, source_target_pairs={{0,2},{1,3},{2,0},{3,1},{4,6},{5,7},{6,4},{7,5},{8,10},{9,11},{10,... | collective-permute-start | bytes 786440 | tf_op jit(solution)/shard_map/ppermute | solution.py:247
  6.2 12.2 %collective-permute-start.3 = (f32[2,2,128,128]{3,2,1,0:T(8,128)}, f32[2,2,128,128]{3,2,1,0:T(8,128)S(1)}, u32[]{:S(2)}, u32[]{:S(2)}) collective-permute-start(f32[2,2,128,128]{3,2,1,0:T(8,128)} %refs_2_.1), channel_id=1, source_target_pairs={{0,1},{1,0},{2,3},{3,2},{4,5},{5,4},{6,7},{7,6},{8,9},{9,8},{10,11... | collective-permute-start | bytes 786440 | tf_op jit(solution)/shard_map/ppermute | solution.py:247
  7.8 10.6 %collective-permute-start.4 = (f32[2,2,128,128]{3,2,1,0:T(8,128)}, f32[2,2,128,128]{3,2,1,0:T(8,128)S(1)}, u32[]{:S(2)}, u32[]{:S(2)}) collective-permute-start(f32[2,2,128,128]{3,2,1,0:T(8,128)} %refs_2_.1), channel_id=1, source_target_pairs={{0,16},{4,20},{8,24},{12,28},{16,0},{20,4},{24,8},{28,12},{1,17},{... | collective-permute-start | bytes 786440 | tf_op jit(solution)/shard_map/ppermute | solution.py:247
  9.3 4.5 %collective-permute-start.6 = (f32[2,1,16]{2,1,0:T(1,128)}, f32[2,1,16]{2,1,0:T(1,128)S(1)}, u32[]{:S(2)}, u32[]{:S(2)}) collective-permute-start(f32[2,1,16]{2,1,0:T(1,128)} %integrals_ref.1), channel_id=1, source_target_pairs={{0,8},{4,12},{8,0},{12,4},{16,24},{20,28},{24,16},{28,20},{1,9},{5... | collective-permute-start | bytes 392 | tf_op jit(solution)/shard_map/ppermute | solution.py:247
  9.9 1.6 %copy-start.1 = (f32[2,4,512,128]{3,2,1,0:T(8,128)S(1)}, f32[2,4,512,128]{3,2,1,0:T(8,128)}, u32[]{:S(2)}) copy-start(f32[2,4,512,128]{3,2,1,0:T(8,128)} %basis_hbm.1) | copy-start | bytes 6291460
  11.5 0.7 %copy-start.2 = (f32[2,1,4,4]{3,2,1,0:T(4,128)S(1)}, f32[2,1,4,4]{3,2,1,0:T(4,128)}, u32[]{:S(2)}) copy-start(f32[2,1,4,4]{3,2,1,0:T(4,128)} %site_hbm.1) | copy-start | bytes 388
  12.1 0.7 %copy-start.3 = (f32[2,1,16]{2,1,0:T(1,128)S(1)}, f32[2,1,16]{2,1,0:T(1,128)}, u32[]{:S(2)}) copy-start(f32[2,1,16]{2,1,0:T(1,128)} %integrals_ref.1) | copy-start | bytes 388
  13.9 7.3 %collective-permute-start.7 = (f32[2,2,136,128]{3,2,1,0:T(8,128)S(1)}, f32[2,2,136,128]{3,2,1,0:T(8,128)S(1)}, u32[]{:S(2)}, u32[]{:S(2)}) collective-permute-start(f32[2,2,136,128]{3,2,1,0:T(8,128)S(1)} %shard_map.65), channel_id=1, source_target_pairs={{0,16},{4,20},{8,24},{12,28},{16,0},{20,4},{24,8},{28,12},{1,17},{... | collective-permute-start | bytes 835592 | tf_op jit(solution)/shard_map/ppermute | solution.py:247
  14.4 1.1 %collective-permute-start.1 = (f32[2,1,16]{2,1,0:T(1,128)S(1)}, f32[2,1,16]{2,1,0:T(1,128)S(1)}, u32[]{:S(2)}, u32[]{:S(2)}) collective-permute-start(f32[2,1,16]{2,1,0:T(1,128)S(1)} %copy-done.3), channel_id=1, source_target_pairs={{0,4},{4,0},{8,12},{12,8},{16,20},{20,16},{24,28},{28,24},{1,5},{5... | collective-permute-start | bytes 392 | tf_op jit(solution)/shard_map/ppermute | solution.py:247
  18.5 3.3 %collective-permute-start.9 = (f32[2,2,128,128]{3,2,1,0:T(8,128)S(1)}, f32[2,2,128,128]{3,2,1,0:T(8,128)S(1)}, u32[]{:S(2)}, u32[]{:S(2)}) collective-permute-start(f32[2,2,128,128]{3,2,1,0:T(8,128)S(1)} %shard_map.62.refs_2_.refs_0_), channel_id=1, source_target_pairs={{0,4},{4,0},{8,12},{12,8},{16,20},{20,16},{24,28},{28,24},{1,5},{5... | collective-permute-start | bytes 786440 | tf_op jit(solution)/shard_map/ppermute | solution.py:247
  18.6 13.0 %collective-permute-start.2 = (f32[2,2,128,128]{3,2,1,0:T(8,128)S(1)}, f32[2,2,128,128]{3,2,1,0:T(8,128)S(1)}, u32[]{:S(2)}, u32[]{:S(2)}) collective-permute-start(f32[2,2,128,128]{3,2,1,0:T(8,128)S(1)} %shard_map.59.x_ref), channel_id=1, source_target_pairs={{0,1},{1,0},{2,3},{3,2},{4,5},{5,4},{6,7},{7,6},{8,9},{9,8},{10,11... | collective-permute-start | bytes 786440 | tf_op jit(solution)/shard_map/ppermute | solution.py:247
  21.7 3.6 %collective-permute-start.8 = (f32[2,1,128,128]{3,2,1,0:T(8,128)S(1)}, f32[2,1,128,128]{3,2,1,0:T(8,128)S(1)}, u32[]{:S(2)}, u32[]{:S(2)}) collective-permute-start(f32[2,1,128,128]{3,2,1,0:T(8,128)S(1)} %get-tuple-element.14), channel_id=1, source_target_pairs={{0,4},{4,0},{8,12},{12,8},{16,20},{20,16},{24,28},{28,24},{1,5},{5... | collective-permute-start | bytes 393224 | tf_op jit(solution)/shard_map/ppermute | solution.py:247
  22.2 6.4 %collective-permute-start.11 = (f32[2,1,128,128]{3,2,1,0:T(8,128)S(1)}, f32[2,1,128,128]{3,2,1,0:T(8,128)S(1)}, u32[]{:S(2)}, u32[]{:S(2)}) collective-permute-start(f32[2,1,128,128]{3,2,1,0:T(8,128)S(1)} %get-tuple-element.16), channel_id=1, source_target_pairs={{0,8},{4,12},{8,0},{12,4},{16,24},{20,28},{24,16},{28,20},{1,9},{5... | collective-permute-start | bytes 393224 | tf_op jit(solution)/shard_map/ppermute | solution.py:247
  23.5 9.6 %collective-permute-start.12 = (f32[2,1,128,128]{3,2,1,0:T(8,128)S(1)}, f32[2,1,128,128]{3,2,1,0:T(8,128)S(1)}, u32[]{:S(2)}, u32[]{:S(2)}) collective-permute-start(f32[2,1,128,128]{3,2,1,0:T(8,128)S(1)} %get-tuple-element.17), channel_id=1, source_target_pairs={{0,24},{4,28},{8,16},{12,20},{16,8},{20,12},{24,0},{28,4},{1,25},{... | collective-permute-start | bytes 393224 | tf_op jit(solution)/shard_map/ppermute | solution.py:247
  25.3 8.2 %collective-permute-start.14 = (f32[2,1,128,128]{3,2,1,0:T(8,128)S(1)}, f32[2,1,128,128]{3,2,1,0:T(8,128)S(1)}, u32[]{:S(2)}, u32[]{:S(2)}) collective-permute-start(f32[2,1,128,128]{3,2,1,0:T(8,128)S(1)} %shard_map.68.refs_0_.refs_1_), channel_id=1, source_target_pairs={{0,3},{1,2},{2,1},{3,0},{4,7},{5,6},{6,5},{7,4},{8,11},{9,10},{10,... | collective-permute-start | bytes 393224 | tf_op jit(solution)/shard_map/ppermute | solution.py:247
  26.9 7.8 %collective-permute-start.10 = (f32[2,1,128,128]{3,2,1,0:T(8,128)S(1)}, f32[2,1,128,128]{3,2,1,0:T(8,128)S(1)}, u32[]{:S(2)}, u32[]{:S(2)}) collective-permute-start(f32[2,1,128,128]{3,2,1,0:T(8,128)S(1)} %shard_map.68.refs_0_.refs_1_), channel_id=1, source_target_pairs={{0,1},{1,0},{2,3},{3,2},{4,5},{5,4},{6,7},{7,6},{8,9},{9,8},{10,11... | collective-permute-start | bytes 393224 | tf_op jit(solution)/shard_map/ppermute | solution.py:247
  28.6 6.1 %collective-permute-start.13 = (f32[2,1,128,128]{3,2,1,0:T(8,128)S(1)}, f32[2,1,128,128]{3,2,1,0:T(8,128)S(1)}, u32[]{:S(2)}, u32[]{:S(2)}) collective-permute-start(f32[2,1,128,128]{3,2,1,0:T(8,128)S(1)} %shard_map.70), channel_id=1, source_target_pairs={{0,16},{4,20},{8,24},{12,28},{16,0},{20,4},{24,8},{28,12},{1,17},{... | collective-permute-start | bytes 393224 | tf_op jit(solution)/shard_map/ppermute | solution.py:247

commit v9 on v8

--- a/solution.py
+++ b/solution.py
@@ -33,7 +33,7 @@
 
 
 def order(sec):
-    return (3, 0, 1, 2) if sec == 4 else tuple(range(sec))
+    return (1, 2, 0, 3) if sec == 4 else tuple(range(sec))
 
 
 def prepare_kernel(depth, basis_hbm, site_hbm, integrals_ref, *refs):
@@ -286,7 +286,7 @@
     two = after(two, sibling)
     three = swap(two, "sec", sec, 1)
     two = after(after(two, one), arrays[2])
-    normals = [three, normal_ops, one, two]
+    normals = [one, two, normal_ops, three]
     held = arrays + [row, sibling]
     here = [(len(arrays), None), (len(arrays) + 1, None)]
     mine, other = combine(held, operators, here, norms, shape)
@@ -296,22 +296,19 @@
     parts = combine(held, operators, tables, norms, shape)
     comp_ops = total([mine, swap(other, "pair", pairs, 1)], [parts[0]])
     far = swap(comp_ops, "sec", sec, 3)
-    near = swap(comp_ops, "sec", sec, 1)
-    last = pairs // 2
-    arrived = {
-        key: swap(parts[key // 2], "pair", pairs, key)
-        for key in range(2, pairs, 2)
-        if key != last
-    }
-    most = total([parts[0]] + list(arrived.values()), [])
-    rest = swap(after(parts[last // 2], comp_ops, arrived[2]), "pair", pairs, last)
+    near = swap(after(comp_ops, three), "sec", sec, 1)
+    summed = [parts[0]] + [
+        swap(after(part, comp_ops), "pair", pairs, key)
+        for part, key in zip(parts[1:], range(2, pairs, 2))
+    ]
     shape = (2, norms, sites, rows, cols)
-    early = renorm(normals, range(1, sec), basis_split, None, shape)
-    new_normal = renorm(normals, range(1), basis_split, early, shape, True)
+    early = renorm(normals, range(sec - 1), basis_split, None, shape)
+    new_normal = renorm(normals, range(sec - 1, sec), basis_split, early, shape, True)
     shape = (2, comps, sites, rows, cols)
-    arrived = [far, comp_ops, near, (most, rest)]
-    early = renorm(arrived, range(2), basis_split, site_part, shape, awaited=[most])
-    return new_normal, renorm(arrived, range(2, sec), basis_split, early, shape, True)
+    arrived = [near, tuple(summed), comp_ops, far]
+    early = renorm(arrived, range(2, sec), basis_split, site_part, shape)
+    early = renorm(arrived, range(1, 2), basis_split, early, shape)
+    return new_normal, renorm(arrived, range(1), basis_split, early, shape, True)
 
 
 def solution(mesh):

time: 36.3 us -> 35.8 us (0.986)
  starting transfers between devices: 18.1 us -> 17.5 us
    ppermute x15, starting transfers between devices: 18.1 us -> 17.5 us  [swap(): return lax.ppermute(x, axis, [(at, at ^ key) for at in range(size)])]
    pallas_call x4 -> x5, Pallas kernels: 4.85 us -> 5.06 us  [renorm(): pl.pallas_call(functools.partial(renorm_kernel, steps, parts, carry is no...]
  transfers between devices with their start and end apart: 15 -> 15, of which waited for: 7 -> 8; matrix products, arithmetic and copies ran while one was open for 0% -> 0% of each run, Pallas kernels for 15% -> 17%
where the time goes in v9:
time: 35.8 us; the launch traced here: 35.6 us
  starting transfers between devices  17.5 us (49%)
  waiting for transfers between devices  7.14 us (20%)
  Pallas kernels  7.11 us (20%)
  local copies, waits for them, and re-layouts  2.96 us (8%)
  between operations  0.81 us (2%)
    ppermute x15, starting transfers between devices, swap(): return lax.ppermute(x, axis, [(at, at ^ key) for at in range(size)])  17.5 us
    ppermute x15, waiting for transfers between devices, swap(): return lax.ppermute(x, axis, [(at, at ^ key) for at in range(size)])  7.14 us
    pallas_call x5, Pallas kernels, renorm(): pl.pallas_call(functools.partial(renorm_kernel, steps, parts, carry is no...  5.06 us
    unnamed x8, local copies, waits for them, and re-layouts  2.96 us
    pallas_call x1, Pallas kernels, prepare(): call(functools.partial(prepare_kernel, depth), (halves, part, jax.ShapeDt...  0.99 us
    pallas_call x2, Pallas kernels, combine(): call(functools.partial(combine_kernel, operators, tables, per), (jax.Shap...  0.93 us
  transfers between devices with their start and end apart: 15, of which 8 were waited for; matrix products, arithmetic and copies ran while one was open for 0% of the time, Pallas kernels for 17%

profile of v9, /device:TPU:0, one launch (start us, length us, event | category | flops | bytes accessed | tf_op | source)
XLA Modules:
  0.0 35.6 jit_solution(3593235381790374013)
XLA Ops:
  0.6 0.0 copy-start
  0.6 3.0 %collective-permute-start.5 = (f32[2,2,128,128]{3,2,1,0:T(8,128)}, f32[2,2,128,128]{3,2,1,0:T(8,128)S(1)}, u32[]{:S(2)}, u32[]{:S(2)}) collective-permute-start(f32[2,2,128,128]{3,2,1,0:T(8,128)} %refs_2_.3), channel_id=1, source_target_pairs={{0,8},{4,12},{8,0},{12,4},{16,24},{20,28},{24,16},{28,20},{1,9},{5... | collective-permute-start | bytes 786440 | tf_op jit(solution)/shard_map/ppermute | solution.py:247
  3.6 2.6 %collective-permute-start = (f32[2,2,128,128]{3,2,1,0:T(8,128)}, f32[2,2,128,128]{3,2,1,0:T(8,128)S(1)}, u32[]{:S(2)}, u32[]{:S(2)}) collective-permute-start(f32[2,2,128,128]{3,2,1,0:T(8,128)} %refs_2_.3), channel_id=1, source_target_pairs={{0,2},{1,3},{2,0},{3,1},{4,6},{5,7},{6,4},{7,5},{8,10},{9,11},{10,... | collective-permute-start | bytes 786440 | tf_op jit(solution)/shard_map/ppermute | solution.py:247
  6.2 1.6 %collective-permute-start.3 = (f32[2,2,128,128]{3,2,1,0:T(8,128)}, f32[2,2,128,128]{3,2,1,0:T(8,128)S(1)}, u32[]{:S(2)}, u32[]{:S(2)}) collective-permute-start(f32[2,2,128,128]{3,2,1,0:T(8,128)} %refs_2_.3), channel_id=1, source_target_pairs={{0,1},{1,0},{2,3},{3,2},{4,5},{5,4},{6,7},{7,6},{8,9},{9,8},{10,11... | collective-permute-start | bytes 786440 | tf_op jit(solution)/shard_map/ppermute | solution.py:247
  7.8 1.5 %collective-permute-start.4 = (f32[2,2,128,128]{3,2,1,0:T(8,128)}, f32[2,2,128,128]{3,2,1,0:T(8,128)S(1)}, u32[]{:S(2)}, u32[]{:S(2)}) collective-permute-start(f32[2,2,128,128]{3,2,1,0:T(8,128)} %refs_2_.3), channel_id=1, source_target_pairs={{0,16},{4,20},{8,24},{12,28},{16,0},{20,4},{24,8},{28,12},{1,17},{... | collective-permute-start | bytes 786440 | tf_op jit(solution)/shard_map/ppermute | solution.py:247
  9.3 0.5 %collective-permute-start.6 = (f32[2,1,16]{2,1,0:T(1,128)}, f32[2,1,16]{2,1,0:T(1,128)S(1)}, u32[]{:S(2)}, u32[]{:S(2)}) collective-permute-start(f32[2,1,16]{2,1,0:T(1,128)} %integrals_ref.1), channel_id=1, source_target_pairs={{0,8},{4,12},{8,0},{12,4},{16,24},{20,28},{24,16},{28,20},{1,9},{5... | collective-permute-start | bytes 392 | tf_op jit(solution)/shard_map/ppermute | solution.py:247
  9.9 0.0 copy-start.1
  9.9 1.6 %copy-done.1 = f32[2,4,512,128]{3,2,1,0:T(8,128)S(1)} copy-done((f32[2,4,512,128]{3,2,1,0:T(8,128)S(1)}, f32[2,4,512,128]{3,2,1,0:T(8,128)}, u32[]{:S(2)}) %copy-start.1) | copy-done | bytes 2097176
  11.5 0.0 copy-start.2
  11.5 0.7 %copy-done.2 = f32[2,1,4,4]{3,2,1,0:T(4,128)S(1)} copy-done((f32[2,1,4,4]{3,2,1,0:T(4,128)S(1)}, f32[2,1,4,4]{3,2,1,0:T(4,128)}, u32[]{:S(2)}) %copy-start.2) | copy-done | bytes 152
  12.1 0.0 copy-start.3
  12.1 0.7 %copy-done.3 = f32[2,1,16]{2,1,0:T(1,128)S(1)} copy-done((f32[2,1,16]{2,1,0:T(1,128)S(1)}, f32[2,1,16]{2,1,0:T(1,128)}, u32[]{:S(2)}) %copy-start.3) | copy-done | bytes 152
  12.8 1.0 %shard_map.60 = (bf16[3072,512]{1,0:T(8,128)(2,1)S(1)}, f32[2,1,4,128,128]{4,3,2,1,0:T(8,128)S(1)}, f32[2,1,16]{2,1,0:T(1,128)S(1)}) custom-call(f32[2,4,512,128]{3,2,1,0:T(8,128)S(1)} %copy-done.1, f32[2,1,4,4]{3,2,1,0:T(4,128)S(1)} %copy-done.2, f32[2,1,16]{2,1,0:T(1,128)S(1)} %copy-done.3), custom_call_target="tpu_custom_call" | custom-call | flops 2097152 | bytes 4194304 | tf_op jit(solution)/shard_map/pallas_call | solution.py:85
  13.8 0.0 collective-permute-done.6.refs_1_.refs_5_.refs_7_
  13.8 0.0 collective-permute-done.5.block_ref.refs_1_.refs_3_
  13.9 0.6 %collective-permute-start.7 = (f32[2,2,136,128]{3,2,1,0:T(8,128)S(1)}, f32[2,2,136,128]{3,2,1,0:T(8,128)S(1)}, u32[]{:S(2)}, u32[]{:S(2)}) collective-permute-start(f32[2,2,136,128]{3,2,1,0:T(8,128)S(1)} %shard_map.65), channel_id=1, source_target_pairs={{0,16},{4,20},{8,24},{12,28},{16,0},{20,4},{24,8},{28,12},{1,17},{... | collective-permute-start | bytes 835592 | tf_op jit(solution)/shard_map/ppermute | solution.py:247
  14.4 0.0 collective-permute-start.1
  14.4 1.1 %collective-permute-done.1.refs_0_.refs_7_ = f32[2,1,16]{2,1,0:T(1,128)S(1)} collective-permute-done((f32[2,1,16]{2,1,0:T(1,128)S(1)}, f32[2,1,16]{2,1,0:T(1,128)S(1)}, u32[]{:S(2)}, u32[]{:S(2)}) %collective-permute-start.1) | collective-permute-done | bytes 160 | tf_op jit(solution)/shard_map/ppermute | solution.py:247
  15.6 2.7 %collective-permute-done.x_ref = f32[2,2,128,128]{3,2,1,0:T(8,128)S(1)} collective-permute-done((f32[2,2,128,128]{3,2,1,0:T(8,128)}, f32[2,2,128,128]{3,2,1,0:T(8,128)S(1)}, u32[]{:S(2)}, u32[]{:S(2)}) %collective-permute-start) | collective-permute-done | bytes 262176 | tf_op jit(solution)/shard_map/ppermute | solution.py:247
  18.3 0.1 collective-permute-done.3.refs_0_
  18.5 0.0 collective-permute-done.4.refs_0_.refs_2_.refs_4_
  18.5 0.1 collective-permute-start.9
  18.6 1.5 %collective-permute-start.2 = (f32[2,2,128,128]{3,2,1,0:T(8,128)S(1)}, f32[2,2,128,128]{3,2,1,0:T(8,128)S(1)}, u32[]{:S(2)}, u32[]{:S(2)}) collective-permute-start(f32[2,2,128,128]{3,2,1,0:T(8,128)S(1)} %shard_map.59.x_ref), channel_id=1, source_target_pairs={{0,1},{1,0},{2,3},{3,2},{4,5},{5,4},{6,7},{7,6},{8,9},{9,8},{10,11... | collective-permute-start | bytes 786440 | tf_op jit(solution)/shard_map/ppermute | solution.py:247
  20.1 1.1 %collective-permute-done.7.refs_3_.refs_5_ = f32[2,2,136,128]{3,2,1,0:T(8,128)S(1)} collective-permute-done((f32[2,2,136,128]{3,2,1,0:T(8,128)S(1)}, f32[2,2,136,128]{3,2,1,0:T(8,128)S(1)}, u32[]{:S(2)}, u32[]{:S(2)}) %collective-permute-start.7) | collective-permute-done | bytes 278560 | tf_op jit(solution)/shard_map/ppermute | solution.py:247
  21.2 0.0 copy-done
  21.2 0.5 %shard_map.66 = (f32[2,1,128,128]{3,2,1,0:T(8,128)S(1)}, f32[2,1,128,128]{3,2,1,0:T(8,128)S(1)}) custom-call(f32[2,2,128,128]{3,2,1,0:T(8,128)S(1)} %copy-done, f32[2,2,128,128]{3,2,1,0:T(8,128)S(1)} %collective-permute-done.5.block_ref.refs_1_.refs_3_, f32[2,2,128,128]{3,2,1,0:T(8,128)S(1)} %collective-permute-done.4.refs_0_.refs_2_.refs_4_, ...), custom_call_target="tpu_custom_call" | custom-call | flops 2097152 | bytes 4194304 | tf_op jit(solution)/shard_map/pallas_call | solution.py:237
  21.7 0.1 collective-permute-start.8
  21.8 0.0 collective-permute-done.9.refs_1_
  21.8 0.5 %shard_map.67 = (f32[2,1,128,128]{3,2,1,0:T(8,128)S(1)}, f32[2,1,128,128]{3,2,1,0:T(8,128)S(1)}, f32[2,1,128,128]{3,2,1,0:T(8,128)S(1)}, f32[2,1,128,128]{3,2,1,0:T(8,128)S(1)}) custom-call(f32[2,2,128,128]{3,2,1,0:T(8,128)S(1)} %shard_map.62.refs_1_.refs_0_, f32[2,2,128,128]{3,2,1,0:T(8,128)S(1)} %collective-permute-done.9.refs_1_, ...), custom_call_target="tpu_custom_call" | custom-call | flops 2097152 | bytes 4194304 | tf_op jit(solution)/shard_map/pallas_call | solution.py:237
  22.2 0.9 %collective-permute-done.8.refs_1_ = f32[2,1,128,128]{3,2,1,0:T(8,128)S(1)} collective-permute-done((f32[2,1,128,128]{3,2,1,0:T(8,128)S(1)}, f32[2,1,128,128]{3,2,1,0:T(8,128)S(1)}, u32[]{:S(2)}, u32[]{:S(2)}) %collective-permute-start.8) | collective-permute-done | bytes 131104 | tf_op jit(solution)/shard_map/ppermute | solution.py:247
  23.1 0.8 %collective-permute-start.14 = (f32[2,1,128,128]{3,2,1,0:T(8,128)S(1)}, f32[2,1,128,128]{3,2,1,0:T(8,128)S(1)}, u32[]{:S(2)}, u32[]{:S(2)}) collective-permute-start(f32[2,1,128,128]{3,2,1,0:T(8,128)S(1)} %shard_map.68.x_ref.refs_0_), channel_id=1, source_target_pairs={{0,3},{1,2},{2,1},{3,0},{4,7},{5,6},{6,5},{7,4},{8,11},{9,10},{10,... | collective-permute-start | bytes 393224 | tf_op jit(solution)/shard_map/ppermute | solution.py:247
  24.0 2.2 %collective-permute-start.13 = (f32[2,1,128,128]{3,2,1,0:T(8,128)S(1)}, f32[2,1,128,128]{3,2,1,0:T(8,128)S(1)}, u32[]{:S(2)}, u32[]{:S(2)}) collective-permute-start(f32[2,1,128,128]{3,2,1,0:T(8,128)S(1)} %shard_map.72), channel_id=1, source_target_pairs={{0,24},{4,28},{8,16},{12,20},{16,8},{20,12},{24,0},{28,4},{1,25},{... | collective-permute-start | bytes 393224 | tf_op jit(solution)/shard_map/ppermute | solution.py:247
  26.2 0.6 %collective-permute-start.12 = (f32[2,1,128,128]{3,2,1,0:T(8,128)S(1)}, f32[2,1,128,128]{3,2,1,0:T(8,128)S(1)}, u32[]{:S(2)}, u32[]{:S(2)}) collective-permute-start(f32[2,1,128,128]{3,2,1,0:T(8,128)S(1)} %shard_map.71), channel_id=1, source_target_pairs={{0,16},{4,20},{8,24},{12,28},{16,0},{20,4},{24,8},{28,12},{1,17},{... | collective-permute-start | bytes 393224 | tf_op jit(solution)/shard_map/ppermute | solution.py:247
  26.8 0.9 %collective-permute-start.11 = (f32[2,1,128,128]{3,2,1,0:T(8,128)S(1)}, f32[2,1,128,128]{3,2,1,0:T(8,128)S(1)}, u32[]{:S(2)}, u32[]{:S(2)}) collective-permute-start(f32[2,1,128,128]{3,2,1,0:T(8,128)S(1)} %shard_map.70), channel_id=1, source_target_pairs={{0,8},{4,12},{8,0},{12,4},{16,24},{20,28},{24,16},{28,20},{1,9},{5... | collective-permute-start | bytes 393224 | tf_op jit(solution)/shard_map/ppermute | solution.py:247
  27.7 0.0 collective-permute-done.2.refs_0_
  27.7 1.6 %collective-permute-start.10 = (f32[2,1,128,128]{3,2,1,0:T(8,128)S(1)}, f32[2,1,128,128]{3,2,1,0:T(8,128)S(1)}, u32[]{:S(2)}, u32[]{:S(2)}) collective-permute-start(f32[2,1,128,128]{3,2,1,0:T(8,128)S(1)} %shard_map.69), channel_id=1, source_target_pairs={{0,1},{1,0},{2,3},{3,2},{4,5},{5,4},{6,7},{7,6},{8,9},{9,8},{10,11... | collective-permute-start | bytes 393224 | tf_op jit(solution)/shard_map/ppermute | solution.py:247
  29.3 1.4 %shard_map.63.refs_2_ = f32[2,2,4,128,128]{4,3,2,1,0:T(8,128)S(1)} custom-call(f32[2,2,128,128]{3,2,1,0:T(8,128)S(1)} %collective-permute-done.3.refs_0_, f32[2,2,128,128]{3,2,1,0:T(8,128)S(1)} %shard_map.62.refs_1_.refs_0_, f32[2,2,128,128]{3,2,1,0:T(8,128)S(1)} %copy-done, bf16[3072,512]{1,0:T(8,128)(2,1)S(1)} %get-tuple-element.11.refs_3_.refs_1_.refs_2_.refs_4_), custom_call_target="tpu_custom_call" | custom-call | flops 1207959552 | bytes 4194304 | tf_op jit(solution)/shard_map/pallas_call | solution.py:182
  30.7 1.5 %shard_map.64 = f32[2,2,4,128,128]{4,3,2,1,0:T(8,128)} custom-call(f32[2,2,128,128]{3,2,1,0:T(8,128)S(1)} %collective-permute-done.2.refs_0_, bf16[3072,512]{1,0:T(8,128)(2,1)S(1)} %get-tuple-element.11.refs_3_.refs_1_.refs_2_.refs_4_, f32[2,2,4,128,128]{4,3,2,1,0:T(8,128)S(1)} %shard_map.63.refs_2_), custom_call_target="tpu_custom_call" | custom-call | flops 402653184 | bytes 4194304 | tf_op jit(solution)/shard_map/pallas_call | solution.py:182
  32.2 0.0 collective-permute-done.14.refs_1_
  32.2 0.6 %shard_map.73.refs_5_ = f32[2,1,4,128,128]{4,3,2,1,0:T(8,128)S(1)} custom-call(f32[2,1,128,128]{3,2,1,0:T(8,128)S(1)} %shard_map.68.x_ref.refs_0_, f32[2,1,128,128]{3,2,1,0:T(8,128)S(1)} %collective-permute-done.14.refs_1_, bf16[3072,512]{1,0:T(8,128)(2,1)S(1)} %get-tuple-element.11.refs_3_.refs_1_.refs_2_.refs_4_, ...), custom_call_target="tpu_custom_call" | custom-call | flops 402653184 | bytes 4194304 | tf_op jit(solution)/shard_map/pallas_call | solution.py:182
  32.8 0.0 collective-permute-done.13.refs_3_
  32.8 0.4 %collective-permute-done.12.refs_2_ = f32[2,1,128,128]{3,2,1,0:T(8,128)S(1)} collective-permute-done((f32[2,1,128,128]{3,2,1,0:T(8,128)S(1)}, f32[2,1,128,128]{3,2,1,0:T(8,128)S(1)}, u32[]{:S(2)}, u32[]{:S(2)}) %collective-permute-start.12) | collective-permute-done | bytes 131104 | tf_op jit(solution)/shard_map/ppermute | solution.py:247
  33.2 0.1 collective-permute-done.11.refs_1_
  33.3 0.4 %shard_map.74.refs_2_ = f32[2,1,4,128,128]{4,3,2,1,0:T(8,128)S(1)} custom-call(f32[2,1,128,128]{3,2,1,0:T(8,128)S(1)} %get-tuple-element.15.refs_2_.refs_0_, f32[2,1,128,128]{3,2,1,0:T(8,128)S(1)} %collective-permute-done.11.refs_1_, f32[2,1,128,128]{3,2,1,0:T(8,128)S(1)} %collective-permute-done.12.refs_2_, ...), custom_call_target="tpu_custom_call" | custom-call | flops 201326592 | bytes 4194304 | tf_op jit(solution)/shard_map/pallas_call | solution.py:182
  33.7 0.7 %collective-permute-done.10.refs_0_ = f32[2,1,128,128]{3,2,1,0:T(8,128)S(1)} collective-permute-done((f32[2,1,128,128]{3,2,1,0:T(8,128)S(1)}, f32[2,1,128,128]{3,2,1,0:T(8,128)S(1)}, u32[]{:S(2)}, u32[]{:S(2)}) %collective-permute-start.10) | collective-permute-done | bytes 131104 | tf_op jit(solution)/shard_map/ppermute | solution.py:247
  34.4 1.2 %shard_map.75 = f32[2,1,4,128,128]{4,3,2,1,0:T(8,128)} custom-call(f32[2,1,128,128]{3,2,1,0:T(8,128)S(1)} %collective-permute-done.10.refs_0_, bf16[3072,512]{1,0:T(8,128)(2,1)S(1)} %get-tuple-element.11.refs_3_.refs_1_.refs_2_.refs_4_, f32[2,1,4,128,128]{4,3,2,1,0:T(8,128)S(1)} %shard_map.74.refs_2_), custom_call_target="tpu_custom_call" | custom-call | flops 201326592 | bytes 4194304 | tf_op jit(solution)/shard_map/pallas_call | solution.py:182
  (9 shorter events, 0.1 us)
Async XLA Ops:
  0.6 20.6 %copy-start = (f32[2,2,128,128]{3,2,1,0:T(8,128)S(1)}, f32[2,2,128,128]{3,2,1,0:T(8,128)}, u32[]{:S(2)}) copy-start(f32[2,2,128,128]{3,2,1,0:T(8,128)} %refs_2_.3) | copy-start | bytes 786436
  0.6 13.2 %collective-permute-start.5 = (f32[2,2,128,128]{3,2,1,0:T(8,128)}, f32[2,2,128,128]{3,2,1,0:T(8,128)S(1)}, u32[]{:S(2)}, u32[]{:S(2)}) collective-permute-start(f32[2,2,128,128]{3,2,1,0:T(8,128)} %refs_2_.3), channel_id=1, source_target_pairs={{0,8},{4,12},{8,0},{12,4},{16,24},{20,28},{24,16},{28,20},{1,9},{5... | collective-permute-start | bytes 786440 | tf_op jit(solution)/shard_map/ppermute | solution.py:247
  3.6 14.6 %collective-permute-start = (f32[2,2,128,128]{3,2,1,0:T(8,128)}, f32[2,2,128,128]{3,2,1,0:T(8,128)S(1)}, u32[]{:S(2)}, u32[]{:S(2)}) collective-permute-start(f32[2,2,128,128]{3,2,1,0:T(8,128)} %refs_2_.3), channel_id=1, source_target_pairs={{0,2},{1,3},{2,0},{3,1},{4,6},{5,7},{6,4},{7,5},{8,10},{9,11},{10,... | collective-permute-start | bytes 786440 | tf_op jit(solution)/shard_map/ppermute | solution.py:247
  6.2 12.2 %collective-permute-start.3 = (f32[2,2,128,128]{3,2,1,0:T(8,128)}, f32[2,2,128,128]{3,2,1,0:T(8,128)S(1)}, u32[]{:S(2)}, u32[]{:S(2)}) collective-permute-start(f32[2,2,128,128]{3,2,1,0:T(8,128)} %refs_2_.3), channel_id=1, source_target_pairs={{0,1},{1,0},{2,3},{3,2},{4,5},{5,4},{6,7},{7,6},{8,9},{9,8},{10,11... | collective-permute-start | bytes 786440 | tf_op jit(solution)/shard_map/ppermute | solution.py:247
  7.8 10.6 %collective-permute-start.4 = (f32[2,2,128,128]{3,2,1,0:T(8,128)}, f32[2,2,128,128]{3,2,1,0:T(8,128)S(1)}, u32[]{:S(2)}, u32[]{:S(2)}) collective-permute-start(f32[2,2,128,128]{3,2,1,0:T(8,128)} %refs_2_.3), channel_id=1, source_target_pairs={{0,16},{4,20},{8,24},{12,28},{16,0},{20,4},{24,8},{28,12},{1,17},{... | collective-permute-start | bytes 786440 | tf_op jit(solution)/shard_map/ppermute | solution.py:247
  9.3 4.5 %collective-permute-start.6 = (f32[2,1,16]{2,1,0:T(1,128)}, f32[2,1,16]{2,1,0:T(1,128)S(1)}, u32[]{:S(2)}, u32[]{:S(2)}) collective-permute-start(f32[2,1,16]{2,1,0:T(1,128)} %integrals_ref.1), channel_id=1, source_target_pairs={{0,8},{4,12},{8,0},{12,4},{16,24},{20,28},{24,16},{28,20},{1,9},{5... | collective-permute-start | bytes 392 | tf_op jit(solution)/shard_map/ppermute | solution.py:247
  9.9 1.6 %copy-start.1 = (f32[2,4,512,128]{3,2,1,0:T(8,128)S(1)}, f32[2,4,512,128]{3,2,1,0:T(8,128)}, u32[]{:S(2)}) copy-start(f32[2,4,512,128]{3,2,1,0:T(8,128)} %basis_hbm.1) | copy-start | bytes 6291460
  11.5 0.7 %copy-start.2 = (f32[2,1,4,4]{3,2,1,0:T(4,128)S(1)}, f32[2,1,4,4]{3,2,1,0:T(4,128)}, u32[]{:S(2)}) copy-start(f32[2,1,4,4]{3,2,1,0:T(4,128)} %site_hbm.1) | copy-start | bytes 388
  12.1 0.7 %copy-start.3 = (f32[2,1,16]{2,1,0:T(1,128)S(1)}, f32[2,1,16]{2,1,0:T(1,128)}, u32[]{:S(2)}) copy-start(f32[2,1,16]{2,1,0:T(1,128)} %integrals_ref.1) | copy-start | bytes 388
  13.9 7.3 %collective-permute-start.7 = (f32[2,2,136,128]{3,2,1,0:T(8,128)S(1)}, f32[2,2,136,128]{3,2,1,0:T(8,128)S(1)}, u32[]{:S(2)}, u32[]{:S(2)}) collective-permute-start(f32[2,2,136,128]{3,2,1,0:T(8,128)S(1)} %shard_map.65), channel_id=1, source_target_pairs={{0,16},{4,20},{8,24},{12,28},{16,0},{20,4},{24,8},{28,12},{1,17},{... | collective-permute-start | bytes 835592 | tf_op jit(solution)/shard_map/ppermute | solution.py:247
  14.4 1.1 %collective-permute-start.1 = (f32[2,1,16]{2,1,0:T(1,128)S(1)}, f32[2,1,16]{2,1,0:T(1,128)S(1)}, u32[]{:S(2)}, u32[]{:S(2)}) collective-permute-start(f32[2,1,16]{2,1,0:T(1,128)S(1)} %copy-done.3), channel_id=1, source_target_pairs={{0,4},{4,0},{8,12},{12,8},{16,20},{20,16},{24,28},{28,24},{1,5},{5... | collective-permute-start | bytes 392 | tf_op jit(solution)/shard_map/ppermute | solution.py:247
  18.5 3.3 %collective-permute-start.9 = (f32[2,2,128,128]{3,2,1,0:T(8,128)S(1)}, f32[2,2,128,128]{3,2,1,0:T(8,128)S(1)}, u32[]{:S(2)}, u32[]{:S(2)}) collective-permute-start(f32[2,2,128,128]{3,2,1,0:T(8,128)S(1)} %shard_map.62.refs_1_.refs_0_), channel_id=1, source_target_pairs={{0,4},{4,0},{8,12},{12,8},{16,20},{20,16},{24,28},{28,24},{1,5},{5... | collective-permute-start | bytes 786440 | tf_op jit(solution)/shard_map/ppermute | solution.py:247
  18.6 9.1 %collective-permute-start.2 = (f32[2,2,128,128]{3,2,1,0:T(8,128)S(1)}, f32[2,2,128,128]{3,2,1,0:T(8,128)S(1)}, u32[]{:S(2)}, u32[]{:S(2)}) collective-permute-start(f32[2,2,128,128]{3,2,1,0:T(8,128)S(1)} %shard_map.59.x_ref), channel_id=1, source_target_pairs={{0,1},{1,0},{2,3},{3,2},{4,5},{5,4},{6,7},{7,6},{8,9},{9,8},{10,11... | collective-permute-start | bytes 786440 | tf_op jit(solution)/shard_map/ppermute | solution.py:247
  21.7 1.4 %collective-permute-start.8 = (f32[2,1,128,128]{3,2,1,0:T(8,128)S(1)}, f32[2,1,128,128]{3,2,1,0:T(8,128)S(1)}, u32[]{:S(2)}, u32[]{:S(2)}) collective-permute-start(f32[2,1,128,128]{3,2,1,0:T(8,128)S(1)} %get-tuple-element.14), channel_id=1, source_target_pairs={{0,4},{4,0},{8,12},{12,8},{16,20},{20,16},{24,28},{28,24},{1,5},{5... | collective-permute-start | bytes 393224 | tf_op jit(solution)/shard_map/ppermute | solution.py:247
  23.1 9.1 %collective-permute-start.14 = (f32[2,1,128,128]{3,2,1,0:T(8,128)S(1)}, f32[2,1,128,128]{3,2,1,0:T(8,128)S(1)}, u32[]{:S(2)}, u32[]{:S(2)}) collective-permute-start(f32[2,1,128,128]{3,2,1,0:T(8,128)S(1)} %shard_map.68.x_ref.refs_0_), channel_id=1, source_target_pairs={{0,3},{1,2},{2,1},{3,0},{4,7},{5,6},{6,5},{7,4},{8,11},{9,10},{10,... | collective-permute-start | bytes 393224 | tf_op jit(solution)/shard_map/ppermute | solution.py:247
  24.0 8.8 %collective-permute-start.13 = (f32[2,1,128,128]{3,2,1,0:T(8,128)S(1)}, f32[2,1,128,128]{3,2,1,0:T(8,128)S(1)}, u32[]{:S(2)}, u32[]{:S(2)}) collective-permute-start(f32[2,1,128,128]{3,2,1,0:T(8,128)S(1)} %shard_map.72), channel_id=1, source_target_pairs={{0,24},{4,28},{8,16},{12,20},{16,8},{20,12},{24,0},{28,4},{1,25},{... | collective-permute-start | bytes 393224 | tf_op jit(solution)/shard_map/ppermute | solution.py:247
  26.2 7.0 %collective-permute-start.12 = (f32[2,1,128,128]{3,2,1,0:T(8,128)S(1)}, f32[2,1,128,128]{3,2,1,0:T(8,128)S(1)}, u32[]{:S(2)}, u32[]{:S(2)}) collective-permute-start(f32[2,1,128,128]{3,2,1,0:T(8,128)S(1)} %shard_map.71), channel_id=1, source_target_pairs={{0,16},{4,20},{8,24},{12,28},{16,0},{20,4},{24,8},{28,12},{1,17},{... | collective-permute-start | bytes 393224 | tf_op jit(solution)/shard_map/ppermute | solution.py:247
  26.8 6.6 %collective-permute-start.11 = (f32[2,1,128,128]{3,2,1,0:T(8,128)S(1)}, f32[2,1,128,128]{3,2,1,0:T(8,128)S(1)}, u32[]{:S(2)}, u32[]{:S(2)}) collective-permute-start(f32[2,1,128,128]{3,2,1,0:T(8,128)S(1)} %shard_map.70), channel_id=1, source_target_pairs={{0,8},{4,12},{8,0},{12,4},{16,24},{20,28},{24,16},{28,20},{1,9},{5... | collective-permute-start | bytes 393224 | tf_op jit(solution)/shard_map/ppermute | solution.py:247
  27.7 6.7 %collective-permute-start.10 = (f32[2,1,128,128]{3,2,1,0:T(8,128)S(1)}, f32[2,1,128,128]{3,2,1,0:T(8,128)S(1)}, u32[]{:S(2)}, u32[]{:S(2)}) collective-permute-start(f32[2,1,128,128]{3,2,1,0:T(8,128)S(1)} %shard_map.69), channel_id=1, source_target_pairs={{0,1},{1,0},{2,3},{3,2},{4,5},{5,4},{6,7},{7,6},{8,9},{9,8},{10,11... | collective-permute-start | bytes 393224 | tf_op jit(solution)/shard_map/ppermute | solution.py:247

commit v10 on v8

--- a/solution.py
+++ b/solution.py
@@ -33,7 +33,7 @@
 
 
 def order(sec):
-    return (3, 0, 1, 2) if sec == 4 else tuple(range(sec))
+    return (3, 1, 2, 0) if sec == 4 else tuple(range(sec))
 
 
 def prepare_kernel(depth, basis_hbm, site_hbm, integrals_ref, *refs):
@@ -286,7 +286,7 @@
     two = after(two, sibling)
     three = swap(two, "sec", sec, 1)
     two = after(after(two, one), arrays[2])
-    normals = [three, normal_ops, one, two]
+    normals = [three, one, two, normal_ops]
     held = arrays + [row, sibling]
     here = [(len(arrays), None), (len(arrays) + 1, None)]
     mine, other = combine(held, operators, here, norms, shape)
@@ -297,21 +297,19 @@
     comp_ops = total([mine, swap(other, "pair", pairs, 1)], [parts[0]])
     far = swap(comp_ops, "sec", sec, 3)
     near = swap(comp_ops, "sec", sec, 1)
-    last = pairs // 2
-    arrived = {
-        key: swap(parts[key // 2], "pair", pairs, key)
-        for key in range(2, pairs, 2)
-        if key != last
-    }
-    most = total([parts[0]] + list(arrived.values()), [])
-    rest = swap(after(parts[last // 2], comp_ops, arrived[2]), "pair", pairs, last)
+    summed = [parts[0]]
+    for key in range(2, pairs, 2):
+        part = after(parts[key // 2], comp_ops)
+        if key == 2:
+            part = after(part, three)
+        summed.append(swap(part, "pair", pairs, key))
     shape = (2, norms, sites, rows, cols)
     early = renorm(normals, range(1, sec), basis_split, None, shape)
     new_normal = renorm(normals, range(1), basis_split, early, shape, True)
     shape = (2, comps, sites, rows, cols)
-    arrived = [far, comp_ops, near, (most, rest)]
-    early = renorm(arrived, range(2), basis_split, site_part, shape, awaited=[most])
-    return new_normal, renorm(arrived, range(2, sec), basis_split, early, shape, True)
+    arrived = [far, near, tuple(summed), comp_ops]
+    early = renorm(arrived, range(3, sec), basis_split, site_part, shape)
+    return new_normal, renorm(arrived, range(3), basis_split, early, shape, True)
 
 
 def solution(mesh):

time: 36.3 us -> 35.6 us (0.981)
  starting transfers between devices: 18.1 us -> 16.4 us
  waiting for transfers between devices: 7.4 us -> 8.38 us
    ppermute x15, starting transfers between devices: 18.1 us -> 16.4 us  [swap(): return lax.ppermute(x, axis, [(at, at ^ key) for at in range(size)])]
    ppermute x15, waiting for transfers between devices: 7.4 us -> 8.38 us  [swap(): return lax.ppermute(x, axis, [(at, at ^ key) for at in range(size)])]
  transfers between devices with their start and end apart: 15 -> 15, of which waited for: 7 -> 8; matrix products, arithmetic and copies ran while one was open for 0% -> 0% of each run, Pallas kernels for 15% -> 15%
where the time goes in v10:
time: 35.6 us; the launch traced here: 35.4 us
  starting transfers between devices  16.4 us (46%)
  waiting for transfers between devices  8.38 us (24%)
  Pallas kernels  6.91 us (19%)
  local copies, waits for them, and re-layouts  2.96 us (8%)
  between operations  0.79 us (2%)
    ppermute x15, starting transfers between devices, swap(): return lax.ppermute(x, axis, [(at, at ^ key) for at in range(size)])  16.4 us
    ppermute x15, waiting for transfers between devices, swap(): return lax.ppermute(x, axis, [(at, at ^ key) for at in range(size)])  8.38 us
    pallas_call x4, Pallas kernels, renorm(): pl.pallas_call(functools.partial(renorm_kernel, steps, parts, carry is no...  4.86 us
    unnamed x8, local copies, waits for them, and re-layouts  2.96 us
    pallas_call x1, Pallas kernels, prepare(): call(functools.partial(prepare_kernel, depth), (halves, part, jax.ShapeDt...  0.99 us
    pallas_call x2, Pallas kernels, combine(): call(functools.partial(combine_kernel, operators, tables, per), (jax.Shap...  0.93 us
  transfers between devices with their start and end apart: 15, of which 8 were waited for; matrix products, arithmetic and copies ran while one was open for 0% of the time, Pallas kernels for 15%

profile of v10, /device:TPU:0, one launch (start us, length us, event | category | flops | bytes accessed | tf_op | source)
XLA Modules:
  0.0 35.4 jit_solution(11433469379902885533)
XLA Ops:
  0.6 0.0 copy-start
  0.6 3.0 %collective-permute-start.5 = (f32[2,2,128,128]{3,2,1,0:T(8,128)}, f32[2,2,128,128]{3,2,1,0:T(8,128)S(1)}, u32[]{:S(2)}, u32[]{:S(2)}) collective-permute-start(f32[2,2,128,128]{3,2,1,0:T(8,128)} %refs_2_.3), channel_id=1, source_target_pairs={{0,8},{4,12},{8,0},{12,4},{16,24},{20,28},{24,16},{28,20},{1,9},{5... | collective-permute-start | bytes 786440 | tf_op jit(solution)/shard_map/ppermute | solution.py:247
  3.6 2.6 %collective-permute-start = (f32[2,2,128,128]{3,2,1,0:T(8,128)}, f32[2,2,128,128]{3,2,1,0:T(8,128)S(1)}, u32[]{:S(2)}, u32[]{:S(2)}) collective-permute-start(f32[2,2,128,128]{3,2,1,0:T(8,128)} %refs_2_.3), channel_id=1, source_target_pairs={{0,2},{1,3},{2,0},{3,1},{4,6},{5,7},{6,4},{7,5},{8,10},{9,11},{10,... | collective-permute-start | bytes 786440 | tf_op jit(solution)/shard_map/ppermute | solution.py:247
  6.2 1.6 %collective-permute-start.3 = (f32[2,2,128,128]{3,2,1,0:T(8,128)}, f32[2,2,128,128]{3,2,1,0:T(8,128)S(1)}, u32[]{:S(2)}, u32[]{:S(2)}) collective-permute-start(f32[2,2,128,128]{3,2,1,0:T(8,128)} %refs_2_.3), channel_id=1, source_target_pairs={{0,1},{1,0},{2,3},{3,2},{4,5},{5,4},{6,7},{7,6},{8,9},{9,8},{10,11... | collective-permute-start | bytes 786440 | tf_op jit(solution)/shard_map/ppermute | solution.py:247
  7.8 1.5 %collective-permute-start.4 = (f32[2,2,128,128]{3,2,1,0:T(8,128)}, f32[2,2,128,128]{3,2,1,0:T(8,128)S(1)}, u32[]{:S(2)}, u32[]{:S(2)}) collective-permute-start(f32[2,2,128,128]{3,2,1,0:T(8,128)} %refs_2_.3), channel_id=1, source_target_pairs={{0,16},{4,20},{8,24},{12,28},{16,0},{20,4},{24,8},{28,12},{1,17},{... | collective-permute-start | bytes 786440 | tf_op jit(solution)/shard_map/ppermute | solution.py:247
  9.3 0.5 %collective-permute-start.6 = (f32[2,1,16]{2,1,0:T(1,128)}, f32[2,1,16]{2,1,0:T(1,128)S(1)}, u32[]{:S(2)}, u32[]{:S(2)}) collective-permute-start(f32[2,1,16]{2,1,0:T(1,128)} %integrals_ref.1), channel_id=1, source_target_pairs={{0,8},{4,12},{8,0},{12,4},{16,24},{20,28},{24,16},{28,20},{1,9},{5... | collective-permute-start | bytes 392 | tf_op jit(solution)/shard_map/ppermute | solution.py:247
  9.9 0.0 copy-start.1
  9.9 1.6 %copy-done.1 = f32[2,4,512,128]{3,2,1,0:T(8,128)S(1)} copy-done((f32[2,4,512,128]{3,2,1,0:T(8,128)S(1)}, f32[2,4,512,128]{3,2,1,0:T(8,128)}, u32[]{:S(2)}) %copy-start.1) | copy-done | bytes 2097176
  11.5 0.0 copy-start.2
  11.5 0.7 %copy-done.2 = f32[2,1,4,4]{3,2,1,0:T(4,128)S(1)} copy-done((f32[2,1,4,4]{3,2,1,0:T(4,128)S(1)}, f32[2,1,4,4]{3,2,1,0:T(4,128)}, u32[]{:S(2)}) %copy-start.2) | copy-done | bytes 152
  12.1 0.0 copy-start.3
  12.1 0.7 %copy-done.3 = f32[2,1,16]{2,1,0:T(1,128)S(1)} copy-done((f32[2,1,16]{2,1,0:T(1,128)S(1)}, f32[2,1,16]{2,1,0:T(1,128)}, u32[]{:S(2)}) %copy-start.3) | copy-done | bytes 152
  12.8 1.0 %shard_map.60 = (bf16[3072,512]{1,0:T(8,128)(2,1)S(1)}, f32[2,1,4,128,128]{4,3,2,1,0:T(8,128)S(1)}, f32[2,1,16]{2,1,0:T(1,128)S(1)}) custom-call(f32[2,4,512,128]{3,2,1,0:T(8,128)S(1)} %copy-done.1, f32[2,1,4,4]{3,2,1,0:T(4,128)S(1)} %copy-done.2, f32[2,1,16]{2,1,0:T(1,128)S(1)} %copy-done.3), custom_call_target="tpu_custom_call" | custom-call | flops 2097152 | bytes 4194304 | tf_op jit(solution)/shard_map/pallas_call | solution.py:85
  13.8 0.0 collective-permute-done.6.refs_1_.refs_5_.refs_7_
  13.8 0.0 collective-permute-done.5.block_ref.refs_1_.refs_3_
  13.9 0.6 %collective-permute-start.7 = (f32[2,2,136,128]{3,2,1,0:T(8,128)S(1)}, f32[2,2,136,128]{3,2,1,0:T(8,128)S(1)}, u32[]{:S(2)}, u32[]{:S(2)}) collective-permute-start(f32[2,2,136,128]{3,2,1,0:T(8,128)S(1)} %shard_map.65), channel_id=1, source_target_pairs={{0,16},{4,20},{8,24},{12,28},{16,0},{20,4},{24,8},{28,12},{1,17},{... | collective-permute-start | bytes 835592 | tf_op jit(solution)/shard_map/ppermute | solution.py:247
  14.4 0.0 collective-permute-start.1
  14.5 1.1 %collective-permute-done.1.refs_0_.refs_7_ = f32[2,1,16]{2,1,0:T(1,128)S(1)} collective-permute-done((f32[2,1,16]{2,1,0:T(1,128)S(1)}, f32[2,1,16]{2,1,0:T(1,128)S(1)}, u32[]{:S(2)}, u32[]{:S(2)}) %collective-permute-start.1) | collective-permute-done | bytes 160 | tf_op jit(solution)/shard_map/ppermute | solution.py:247
  15.6 2.7 %collective-permute-done.x_ref = f32[2,2,128,128]{3,2,1,0:T(8,128)S(1)} collective-permute-done((f32[2,2,128,128]{3,2,1,0:T(8,128)}, f32[2,2,128,128]{3,2,1,0:T(8,128)S(1)}, u32[]{:S(2)}, u32[]{:S(2)}) %collective-permute-start) | collective-permute-done | bytes 262176 | tf_op jit(solution)/shard_map/ppermute | solution.py:247
  18.3 0.1 collective-permute-done.3.refs_0_
  18.5 0.0 collective-permute-done.4.refs_0_.refs_2_.refs_4_
  18.5 0.1 collective-permute-start.9
  18.6 1.5 %collective-permute-start.2 = (f32[2,2,128,128]{3,2,1,0:T(8,128)S(1)}, f32[2,2,128,128]{3,2,1,0:T(8,128)S(1)}, u32[]{:S(2)}, u32[]{:S(2)}) collective-permute-start(f32[2,2,128,128]{3,2,1,0:T(8,128)S(1)} %shard_map.59.x_ref), channel_id=1, source_target_pairs={{0,1},{1,0},{2,3},{3,2},{4,5},{5,4},{6,7},{7,6},{8,9},{9,8},{10,11... | collective-permute-start | bytes 786440 | tf_op jit(solution)/shard_map/ppermute | solution.py:247
  20.1 1.1 %collective-permute-done.7.refs_3_.refs_5_ = f32[2,2,136,128]{3,2,1,0:T(8,128)S(1)} collective-permute-done((f32[2,2,136,128]{3,2,1,0:T(8,128)S(1)}, f32[2,2,136,128]{3,2,1,0:T(8,128)S(1)}, u32[]{:S(2)}, u32[]{:S(2)}) %collective-permute-start.7) | collective-permute-done | bytes 278560 | tf_op jit(solution)/shard_map/ppermute | solution.py:247
  21.2 0.0 copy-done
  21.2 0.5 %shard_map.66 = (f32[2,1,128,128]{3,2,1,0:T(8,128)S(1)}, f32[2,1,128,128]{3,2,1,0:T(8,128)S(1)}) custom-call(f32[2,2,128,128]{3,2,1,0:T(8,128)S(1)} %copy-done, f32[2,2,128,128]{3,2,1,0:T(8,128)S(1)} %collective-permute-done.5.block_ref.refs_1_.refs_3_, f32[2,2,128,128]{3,2,1,0:T(8,128)S(1)} %collective-permute-done.4.refs_0_.refs_2_.refs_4_, ...), custom_call_target="tpu_custom_call" | custom-call | flops 2097152 | bytes 4194304 | tf_op jit(solution)/shard_map/pallas_call | solution.py:237
  21.7 0.1 collective-permute-start.8
  21.8 0.0 collective-permute-done.9.refs_1_
  21.8 0.5 %shard_map.67 = (f32[2,1,128,128]{3,2,1,0:T(8,128)S(1)}, f32[2,1,128,128]{3,2,1,0:T(8,128)S(1)}, f32[2,1,128,128]{3,2,1,0:T(8,128)S(1)}, f32[2,1,128,128]{3,2,1,0:T(8,128)S(1)}) custom-call(f32[2,2,128,128]{3,2,1,0:T(8,128)S(1)} %shard_map.62.refs_1_.refs_0_, f32[2,2,128,128]{3,2,1,0:T(8,128)S(1)} %collective-permute-done.9.refs_1_, ...), custom_call_target="tpu_custom_call" | custom-call | flops 2097152 | bytes 4194304 | tf_op jit(solution)/shard_map/pallas_call | solution.py:237
  22.2 0.9 %collective-permute-done.8.refs_1_ = f32[2,1,128,128]{3,2,1,0:T(8,128)S(1)} collective-permute-done((f32[2,1,128,128]{3,2,1,0:T(8,128)S(1)}, f32[2,1,128,128]{3,2,1,0:T(8,128)S(1)}, u32[]{:S(2)}, u32[]{:S(2)}) %collective-permute-start.8) | collective-permute-done | bytes 131104 | tf_op jit(solution)/shard_map/ppermute | solution.py:247
  23.1 0.8 %collective-permute-start.10 = (f32[2,1,128,128]{3,2,1,0:T(8,128)S(1)}, f32[2,1,128,128]{3,2,1,0:T(8,128)S(1)}, u32[]{:S(2)}, u32[]{:S(2)}) collective-permute-start(f32[2,1,128,128]{3,2,1,0:T(8,128)S(1)} %shard_map.68.refs_0_), channel_id=1, source_target_pairs={{0,3},{1,2},{2,1},{3,0},{4,7},{5,6},{6,5},{7,4},{8,11},{9,10},{10,... | collective-permute-start | bytes 393224 | tf_op jit(solution)/shard_map/ppermute | solution.py:247
  23.9 1.0 %collective-permute-start.11 = (f32[2,1,128,128]{3,2,1,0:T(8,128)S(1)}, f32[2,1,128,128]{3,2,1,0:T(8,128)S(1)}, u32[]{:S(2)}, u32[]{:S(2)}) collective-permute-start(f32[2,1,128,128]{3,2,1,0:T(8,128)S(1)} %shard_map.68.refs_0_), channel_id=1, source_target_pairs={{0,1},{1,0},{2,3},{3,2},{4,5},{5,4},{6,7},{7,6},{8,9},{9,8},{10,11... | collective-permute-start | bytes 393224 | tf_op jit(solution)/shard_map/ppermute | solution.py:247
  25.0 1.6 %collective-permute-start.14 = (f32[2,1,128,128]{3,2,1,0:T(8,128)S(1)}, f32[2,1,128,128]{3,2,1,0:T(8,128)S(1)}, u32[]{:S(2)}, u32[]{:S(2)}) collective-permute-start(f32[2,1,128,128]{3,2,1,0:T(8,128)S(1)} %shard_map.72), channel_id=1, source_target_pairs={{0,24},{4,28},{8,16},{12,20},{16,8},{20,12},{24,0},{28,4},{1,25},{... | collective-permute-start | bytes 393224 | tf_op jit(solution)/shard_map/ppermute | solution.py:247
  26.6 0.6 %collective-permute-start.13 = (f32[2,1,128,128]{3,2,1,0:T(8,128)S(1)}, f32[2,1,128,128]{3,2,1,0:T(8,128)S(1)}, u32[]{:S(2)}, u32[]{:S(2)}) collective-permute-start(f32[2,1,128,128]{3,2,1,0:T(8,128)S(1)} %shard_map.71), channel_id=1, source_target_pairs={{0,16},{4,20},{8,24},{12,28},{16,0},{20,4},{24,8},{28,12},{1,17},{... | collective-permute-start | bytes 393224 | tf_op jit(solution)/shard_map/ppermute | solution.py:247
  27.1 0.6 %collective-permute-done.2.refs_0_ = f32[2,2,128,128]{3,2,1,0:T(8,128)S(1)} collective-permute-done((f32[2,2,128,128]{3,2,1,0:T(8,128)S(1)}, f32[2,2,128,128]{3,2,1,0:T(8,128)S(1)}, u32[]{:S(2)}, u32[]{:S(2)}) %collective-permute-start.2) | collective-permute-done | bytes 262176 | tf_op jit(solution)/shard_map/ppermute | solution.py:247
  27.8 1.0 %collective-permute-start.12 = (f32[2,1,128,128]{3,2,1,0:T(8,128)S(1)}, f32[2,1,128,128]{3,2,1,0:T(8,128)S(1)}, u32[]{:S(2)}, u32[]{:S(2)}) collective-permute-start(f32[2,1,128,128]{3,2,1,0:T(8,128)S(1)} %shard_map.70), channel_id=1, source_target_pairs={{0,8},{4,12},{8,0},{12,4},{16,24},{20,28},{24,16},{28,20},{1,9},{5... | collective-permute-start | bytes 393224 | tf_op jit(solution)/shard_map/ppermute | solution.py:247
  28.7 1.4 %shard_map.63.refs_2_ = f32[2,2,4,128,128]{4,3,2,1,0:T(8,128)S(1)} custom-call(f32[2,2,128,128]{3,2,1,0:T(8,128)S(1)} %collective-permute-done.3.refs_0_, f32[2,2,128,128]{3,2,1,0:T(8,128)S(1)} %shard_map.62.refs_1_.refs_0_, f32[2,2,128,128]{3,2,1,0:T(8,128)S(1)} %copy-done, bf16[3072,512]{1,0:T(8,128)(2,1)S(1)} %get-tuple-element.11.refs_3_.refs_1_.refs_6_), custom_call_target="tpu_custom_call" | custom-call | flops 1207959552 | bytes 4194304 | tf_op jit(solution)/shard_map/pallas_call | solution.py:182
  30.1 1.5 %shard_map.64 = f32[2,2,4,128,128]{4,3,2,1,0:T(8,128)} custom-call(f32[2,2,128,128]{3,2,1,0:T(8,128)S(1)} %collective-permute-done.2.refs_0_, bf16[3072,512]{1,0:T(8,128)(2,1)S(1)} %get-tuple-element.11.refs_3_.refs_1_.refs_6_, f32[2,2,4,128,128]{4,3,2,1,0:T(8,128)S(1)} %shard_map.63.refs_2_), custom_call_target="tpu_custom_call" | custom-call | flops 402653184 | bytes 4194304 | tf_op jit(solution)/shard_map/pallas_call | solution.py:182
  31.6 0.4 %shard_map.73.refs_7_ = f32[2,1,4,128,128]{4,3,2,1,0:T(8,128)S(1)} custom-call(f32[2,1,128,128]{3,2,1,0:T(8,128)S(1)} %shard_map.68.refs_0_, bf16[3072,512]{1,0:T(8,128)(2,1)S(1)} %get-tuple-element.11.refs_3_.refs_1_.refs_6_, f32[2,1,4,128,128]{4,3,2,1,0:T(8,128)S(1)} %get-tuple-element.19.refs_2_), custom_call_target="tpu_custom_call" | custom-call | flops 201326592 | bytes 4194304 | tf_op jit(solution)/shard_map/pallas_call | solution.py:182
  32.0 0.0 collective-permute-done.14.refs_5_
  32.1 1.7 %collective-permute-done.13.refs_4_ = f32[2,1,128,128]{3,2,1,0:T(8,128)S(1)} collective-permute-done((f32[2,1,128,128]{3,2,1,0:T(8,128)S(1)}, f32[2,1,128,128]{3,2,1,0:T(8,128)S(1)}, u32[]{:S(2)}, u32[]{:S(2)}) %collective-permute-start.13) | collective-permute-done | bytes 131104 | tf_op jit(solution)/shard_map/ppermute | solution.py:247
  33.8 0.1 collective-permute-done.12.refs_3_
  33.9 0.0 collective-permute-done.10.refs_0_
  33.9 0.0 collective-permute-done.11.refs_1_
  33.9 1.6 %shard_map.74 = f32[2,1,4,128,128]{4,3,2,1,0:T(8,128)} custom-call(f32[2,1,128,128]{3,2,1,0:T(8,128)S(1)} %collective-permute-done.10.refs_0_, f32[2,1,128,128]{3,2,1,0:T(8,128)S(1)} %collective-permute-done.11.refs_1_, f32[2,1,128,128]{3,2,1,0:T(8,128)S(1)} %get-tuple-element.15.refs_2_, f32[2,1,128,128]{3,2,1,0:T(8,128)S(1)} %collective-permute-done.12.refs_3_, ...), custom_call_target="tpu_custom_call" | custom-call | flops 603979776 | bytes 4194304 | tf_op jit(solution)/shard_map/pallas_call | solution.py:182
  (9 shorter events, 0.1 us)
Async XLA Ops:
  0.6 20.6 %copy-start = (f32[2,2,128,128]{3,2,1,0:T(8,128)S(1)}, f32[2,2,128,128]{3,2,1,0:T(8,128)}, u32[]{:S(2)}) copy-start(f32[2,2,128,128]{3,2,1,0:T(8,128)} %refs_2_.3) | copy-start | bytes 786436
  0.6 13.2 %collective-permute-start.5 = (f32[2,2,128,128]{3,2,1,0:T(8,128)}, f32[2,2,128,128]{3,2,1,0:T(8,128)S(1)}, u32[]{:S(2)}, u32[]{:S(2)}) collective-permute-start(f32[2,2,128,128]{3,2,1,0:T(8,128)} %refs_2_.3), channel_id=1, source_target_pairs={{0,8},{4,12},{8,0},{12,4},{16,24},{20,28},{24,16},{28,20},{1,9},{5... | collective-permute-start | bytes 786440 | tf_op jit(solution)/shard_map/ppermute | solution.py:247
  3.6 14.6 %collective-permute-start = (f32[2,2,128,128]{3,2,1,0:T(8,128)}, f32[2,2,128,128]{3,2,1,0:T(8,128)S(1)}, u32[]{:S(2)}, u32[]{:S(2)}) collective-permute-start(f32[2,2,128,128]{3,2,1,0:T(8,128)} %refs_2_.3), channel_id=1, source_target_pairs={{0,2},{1,3},{2,0},{3,1},{4,6},{5,7},{6,4},{7,5},{8,10},{9,11},{10,... | collective-permute-start | bytes 786440 | tf_op jit(solution)/shard_map/ppermute | solution.py:247
  6.2 12.2 %collective-permute-start.3 = (f32[2,2,128,128]{3,2,1,0:T(8,128)}, f32[2,2,128,128]{3,2,1,0:T(8,128)S(1)}, u32[]{:S(2)}, u32[]{:S(2)}) collective-permute-start(f32[2,2,128,128]{3,2,1,0:T(8,128)} %refs_2_.3), channel_id=1, source_target_pairs={{0,1},{1,0},{2,3},{3,2},{4,5},{5,4},{6,7},{7,6},{8,9},{9,8},{10,11... | collective-permute-start | bytes 786440 | tf_op jit(solution)/shard_map/ppermute | solution.py:247
  7.8 10.6 %collective-permute-start.4 = (f32[2,2,128,128]{3,2,1,0:T(8,128)}, f32[2,2,128,128]{3,2,1,0:T(8,128)S(1)}, u32[]{:S(2)}, u32[]{:S(2)}) collective-permute-start(f32[2,2,128,128]{3,2,1,0:T(8,128)} %refs_2_.3), channel_id=1, source_target_pairs={{0,16},{4,20},{8,24},{12,28},{16,0},{20,4},{24,8},{28,12},{1,17},{... | collective-permute-start | bytes 786440 | tf_op jit(solution)/shard_map/ppermute | solution.py:247
  9.3 4.5 %collective-permute-start.6 = (f32[2,1,16]{2,1,0:T(1,128)}, f32[2,1,16]{2,1,0:T(1,128)S(1)}, u32[]{:S(2)}, u32[]{:S(2)}) collective-permute-start(f32[2,1,16]{2,1,0:T(1,128)} %integrals_ref.1), channel_id=1, source_target_pairs={{0,8},{4,12},{8,0},{12,4},{16,24},{20,28},{24,16},{28,20},{1,9},{5... | collective-permute-start | bytes 392 | tf_op jit(solution)/shard_map/ppermute | solution.py:247
  9.9 1.6 %copy-start.1 = (f32[2,4,512,128]{3,2,1,0:T(8,128)S(1)}, f32[2,4,512,128]{3,2,1,0:T(8,128)}, u32[]{:S(2)}) copy-start(f32[2,4,512,128]{3,2,1,0:T(8,128)} %basis_hbm.1) | copy-start | bytes 6291460
  11.5 0.7 %copy-start.2 = (f32[2,1,4,4]{3,2,1,0:T(4,128)S(1)}, f32[2,1,4,4]{3,2,1,0:T(4,128)}, u32[]{:S(2)}) copy-start(f32[2,1,4,4]{3,2,1,0:T(4,128)} %site_hbm.1) | copy-start | bytes 388
  12.1 0.7 %copy-start.3 = (f32[2,1,16]{2,1,0:T(1,128)S(1)}, f32[2,1,16]{2,1,0:T(1,128)}, u32[]{:S(2)}) copy-start(f32[2,1,16]{2,1,0:T(1,128)} %integrals_ref.1) | copy-start | bytes 388
  13.9 7.3 %collective-permute-start.7 = (f32[2,2,136,128]{3,2,1,0:T(8,128)S(1)}, f32[2,2,136,128]{3,2,1,0:T(8,128)S(1)}, u32[]{:S(2)}, u32[]{:S(2)}) collective-permute-start(f32[2,2,136,128]{3,2,1,0:T(8,128)S(1)} %shard_map.65), channel_id=1, source_target_pairs={{0,16},{4,20},{8,24},{12,28},{16,0},{20,4},{24,8},{28,12},{1,17},{... | collective-permute-start | bytes 835592 | tf_op jit(solution)/shard_map/ppermute | solution.py:247
  14.4 1.1 %collective-permute-start.1 = (f32[2,1,16]{2,1,0:T(1,128)S(1)}, f32[2,1,16]{2,1,0:T(1,128)S(1)}, u32[]{:S(2)}, u32[]{:S(2)}) collective-permute-start(f32[2,1,16]{2,1,0:T(1,128)S(1)} %copy-done.3), channel_id=1, source_target_pairs={{0,4},{4,0},{8,12},{12,8},{16,20},{20,16},{24,28},{28,24},{1,5},{5... | collective-permute-start | bytes 392 | tf_op jit(solution)/shard_map/ppermute | solution.py:247
  18.5 3.3 %collective-permute-start.9 = (f32[2,2,128,128]{3,2,1,0:T(8,128)S(1)}, f32[2,2,128,128]{3,2,1,0:T(8,128)S(1)}, u32[]{:S(2)}, u32[]{:S(2)}) collective-permute-start(f32[2,2,128,128]{3,2,1,0:T(8,128)S(1)} %shard_map.62.refs_1_.refs_0_), channel_id=1, source_target_pairs={{0,4},{4,0},{8,12},{12,8},{16,20},{20,16},{24,28},{28,24},{1,5},{5... | collective-permute-start | bytes 786440 | tf_op jit(solution)/shard_map/ppermute | solution.py:247
  18.6 9.2 %collective-permute-start.2 = (f32[2,2,128,128]{3,2,1,0:T(8,128)S(1)}, f32[2,2,128,128]{3,2,1,0:T(8,128)S(1)}, u32[]{:S(2)}, u32[]{:S(2)}) collective-permute-start(f32[2,2,128,128]{3,2,1,0:T(8,128)S(1)} %shard_map.59.x_ref), channel_id=1, source_target_pairs={{0,1},{1,0},{2,3},{3,2},{4,5},{5,4},{6,7},{7,6},{8,9},{9,8},{10,11... | collective-permute-start | bytes 786440 | tf_op jit(solution)/shard_map/ppermute | solution.py:247
  21.7 1.4 %collective-permute-start.8 = (f32[2,1,128,128]{3,2,1,0:T(8,128)S(1)}, f32[2,1,128,128]{3,2,1,0:T(8,128)S(1)}, u32[]{:S(2)}, u32[]{:S(2)}) collective-permute-start(f32[2,1,128,128]{3,2,1,0:T(8,128)S(1)} %get-tuple-element.14), channel_id=1, source_target_pairs={{0,4},{4,0},{8,12},{12,8},{16,20},{20,16},{24,28},{28,24},{1,5},{5... | collective-permute-start | bytes 393224 | tf_op jit(solution)/shard_map/ppermute | solution.py:247
  23.1 10.8 %collective-permute-start.10 = (f32[2,1,128,128]{3,2,1,0:T(8,128)S(1)}, f32[2,1,128,128]{3,2,1,0:T(8,128)S(1)}, u32[]{:S(2)}, u32[]{:S(2)}) collective-permute-start(f32[2,1,128,128]{3,2,1,0:T(8,128)S(1)} %shard_map.68.refs_0_), channel_id=1, source_target_pairs={{0,3},{1,2},{2,1},{3,0},{4,7},{5,6},{6,5},{7,4},{8,11},{9,10},{10,... | collective-permute-start | bytes 393224 | tf_op jit(solution)/shard_map/ppermute | solution.py:247
  23.9 9.9 %collective-permute-start.11 = (f32[2,1,128,128]{3,2,1,0:T(8,128)S(1)}, f32[2,1,128,128]{3,2,1,0:T(8,128)S(1)}, u32[]{:S(2)}, u32[]{:S(2)}) collective-permute-start(f32[2,1,128,128]{3,2,1,0:T(8,128)S(1)} %shard_map.68.refs_0_), channel_id=1, source_target_pairs={{0,1},{1,0},{2,3},{3,2},{4,5},{5,4},{6,7},{7,6},{8,9},{9,8},{10,11... | collective-permute-start | bytes 393224 | tf_op jit(solution)/shard_map/ppermute | solution.py:247
  25.0 7.1 %collective-permute-start.14 = (f32[2,1,128,128]{3,2,1,0:T(8,128)S(1)}, f32[2,1,128,128]{3,2,1,0:T(8,128)S(1)}, u32[]{:S(2)}, u32[]{:S(2)}) collective-permute-start(f32[2,1,128,128]{3,2,1,0:T(8,128)S(1)} %shard_map.72), channel_id=1, source_target_pairs={{0,24},{4,28},{8,16},{12,20},{16,8},{20,12},{24,0},{28,4},{1,25},{... | collective-permute-start | bytes 393224 | tf_op jit(solution)/shard_map/ppermute | solution.py:247
  26.6 7.2 %collective-permute-start.13 = (f32[2,1,128,128]{3,2,1,0:T(8,128)S(1)}, f32[2,1,128,128]{3,2,1,0:T(8,128)S(1)}, u32[]{:S(2)}, u32[]{:S(2)}) collective-permute-start(f32[2,1,128,128]{3,2,1,0:T(8,128)S(1)} %shard_map.71), channel_id=1, source_target_pairs={{0,16},{4,20},{8,24},{12,28},{16,0},{20,4},{24,8},{28,12},{1,17},{... | collective-permute-start | bytes 393224 | tf_op jit(solution)/shard_map/ppermute | solution.py:247
  27.8 6.1 %collective-permute-start.12 = (f32[2,1,128,128]{3,2,1,0:T(8,128)S(1)}, f32[2,1,128,128]{3,2,1,0:T(8,128)S(1)}, u32[]{:S(2)}, u32[]{:S(2)}) collective-permute-start(f32[2,1,128,128]{3,2,1,0:T(8,128)S(1)} %shard_map.70), channel_id=1, source_target_pairs={{0,8},{4,12},{8,0},{12,4},{16,24},{20,28},{24,16},{28,20},{1,9},{5... | collective-permute-start | bytes 393224 | tf_op jit(solution)/shard_map/ppermute | solution.py:247

commit v11 on v10

--- a/solution.py
+++ b/solution.py
@@ -297,11 +297,12 @@
     comp_ops = total([mine, swap(other, "pair", pairs, 1)], [parts[0]])
     far = swap(comp_ops, "sec", sec, 3)
     near = swap(comp_ops, "sec", sec, 1)
-    summed = [parts[0]]
-    for key in range(2, pairs, 2):
+    first = swap(parts[-1], "pair", pairs, pairs - 2)
+    summed = [parts[0], first]
+    for key in range(2, pairs - 2, 2):
         part = after(parts[key // 2], comp_ops)
         if key == 2:
-            part = after(part, three)
+            part = after(part, first)
         summed.append(swap(part, "pair", pairs, key))
     shape = (2, norms, sites, rows, cols)
     early = renorm(normals, range(1, sec), basis_split, None, shape)

time: 35.6 us -> 36 us (1.011)
  starting transfers between devices: 16.4 us -> 17 us
    ppermute x15, starting transfers between devices: 16.4 us -> 17 us  [swap(): return lax.ppermute(x, axis, [(at, at ^ key) for at in range(size)])]
  transfers between devices with their start and end apart: 15 -> 15, of which waited for: 8 -> 6; matrix products, arithmetic and copies ran while one was open for 0% -> 0% of each run, Pallas kernels for 15% -> 15%
where the time goes in v11:
time: 36 us; the launch traced here: 35.8 us
  starting transfers between devices  17 us (47%)
  waiting for transfers between devices  8.15 us (23%)
  Pallas kernels  6.89 us (19%)
  local copies, waits for them, and re-layouts  2.96 us (8%)
  between operations  0.8 us (2%)
    ppermute x15, starting transfers between devices, swap(): return lax.ppermute(x, axis, [(at, at ^ key) for at in range(size)])  17 us
    ppermute x15, waiting for transfers between devices, swap(): return lax.ppermute(x, axis, [(at, at ^ key) for at in range(size)])  8.15 us
    pallas_call x4, Pallas kernels, renorm(): pl.pallas_call(functools.partial(renorm_kernel, steps, parts, carry is no...  4.85 us
    unnamed x8, local copies, waits for them, and re-layouts  2.96 us
    pallas_call x1, Pallas kernels, prepare(): call(functools.partial(prepare_kernel, depth), (halves, part, jax.ShapeDt...  0.99 us
    pallas_call x2, Pallas kernels, combine(): call(functools.partial(combine_kernel, operators, tables, per), (jax.Shap...  0.93 us
  transfers between devices with their start and end apart: 15, of which 6 were waited for; matrix products, arithmetic and copies ran while one was open for 0% of the time, Pallas kernels for 15%

profile of v11, /device:TPU:0, one launch (start us, length us, event | category | flops | bytes accessed | tf_op | source)
XLA Modules:
  0.0 35.8 jit_solution(11258219990950407989)
XLA Ops:
  0.6 0.0 copy-start
  0.6 3.0 %collective-permute-start.5 = (f32[2,2,128,128]{3,2,1,0:T(8,128)}, f32[2,2,128,128]{3,2,1,0:T(8,128)S(1)}, u32[]{:S(2)}, u32[]{:S(2)}) collective-permute-start(f32[2,2,128,128]{3,2,1,0:T(8,128)} %refs_2_.3), channel_id=1, source_target_pairs={{0,8},{4,12},{8,0},{12,4},{16,24},{20,28},{24,16},{28,20},{1,9},{5... | collective-permute-start | bytes 786440 | tf_op jit(solution)/shard_map/ppermute | solution.py:247
  3.6 2.6 %collective-permute-start = (f32[2,2,128,128]{3,2,1,0:T(8,128)}, f32[2,2,128,128]{3,2,1,0:T(8,128)S(1)}, u32[]{:S(2)}, u32[]{:S(2)}) collective-permute-start(f32[2,2,128,128]{3,2,1,0:T(8,128)} %refs_2_.3), channel_id=1, source_target_pairs={{0,2},{1,3},{2,0},{3,1},{4,6},{5,7},{6,4},{7,5},{8,10},{9,11},{10,... | collective-permute-start | bytes 786440 | tf_op jit(solution)/shard_map/ppermute | solution.py:247
  6.2 1.6 %collective-permute-start.3 = (f32[2,2,128,128]{3,2,1,0:T(8,128)}, f32[2,2,128,128]{3,2,1,0:T(8,128)S(1)}, u32[]{:S(2)}, u32[]{:S(2)}) collective-permute-start(f32[2,2,128,128]{3,2,1,0:T(8,128)} %refs_2_.3), channel_id=1, source_target_pairs={{0,1},{1,0},{2,3},{3,2},{4,5},{5,4},{6,7},{7,6},{8,9},{9,8},{10,11... | collective-permute-start | bytes 786440 | tf_op jit(solution)/shard_map/ppermute | solution.py:247
  7.8 1.5 %collective-permute-start.4 = (f32[2,2,128,128]{3,2,1,0:T(8,128)}, f32[2,2,128,128]{3,2,1,0:T(8,128)S(1)}, u32[]{:S(2)}, u32[]{:S(2)}) collective-permute-start(f32[2,2,128,128]{3,2,1,0:T(8,128)} %refs_2_.3), channel_id=1, source_target_pairs={{0,16},{4,20},{8,24},{12,28},{16,0},{20,4},{24,8},{28,12},{1,17},{... | collective-permute-start | bytes 786440 | tf_op jit(solution)/shard_map/ppermute | solution.py:247
  9.3 0.5 %collective-permute-start.6 = (f32[2,1,16]{2,1,0:T(1,128)}, f32[2,1,16]{2,1,0:T(1,128)S(1)}, u32[]{:S(2)}, u32[]{:S(2)}) collective-permute-start(f32[2,1,16]{2,1,0:T(1,128)} %integrals_ref.1), channel_id=1, source_target_pairs={{0,8},{4,12},{8,0},{12,4},{16,24},{20,28},{24,16},{28,20},{1,9},{5... | collective-permute-start | bytes 392 | tf_op jit(solution)/shard_map/ppermute | solution.py:247
  9.9 0.0 copy-start.1
  9.9 1.6 %copy-done.1 = f32[2,4,512,128]{3,2,1,0:T(8,128)S(1)} copy-done((f32[2,4,512,128]{3,2,1,0:T(8,128)S(1)}, f32[2,4,512,128]{3,2,1,0:T(8,128)}, u32[]{:S(2)}) %copy-start.1) | copy-done | bytes 2097176
  11.5 0.0 copy-start.2
  11.5 0.7 %copy-done.2 = f32[2,1,4,4]{3,2,1,0:T(4,128)S(1)} copy-done((f32[2,1,4,4]{3,2,1,0:T(4,128)S(1)}, f32[2,1,4,4]{3,2,1,0:T(4,128)}, u32[]{:S(2)}) %copy-start.2) | copy-done | bytes 152
  12.1 0.0 copy-start.3
  12.1 0.7 %copy-done.3 = f32[2,1,16]{2,1,0:T(1,128)S(1)} copy-done((f32[2,1,16]{2,1,0:T(1,128)S(1)}, f32[2,1,16]{2,1,0:T(1,128)}, u32[]{:S(2)}) %copy-start.3) | copy-done | bytes 152
  12.8 1.0 %shard_map.60 = (bf16[3072,512]{1,0:T(8,128)(2,1)S(1)}, f32[2,1,4,128,128]{4,3,2,1,0:T(8,128)S(1)}, f32[2,1,16]{2,1,0:T(1,128)S(1)}) custom-call(f32[2,4,512,128]{3,2,1,0:T(8,128)S(1)} %copy-done.1, f32[2,1,4,4]{3,2,1,0:T(4,128)S(1)} %copy-done.2, f32[2,1,16]{2,1,0:T(1,128)S(1)} %copy-done.3), custom_call_target="tpu_custom_call" | custom-call | flops 2097152 | bytes 4194304 | tf_op jit(solution)/shard_map/pallas_call | solution.py:85
  13.8 0.0 collective-permute-done.6.refs_1_.refs_5_.refs_7_
  13.8 0.0 collective-permute-done.5.block_ref.refs_1_.refs_3_
  13.9 0.6 %collective-permute-start.7 = (f32[2,2,136,128]{3,2,1,0:T(8,128)S(1)}, f32[2,2,136,128]{3,2,1,0:T(8,128)S(1)}, u32[]{:S(2)}, u32[]{:S(2)}) collective-permute-start(f32[2,2,136,128]{3,2,1,0:T(8,128)S(1)} %shard_map.65), channel_id=1, source_target_pairs={{0,16},{4,20},{8,24},{12,28},{16,0},{20,4},{24,8},{28,12},{1,17},{... | collective-permute-start | bytes 835592 | tf_op jit(solution)/shard_map/ppermute | solution.py:247
  14.4 0.0 collective-permute-start.1
  14.5 1.1 %collective-permute-done.1.refs_0_.refs_7_ = f32[2,1,16]{2,1,0:T(1,128)S(1)} collective-permute-done((f32[2,1,16]{2,1,0:T(1,128)S(1)}, f32[2,1,16]{2,1,0:T(1,128)S(1)}, u32[]{:S(2)}, u32[]{:S(2)}) %collective-permute-start.1) | collective-permute-done | bytes 160 | tf_op jit(solution)/shard_map/ppermute | solution.py:247
  15.6 2.7 %collective-permute-done.x_ref = f32[2,2,128,128]{3,2,1,0:T(8,128)S(1)} collective-permute-done((f32[2,2,128,128]{3,2,1,0:T(8,128)}, f32[2,2,128,128]{3,2,1,0:T(8,128)S(1)}, u32[]{:S(2)}, u32[]{:S(2)}) %collective-permute-start) | collective-permute-done | bytes 262176 | tf_op jit(solution)/shard_map/ppermute | solution.py:247
  18.3 0.1 collective-permute-done.3.refs_0_
  18.5 0.0 collective-permute-done.4.refs_0_.refs_2_.refs_4_
  18.5 0.1 collective-permute-start.9
  18.6 1.5 %collective-permute-start.2 = (f32[2,2,128,128]{3,2,1,0:T(8,128)S(1)}, f32[2,2,128,128]{3,2,1,0:T(8,128)S(1)}, u32[]{:S(2)}, u32[]{:S(2)}) collective-permute-start(f32[2,2,128,128]{3,2,1,0:T(8,128)S(1)} %shard_map.59.x_ref), channel_id=1, source_target_pairs={{0,1},{1,0},{2,3},{3,2},{4,5},{5,4},{6,7},{7,6},{8,9},{9,8},{10,11... | collective-permute-start | bytes 786440 | tf_op jit(solution)/shard_map/ppermute | solution.py:247
  20.1 1.1 %collective-permute-done.7.refs_3_.refs_5_ = f32[2,2,136,128]{3,2,1,0:T(8,128)S(1)} collective-permute-done((f32[2,2,136,128]{3,2,1,0:T(8,128)S(1)}, f32[2,2,136,128]{3,2,1,0:T(8,128)S(1)}, u32[]{:S(2)}, u32[]{:S(2)}) %collective-permute-start.7) | collective-permute-done | bytes 278560 | tf_op jit(solution)/shard_map/ppermute | solution.py:247
  21.2 0.0 copy-done
  21.2 0.5 %shard_map.66 = (f32[2,1,128,128]{3,2,1,0:T(8,128)S(1)}, f32[2,1,128,128]{3,2,1,0:T(8,128)S(1)}) custom-call(f32[2,2,128,128]{3,2,1,0:T(8,128)S(1)} %copy-done, f32[2,2,128,128]{3,2,1,0:T(8,128)S(1)} %collective-permute-done.5.block_ref.refs_1_.refs_3_, f32[2,2,128,128]{3,2,1,0:T(8,128)S(1)} %collective-permute-done.4.refs_0_.refs_2_.refs_4_, ...), custom_call_target="tpu_custom_call" | custom-call | flops 2097152 | bytes 4194304 | tf_op jit(solution)/shard_map/pallas_call | solution.py:237
  21.7 0.1 collective-permute-start.8
  21.8 0.0 collective-permute-done.9.refs_1_
  21.8 0.5 %shard_map.67 = (f32[2,1,128,128]{3,2,1,0:T(8,128)S(1)}, f32[2,1,128,128]{3,2,1,0:T(8,128)S(1)}, f32[2,1,128,128]{3,2,1,0:T(8,128)S(1)}, f32[2,1,128,128]{3,2,1,0:T(8,128)S(1)}) custom-call(f32[2,2,128,128]{3,2,1,0:T(8,128)S(1)} %shard_map.62.refs_1_.refs_0_, f32[2,2,128,128]{3,2,1,0:T(8,128)S(1)} %collective-permute-done.9.refs_1_, ...), custom_call_target="tpu_custom_call" | custom-call | flops 2097152 | bytes 4194304 | tf_op jit(solution)/shard_map/pallas_call | solution.py:237
  22.2 1.6 %collective-permute-start.12 = (f32[2,1,128,128]{3,2,1,0:T(8,128)S(1)}, f32[2,1,128,128]{3,2,1,0:T(8,128)S(1)}, u32[]{:S(2)}, u32[]{:S(2)}) collective-permute-start(f32[2,1,128,128]{3,2,1,0:T(8,128)S(1)} %get-tuple-element.16), channel_id=1, source_target_pairs={{0,24},{4,28},{8,16},{12,20},{16,8},{20,12},{24,0},{28,4},{1,25},{... | collective-permute-start | bytes 393224 | tf_op jit(solution)/shard_map/ppermute | solution.py:247
  23.8 0.0 collective-permute-done.8.refs_1_
  23.8 1.6 %collective-permute-start.10 = (f32[2,1,128,128]{3,2,1,0:T(8,128)S(1)}, f32[2,1,128,128]{3,2,1,0:T(8,128)S(1)}, u32[]{:S(2)}, u32[]{:S(2)}) collective-permute-start(f32[2,1,128,128]{3,2,1,0:T(8,128)S(1)} %shard_map.68.refs_0_), channel_id=1, source_target_pairs={{0,3},{1,2},{2,1},{3,0},{4,7},{5,6},{6,5},{7,4},{8,11},{9,10},{10,... | collective-permute-start | bytes 393224 | tf_op jit(solution)/shard_map/ppermute | solution.py:247
  25.4 0.4 %collective-permute-start.11 = (f32[2,1,128,128]{3,2,1,0:T(8,128)S(1)}, f32[2,1,128,128]{3,2,1,0:T(8,128)S(1)}, u32[]{:S(2)}, u32[]{:S(2)}) collective-permute-start(f32[2,1,128,128]{3,2,1,0:T(8,128)S(1)} %shard_map.68.refs_0_), channel_id=1, source_target_pairs={{0,1},{1,0},{2,3},{3,2},{4,5},{5,4},{6,7},{7,6},{8,9},{9,8},{10,11... | collective-permute-start | bytes 393224 | tf_op jit(solution)/shard_map/ppermute | solution.py:247
  25.8 0.7 %collective-permute-start.14 = (f32[2,1,128,128]{3,2,1,0:T(8,128)S(1)}, f32[2,1,128,128]{3,2,1,0:T(8,128)S(1)}, u32[]{:S(2)}, u32[]{:S(2)}) collective-permute-start(f32[2,1,128,128]{3,2,1,0:T(8,128)S(1)} %shard_map.71), channel_id=1, source_target_pairs={{0,16},{4,20},{8,24},{12,28},{16,0},{20,4},{24,8},{28,12},{1,17},{... | collective-permute-start | bytes 393224 | tf_op jit(solution)/shard_map/ppermute | solution.py:247
  26.6 2.6 %collective-permute-done.12.refs_0_.refs_3_ = f32[2,1,128,128]{3,2,1,0:T(8,128)S(1)} collective-permute-done((f32[2,1,128,128]{3,2,1,0:T(8,128)S(1)}, f32[2,1,128,128]{3,2,1,0:T(8,128)S(1)}, u32[]{:S(2)}, u32[]{:S(2)}) %collective-permute-start.12) | collective-permute-done | bytes 131104 | tf_op jit(solution)/shard_map/ppermute | solution.py:247
  29.2 1.3 %collective-permute-start.13 = (f32[2,1,128,128]{3,2,1,0:T(8,128)S(1)}, f32[2,1,128,128]{3,2,1,0:T(8,128)S(1)}, u32[]{:S(2)}, u32[]{:S(2)}) collective-permute-start(f32[2,1,128,128]{3,2,1,0:T(8,128)S(1)} %shard_map.70), channel_id=1, source_target_pairs={{0,8},{4,12},{8,0},{12,4},{16,24},{20,28},{24,16},{28,20},{1,9},{5... | collective-permute-start | bytes 393224 | tf_op jit(solution)/shard_map/ppermute | solution.py:247
  30.5 1.4 %shard_map.63.refs_2_ = f32[2,2,4,128,128]{4,3,2,1,0:T(8,128)S(1)} custom-call(f32[2,2,128,128]{3,2,1,0:T(8,128)S(1)} %collective-permute-done.3.refs_0_, f32[2,2,128,128]{3,2,1,0:T(8,128)S(1)} %shard_map.62.refs_1_.refs_0_, f32[2,2,128,128]{3,2,1,0:T(8,128)S(1)} %copy-done, bf16[3072,512]{1,0:T(8,128)(2,1)S(1)} %get-tuple-element.11.refs_3_.refs_1_.refs_6_), custom_call_target="tpu_custom_call" | custom-call | flops 1207959552 | bytes 4194304 | tf_op jit(solution)/shard_map/pallas_call | solution.py:182
  31.9 0.0 collective-permute-done.2.refs_0_
  31.9 1.5 %shard_map.64 = f32[2,2,4,128,128]{4,3,2,1,0:T(8,128)} custom-call(f32[2,2,128,128]{3,2,1,0:T(8,128)S(1)} %collective-permute-done.2.refs_0_, bf16[3072,512]{1,0:T(8,128)(2,1)S(1)} %get-tuple-element.11.refs_3_.refs_1_.refs_6_, f32[2,2,4,128,128]{4,3,2,1,0:T(8,128)S(1)} %shard_map.63.refs_2_), custom_call_target="tpu_custom_call" | custom-call | flops 402653184 | bytes 4194304 | tf_op jit(solution)/shard_map/pallas_call | solution.py:182
  33.4 0.4 %shard_map.72.refs_7_ = f32[2,1,4,128,128]{4,3,2,1,0:T(8,128)S(1)} custom-call(f32[2,1,128,128]{3,2,1,0:T(8,128)S(1)} %shard_map.68.refs_0_, bf16[3072,512]{1,0:T(8,128)(2,1)S(1)} %get-tuple-element.11.refs_3_.refs_1_.refs_6_, f32[2,1,4,128,128]{4,3,2,1,0:T(8,128)S(1)} %get-tuple-element.19.refs_2_), custom_call_target="tpu_custom_call" | custom-call | flops 201326592 | bytes 4194304 | tf_op jit(solution)/shard_map/pallas_call | solution.py:182
  33.8 0.0 collective-permute-done.14.refs_5_
  33.8 0.5 %collective-permute-done.13.refs_4_ = f32[2,1,128,128]{3,2,1,0:T(8,128)S(1)} collective-permute-done((f32[2,1,128,128]{3,2,1,0:T(8,128)S(1)}, f32[2,1,128,128]{3,2,1,0:T(8,128)S(1)}, u32[]{:S(2)}, u32[]{:S(2)}) %collective-permute-start.13) | collective-permute-done | bytes 131104 | tf_op jit(solution)/shard_map/ppermute | solution.py:247
  34.3 0.0 collective-permute-done.10.refs_0_
  34.3 0.0 collective-permute-done.11.refs_1_
  34.3 1.6 %shard_map.73 = f32[2,1,4,128,128]{4,3,2,1,0:T(8,128)} custom-call(f32[2,1,128,128]{3,2,1,0:T(8,128)S(1)} %collective-permute-done.10.refs_0_, f32[2,1,128,128]{3,2,1,0:T(8,128)S(1)} %collective-permute-done.11.refs_1_, f32[2,1,128,128]{3,2,1,0:T(8,128)S(1)} %get-tuple-element.15.refs_2_, f32[2,1,128,128]{3,2,1,0:T(8,128)S(1)} %collective-permute-done.12.refs_0_.refs_3_, ...), custom_call_target="tpu_custom_call" | custom-call | flops 603979776 | bytes 4194304 | tf_op jit(solution)/shard_map/pallas_call | solution.py:182
  (8 shorter events, 0.1 us)
Async XLA Ops:
  0.6 20.6 %copy-start = (f32[2,2,128,128]{3,2,1,0:T(8,128)S(1)}, f32[2,2,128,128]{3,2,1,0:T(8,128)}, u32[]{:S(2)}) copy-start(f32[2,2,128,128]{3,2,1,0:T(8,128)} %refs_2_.3) | copy-start | bytes 786436
  0.6 13.2 %collective-permute-start.5 = (f32[2,2,128,128]{3,2,1,0:T(8,128)}, f32[2,2,128,128]{3,2,1,0:T(8,128)S(1)}, u32[]{:S(2)}, u32[]{:S(2)}) collective-permute-start(f32[2,2,128,128]{3,2,1,0:T(8,128)} %refs_2_.3), channel_id=1, source_target_pairs={{0,8},{4,12},{8,0},{12,4},{16,24},{20,28},{24,16},{28,20},{1,9},{5... | collective-permute-start | bytes 786440 | tf_op jit(solution)/shard_map/ppermute | solution.py:247
  3.6 14.6 %collective-permute-start = (f32[2,2,128,128]{3,2,1,0:T(8,128)}, f32[2,2,128,128]{3,2,1,0:T(8,128)S(1)}, u32[]{:S(2)}, u32[]{:S(2)}) collective-permute-start(f32[2,2,128,128]{3,2,1,0:T(8,128)} %refs_2_.3), channel_id=1, source_target_pairs={{0,2},{1,3},{2,0},{3,1},{4,6},{5,7},{6,4},{7,5},{8,10},{9,11},{10,... | collective-permute-start | bytes 786440 | tf_op jit(solution)/shard_map/ppermute | solution.py:247
  6.2 12.2 %collective-permute-start.3 = (f32[2,2,128,128]{3,2,1,0:T(8,128)}, f32[2,2,128,128]{3,2,1,0:T(8,128)S(1)}, u32[]{:S(2)}, u32[]{:S(2)}) collective-permute-start(f32[2,2,128,128]{3,2,1,0:T(8,128)} %refs_2_.3), channel_id=1, source_target_pairs={{0,1},{1,0},{2,3},{3,2},{4,5},{5,4},{6,7},{7,6},{8,9},{9,8},{10,11... | collective-permute-start | bytes 786440 | tf_op jit(solution)/shard_map/ppermute | solution.py:247
  7.8 10.6 %collective-permute-start.4 = (f32[2,2,128,128]{3,2,1,0:T(8,128)}, f32[2,2,128,128]{3,2,1,0:T(8,128)S(1)}, u32[]{:S(2)}, u32[]{:S(2)}) collective-permute-start(f32[2,2,128,128]{3,2,1,0:T(8,128)} %refs_2_.3), channel_id=1, source_target_pairs={{0,16},{4,20},{8,24},{12,28},{16,0},{20,4},{24,8},{28,12},{1,17},{... | collective-permute-start | bytes 786440 | tf_op jit(solution)/shard_map/ppermute | solution.py:247
  9.3 4.5 %collective-permute-start.6 = (f32[2,1,16]{2,1,0:T(1,128)}, f32[2,1,16]{2,1,0:T(1,128)S(1)}, u32[]{:S(2)}, u32[]{:S(2)}) collective-permute-start(f32[2,1,16]{2,1,0:T(1,128)} %integrals_ref.1), channel_id=1, source_target_pairs={{0,8},{4,12},{8,0},{12,4},{16,24},{20,28},{24,16},{28,20},{1,9},{5... | collective-permute-start | bytes 392 | tf_op jit(solution)/shard_map/ppermute | solution.py:247
  9.9 1.6 %copy-start.1 = (f32[2,4,512,128]{3,2,1,0:T(8,128)S(1)}, f32[2,4,512,128]{3,2,1,0:T(8,128)}, u32[]{:S(2)}) copy-start(f32[2,4,512,128]{3,2,1,0:T(8,128)} %basis_hbm.1) | copy-start | bytes 6291460
  11.5 0.7 %copy-start.2 = (f32[2,1,4,4]{3,2,1,0:T(4,128)S(1)}, f32[2,1,4,4]{3,2,1,0:T(4,128)}, u32[]{:S(2)}) copy-start(f32[2,1,4,4]{3,2,1,0:T(4,128)} %site_hbm.1) | copy-start | bytes 388
  12.1 0.7 %copy-start.3 = (f32[2,1,16]{2,1,0:T(1,128)S(1)}, f32[2,1,16]{2,1,0:T(1,128)}, u32[]{:S(2)}) copy-start(f32[2,1,16]{2,1,0:T(1,128)} %integrals_ref.1) | copy-start | bytes 388
  13.9 7.3 %collective-permute-start.7 = (f32[2,2,136,128]{3,2,1,0:T(8,128)S(1)}, f32[2,2,136,128]{3,2,1,0:T(8,128)S(1)}, u32[]{:S(2)}, u32[]{:S(2)}) collective-permute-start(f32[2,2,136,128]{3,2,1,0:T(8,128)S(1)} %shard_map.65), channel_id=1, source_target_pairs={{0,16},{4,20},{8,24},{12,28},{16,0},{20,4},{24,8},{28,12},{1,17},{... | collective-permute-start | bytes 835592 | tf_op jit(solution)/shard_map/ppermute | solution.py:247
  14.4 1.1 %collective-permute-start.1 = (f32[2,1,16]{2,1,0:T(1,128)S(1)}, f32[2,1,16]{2,1,0:T(1,128)S(1)}, u32[]{:S(2)}, u32[]{:S(2)}) collective-permute-start(f32[2,1,16]{2,1,0:T(1,128)S(1)} %copy-done.3), channel_id=1, source_target_pairs={{0,4},{4,0},{8,12},{12,8},{16,20},{20,16},{24,28},{28,24},{1,5},{5... | collective-permute-start | bytes 392 | tf_op jit(solution)/shard_map/ppermute | solution.py:247
  18.5 3.3 %collective-permute-start.9 = (f32[2,2,128,128]{3,2,1,0:T(8,128)S(1)}, f32[2,2,128,128]{3,2,1,0:T(8,128)S(1)}, u32[]{:S(2)}, u32[]{:S(2)}) collective-permute-start(f32[2,2,128,128]{3,2,1,0:T(8,128)S(1)} %shard_map.62.refs_1_.refs_0_), channel_id=1, source_target_pairs={{0,4},{4,0},{8,12},{12,8},{16,20},{20,16},{24,28},{28,24},{1,5},{5... | collective-permute-start | bytes 786440 | tf_op jit(solution)/shard_map/ppermute | solution.py:247
  18.6 13.3 %collective-permute-start.2 = (f32[2,2,128,128]{3,2,1,0:T(8,128)S(1)}, f32[2,2,128,128]{3,2,1,0:T(8,128)S(1)}, u32[]{:S(2)}, u32[]{:S(2)}) collective-permute-start(f32[2,2,128,128]{3,2,1,0:T(8,128)S(1)} %shard_map.59.x_ref), channel_id=1, source_target_pairs={{0,1},{1,0},{2,3},{3,2},{4,5},{5,4},{6,7},{7,6},{8,9},{9,8},{10,11... | collective-permute-start | bytes 786440 | tf_op jit(solution)/shard_map/ppermute | solution.py:247
  21.7 2.1 %collective-permute-start.8 = (f32[2,1,128,128]{3,2,1,0:T(8,128)S(1)}, f32[2,1,128,128]{3,2,1,0:T(8,128)S(1)}, u32[]{:S(2)}, u32[]{:S(2)}) collective-permute-start(f32[2,1,128,128]{3,2,1,0:T(8,128)S(1)} %get-tuple-element.14), channel_id=1, source_target_pairs={{0,4},{4,0},{8,12},{12,8},{16,20},{20,16},{24,28},{28,24},{1,5},{5... | collective-permute-start | bytes 393224 | tf_op jit(solution)/shard_map/ppermute | solution.py:247
  22.2 7.0 %collective-permute-start.12 = (f32[2,1,128,128]{3,2,1,0:T(8,128)S(1)}, f32[2,1,128,128]{3,2,1,0:T(8,128)S(1)}, u32[]{:S(2)}, u32[]{:S(2)}) collective-permute-start(f32[2,1,128,128]{3,2,1,0:T(8,128)S(1)} %get-tuple-element.16), channel_id=1, source_target_pairs={{0,24},{4,28},{8,16},{12,20},{16,8},{20,12},{24,0},{28,4},{1,25},{... | collective-permute-start | bytes 393224 | tf_op jit(solution)/shard_map/ppermute | solution.py:247
  23.8 10.4 %collective-permute-start.10 = (f32[2,1,128,128]{3,2,1,0:T(8,128)S(1)}, f32[2,1,128,128]{3,2,1,0:T(8,128)S(1)}, u32[]{:S(2)}, u32[]{:S(2)}) collective-permute-start(f32[2,1,128,128]{3,2,1,0:T(8,128)S(1)} %shard_map.68.refs_0_), channel_id=1, source_target_pairs={{0,3},{1,2},{2,1},{3,0},{4,7},{5,6},{6,5},{7,4},{8,11},{9,10},{10,... | collective-permute-start | bytes 393224 | tf_op jit(solution)/shard_map/ppermute | solution.py:247
  25.4 8.8 %collective-permute-start.11 = (f32[2,1,128,128]{3,2,1,0:T(8,128)S(1)}, f32[2,1,128,128]{3,2,1,0:T(8,128)S(1)}, u32[]{:S(2)}, u32[]{:S(2)}) collective-permute-start(f32[2,1,128,128]{3,2,1,0:T(8,128)S(1)} %shard_map.68.refs_0_), channel_id=1, source_target_pairs={{0,1},{1,0},{2,3},{3,2},{4,5},{5,4},{6,7},{7,6},{8,9},{9,8},{10,11... | collective-permute-start | bytes 393224 | tf_op jit(solution)/shard_map/ppermute | solution.py:247
  25.8 8.0 %collective-permute-start.14 = (f32[2,1,128,128]{3,2,1,0:T(8,128)S(1)}, f32[2,1,128,128]{3,2,1,0:T(8,128)S(1)}, u32[]{:S(2)}, u32[]{:S(2)}) collective-permute-start(f32[2,1,128,128]{3,2,1,0:T(8,128)S(1)} %shard_map.71), channel_id=1, source_target_pairs={{0,16},{4,20},{8,24},{12,28},{16,0},{20,4},{24,8},{28,12},{1,17},{... | collective-permute-start | bytes 393224 | tf_op jit(solution)/shard_map/ppermute | solution.py:247
  29.2 5.1 %collective-permute-start.13 = (f32[2,1,128,128]{3,2,1,0:T(8,128)S(1)}, f32[2,1,128,128]{3,2,1,0:T(8,128)S(1)}, u32[]{:S(2)}, u32[]{:S(2)}) collective-permute-start(f32[2,1,128,128]{3,2,1,0:T(8,128)S(1)} %shard_map.70), channel_id=1, source_target_pairs={{0,8},{4,12},{8,0},{12,4},{16,24},{20,28},{24,16},{28,20},{1,9},{5... | collective-permute-start | bytes 393224 | tf_op jit(solution)/shard_map/ppermute | solution.py:247

commit v12 on v10

--- a/solution.py
+++ b/solution.py
@@ -299,7 +299,9 @@
     near = swap(comp_ops, "sec", sec, 1)
     summed = [parts[0]]
     for key in range(2, pairs, 2):
-        part = after(parts[key // 2], comp_ops)
+        part = parts[key // 2]
+        if key < pairs - 2:
+            part = after(part, comp_ops)
         if key == 2:
             part = after(part, three)
         summed.append(swap(part, "pair", pairs, key))

time: 35.6 us -> 35.5 us (level); the launches traced: 35.4 us -> 35 us
  waiting for transfers between devices: 8.38 us -> 7.9 us
    ppermute x15, waiting for transfers between devices: 8.38 us -> 7.9 us  [swap(): return lax.ppermute(x, axis, [(at, at ^ key) for at in range(size)])]
where the time goes in v12:
time: 35.5 us; the launch traced here: 35 us
  starting transfers between devices  16.4 us (46%)
  waiting for transfers between devices  7.9 us (22%)
  Pallas kernels  6.89 us (19%)
  local copies, waits for them, and re-layouts  2.96 us (8%)
  between operations  0.79 us (2%)
    ppermute x15, starting transfers between devices, swap(): return lax.ppermute(x, axis, [(at, at ^ key) for at in range(size)])  16.4 us
    ppermute x15, waiting for transfers between devices, swap(): return lax.ppermute(x, axis, [(at, at ^ key) for at in range(size)])  7.9 us
    pallas_call x4, Pallas kernels, renorm(): pl.pallas_call(functools.partial(renorm_kernel, steps, parts, carry is no...  4.85 us
    unnamed x8, local copies, waits for them, and re-layouts  2.96 us
    pallas_call x1, Pallas kernels, prepare(): call(functools.partial(prepare_kernel, depth), (halves, part, jax.ShapeDt...  0.99 us
    pallas_call x2, Pallas kernels, combine(): call(functools.partial(combine_kernel, operators, tables, per), (jax.Shap...  0.93 us
  transfers between devices with their start and end apart: 15, of which 8 were waited for; matrix products, arithmetic and copies ran while one was open for 0% of the time, Pallas kernels for 15%

profile of v12, /device:TPU:0, one launch (start us, length us, event | category | flops | bytes accessed | tf_op | source)
XLA Modules:
  0.0 35.0 jit_solution(701452846214069498)
XLA Ops:
  0.6 0.0 copy-start
  0.6 3.0 %collective-permute-start.5 = (f32[2,2,128,128]{3,2,1,0:T(8,128)}, f32[2,2,128,128]{3,2,1,0:T(8,128)S(1)}, u32[]{:S(2)}, u32[]{:S(2)}) collective-permute-start(f32[2,2,128,128]{3,2,1,0:T(8,128)} %refs_2_.3), channel_id=1, source_target_pairs={{0,8},{4,12},{8,0},{12,4},{16,24},{20,28},{24,16},{28,20},{1,9},{5... | collective-permute-start | bytes 786440 | tf_op jit(solution)/shard_map/ppermute | solution.py:247
  3.6 2.6 %collective-permute-start = (f32[2,2,128,128]{3,2,1,0:T(8,128)}, f32[2,2,128,128]{3,2,1,0:T(8,128)S(1)}, u32[]{:S(2)}, u32[]{:S(2)}) collective-permute-start(f32[2,2,128,128]{3,2,1,0:T(8,128)} %refs_2_.3), channel_id=1, source_target_pairs={{0,2},{1,3},{2,0},{3,1},{4,6},{5,7},{6,4},{7,5},{8,10},{9,11},{10,... | collective-permute-start | bytes 786440 | tf_op jit(solution)/shard_map/ppermute | solution.py:247
  6.2 1.6 %collective-permute-start.3 = (f32[2,2,128,128]{3,2,1,0:T(8,128)}, f32[2,2,128,128]{3,2,1,0:T(8,128)S(1)}, u32[]{:S(2)}, u32[]{:S(2)}) collective-permute-start(f32[2,2,128,128]{3,2,1,0:T(8,128)} %refs_2_.3), channel_id=1, source_target_pairs={{0,1},{1,0},{2,3},{3,2},{4,5},{5,4},{6,7},{7,6},{8,9},{9,8},{10,11... | collective-permute-start | bytes 786440 | tf_op jit(solution)/shard_map/ppermute | solution.py:247
  7.8 1.5 %collective-permute-start.4 = (f32[2,2,128,128]{3,2,1,0:T(8,128)}, f32[2,2,128,128]{3,2,1,0:T(8,128)S(1)}, u32[]{:S(2)}, u32[]{:S(2)}) collective-permute-start(f32[2,2,128,128]{3,2,1,0:T(8,128)} %refs_2_.3), channel_id=1, source_target_pairs={{0,16},{4,20},{8,24},{12,28},{16,0},{20,4},{24,8},{28,12},{1,17},{... | collective-permute-start | bytes 786440 | tf_op jit(solution)/shard_map/ppermute | solution.py:247
  9.3 0.5 %collective-permute-start.6 = (f32[2,1,16]{2,1,0:T(1,128)}, f32[2,1,16]{2,1,0:T(1,128)S(1)}, u32[]{:S(2)}, u32[]{:S(2)}) collective-permute-start(f32[2,1,16]{2,1,0:T(1,128)} %integrals_ref.1), channel_id=1, source_target_pairs={{0,8},{4,12},{8,0},{12,4},{16,24},{20,28},{24,16},{28,20},{1,9},{5... | collective-permute-start | bytes 392 | tf_op jit(solution)/shard_map/ppermute | solution.py:247
  9.9 0.0 copy-start.1
  9.9 1.6 %copy-done.1 = f32[2,4,512,128]{3,2,1,0:T(8,128)S(1)} copy-done((f32[2,4,512,128]{3,2,1,0:T(8,128)S(1)}, f32[2,4,512,128]{3,2,1,0:T(8,128)}, u32[]{:S(2)}) %copy-start.1) | copy-done | bytes 2097176
  11.5 0.0 copy-start.2
  11.5 0.7 %copy-done.2 = f32[2,1,4,4]{3,2,1,0:T(4,128)S(1)} copy-done((f32[2,1,4,4]{3,2,1,0:T(4,128)S(1)}, f32[2,1,4,4]{3,2,1,0:T(4,128)}, u32[]{:S(2)}) %copy-start.2) | copy-done | bytes 152
  12.1 0.0 copy-start.3
  12.1 0.7 %copy-done.3 = f32[2,1,16]{2,1,0:T(1,128)S(1)} copy-done((f32[2,1,16]{2,1,0:T(1,128)S(1)}, f32[2,1,16]{2,1,0:T(1,128)}, u32[]{:S(2)}) %copy-start.3) | copy-done | bytes 152
  12.8 1.0 %shard_map.60 = (bf16[3072,512]{1,0:T(8,128)(2,1)S(1)}, f32[2,1,4,128,128]{4,3,2,1,0:T(8,128)S(1)}, f32[2,1,16]{2,1,0:T(1,128)S(1)}) custom-call(f32[2,4,512,128]{3,2,1,0:T(8,128)S(1)} %copy-done.1, f32[2,1,4,4]{3,2,1,0:T(4,128)S(1)} %copy-done.2, f32[2,1,16]{2,1,0:T(1,128)S(1)} %copy-done.3), custom_call_target="tpu_custom_call" | custom-call | flops 2097152 | bytes 4194304 | tf_op jit(solution)/shard_map/pallas_call | solution.py:85
  13.8 0.0 collective-permute-done.6.refs_1_.refs_5_.refs_7_
  13.8 0.0 collective-permute-done.5.block_ref.refs_1_.refs_3_
  13.9 0.6 %collective-permute-start.7 = (f32[2,2,136,128]{3,2,1,0:T(8,128)S(1)}, f32[2,2,136,128]{3,2,1,0:T(8,128)S(1)}, u32[]{:S(2)}, u32[]{:S(2)}) collective-permute-start(f32[2,2,136,128]{3,2,1,0:T(8,128)S(1)} %shard_map.65), channel_id=1, source_target_pairs={{0,16},{4,20},{8,24},{12,28},{16,0},{20,4},{24,8},{28,12},{1,17},{... | collective-permute-start | bytes 835592 | tf_op jit(solution)/shard_map/ppermute | solution.py:247
  14.4 0.0 collective-permute-start.1
  14.5 1.1 %collective-permute-done.1.refs_0_.refs_7_ = f32[2,1,16]{2,1,0:T(1,128)S(1)} collective-permute-done((f32[2,1,16]{2,1,0:T(1,128)S(1)}, f32[2,1,16]{2,1,0:T(1,128)S(1)}, u32[]{:S(2)}, u32[]{:S(2)}) %collective-permute-start.1) | collective-permute-done | bytes 160 | tf_op jit(solution)/shard_map/ppermute | solution.py:247
  15.6 2.7 %collective-permute-done.x_ref = f32[2,2,128,128]{3,2,1,0:T(8,128)S(1)} collective-permute-done((f32[2,2,128,128]{3,2,1,0:T(8,128)}, f32[2,2,128,128]{3,2,1,0:T(8,128)S(1)}, u32[]{:S(2)}, u32[]{:S(2)}) %collective-permute-start) | collective-permute-done | bytes 262176 | tf_op jit(solution)/shard_map/ppermute | solution.py:247
  18.3 0.1 collective-permute-done.3.refs_0_
  18.5 0.0 collective-permute-done.4.refs_0_.refs_2_.refs_4_
  18.5 0.1 collective-permute-start.9
  18.6 1.5 %collective-permute-start.2 = (f32[2,2,128,128]{3,2,1,0:T(8,128)S(1)}, f32[2,2,128,128]{3,2,1,0:T(8,128)S(1)}, u32[]{:S(2)}, u32[]{:S(2)}) collective-permute-start(f32[2,2,128,128]{3,2,1,0:T(8,128)S(1)} %shard_map.59.x_ref), channel_id=1, source_target_pairs={{0,1},{1,0},{2,3},{3,2},{4,5},{5,4},{6,7},{7,6},{8,9},{9,8},{10,11... | collective-permute-start | bytes 786440 | tf_op jit(solution)/shard_map/ppermute | solution.py:247
  20.1 1.1 %collective-permute-done.7.refs_3_.refs_5_ = f32[2,2,136,128]{3,2,1,0:T(8,128)S(1)} collective-permute-done((f32[2,2,136,128]{3,2,1,0:T(8,128)S(1)}, f32[2,2,136,128]{3,2,1,0:T(8,128)S(1)}, u32[]{:S(2)}, u32[]{:S(2)}) %collective-permute-start.7) | collective-permute-done | bytes 278560 | tf_op jit(solution)/shard_map/ppermute | solution.py:247
  21.2 0.0 copy-done
  21.2 0.5 %shard_map.66 = (f32[2,1,128,128]{3,2,1,0:T(8,128)S(1)}, f32[2,1,128,128]{3,2,1,0:T(8,128)S(1)}) custom-call(f32[2,2,128,128]{3,2,1,0:T(8,128)S(1)} %copy-done, f32[2,2,128,128]{3,2,1,0:T(8,128)S(1)} %collective-permute-done.5.block_ref.refs_1_.refs_3_, f32[2,2,128,128]{3,2,1,0:T(8,128)S(1)} %collective-permute-done.4.refs_0_.refs_2_.refs_4_, ...), custom_call_target="tpu_custom_call" | custom-call | flops 2097152 | bytes 4194304 | tf_op jit(solution)/shard_map/pallas_call | solution.py:237
  21.7 0.1 collective-permute-start.8
  21.8 0.0 collective-permute-done.9.refs_1_
  21.8 0.5 %shard_map.67 = (f32[2,1,128,128]{3,2,1,0:T(8,128)S(1)}, f32[2,1,128,128]{3,2,1,0:T(8,128)S(1)}, f32[2,1,128,128]{3,2,1,0:T(8,128)S(1)}, f32[2,1,128,128]{3,2,1,0:T(8,128)S(1)}) custom-call(f32[2,2,128,128]{3,2,1,0:T(8,128)S(1)} %shard_map.62.refs_1_.refs_0_, f32[2,2,128,128]{3,2,1,0:T(8,128)S(1)} %collective-permute-done.9.refs_1_, ...), custom_call_target="tpu_custom_call" | custom-call | flops 2097152 | bytes 4194304 | tf_op jit(solution)/shard_map/pallas_call | solution.py:237
  22.2 1.6 %collective-permute-start.14 = (f32[2,1,128,128]{3,2,1,0:T(8,128)S(1)}, f32[2,1,128,128]{3,2,1,0:T(8,128)S(1)}, u32[]{:S(2)}, u32[]{:S(2)}) collective-permute-start(f32[2,1,128,128]{3,2,1,0:T(8,128)S(1)} %get-tuple-element.18), channel_id=1, source_target_pairs={{0,24},{4,28},{8,16},{12,20},{16,8},{20,12},{24,0},{28,4},{1,25},{... | collective-permute-start | bytes 393224 | tf_op jit(solution)/shard_map/ppermute | solution.py:247
  23.8 0.0 collective-permute-done.8.refs_1_
  23.8 1.6 %collective-permute-start.10 = (f32[2,1,128,128]{3,2,1,0:T(8,128)S(1)}, f32[2,1,128,128]{3,2,1,0:T(8,128)S(1)}, u32[]{:S(2)}, u32[]{:S(2)}) collective-permute-start(f32[2,1,128,128]{3,2,1,0:T(8,128)S(1)} %shard_map.68.refs_0_), channel_id=1, source_target_pairs={{0,3},{1,2},{2,1},{3,0},{4,7},{5,6},{6,5},{7,4},{8,11},{9,10},{10,... | collective-permute-start | bytes 393224 | tf_op jit(solution)/shard_map/ppermute | solution.py:247
  25.4 0.4 %collective-permute-start.11 = (f32[2,1,128,128]{3,2,1,0:T(8,128)S(1)}, f32[2,1,128,128]{3,2,1,0:T(8,128)S(1)}, u32[]{:S(2)}, u32[]{:S(2)}) collective-permute-start(f32[2,1,128,128]{3,2,1,0:T(8,128)S(1)} %shard_map.68.refs_0_), channel_id=1, source_target_pairs={{0,1},{1,0},{2,3},{3,2},{4,5},{5,4},{6,7},{7,6},{8,9},{9,8},{10,11... | collective-permute-start | bytes 393224 | tf_op jit(solution)/shard_map/ppermute | solution.py:247
  25.8 0.7 %collective-permute-start.13 = (f32[2,1,128,128]{3,2,1,0:T(8,128)S(1)}, f32[2,1,128,128]{3,2,1,0:T(8,128)S(1)}, u32[]{:S(2)}, u32[]{:S(2)}) collective-permute-start(f32[2,1,128,128]{3,2,1,0:T(8,128)S(1)} %shard_map.71), channel_id=1, source_target_pairs={{0,16},{4,20},{8,24},{12,28},{16,0},{20,4},{24,8},{28,12},{1,17},{... | collective-permute-start | bytes 393224 | tf_op jit(solution)/shard_map/ppermute | solution.py:247
  26.6 0.7 %collective-permute-done.2.refs_0_ = f32[2,2,128,128]{3,2,1,0:T(8,128)S(1)} collective-permute-done((f32[2,2,128,128]{3,2,1,0:T(8,128)S(1)}, f32[2,2,128,128]{3,2,1,0:T(8,128)S(1)}, u32[]{:S(2)}, u32[]{:S(2)}) %collective-permute-start.2) | collective-permute-done | bytes 262176 | tf_op jit(solution)/shard_map/ppermute | solution.py:247
  27.3 0.7 %collective-permute-start.12 = (f32[2,1,128,128]{3,2,1,0:T(8,128)S(1)}, f32[2,1,128,128]{3,2,1,0:T(8,128)S(1)}, u32[]{:S(2)}, u32[]{:S(2)}) collective-permute-start(f32[2,1,128,128]{3,2,1,0:T(8,128)S(1)} %shard_map.70), channel_id=1, source_target_pairs={{0,8},{4,12},{8,0},{12,4},{16,24},{20,28},{24,16},{28,20},{1,9},{5... | collective-permute-start | bytes 393224 | tf_op jit(solution)/shard_map/ppermute | solution.py:247
  28.0 1.4 %shard_map.63.refs_2_ = f32[2,2,4,128,128]{4,3,2,1,0:T(8,128)S(1)} custom-call(f32[2,2,128,128]{3,2,1,0:T(8,128)S(1)} %collective-permute-done.3.refs_0_, f32[2,2,128,128]{3,2,1,0:T(8,128)S(1)} %shard_map.62.refs_1_.refs_0_, f32[2,2,128,128]{3,2,1,0:T(8,128)S(1)} %copy-done, bf16[3072,512]{1,0:T(8,128)(2,1)S(1)} %get-tuple-element.11.refs_3_.refs_1_.refs_6_), custom_call_target="tpu_custom_call" | custom-call | flops 1207959552 | bytes 4194304 | tf_op jit(solution)/shard_map/pallas_call | solution.py:182
  29.4 1.5 %shard_map.64 = f32[2,2,4,128,128]{4,3,2,1,0:T(8,128)} custom-call(f32[2,2,128,128]{3,2,1,0:T(8,128)S(1)} %collective-permute-done.2.refs_0_, bf16[3072,512]{1,0:T(8,128)(2,1)S(1)} %get-tuple-element.11.refs_3_.refs_1_.refs_6_, f32[2,2,4,128,128]{4,3,2,1,0:T(8,128)S(1)} %shard_map.63.refs_2_), custom_call_target="tpu_custom_call" | custom-call | flops 402653184 | bytes 4194304 | tf_op jit(solution)/shard_map/pallas_call | solution.py:182
  30.9 0.4 %shard_map.72.refs_7_ = f32[2,1,4,128,128]{4,3,2,1,0:T(8,128)S(1)} custom-call(f32[2,1,128,128]{3,2,1,0:T(8,128)S(1)} %shard_map.68.refs_0_, bf16[3072,512]{1,0:T(8,128)(2,1)S(1)} %get-tuple-element.11.refs_3_.refs_1_.refs_6_, f32[2,1,4,128,128]{4,3,2,1,0:T(8,128)S(1)} %get-tuple-element.19.refs_2_), custom_call_target="tpu_custom_call" | custom-call | flops 201326592 | bytes 4194304 | tf_op jit(solution)/shard_map/pallas_call | solution.py:182
  31.3 0.0 collective-permute-done.14.refs_5_
  31.3 0.6 %collective-permute-done.13.refs_4_ = f32[2,1,128,128]{3,2,1,0:T(8,128)S(1)} collective-permute-done((f32[2,1,128,128]{3,2,1,0:T(8,128)S(1)}, f32[2,1,128,128]{3,2,1,0:T(8,128)S(1)}, u32[]{:S(2)}, u32[]{:S(2)}) %collective-permute-start.13) | collective-permute-done | bytes 131104 | tf_op jit(solution)/shard_map/ppermute | solution.py:247
  31.9 0.5 %collective-permute-done.12.refs_3_ = f32[2,1,128,128]{3,2,1,0:T(8,128)S(1)} collective-permute-done((f32[2,1,128,128]{3,2,1,0:T(8,128)S(1)}, f32[2,1,128,128]{3,2,1,0:T(8,128)S(1)}, u32[]{:S(2)}, u32[]{:S(2)}) %collective-permute-start.12) | collective-permute-done | bytes 131104 | tf_op jit(solution)/shard_map/ppermute | solution.py:247
  32.4 0.0 collective-permute-done.10.refs_0_
  32.4 1.0 %collective-permute-done.11.refs_1_ = f32[2,1,128,128]{3,2,1,0:T(8,128)S(1)} collective-permute-done((f32[2,1,128,128]{3,2,1,0:T(8,128)S(1)}, f32[2,1,128,128]{3,2,1,0:T(8,128)S(1)}, u32[]{:S(2)}, u32[]{:S(2)}) %collective-permute-start.11) | collective-permute-done | bytes 131104 | tf_op jit(solution)/shard_map/ppermute | solution.py:247
  33.4 1.6 %shard_map.73 = f32[2,1,4,128,128]{4,3,2,1,0:T(8,128)} custom-call(f32[2,1,128,128]{3,2,1,0:T(8,128)S(1)} %collective-permute-done.10.refs_0_, f32[2,1,128,128]{3,2,1,0:T(8,128)S(1)} %collective-permute-done.11.refs_1_, f32[2,1,128,128]{3,2,1,0:T(8,128)S(1)} %get-tuple-element.15.refs_2_, f32[2,1,128,128]{3,2,1,0:T(8,128)S(1)} %collective-permute-done.12.refs_3_, ...), custom_call_target="tpu_custom_call" | custom-call | flops 603979776 | bytes 4194304 | tf_op jit(solution)/shard_map/pallas_call | solution.py:182
  (8 shorter events, 0.1 us)
Async XLA Ops:
  0.6 20.6 %copy-start = (f32[2,2,128,128]{3,2,1,0:T(8,128)S(1)}, f32[2,2,128,128]{3,2,1,0:T(8,128)}, u32[]{:S(2)}) copy-start(f32[2,2,128,128]{3,2,1,0:T(8,128)} %refs_2_.3) | copy-start | bytes 786436
  0.6 13.2 %collective-permute-start.5 = (f32[2,2,128,128]{3,2,1,0:T(8,128)}, f32[2,2,128,128]{3,2,1,0:T(8,128)S(1)}, u32[]{:S(2)}, u32[]{:S(2)}) collective-permute-start(f32[2,2,128,128]{3,2,1,0:T(8,128)} %refs_2_.3), channel_id=1, source_target_pairs={{0,8},{4,12},{8,0},{12,4},{16,24},{20,28},{24,16},{28,20},{1,9},{5... | collective-permute-start | bytes 786440 | tf_op jit(solution)/shard_map/ppermute | solution.py:247
  3.6 14.6 %collective-permute-start = (f32[2,2,128,128]{3,2,1,0:T(8,128)}, f32[2,2,128,128]{3,2,1,0:T(8,128)S(1)}, u32[]{:S(2)}, u32[]{:S(2)}) collective-permute-start(f32[2,2,128,128]{3,2,1,0:T(8,128)} %refs_2_.3), channel_id=1, source_target_pairs={{0,2},{1,3},{2,0},{3,1},{4,6},{5,7},{6,4},{7,5},{8,10},{9,11},{10,... | collective-permute-start | bytes 786440 | tf_op jit(solution)/shard_map/ppermute | solution.py:247
  6.2 12.2 %collective-permute-start.3 = (f32[2,2,128,128]{3,2,1,0:T(8,128)}, f32[2,2,128,128]{3,2,1,0:T(8,128)S(1)}, u32[]{:S(2)}, u32[]{:S(2)}) collective-permute-start(f32[2,2,128,128]{3,2,1,0:T(8,128)} %refs_2_.3), channel_id=1, source_target_pairs={{0,1},{1,0},{2,3},{3,2},{4,5},{5,4},{6,7},{7,6},{8,9},{9,8},{10,11... | collective-permute-start | bytes 786440 | tf_op jit(solution)/shard_map/ppermute | solution.py:247
  7.8 10.6 %collective-permute-start.4 = (f32[2,2,128,128]{3,2,1,0:T(8,128)}, f32[2,2,128,128]{3,2,1,0:T(8,128)S(1)}, u32[]{:S(2)}, u32[]{:S(2)}) collective-permute-start(f32[2,2,128,128]{3,2,1,0:T(8,128)} %refs_2_.3), channel_id=1, source_target_pairs={{0,16},{4,20},{8,24},{12,28},{16,0},{20,4},{24,8},{28,12},{1,17},{... | collective-permute-start | bytes 786440 | tf_op jit(solution)/shard_map/ppermute | solution.py:247
  9.3 4.5 %collective-permute-start.6 = (f32[2,1,16]{2,1,0:T(1,128)}, f32[2,1,16]{2,1,0:T(1,128)S(1)}, u32[]{:S(2)}, u32[]{:S(2)}) collective-permute-start(f32[2,1,16]{2,1,0:T(1,128)} %integrals_ref.1), channel_id=1, source_target_pairs={{0,8},{4,12},{8,0},{12,4},{16,24},{20,28},{24,16},{28,20},{1,9},{5... | collective-permute-start | bytes 392 | tf_op jit(solution)/shard_map/ppermute | solution.py:247
  9.9 1.6 %copy-start.1 = (f32[2,4,512,128]{3,2,1,0:T(8,128)S(1)}, f32[2,4,512,128]{3,2,1,0:T(8,128)}, u32[]{:S(2)}) copy-start(f32[2,4,512,128]{3,2,1,0:T(8,128)} %basis_hbm.1) | copy-start | bytes 6291460
  11.5 0.7 %copy-start.2 = (f32[2,1,4,4]{3,2,1,0:T(4,128)S(1)}, f32[2,1,4,4]{3,2,1,0:T(4,128)}, u32[]{:S(2)}) copy-start(f32[2,1,4,4]{3,2,1,0:T(4,128)} %site_hbm.1) | copy-start | bytes 388
  12.1 0.7 %copy-start.3 = (f32[2,1,16]{2,1,0:T(1,128)S(1)}, f32[2,1,16]{2,1,0:T(1,128)}, u32[]{:S(2)}) copy-start(f32[2,1,16]{2,1,0:T(1,128)} %integrals_ref.1) | copy-start | bytes 388
  13.9 7.3 %collective-permute-start.7 = (f32[2,2,136,128]{3,2,1,0:T(8,128)S(1)}, f32[2,2,136,128]{3,2,1,0:T(8,128)S(1)}, u32[]{:S(2)}, u32[]{:S(2)}) collective-permute-start(f32[2,2,136,128]{3,2,1,0:T(8,128)S(1)} %shard_map.65), channel_id=1, source_target_pairs={{0,16},{4,20},{8,24},{12,28},{16,0},{20,4},{24,8},{28,12},{1,17},{... | collective-permute-start | bytes 835592 | tf_op jit(solution)/shard_map/ppermute | solution.py:247
  14.4 1.1 %collective-permute-start.1 = (f32[2,1,16]{2,1,0:T(1,128)S(1)}, f32[2,1,16]{2,1,0:T(1,128)S(1)}, u32[]{:S(2)}, u32[]{:S(2)}) collective-permute-start(f32[2,1,16]{2,1,0:T(1,128)S(1)} %copy-done.3), channel_id=1, source_target_pairs={{0,4},{4,0},{8,12},{12,8},{16,20},{20,16},{24,28},{28,24},{1,5},{5... | collective-permute-start | bytes 392 | tf_op jit(solution)/shard_map/ppermute | solution.py:247
  18.5 3.3 %collective-permute-start.9 = (f32[2,2,128,128]{3,2,1,0:T(8,128)S(1)}, f32[2,2,128,128]{3,2,1,0:T(8,128)S(1)}, u32[]{:S(2)}, u32[]{:S(2)}) collective-permute-start(f32[2,2,128,128]{3,2,1,0:T(8,128)S(1)} %shard_map.62.refs_1_.refs_0_), channel_id=1, source_target_pairs={{0,4},{4,0},{8,12},{12,8},{16,20},{20,16},{24,28},{28,24},{1,5},{5... | collective-permute-start | bytes 786440 | tf_op jit(solution)/shard_map/ppermute | solution.py:247
  18.6 8.7 %collective-permute-start.2 = (f32[2,2,128,128]{3,2,1,0:T(8,128)S(1)}, f32[2,2,128,128]{3,2,1,0:T(8,128)S(1)}, u32[]{:S(2)}, u32[]{:S(2)}) collective-permute-start(f32[2,2,128,128]{3,2,1,0:T(8,128)S(1)} %shard_map.59.x_ref), channel_id=1, source_target_pairs={{0,1},{1,0},{2,3},{3,2},{4,5},{5,4},{6,7},{7,6},{8,9},{9,8},{10,11... | collective-permute-start | bytes 786440 | tf_op jit(solution)/shard_map/ppermute | solution.py:247
  21.7 2.1 %collective-permute-start.8 = (f32[2,1,128,128]{3,2,1,0:T(8,128)S(1)}, f32[2,1,128,128]{3,2,1,0:T(8,128)S(1)}, u32[]{:S(2)}, u32[]{:S(2)}) collective-permute-start(f32[2,1,128,128]{3,2,1,0:T(8,128)S(1)} %get-tuple-element.14), channel_id=1, source_target_pairs={{0,4},{4,0},{8,12},{12,8},{16,20},{20,16},{24,28},{28,24},{1,5},{5... | collective-permute-start | bytes 393224 | tf_op jit(solution)/shard_map/ppermute | solution.py:247
  22.2 9.1 %collective-permute-start.14 = (f32[2,1,128,128]{3,2,1,0:T(8,128)S(1)}, f32[2,1,128,128]{3,2,1,0:T(8,128)S(1)}, u32[]{:S(2)}, u32[]{:S(2)}) collective-permute-start(f32[2,1,128,128]{3,2,1,0:T(8,128)S(1)} %get-tuple-element.18), channel_id=1, source_target_pairs={{0,24},{4,28},{8,16},{12,20},{16,8},{20,12},{24,0},{28,4},{1,25},{... | collective-permute-start | bytes 393224 | tf_op jit(solution)/shard_map/ppermute | solution.py:247
  23.8 8.6 %collective-permute-start.10 = (f32[2,1,128,128]{3,2,1,0:T(8,128)S(1)}, f32[2,1,128,128]{3,2,1,0:T(8,128)S(1)}, u32[]{:S(2)}, u32[]{:S(2)}) collective-permute-start(f32[2,1,128,128]{3,2,1,0:T(8,128)S(1)} %shard_map.68.refs_0_), channel_id=1, source_target_pairs={{0,3},{1,2},{2,1},{3,0},{4,7},{5,6},{6,5},{7,4},{8,11},{9,10},{10,... | collective-permute-start | bytes 393224 | tf_op jit(solution)/shard_map/ppermute | solution.py:247
  25.4 8.0 %collective-permute-start.11 = (f32[2,1,128,128]{3,2,1,0:T(8,128)S(1)}, f32[2,1,128,128]{3,2,1,0:T(8,128)S(1)}, u32[]{:S(2)}, u32[]{:S(2)}) collective-permute-start(f32[2,1,128,128]{3,2,1,0:T(8,128)S(1)} %shard_map.68.refs_0_), channel_id=1, source_target_pairs={{0,1},{1,0},{2,3},{3,2},{4,5},{5,4},{6,7},{7,6},{8,9},{9,8},{10,11... | collective-permute-start | bytes 393224 | tf_op jit(solution)/shard_map/ppermute | solution.py:247
  25.8 6.1 %collective-permute-start.13 = (f32[2,1,128,128]{3,2,1,0:T(8,128)S(1)}, f32[2,1,128,128]{3,2,1,0:T(8,128)S(1)}, u32[]{:S(2)}, u32[]{:S(2)}) collective-permute-start(f32[2,1,128,128]{3,2,1,0:T(8,128)S(1)} %shard_map.71), channel_id=1, source_target_pairs={{0,16},{4,20},{8,24},{12,28},{16,0},{20,4},{24,8},{28,12},{1,17},{... | collective-permute-start | bytes 393224 | tf_op jit(solution)/shard_map/ppermute | solution.py:247
  27.3 5.1 %collective-permute-start.12 = (f32[2,1,128,128]{3,2,1,0:T(8,128)S(1)}, f32[2,1,128,128]{3,2,1,0:T(8,128)S(1)}, u32[]{:S(2)}, u32[]{:S(2)}) collective-permute-start(f32[2,1,128,128]{3,2,1,0:T(8,128)S(1)} %shard_map.70), channel_id=1, source_target_pairs={{0,8},{4,12},{8,0},{12,4},{16,24},{20,28},{24,16},{28,20},{1,9},{5... | collective-permute-start | bytes 393224 | tf_op jit(solution)/shard_map/ppermute | solution.py:247

commit v13 on v12

--- a/solution.py
+++ b/solution.py
@@ -300,7 +300,7 @@
     summed = [parts[0]]
     for key in range(2, pairs, 2):
         part = parts[key // 2]
-        if key < pairs - 2:
+        if key == 2:
             part = after(part, comp_ops)
         if key == 2:
             part = after(part, three)

time: 35.5 us -> 35.5 us (level)
  waiting for transfers between devices: 7.9 us -> 8.51 us
    ppermute x15, waiting for transfers between devices: 7.9 us -> 8.51 us  [swap(): return lax.ppermute(x, axis, [(at, at ^ key) for at in range(size)])]
where the time goes in v13:
time: 35.5 us; the launch traced here: 35.3 us
  starting transfers between devices  16.1 us (45%)
  waiting for transfers between devices  8.51 us (24%)
  Pallas kernels  6.87 us (19%)
  local copies, waits for them, and re-layouts  2.96 us (8%)
  between operations  0.79 us (2%)
    ppermute x15, starting transfers between devices, swap(): return lax.ppermute(x, axis, [(at, at ^ key) for at in range(size)])  16.1 us
    ppermute x15, waiting for transfers between devices, swap(): return lax.ppermute(x, axis, [(at, at ^ key) for at in range(size)])  8.51 us
    pallas_call x4, Pallas kernels, renorm(): pl.pallas_call(functools.partial(renorm_kernel, steps, parts, carry is no...  4.84 us
    unnamed x8, local copies, waits for them, and re-layouts  2.96 us
    pallas_call x1, Pallas kernels, prepare(): call(functools.partial(prepare_kernel, depth), (halves, part, jax.ShapeDt...  0.99 us
    pallas_call x2, Pallas kernels, combine(): call(functools.partial(combine_kernel, operators, tables, per), (jax.Shap...  0.93 us
  transfers between devices with their start and end apart: 15, of which 8 were waited for; matrix products, arithmetic and copies ran while one was open for 0% of the time, Pallas kernels for 15%

profile of v13, /device:TPU:0, one launch (start us, length us, event | category | flops | bytes accessed | tf_op | source)
XLA Modules:
  0.0 35.3 jit_solution(561600089869469098)
XLA Ops:
  0.6 0.0 copy-start
  0.6 3.0 %collective-permute-start.5 = (f32[2,2,128,128]{3,2,1,0:T(8,128)}, f32[2,2,128,128]{3,2,1,0:T(8,128)S(1)}, u32[]{:S(2)}, u32[]{:S(2)}) collective-permute-start(f32[2,2,128,128]{3,2,1,0:T(8,128)} %refs_2_.3), channel_id=1, source_target_pairs={{0,8},{4,12},{8,0},{12,4},{16,24},{20,28},{24,16},{28,20},{1,9},{5... | collective-permute-start | bytes 786440 | tf_op jit(solution)/shard_map/ppermute | solution.py:247
  3.6 2.6 %collective-permute-start = (f32[2,2,128,128]{3,2,1,0:T(8,128)}, f32[2,2,128,128]{3,2,1,0:T(8,128)S(1)}, u32[]{:S(2)}, u32[]{:S(2)}) collective-permute-start(f32[2,2,128,128]{3,2,1,0:T(8,128)} %refs_2_.3), channel_id=1, source_target_pairs={{0,2},{1,3},{2,0},{3,1},{4,6},{5,7},{6,4},{7,5},{8,10},{9,11},{10,... | collective-permute-start | bytes 786440 | tf_op jit(solution)/shard_map/ppermute | solution.py:247
  6.2 1.6 %collective-permute-start.3 = (f32[2,2,128,128]{3,2,1,0:T(8,128)}, f32[2,2,128,128]{3,2,1,0:T(8,128)S(1)}, u32[]{:S(2)}, u32[]{:S(2)}) collective-permute-start(f32[2,2,128,128]{3,2,1,0:T(8,128)} %refs_2_.3), channel_id=1, source_target_pairs={{0,1},{1,0},{2,3},{3,2},{4,5},{5,4},{6,7},{7,6},{8,9},{9,8},{10,11... | collective-permute-start | bytes 786440 | tf_op jit(solution)/shard_map/ppermute | solution.py:247
  7.8 1.5 %collective-permute-start.4 = (f32[2,2,128,128]{3,2,1,0:T(8,128)}, f32[2,2,128,128]{3,2,1,0:T(8,128)S(1)}, u32[]{:S(2)}, u32[]{:S(2)}) collective-permute-start(f32[2,2,128,128]{3,2,1,0:T(8,128)} %refs_2_.3), channel_id=1, source_target_pairs={{0,16},{4,20},{8,24},{12,28},{16,0},{20,4},{24,8},{28,12},{1,17},{... | collective-permute-start | bytes 786440 | tf_op jit(solution)/shard_map/ppermute | solution.py:247
  9.3 0.5 %collective-permute-start.6 = (f32[2,1,16]{2,1,0:T(1,128)}, f32[2,1,16]{2,1,0:T(1,128)S(1)}, u32[]{:S(2)}, u32[]{:S(2)}) collective-permute-start(f32[2,1,16]{2,1,0:T(1,128)} %integrals_ref.1), channel_id=1, source_target_pairs={{0,8},{4,12},{8,0},{12,4},{16,24},{20,28},{24,16},{28,20},{1,9},{5... | collective-permute-start | bytes 392 | tf_op jit(solution)/shard_map/ppermute | solution.py:247
  9.9 0.0 copy-start.1
  9.9 1.6 %copy-done.1 = f32[2,4,512,128]{3,2,1,0:T(8,128)S(1)} copy-done((f32[2,4,512,128]{3,2,1,0:T(8,128)S(1)}, f32[2,4,512,128]{3,2,1,0:T(8,128)}, u32[]{:S(2)}) %copy-start.1) | copy-done | bytes 2097176
  11.5 0.0 copy-start.2
  11.5 0.7 %copy-done.2 = f32[2,1,4,4]{3,2,1,0:T(4,128)S(1)} copy-done((f32[2,1,4,4]{3,2,1,0:T(4,128)S(1)}, f32[2,1,4,4]{3,2,1,0:T(4,128)}, u32[]{:S(2)}) %copy-start.2) | copy-done | bytes 152
  12.1 0.0 copy-start.3
  12.1 0.7 %copy-done.3 = f32[2,1,16]{2,1,0:T(1,128)S(1)} copy-done((f32[2,1,16]{2,1,0:T(1,128)S(1)}, f32[2,1,16]{2,1,0:T(1,128)}, u32[]{:S(2)}) %copy-start.3) | copy-done | bytes 152
  12.8 1.0 %shard_map.60 = (bf16[3072,512]{1,0:T(8,128)(2,1)S(1)}, f32[2,1,4,128,128]{4,3,2,1,0:T(8,128)S(1)}, f32[2,1,16]{2,1,0:T(1,128)S(1)}) custom-call(f32[2,4,512,128]{3,2,1,0:T(8,128)S(1)} %copy-done.1, f32[2,1,4,4]{3,2,1,0:T(4,128)S(1)} %copy-done.2, f32[2,1,16]{2,1,0:T(1,128)S(1)} %copy-done.3), custom_call_target="tpu_custom_call" | custom-call | flops 2097152 | bytes 4194304 | tf_op jit(solution)/shard_map/pallas_call | solution.py:85
  13.8 0.0 collective-permute-done.6.refs_1_.refs_5_.refs_7_
  13.8 0.0 collective-permute-done.5.block_ref.refs_1_.refs_3_
  13.9 0.6 %collective-permute-start.7 = (f32[2,2,136,128]{3,2,1,0:T(8,128)S(1)}, f32[2,2,136,128]{3,2,1,0:T(8,128)S(1)}, u32[]{:S(2)}, u32[]{:S(2)}) collective-permute-start(f32[2,2,136,128]{3,2,1,0:T(8,128)S(1)} %shard_map.65), channel_id=1, source_target_pairs={{0,16},{4,20},{8,24},{12,28},{16,0},{20,4},{24,8},{28,12},{1,17},{... | collective-permute-start | bytes 835592 | tf_op jit(solution)/shard_map/ppermute | solution.py:247
  14.4 0.0 collective-permute-start.1
  14.5 1.1 %collective-permute-done.1.refs_0_.refs_7_ = f32[2,1,16]{2,1,0:T(1,128)S(1)} collective-permute-done((f32[2,1,16]{2,1,0:T(1,128)S(1)}, f32[2,1,16]{2,1,0:T(1,128)S(1)}, u32[]{:S(2)}, u32[]{:S(2)}) %collective-permute-start.1) | collective-permute-done | bytes 160 | tf_op jit(solution)/shard_map/ppermute | solution.py:247
  15.6 2.7 %collective-permute-done.x_ref = f32[2,2,128,128]{3,2,1,0:T(8,128)S(1)} collective-permute-done((f32[2,2,128,128]{3,2,1,0:T(8,128)}, f32[2,2,128,128]{3,2,1,0:T(8,128)S(1)}, u32[]{:S(2)}, u32[]{:S(2)}) %collective-permute-start) | collective-permute-done | bytes 262176 | tf_op jit(solution)/shard_map/ppermute | solution.py:247
  18.3 0.1 collective-permute-done.3.refs_0_
  18.5 0.0 collective-permute-done.4.refs_0_.refs_2_.refs_4_
  18.5 0.1 collective-permute-start.9
  18.6 1.5 %collective-permute-start.2 = (f32[2,2,128,128]{3,2,1,0:T(8,128)S(1)}, f32[2,2,128,128]{3,2,1,0:T(8,128)S(1)}, u32[]{:S(2)}, u32[]{:S(2)}) collective-permute-start(f32[2,2,128,128]{3,2,1,0:T(8,128)S(1)} %shard_map.59.x_ref), channel_id=1, source_target_pairs={{0,1},{1,0},{2,3},{3,2},{4,5},{5,4},{6,7},{7,6},{8,9},{9,8},{10,11... | collective-permute-start | bytes 786440 | tf_op jit(solution)/shard_map/ppermute | solution.py:247
  20.1 1.1 %collective-permute-done.7.refs_3_.refs_5_ = f32[2,2,136,128]{3,2,1,0:T(8,128)S(1)} collective-permute-done((f32[2,2,136,128]{3,2,1,0:T(8,128)S(1)}, f32[2,2,136,128]{3,2,1,0:T(8,128)S(1)}, u32[]{:S(2)}, u32[]{:S(2)}) %collective-permute-start.7) | collective-permute-done | bytes 278560 | tf_op jit(solution)/shard_map/ppermute | solution.py:247
  21.2 0.0 copy-done
  21.2 0.5 %shard_map.66 = (f32[2,1,128,128]{3,2,1,0:T(8,128)S(1)}, f32[2,1,128,128]{3,2,1,0:T(8,128)S(1)}) custom-call(f32[2,2,128,128]{3,2,1,0:T(8,128)S(1)} %copy-done, f32[2,2,128,128]{3,2,1,0:T(8,128)S(1)} %collective-permute-done.5.block_ref.refs_1_.refs_3_, f32[2,2,128,128]{3,2,1,0:T(8,128)S(1)} %collective-permute-done.4.refs_0_.refs_2_.refs_4_, ...), custom_call_target="tpu_custom_call" | custom-call | flops 2097152 | bytes 4194304 | tf_op jit(solution)/shard_map/pallas_call | solution.py:237
  21.7 0.1 collective-permute-start.8
  21.8 0.0 collective-permute-done.9.refs_1_
  21.8 0.5 %shard_map.67 = (f32[2,1,128,128]{3,2,1,0:T(8,128)S(1)}, f32[2,1,128,128]{3,2,1,0:T(8,128)S(1)}, f32[2,1,128,128]{3,2,1,0:T(8,128)S(1)}, f32[2,1,128,128]{3,2,1,0:T(8,128)S(1)}) custom-call(f32[2,2,128,128]{3,2,1,0:T(8,128)S(1)} %shard_map.62.refs_1_.refs_0_, f32[2,2,128,128]{3,2,1,0:T(8,128)S(1)} %collective-permute-done.9.refs_1_, ...), custom_call_target="tpu_custom_call" | custom-call | flops 2097152 | bytes 4194304 | tf_op jit(solution)/shard_map/pallas_call | solution.py:237
  22.2 1.6 %collective-permute-start.13 = (f32[2,1,128,128]{3,2,1,0:T(8,128)S(1)}, f32[2,1,128,128]{3,2,1,0:T(8,128)S(1)}, u32[]{:S(2)}, u32[]{:S(2)}) collective-permute-start(f32[2,1,128,128]{3,2,1,0:T(8,128)S(1)} %get-tuple-element.17), channel_id=1, source_target_pairs={{0,16},{4,20},{8,24},{12,28},{16,0},{20,4},{24,8},{28,12},{1,17},{... | collective-permute-start | bytes 393224 | tf_op jit(solution)/shard_map/ppermute | solution.py:247
  23.8 1.2 %collective-permute-start.14 = (f32[2,1,128,128]{3,2,1,0:T(8,128)S(1)}, f32[2,1,128,128]{3,2,1,0:T(8,128)S(1)}, u32[]{:S(2)}, u32[]{:S(2)}) collective-permute-start(f32[2,1,128,128]{3,2,1,0:T(8,128)S(1)} %get-tuple-element.18), channel_id=1, source_target_pairs={{0,24},{4,28},{8,16},{12,20},{16,8},{20,12},{24,0},{28,4},{1,25},{... | collective-permute-start | bytes 393224 | tf_op jit(solution)/shard_map/ppermute | solution.py:247
  25.0 0.0 collective-permute-done.8.refs_1_
  25.0 0.9 %collective-permute-start.10 = (f32[2,1,128,128]{3,2,1,0:T(8,128)S(1)}, f32[2,1,128,128]{3,2,1,0:T(8,128)S(1)}, u32[]{:S(2)}, u32[]{:S(2)}) collective-permute-start(f32[2,1,128,128]{3,2,1,0:T(8,128)S(1)} %shard_map.68.refs_0_), channel_id=1, source_target_pairs={{0,3},{1,2},{2,1},{3,0},{4,7},{5,6},{6,5},{7,4},{8,11},{9,10},{10,... | collective-permute-start | bytes 393224 | tf_op jit(solution)/shard_map/ppermute | solution.py:247
  25.9 0.4 %collective-permute-start.11 = (f32[2,1,128,128]{3,2,1,0:T(8,128)S(1)}, f32[2,1,128,128]{3,2,1,0:T(8,128)S(1)}, u32[]{:S(2)}, u32[]{:S(2)}) collective-permute-start(f32[2,1,128,128]{3,2,1,0:T(8,128)S(1)} %shard_map.68.refs_0_), channel_id=1, source_target_pairs={{0,1},{1,0},{2,3},{3,2},{4,5},{5,4},{6,7},{7,6},{8,9},{9,8},{10,11... | collective-permute-start | bytes 393224 | tf_op jit(solution)/shard_map/ppermute | solution.py:247
  26.3 1.0 %collective-permute-done.2.refs_0_ = f32[2,2,128,128]{3,2,1,0:T(8,128)S(1)} collective-permute-done((f32[2,2,128,128]{3,2,1,0:T(8,128)S(1)}, f32[2,2,128,128]{3,2,1,0:T(8,128)S(1)}, u32[]{:S(2)}, u32[]{:S(2)}) %collective-permute-start.2) | collective-permute-done | bytes 262176 | tf_op jit(solution)/shard_map/ppermute | solution.py:247
  27.3 0.6 %collective-permute-start.12 = (f32[2,1,128,128]{3,2,1,0:T(8,128)S(1)}, f32[2,1,128,128]{3,2,1,0:T(8,128)S(1)}, u32[]{:S(2)}, u32[]{:S(2)}) collective-permute-start(f32[2,1,128,128]{3,2,1,0:T(8,128)S(1)} %shard_map.70), channel_id=1, source_target_pairs={{0,8},{4,12},{8,0},{12,4},{16,24},{20,28},{24,16},{28,20},{1,9},{5... | collective-permute-start | bytes 393224 | tf_op jit(solution)/shard_map/ppermute | solution.py:247
  27.9 1.4 %shard_map.63.refs_2_ = f32[2,2,4,128,128]{4,3,2,1,0:T(8,128)S(1)} custom-call(f32[2,2,128,128]{3,2,1,0:T(8,128)S(1)} %collective-permute-done.3.refs_0_, f32[2,2,128,128]{3,2,1,0:T(8,128)S(1)} %shard_map.62.refs_1_.refs_0_, f32[2,2,128,128]{3,2,1,0:T(8,128)S(1)} %copy-done, bf16[3072,512]{1,0:T(8,128)(2,1)S(1)} %get-tuple-element.11.refs_3_.refs_1_.refs_6_), custom_call_target="tpu_custom_call" | custom-call | flops 1207959552 | bytes 4194304 | tf_op jit(solution)/shard_map/pallas_call | solution.py:182
  29.3 1.5 %shard_map.64 = f32[2,2,4,128,128]{4,3,2,1,0:T(8,128)} custom-call(f32[2,2,128,128]{3,2,1,0:T(8,128)S(1)} %collective-permute-done.2.refs_0_, bf16[3072,512]{1,0:T(8,128)(2,1)S(1)} %get-tuple-element.11.refs_3_.refs_1_.refs_6_, f32[2,2,4,128,128]{4,3,2,1,0:T(8,128)S(1)} %shard_map.63.refs_2_), custom_call_target="tpu_custom_call" | custom-call | flops 402653184 | bytes 4194304 | tf_op jit(solution)/shard_map/pallas_call | solution.py:182
  30.8 0.4 %shard_map.71.refs_7_ = f32[2,1,4,128,128]{4,3,2,1,0:T(8,128)S(1)} custom-call(f32[2,1,128,128]{3,2,1,0:T(8,128)S(1)} %shard_map.68.refs_0_, bf16[3072,512]{1,0:T(8,128)(2,1)S(1)} %get-tuple-element.11.refs_3_.refs_1_.refs_6_, f32[2,1,4,128,128]{4,3,2,1,0:T(8,128)S(1)} %get-tuple-element.19.refs_2_), custom_call_target="tpu_custom_call" | custom-call | flops 201326592 | bytes 4194304 | tf_op jit(solution)/shard_map/pallas_call | solution.py:182
  31.2 0.0 collective-permute-done.13.refs_4_
  31.2 0.0 collective-permute-done.14.refs_5_
  31.2 1.2 %collective-permute-done.12.refs_3_ = f32[2,1,128,128]{3,2,1,0:T(8,128)S(1)} collective-permute-done((f32[2,1,128,128]{3,2,1,0:T(8,128)S(1)}, f32[2,1,128,128]{3,2,1,0:T(8,128)S(1)}, u32[]{:S(2)}, u32[]{:S(2)}) %collective-permute-start.12) | collective-permute-done | bytes 131104 | tf_op jit(solution)/shard_map/ppermute | solution.py:247
  32.4 0.8 %collective-permute-done.10.refs_0_ = f32[2,1,128,128]{3,2,1,0:T(8,128)S(1)} collective-permute-done((f32[2,1,128,128]{3,2,1,0:T(8,128)S(1)}, f32[2,1,128,128]{3,2,1,0:T(8,128)S(1)}, u32[]{:S(2)}, u32[]{:S(2)}) %collective-permute-start.10) | collective-permute-done | bytes 131104 | tf_op jit(solution)/shard_map/ppermute | solution.py:247
  33.3 0.4 %collective-permute-done.11.refs_1_ = f32[2,1,128,128]{3,2,1,0:T(8,128)S(1)} collective-permute-done((f32[2,1,128,128]{3,2,1,0:T(8,128)S(1)}, f32[2,1,128,128]{3,2,1,0:T(8,128)S(1)}, u32[]{:S(2)}, u32[]{:S(2)}) %collective-permute-start.11) | collective-permute-done | bytes 131104 | tf_op jit(solution)/shard_map/ppermute | solution.py:247
  33.7 1.6 %shard_map.72 = f32[2,1,4,128,128]{4,3,2,1,0:T(8,128)} custom-call(f32[2,1,128,128]{3,2,1,0:T(8,128)S(1)} %collective-permute-done.10.refs_0_, f32[2,1,128,128]{3,2,1,0:T(8,128)S(1)} %collective-permute-done.11.refs_1_, f32[2,1,128,128]{3,2,1,0:T(8,128)S(1)} %get-tuple-element.15.refs_2_, f32[2,1,128,128]{3,2,1,0:T(8,128)S(1)} %collective-permute-done.12.refs_3_, ...), custom_call_target="tpu_custom_call" | custom-call | flops 603979776 | bytes 4194304 | tf_op jit(solution)/shard_map/pallas_call | solution.py:182
  (7 shorter events, 0.1 us)
Async XLA Ops:
  0.6 20.6 %copy-start = (f32[2,2,128,128]{3,2,1,0:T(8,128)S(1)}, f32[2,2,128,128]{3,2,1,0:T(8,128)}, u32[]{:S(2)}) copy-start(f32[2,2,128,128]{3,2,1,0:T(8,128)} %refs_2_.3) | copy-start | bytes 786436
  0.6 13.2 %collective-permute-start.5 = (f32[2,2,128,128]{3,2,1,0:T(8,128)}, f32[2,2,128,128]{3,2,1,0:T(8,128)S(1)}, u32[]{:S(2)}, u32[]{:S(2)}) collective-permute-start(f32[2,2,128,128]{3,2,1,0:T(8,128)} %refs_2_.3), channel_id=1, source_target_pairs={{0,8},{4,12},{8,0},{12,4},{16,24},{20,28},{24,16},{28,20},{1,9},{5... | collective-permute-start | bytes 786440 | tf_op jit(solution)/shard_map/ppermute | solution.py:247
  3.6 14.6 %collective-permute-start = (f32[2,2,128,128]{3,2,1,0:T(8,128)}, f32[2,2,128,128]{3,2,1,0:T(8,128)S(1)}, u32[]{:S(2)}, u32[]{:S(2)}) collective-permute-start(f32[2,2,128,128]{3,2,1,0:T(8,128)} %refs_2_.3), channel_id=1, source_target_pairs={{0,2},{1,3},{2,0},{3,1},{4,6},{5,7},{6,4},{7,5},{8,10},{9,11},{10,... | collective-permute-start | bytes 786440 | tf_op jit(solution)/shard_map/ppermute | solution.py:247
  6.2 12.2 %collective-permute-start.3 = (f32[2,2,128,128]{3,2,1,0:T(8,128)}, f32[2,2,128,128]{3,2,1,0:T(8,128)S(1)}, u32[]{:S(2)}, u32[]{:S(2)}) collective-permute-start(f32[2,2,128,128]{3,2,1,0:T(8,128)} %refs_2_.3), channel_id=1, source_target_pairs={{0,1},{1,0},{2,3},{3,2},{4,5},{5,4},{6,7},{7,6},{8,9},{9,8},{10,11... | collective-permute-start | bytes 786440 | tf_op jit(solution)/shard_map/ppermute | solution.py:247
  7.8 10.6 %collective-permute-start.4 = (f32[2,2,128,128]{3,2,1,0:T(8,128)}, f32[2,2,128,128]{3,2,1,0:T(8,128)S(1)}, u32[]{:S(2)}, u32[]{:S(2)}) collective-permute-start(f32[2,2,128,128]{3,2,1,0:T(8,128)} %refs_2_.3), channel_id=1, source_target_pairs={{0,16},{4,20},{8,24},{12,28},{16,0},{20,4},{24,8},{28,12},{1,17},{... | collective-permute-start | bytes 786440 | tf_op jit(solution)/shard_map/ppermute | solution.py:247
  9.3 4.5 %collective-permute-start.6 = (f32[2,1,16]{2,1,0:T(1,128)}, f32[2,1,16]{2,1,0:T(1,128)S(1)}, u32[]{:S(2)}, u32[]{:S(2)}) collective-permute-start(f32[2,1,16]{2,1,0:T(1,128)} %integrals_ref.1), channel_id=1, source_target_pairs={{0,8},{4,12},{8,0},{12,4},{16,24},{20,28},{24,16},{28,20},{1,9},{5... | collective-permute-start | bytes 392 | tf_op jit(solution)/shard_map/ppermute | solution.py:247
  9.9 1.6 %copy-start.1 = (f32[2,4,512,128]{3,2,1,0:T(8,128)S(1)}, f32[2,4,512,128]{3,2,1,0:T(8,128)}, u32[]{:S(2)}) copy-start(f32[2,4,512,128]{3,2,1,0:T(8,128)} %basis_hbm.1) | copy-start | bytes 6291460
  11.5 0.7 %copy-start.2 = (f32[2,1,4,4]{3,2,1,0:T(4,128)S(1)}, f32[2,1,4,4]{3,2,1,0:T(4,128)}, u32[]{:S(2)}) copy-start(f32[2,1,4,4]{3,2,1,0:T(4,128)} %site_hbm.1) | copy-start | bytes 388
  12.1 0.7 %copy-start.3 = (f32[2,1,16]{2,1,0:T(1,128)S(1)}, f32[2,1,16]{2,1,0:T(1,128)}, u32[]{:S(2)}) copy-start(f32[2,1,16]{2,1,0:T(1,128)} %integrals_ref.1) | copy-start | bytes 388
  13.9 7.3 %collective-permute-start.7 = (f32[2,2,136,128]{3,2,1,0:T(8,128)S(1)}, f32[2,2,136,128]{3,2,1,0:T(8,128)S(1)}, u32[]{:S(2)}, u32[]{:S(2)}) collective-permute-start(f32[2,2,136,128]{3,2,1,0:T(8,128)S(1)} %shard_map.65), channel_id=1, source_target_pairs={{0,16},{4,20},{8,24},{12,28},{16,0},{20,4},{24,8},{28,12},{1,17},{... | collective-permute-start | bytes 835592 | tf_op jit(solution)/shard_map/ppermute | solution.py:247
  14.4 1.1 %collective-permute-start.1 = (f32[2,1,16]{2,1,0:T(1,128)S(1)}, f32[2,1,16]{2,1,0:T(1,128)S(1)}, u32[]{:S(2)}, u32[]{:S(2)}) collective-permute-start(f32[2,1,16]{2,1,0:T(1,128)S(1)} %copy-done.3), channel_id=1, source_target_pairs={{0,4},{4,0},{8,12},{12,8},{16,20},{20,16},{24,28},{28,24},{1,5},{5... | collective-permute-start | bytes 392 | tf_op jit(solution)/shard_map/ppermute | solution.py:247
  18.5 3.3 %collective-permute-start.9 = (f32[2,2,128,128]{3,2,1,0:T(8,128)S(1)}, f32[2,2,128,128]{3,2,1,0:T(8,128)S(1)}, u32[]{:S(2)}, u32[]{:S(2)}) collective-permute-start(f32[2,2,128,128]{3,2,1,0:T(8,128)S(1)} %shard_map.62.refs_1_.refs_0_), channel_id=1, source_target_pairs={{0,4},{4,0},{8,12},{12,8},{16,20},{20,16},{24,28},{28,24},{1,5},{5... | collective-permute-start | bytes 786440 | tf_op jit(solution)/shard_map/ppermute | solution.py:247
  18.6 8.7 %collective-permute-start.2 = (f32[2,2,128,128]{3,2,1,0:T(8,128)S(1)}, f32[2,2,128,128]{3,2,1,0:T(8,128)S(1)}, u32[]{:S(2)}, u32[]{:S(2)}) collective-permute-start(f32[2,2,128,128]{3,2,1,0:T(8,128)S(1)} %shard_map.59.x_ref), channel_id=1, source_target_pairs={{0,1},{1,0},{2,3},{3,2},{4,5},{5,4},{6,7},{7,6},{8,9},{9,8},{10,11... | collective-permute-start | bytes 786440 | tf_op jit(solution)/shard_map/ppermute | solution.py:247
  21.7 3.3 %collective-permute-start.8 = (f32[2,1,128,128]{3,2,1,0:T(8,128)S(1)}, f32[2,1,128,128]{3,2,1,0:T(8,128)S(1)}, u32[]{:S(2)}, u32[]{:S(2)}) collective-permute-start(f32[2,1,128,128]{3,2,1,0:T(8,128)S(1)} %get-tuple-element.14), channel_id=1, source_target_pairs={{0,4},{4,0},{8,12},{12,8},{16,20},{20,16},{24,28},{28,24},{1,5},{5... | collective-permute-start | bytes 393224 | tf_op jit(solution)/shard_map/ppermute | solution.py:247
  22.2 9.0 %collective-permute-start.13 = (f32[2,1,128,128]{3,2,1,0:T(8,128)S(1)}, f32[2,1,128,128]{3,2,1,0:T(8,128)S(1)}, u32[]{:S(2)}, u32[]{:S(2)}) collective-permute-start(f32[2,1,128,128]{3,2,1,0:T(8,128)S(1)} %get-tuple-element.17), channel_id=1, source_target_pairs={{0,16},{4,20},{8,24},{12,28},{16,0},{20,4},{24,8},{28,12},{1,17},{... | collective-permute-start | bytes 393224 | tf_op jit(solution)/shard_map/ppermute | solution.py:247
  23.8 7.4 %collective-permute-start.14 = (f32[2,1,128,128]{3,2,1,0:T(8,128)S(1)}, f32[2,1,128,128]{3,2,1,0:T(8,128)S(1)}, u32[]{:S(2)}, u32[]{:S(2)}) collective-permute-start(f32[2,1,128,128]{3,2,1,0:T(8,128)S(1)} %get-tuple-element.18), channel_id=1, source_target_pairs={{0,24},{4,28},{8,16},{12,20},{16,8},{20,12},{24,0},{28,4},{1,25},{... | collective-permute-start | bytes 393224 | tf_op jit(solution)/shard_map/ppermute | solution.py:247
  25.0 8.2 %collective-permute-start.10 = (f32[2,1,128,128]{3,2,1,0:T(8,128)S(1)}, f32[2,1,128,128]{3,2,1,0:T(8,128)S(1)}, u32[]{:S(2)}, u32[]{:S(2)}) collective-permute-start(f32[2,1,128,128]{3,2,1,0:T(8,128)S(1)} %shard_map.68.refs_0_), channel_id=1, source_target_pairs={{0,3},{1,2},{2,1},{3,0},{4,7},{5,6},{6,5},{7,4},{8,11},{9,10},{10,... | collective-permute-start | bytes 393224 | tf_op jit(solution)/shard_map/ppermute | solution.py:247
  25.9 7.8 %collective-permute-start.11 = (f32[2,1,128,128]{3,2,1,0:T(8,128)S(1)}, f32[2,1,128,128]{3,2,1,0:T(8,128)S(1)}, u32[]{:S(2)}, u32[]{:S(2)}) collective-permute-start(f32[2,1,128,128]{3,2,1,0:T(8,128)S(1)} %shard_map.68.refs_0_), channel_id=1, source_target_pairs={{0,1},{1,0},{2,3},{3,2},{4,5},{5,4},{6,7},{7,6},{8,9},{9,8},{10,11... | collective-permute-start | bytes 393224 | tf_op jit(solution)/shard_map/ppermute | solution.py:247
  27.3 5.1 %collective-permute-start.12 = (f32[2,1,128,128]{3,2,1,0:T(8,128)S(1)}, f32[2,1,128,128]{3,2,1,0:T(8,128)S(1)}, u32[]{:S(2)}, u32[]{:S(2)}) collective-permute-start(f32[2,1,128,128]{3,2,1,0:T(8,128)S(1)} %shard_map.70), channel_id=1, source_target_pairs={{0,8},{4,12},{8,0},{12,4},{16,24},{20,28},{24,16},{28,20},{1,9},{5... | collective-permute-start | bytes 393224 | tf_op jit(solution)/shard_map/ppermute | solution.py:247

commit v14 on v13

--- a/solution.py
+++ b/solution.py
@@ -33,7 +33,7 @@
 
 
 def order(sec):
-    return (3, 1, 2, 0) if sec == 4 else tuple(range(sec))
+    return (3, 2, 1, 0) if sec == 4 else tuple(range(sec))
 
 
 def prepare_kernel(depth, basis_hbm, site_hbm, integrals_ref, *refs):
@@ -286,7 +286,7 @@
     two = after(two, sibling)
     three = swap(two, "sec", sec, 1)
     two = after(after(two, one), arrays[2])
-    normals = [three, one, two, normal_ops]
+    normals = [three, two, one, normal_ops]
     held = arrays + [row, sibling]
     here = [(len(arrays), None), (len(arrays) + 1, None)]
     mine, other = combine(held, operators, here, norms, shape)
@@ -309,9 +309,10 @@
     early = renorm(normals, range(1, sec), basis_split, None, shape)
     new_normal = renorm(normals, range(1), basis_split, early, shape, True)
     shape = (2, comps, sites, rows, cols)
-    arrived = [far, near, tuple(summed), comp_ops]
+    arrived = [far, tuple(summed), near, comp_ops]
     early = renorm(arrived, range(3, sec), basis_split, site_part, shape)
-    return new_normal, renorm(arrived, range(3), basis_split, early, shape, True)
+    early = renorm(arrived, range(2), basis_split, early, shape)
+    return new_normal, renorm(arrived, range(2, 3), basis_split, early, shape, True)
 
 
 def solution(mesh):

time: 35.5 us -> 35.2 us (level)
  waiting for transfers between devices: 8.51 us -> 8.08 us
    ppermute x15, waiting for transfers between devices: 8.51 us -> 8.08 us  [swap(): return lax.ppermute(x, axis, [(at, at ^ key) for at in range(size)])]
    pallas_call x4 -> x5, Pallas kernels: 4.84 us -> 5.02 us  [renorm(): pl.pallas_call(functools.partial(renorm_kernel, steps, parts, carry is no...]
  transfers between devices with their start and end apart: 15 -> 15, of which waited for: 8 -> 7; matrix products, arithmetic and copies ran while one was open for 0% -> 0% of each run, Pallas kernels for 15% -> 17%
where the time goes in v14:
time: 35.2 us; the launch traced here: 35 us
  starting transfers between devices  16.1 us (46%)
  waiting for transfers between devices  8.08 us (23%)
  Pallas kernels  7.05 us (20%)
  local copies, waits for them, and re-layouts  2.96 us (8%)
  between operations  0.81 us (2%)
    ppermute x15, starting transfers between devices, swap(): return lax.ppermute(x, axis, [(at, at ^ key) for at in range(size)])  16.1 us
    ppermute x15, waiting for transfers between devices, swap(): return lax.ppermute(x, axis, [(at, at ^ key) for at in range(size)])  8.08 us
    pallas_call x5, Pallas kernels, renorm(): pl.pallas_call(functools.partial(renorm_kernel, steps, parts, carry is no...  5.02 us
    unnamed x8, local copies, waits for them, and re-layouts  2.96 us
    pallas_call x1, Pallas kernels, prepare(): call(functools.partial(prepare_kernel, depth), (halves, part, jax.ShapeDt...  0.99 us
    pallas_call x2, Pallas kernels, combine(): call(functools.partial(combine_kernel, operators, tables, per), (jax.Shap...  0.93 us
  transfers between devices with their start and end apart: 15, of which 7 were waited for; matrix products, arithmetic and copies ran while one was open for 0% of the time, Pallas kernels for 17%

profile of v14, /device:TPU:0, one launch (start us, length us, event | category | flops | bytes accessed | tf_op | source)
XLA Modules:
  0.0 35.0 jit_solution(12072867775258512767)
XLA Ops:
  0.6 0.0 copy-start
  0.6 3.0 %collective-permute-start.5 = (f32[2,2,128,128]{3,2,1,0:T(8,128)}, f32[2,2,128,128]{3,2,1,0:T(8,128)S(1)}, u32[]{:S(2)}, u32[]{:S(2)}) collective-permute-start(f32[2,2,128,128]{3,2,1,0:T(8,128)} %refs_2_.3), channel_id=1, source_target_pairs={{0,8},{4,12},{8,0},{12,4},{16,24},{20,28},{24,16},{28,20},{1,9},{5... | collective-permute-start | bytes 786440 | tf_op jit(solution)/shard_map/ppermute | solution.py:247
  3.6 2.6 %collective-permute-start = (f32[2,2,128,128]{3,2,1,0:T(8,128)}, f32[2,2,128,128]{3,2,1,0:T(8,128)S(1)}, u32[]{:S(2)}, u32[]{:S(2)}) collective-permute-start(f32[2,2,128,128]{3,2,1,0:T(8,128)} %refs_2_.3), channel_id=1, source_target_pairs={{0,2},{1,3},{2,0},{3,1},{4,6},{5,7},{6,4},{7,5},{8,10},{9,11},{10,... | collective-permute-start | bytes 786440 | tf_op jit(solution)/shard_map/ppermute | solution.py:247
  6.2 1.6 %collective-permute-start.3 = (f32[2,2,128,128]{3,2,1,0:T(8,128)}, f32[2,2,128,128]{3,2,1,0:T(8,128)S(1)}, u32[]{:S(2)}, u32[]{:S(2)}) collective-permute-start(f32[2,2,128,128]{3,2,1,0:T(8,128)} %refs_2_.3), channel_id=1, source_target_pairs={{0,1},{1,0},{2,3},{3,2},{4,5},{5,4},{6,7},{7,6},{8,9},{9,8},{10,11... | collective-permute-start | bytes 786440 | tf_op jit(solution)/shard_map/ppermute | solution.py:247
  7.8 1.5 %collective-permute-start.4 = (f32[2,2,128,128]{3,2,1,0:T(8,128)}, f32[2,2,128,128]{3,2,1,0:T(8,128)S(1)}, u32[]{:S(2)}, u32[]{:S(2)}) collective-permute-start(f32[2,2,128,128]{3,2,1,0:T(8,128)} %refs_2_.3), channel_id=1, source_target_pairs={{0,16},{4,20},{8,24},{12,28},{16,0},{20,4},{24,8},{28,12},{1,17},{... | collective-permute-start | bytes 786440 | tf_op jit(solution)/shard_map/ppermute | solution.py:247
  9.3 0.5 %collective-permute-start.6 = (f32[2,1,16]{2,1,0:T(1,128)}, f32[2,1,16]{2,1,0:T(1,128)S(1)}, u32[]{:S(2)}, u32[]{:S(2)}) collective-permute-start(f32[2,1,16]{2,1,0:T(1,128)} %integrals_ref.1), channel_id=1, source_target_pairs={{0,8},{4,12},{8,0},{12,4},{16,24},{20,28},{24,16},{28,20},{1,9},{5... | collective-permute-start | bytes 392 | tf_op jit(solution)/shard_map/ppermute | solution.py:247
  9.9 0.0 copy-start.1
  9.9 1.6 %copy-done.1 = f32[2,4,512,128]{3,2,1,0:T(8,128)S(1)} copy-done((f32[2,4,512,128]{3,2,1,0:T(8,128)S(1)}, f32[2,4,512,128]{3,2,1,0:T(8,128)}, u32[]{:S(2)}) %copy-start.1) | copy-done | bytes 2097176
  11.5 0.0 copy-start.2
  11.5 0.7 %copy-done.2 = f32[2,1,4,4]{3,2,1,0:T(4,128)S(1)} copy-done((f32[2,1,4,4]{3,2,1,0:T(4,128)S(1)}, f32[2,1,4,4]{3,2,1,0:T(4,128)}, u32[]{:S(2)}) %copy-start.2) | copy-done | bytes 152
  12.1 0.0 copy-start.3
  12.1 0.7 %copy-done.3 = f32[2,1,16]{2,1,0:T(1,128)S(1)} copy-done((f32[2,1,16]{2,1,0:T(1,128)S(1)}, f32[2,1,16]{2,1,0:T(1,128)}, u32[]{:S(2)}) %copy-start.3) | copy-done | bytes 152
  12.8 1.0 %shard_map.60 = (bf16[3072,512]{1,0:T(8,128)(2,1)S(1)}, f32[2,1,4,128,128]{4,3,2,1,0:T(8,128)S(1)}, f32[2,1,16]{2,1,0:T(1,128)S(1)}) custom-call(f32[2,4,512,128]{3,2,1,0:T(8,128)S(1)} %copy-done.1, f32[2,1,4,4]{3,2,1,0:T(4,128)S(1)} %copy-done.2, f32[2,1,16]{2,1,0:T(1,128)S(1)} %copy-done.3), custom_call_target="tpu_custom_call" | custom-call | flops 2097152 | bytes 4194304 | tf_op jit(solution)/shard_map/pallas_call | solution.py:85
  13.8 0.0 collective-permute-done.6.refs_1_.refs_5_.refs_7_
  13.8 0.0 collective-permute-done.5.block_ref.refs_1_.refs_3_
  13.9 0.6 %collective-permute-start.7 = (f32[2,2,136,128]{3,2,1,0:T(8,128)S(1)}, f32[2,2,136,128]{3,2,1,0:T(8,128)S(1)}, u32[]{:S(2)}, u32[]{:S(2)}) collective-permute-start(f32[2,2,136,128]{3,2,1,0:T(8,128)S(1)} %shard_map.65), channel_id=1, source_target_pairs={{0,16},{4,20},{8,24},{12,28},{16,0},{20,4},{24,8},{28,12},{1,17},{... | collective-permute-start | bytes 835592 | tf_op jit(solution)/shard_map/ppermute | solution.py:247
  14.4 0.0 collective-permute-start.1
  14.5 1.1 %collective-permute-done.1.refs_0_.refs_7_ = f32[2,1,16]{2,1,0:T(1,128)S(1)} collective-permute-done((f32[2,1,16]{2,1,0:T(1,128)S(1)}, f32[2,1,16]{2,1,0:T(1,128)S(1)}, u32[]{:S(2)}, u32[]{:S(2)}) %collective-permute-start.1) | collective-permute-done | bytes 160 | tf_op jit(solution)/shard_map/ppermute | solution.py:247
  15.6 2.7 %collective-permute-done.x_ref = f32[2,2,128,128]{3,2,1,0:T(8,128)S(1)} collective-permute-done((f32[2,2,128,128]{3,2,1,0:T(8,128)}, f32[2,2,128,128]{3,2,1,0:T(8,128)S(1)}, u32[]{:S(2)}, u32[]{:S(2)}) %collective-permute-start) | collective-permute-done | bytes 262176 | tf_op jit(solution)/shard_map/ppermute | solution.py:247
  18.3 0.1 collective-permute-done.3.refs_0_.refs_1_
  18.5 0.0 collective-permute-done.4.refs_0_.refs_2_.refs_4_
  18.5 0.1 collective-permute-start.9
  18.6 1.5 %collective-permute-start.2 = (f32[2,2,128,128]{3,2,1,0:T(8,128)S(1)}, f32[2,2,128,128]{3,2,1,0:T(8,128)S(1)}, u32[]{:S(2)}, u32[]{:S(2)}) collective-permute-start(f32[2,2,128,128]{3,2,1,0:T(8,128)S(1)} %shard_map.59.x_ref), channel_id=1, source_target_pairs={{0,1},{1,0},{2,3},{3,2},{4,5},{5,4},{6,7},{7,6},{8,9},{9,8},{10,11... | collective-permute-start | bytes 786440 | tf_op jit(solution)/shard_map/ppermute | solution.py:247
  20.1 1.1 %collective-permute-done.7.refs_3_.refs_5_ = f32[2,2,136,128]{3,2,1,0:T(8,128)S(1)} collective-permute-done((f32[2,2,136,128]{3,2,1,0:T(8,128)S(1)}, f32[2,2,136,128]{3,2,1,0:T(8,128)S(1)}, u32[]{:S(2)}, u32[]{:S(2)}) %collective-permute-start.7) | collective-permute-done | bytes 278560 | tf_op jit(solution)/shard_map/ppermute | solution.py:247
  21.2 0.0 copy-done
  21.2 0.5 %shard_map.66 = (f32[2,1,128,128]{3,2,1,0:T(8,128)S(1)}, f32[2,1,128,128]{3,2,1,0:T(8,128)S(1)}) custom-call(f32[2,2,128,128]{3,2,1,0:T(8,128)S(1)} %copy-done, f32[2,2,128,128]{3,2,1,0:T(8,128)S(1)} %collective-permute-done.5.block_ref.refs_1_.refs_3_, f32[2,2,128,128]{3,2,1,0:T(8,128)S(1)} %collective-permute-done.4.refs_0_.refs_2_.refs_4_, ...), custom_call_target="tpu_custom_call" | custom-call | flops 2097152 | bytes 4194304 | tf_op jit(solution)/shard_map/pallas_call | solution.py:237
  21.7 0.1 collective-permute-start.8
  21.8 0.0 collective-permute-done.9.refs_1_
  21.8 0.5 %shard_map.67 = (f32[2,1,128,128]{3,2,1,0:T(8,128)S(1)}, f32[2,1,128,128]{3,2,1,0:T(8,128)S(1)}, f32[2,1,128,128]{3,2,1,0:T(8,128)S(1)}, f32[2,1,128,128]{3,2,1,0:T(8,128)S(1)}) custom-call(f32[2,2,128,128]{3,2,1,0:T(8,128)S(1)} %shard_map.62.refs_0_, f32[2,2,128,128]{3,2,1,0:T(8,128)S(1)} %collective-permute-done.9.refs_1_, f32[2,2,128,128]{3,2,1,0:T(8,128)S(1)} %copy-done, ...), custom_call_target="tpu_custom_call" | custom-call | flops 2097152 | bytes 4194304 | tf_op jit(solution)/shard_map/pallas_call | solution.py:237
  22.2 1.6 %collective-permute-start.13 = (f32[2,1,128,128]{3,2,1,0:T(8,128)S(1)}, f32[2,1,128,128]{3,2,1,0:T(8,128)S(1)}, u32[]{:S(2)}, u32[]{:S(2)}) collective-permute-start(f32[2,1,128,128]{3,2,1,0:T(8,128)S(1)} %get-tuple-element.17), channel_id=1, source_target_pairs={{0,16},{4,20},{8,24},{12,28},{16,0},{20,4},{24,8},{28,12},{1,17},{... | collective-permute-start | bytes 393224 | tf_op jit(solution)/shard_map/ppermute | solution.py:247
  23.8 1.2 %collective-permute-start.14 = (f32[2,1,128,128]{3,2,1,0:T(8,128)S(1)}, f32[2,1,128,128]{3,2,1,0:T(8,128)S(1)}, u32[]{:S(2)}, u32[]{:S(2)}) collective-permute-start(f32[2,1,128,128]{3,2,1,0:T(8,128)S(1)} %get-tuple-element.18), channel_id=1, source_target_pairs={{0,24},{4,28},{8,16},{12,20},{16,8},{20,12},{24,0},{28,4},{1,25},{... | collective-permute-start | bytes 393224 | tf_op jit(solution)/shard_map/ppermute | solution.py:247
  25.0 0.0 collective-permute-done.8.refs_1_
  25.0 0.9 %collective-permute-start.11 = (f32[2,1,128,128]{3,2,1,0:T(8,128)S(1)}, f32[2,1,128,128]{3,2,1,0:T(8,128)S(1)}, u32[]{:S(2)}, u32[]{:S(2)}) collective-permute-start(f32[2,1,128,128]{3,2,1,0:T(8,128)S(1)} %shard_map.68.refs_0_), channel_id=1, source_target_pairs={{0,3},{1,2},{2,1},{3,0},{4,7},{5,6},{6,5},{7,4},{8,11},{9,10},{10,... | collective-permute-start | bytes 393224 | tf_op jit(solution)/shard_map/ppermute | solution.py:247
  25.9 0.4 %collective-permute-start.10 = (f32[2,1,128,128]{3,2,1,0:T(8,128)S(1)}, f32[2,1,128,128]{3,2,1,0:T(8,128)S(1)}, u32[]{:S(2)}, u32[]{:S(2)}) collective-permute-start(f32[2,1,128,128]{3,2,1,0:T(8,128)S(1)} %shard_map.68.refs_0_), channel_id=1, source_target_pairs={{0,1},{1,0},{2,3},{3,2},{4,5},{5,4},{6,7},{7,6},{8,9},{9,8},{10,11... | collective-permute-start | bytes 393224 | tf_op jit(solution)/shard_map/ppermute | solution.py:247
  26.3 1.0 %collective-permute-done.2.refs_0_ = f32[2,2,128,128]{3,2,1,0:T(8,128)S(1)} collective-permute-done((f32[2,2,128,128]{3,2,1,0:T(8,128)S(1)}, f32[2,2,128,128]{3,2,1,0:T(8,128)S(1)}, u32[]{:S(2)}, u32[]{:S(2)}) %collective-permute-start.2) | collective-permute-done | bytes 262176 | tf_op jit(solution)/shard_map/ppermute | solution.py:247
  27.3 0.6 %collective-permute-start.12 = (f32[2,1,128,128]{3,2,1,0:T(8,128)S(1)}, f32[2,1,128,128]{3,2,1,0:T(8,128)S(1)}, u32[]{:S(2)}, u32[]{:S(2)}) collective-permute-start(f32[2,1,128,128]{3,2,1,0:T(8,128)S(1)} %shard_map.70), channel_id=1, source_target_pairs={{0,8},{4,12},{8,0},{12,4},{16,24},{20,28},{24,16},{28,20},{1,9},{5... | collective-permute-start | bytes 393224 | tf_op jit(solution)/shard_map/ppermute | solution.py:247
  27.9 1.4 %shard_map.63.refs_2_ = f32[2,2,4,128,128]{4,3,2,1,0:T(8,128)S(1)} custom-call(f32[2,2,128,128]{3,2,1,0:T(8,128)S(1)} %shard_map.62.refs_0_, f32[2,2,128,128]{3,2,1,0:T(8,128)S(1)} %collective-permute-done.3.refs_0_.refs_1_, f32[2,2,128,128]{3,2,1,0:T(8,128)S(1)} %copy-done, bf16[3072,512]{1,0:T(8,128)(2,1)S(1)} %get-tuple-element.11.refs_3_.refs_1_.refs_5_), custom_call_target="tpu_custom_call" | custom-call | flops 1207959552 | bytes 4194304 | tf_op jit(solution)/shard_map/pallas_call | solution.py:182
  29.3 1.5 %shard_map.64 = f32[2,2,4,128,128]{4,3,2,1,0:T(8,128)} custom-call(f32[2,2,128,128]{3,2,1,0:T(8,128)S(1)} %collective-permute-done.2.refs_0_, bf16[3072,512]{1,0:T(8,128)(2,1)S(1)} %get-tuple-element.11.refs_3_.refs_1_.refs_5_, f32[2,2,4,128,128]{4,3,2,1,0:T(8,128)S(1)} %shard_map.63.refs_2_), custom_call_target="tpu_custom_call" | custom-call | flops 402653184 | bytes 4194304 | tf_op jit(solution)/shard_map/pallas_call | solution.py:182
  30.8 0.4 %shard_map.71.refs_6_ = f32[2,1,4,128,128]{4,3,2,1,0:T(8,128)S(1)} custom-call(f32[2,1,128,128]{3,2,1,0:T(8,128)S(1)} %shard_map.68.refs_0_, bf16[3072,512]{1,0:T(8,128)(2,1)S(1)} %get-tuple-element.11.refs_3_.refs_1_.refs_5_, f32[2,1,4,128,128]{4,3,2,1,0:T(8,128)S(1)} %get-tuple-element.19.refs_2_), custom_call_target="tpu_custom_call" | custom-call | flops 201326592 | bytes 4194304 | tf_op jit(solution)/shard_map/pallas_call | solution.py:182
  31.2 0.0 collective-permute-done.13.refs_3_
  31.2 0.0 collective-permute-done.14.refs_4_
  31.2 1.2 %collective-permute-done.12.refs_2_ = f32[2,1,128,128]{3,2,1,0:T(8,128)S(1)} collective-permute-done((f32[2,1,128,128]{3,2,1,0:T(8,128)S(1)}, f32[2,1,128,128]{3,2,1,0:T(8,128)S(1)}, u32[]{:S(2)}, u32[]{:S(2)}) %collective-permute-start.12) | collective-permute-done | bytes 131104 | tf_op jit(solution)/shard_map/ppermute | solution.py:247
  32.4 0.8 %collective-permute-done.11.refs_0_ = f32[2,1,128,128]{3,2,1,0:T(8,128)S(1)} collective-permute-done((f32[2,1,128,128]{3,2,1,0:T(8,128)S(1)}, f32[2,1,128,128]{3,2,1,0:T(8,128)S(1)}, u32[]{:S(2)}, u32[]{:S(2)}) %collective-permute-start.11) | collective-permute-done | bytes 131104 | tf_op jit(solution)/shard_map/ppermute | solution.py:247
  33.3 0.6 %shard_map.72.refs_2_ = f32[2,1,4,128,128]{4,3,2,1,0:T(8,128)S(1)} custom-call(f32[2,1,128,128]{3,2,1,0:T(8,128)S(1)} %collective-permute-done.11.refs_0_, f32[2,1,128,128]{3,2,1,0:T(8,128)S(1)} %get-tuple-element.15.refs_2_.refs_1_, f32[2,1,128,128]{3,2,1,0:T(8,128)S(1)} %collective-permute-done.12.refs_2_, ...), custom_call_target="tpu_custom_call" | custom-call | flops 402653184 | bytes 4194304 | tf_op jit(solution)/shard_map/pallas_call | solution.py:182
  33.8 0.0 collective-permute-done.10.refs_0_
  33.8 1.2 %shard_map.73 = f32[2,1,4,128,128]{4,3,2,1,0:T(8,128)} custom-call(f32[2,1,128,128]{3,2,1,0:T(8,128)S(1)} %collective-permute-done.10.refs_0_, bf16[3072,512]{1,0:T(8,128)(2,1)S(1)} %get-tuple-element.11.refs_3_.refs_1_.refs_5_, f32[2,1,4,128,128]{4,3,2,1,0:T(8,128)S(1)} %shard_map.72.refs_2_), custom_call_target="tpu_custom_call" | custom-call | flops 201326592 | bytes 4194304 | tf_op jit(solution)/shard_map/pallas_call | solution.py:182
  (7 shorter events, 0.1 us)
Async XLA Ops:
  0.6 20.6 %copy-start = (f32[2,2,128,128]{3,2,1,0:T(8,128)S(1)}, f32[2,2,128,128]{3,2,1,0:T(8,128)}, u32[]{:S(2)}) copy-start(f32[2,2,128,128]{3,2,1,0:T(8,128)} %refs_2_.3) | copy-start | bytes 786436
  0.6 13.2 %collective-permute-start.5 = (f32[2,2,128,128]{3,2,1,0:T(8,128)}, f32[2,2,128,128]{3,2,1,0:T(8,128)S(1)}, u32[]{:S(2)}, u32[]{:S(2)}) collective-permute-start(f32[2,2,128,128]{3,2,1,0:T(8,128)} %refs_2_.3), channel_id=1, source_target_pairs={{0,8},{4,12},{8,0},{12,4},{16,24},{20,28},{24,16},{28,20},{1,9},{5... | collective-permute-start | bytes 786440 | tf_op jit(solution)/shard_map/ppermute | solution.py:247
  3.6 14.6 %collective-permute-start = (f32[2,2,128,128]{3,2,1,0:T(8,128)}, f32[2,2,128,128]{3,2,1,0:T(8,128)S(1)}, u32[]{:S(2)}, u32[]{:S(2)}) collective-permute-start(f32[2,2,128,128]{3,2,1,0:T(8,128)} %refs_2_.3), channel_id=1, source_target_pairs={{0,2},{1,3},{2,0},{3,1},{4,6},{5,7},{6,4},{7,5},{8,10},{9,11},{10,... | collective-permute-start | bytes 786440 | tf_op jit(solution)/shard_map/ppermute | solution.py:247
  6.2 12.2 %collective-permute-start.3 = (f32[2,2,128,128]{3,2,1,0:T(8,128)}, f32[2,2,128,128]{3,2,1,0:T(8,128)S(1)}, u32[]{:S(2)}, u32[]{:S(2)}) collective-permute-start(f32[2,2,128,128]{3,2,1,0:T(8,128)} %refs_2_.3), channel_id=1, source_target_pairs={{0,1},{1,0},{2,3},{3,2},{4,5},{5,4},{6,7},{7,6},{8,9},{9,8},{10,11... | collective-permute-start | bytes 786440 | tf_op jit(solution)/shard_map/ppermute | solution.py:247
  7.8 10.6 %collective-permute-start.4 = (f32[2,2,128,128]{3,2,1,0:T(8,128)}, f32[2,2,128,128]{3,2,1,0:T(8,128)S(1)}, u32[]{:S(2)}, u32[]{:S(2)}) collective-permute-start(f32[2,2,128,128]{3,2,1,0:T(8,128)} %refs_2_.3), channel_id=1, source_target_pairs={{0,16},{4,20},{8,24},{12,28},{16,0},{20,4},{24,8},{28,12},{1,17},{... | collective-permute-start | bytes 786440 | tf_op jit(solution)/shard_map/ppermute | solution.py:247
  9.3 4.5 %collective-permute-start.6 = (f32[2,1,16]{2,1,0:T(1,128)}, f32[2,1,16]{2,1,0:T(1,128)S(1)}, u32[]{:S(2)}, u32[]{:S(2)}) collective-permute-start(f32[2,1,16]{2,1,0:T(1,128)} %integrals_ref.1), channel_id=1, source_target_pairs={{0,8},{4,12},{8,0},{12,4},{16,24},{20,28},{24,16},{28,20},{1,9},{5... | collective-permute-start | bytes 392 | tf_op jit(solution)/shard_map/ppermute | solution.py:247
  9.9 1.6 %copy-start.1 = (f32[2,4,512,128]{3,2,1,0:T(8,128)S(1)}, f32[2,4,512,128]{3,2,1,0:T(8,128)}, u32[]{:S(2)}) copy-start(f32[2,4,512,128]{3,2,1,0:T(8,128)} %basis_hbm.1) | copy-start | bytes 6291460
  11.5 0.7 %copy-start.2 = (f32[2,1,4,4]{3,2,1,0:T(4,128)S(1)}, f32[2,1,4,4]{3,2,1,0:T(4,128)}, u32[]{:S(2)}) copy-start(f32[2,1,4,4]{3,2,1,0:T(4,128)} %site_hbm.1) | copy-start | bytes 388
  12.1 0.7 %copy-start.3 = (f32[2,1,16]{2,1,0:T(1,128)S(1)}, f32[2,1,16]{2,1,0:T(1,128)}, u32[]{:S(2)}) copy-start(f32[2,1,16]{2,1,0:T(1,128)} %integrals_ref.1) | copy-start | bytes 388
  13.9 7.3 %collective-permute-start.7 = (f32[2,2,136,128]{3,2,1,0:T(8,128)S(1)}, f32[2,2,136,128]{3,2,1,0:T(8,128)S(1)}, u32[]{:S(2)}, u32[]{:S(2)}) collective-permute-start(f32[2,2,136,128]{3,2,1,0:T(8,128)S(1)} %shard_map.65), channel_id=1, source_target_pairs={{0,16},{4,20},{8,24},{12,28},{16,0},{20,4},{24,8},{28,12},{1,17},{... | collective-permute-start | bytes 835592 | tf_op jit(solution)/shard_map/ppermute | solution.py:247
  14.4 1.1 %collective-permute-start.1 = (f32[2,1,16]{2,1,0:T(1,128)S(1)}, f32[2,1,16]{2,1,0:T(1,128)S(1)}, u32[]{:S(2)}, u32[]{:S(2)}) collective-permute-start(f32[2,1,16]{2,1,0:T(1,128)S(1)} %copy-done.3), channel_id=1, source_target_pairs={{0,4},{4,0},{8,12},{12,8},{16,20},{20,16},{24,28},{28,24},{1,5},{5... | collective-permute-start | bytes 392 | tf_op jit(solution)/shard_map/ppermute | solution.py:247
  18.5 3.3 %collective-permute-start.9 = (f32[2,2,128,128]{3,2,1,0:T(8,128)S(1)}, f32[2,2,128,128]{3,2,1,0:T(8,128)S(1)}, u32[]{:S(2)}, u32[]{:S(2)}) collective-permute-start(f32[2,2,128,128]{3,2,1,0:T(8,128)S(1)} %shard_map.62.refs_0_), channel_id=1, source_target_pairs={{0,4},{4,0},{8,12},{12,8},{16,20},{20,16},{24,28},{28,24},{1,5},{5... | collective-permute-start | bytes 786440 | tf_op jit(solution)/shard_map/ppermute | solution.py:247
  18.6 8.7 %collective-permute-start.2 = (f32[2,2,128,128]{3,2,1,0:T(8,128)S(1)}, f32[2,2,128,128]{3,2,1,0:T(8,128)S(1)}, u32[]{:S(2)}, u32[]{:S(2)}) collective-permute-start(f32[2,2,128,128]{3,2,1,0:T(8,128)S(1)} %shard_map.59.x_ref), channel_id=1, source_target_pairs={{0,1},{1,0},{2,3},{3,2},{4,5},{5,4},{6,7},{7,6},{8,9},{9,8},{10,11... | collective-permute-start | bytes 786440 | tf_op jit(solution)/shard_map/ppermute | solution.py:247
  21.7 3.3 %collective-permute-start.8 = (f32[2,1,128,128]{3,2,1,0:T(8,128)S(1)}, f32[2,1,128,128]{3,2,1,0:T(8,128)S(1)}, u32[]{:S(2)}, u32[]{:S(2)}) collective-permute-start(f32[2,1,128,128]{3,2,1,0:T(8,128)S(1)} %get-tuple-element.14), channel_id=1, source_target_pairs={{0,4},{4,0},{8,12},{12,8},{16,20},{20,16},{24,28},{28,24},{1,5},{5... | collective-permute-start | bytes 393224 | tf_op jit(solution)/shard_map/ppermute | solution.py:247
  22.2 9.0 %collective-permute-start.13 = (f32[2,1,128,128]{3,2,1,0:T(8,128)S(1)}, f32[2,1,128,128]{3,2,1,0:T(8,128)S(1)}, u32[]{:S(2)}, u32[]{:S(2)}) collective-permute-start(f32[2,1,128,128]{3,2,1,0:T(8,128)S(1)} %get-tuple-element.17), channel_id=1, source_target_pairs={{0,16},{4,20},{8,24},{12,28},{16,0},{20,4},{24,8},{28,12},{1,17},{... | collective-permute-start | bytes 393224 | tf_op jit(solution)/shard_map/ppermute | solution.py:247
  23.8 7.4 %collective-permute-start.14 = (f32[2,1,128,128]{3,2,1,0:T(8,128)S(1)}, f32[2,1,128,128]{3,2,1,0:T(8,128)S(1)}, u32[]{:S(2)}, u32[]{:S(2)}) collective-permute-start(f32[2,1,128,128]{3,2,1,0:T(8,128)S(1)} %get-tuple-element.18), channel_id=1, source_target_pairs={{0,24},{4,28},{8,16},{12,20},{16,8},{20,12},{24,0},{28,4},{1,25},{... | collective-permute-start | bytes 393224 | tf_op jit(solution)/shard_map/ppermute | solution.py:247
  25.0 8.2 %collective-permute-start.11 = (f32[2,1,128,128]{3,2,1,0:T(8,128)S(1)}, f32[2,1,128,128]{3,2,1,0:T(8,128)S(1)}, u32[]{:S(2)}, u32[]{:S(2)}) collective-permute-start(f32[2,1,128,128]{3,2,1,0:T(8,128)S(1)} %shard_map.68.refs_0_), channel_id=1, source_target_pairs={{0,3},{1,2},{2,1},{3,0},{4,7},{5,6},{6,5},{7,4},{8,11},{9,10},{10,... | collective-permute-start | bytes 393224 | tf_op jit(solution)/shard_map/ppermute | solution.py:247
  25.9 7.9 %collective-permute-start.10 = (f32[2,1,128,128]{3,2,1,0:T(8,128)S(1)}, f32[2,1,128,128]{3,2,1,0:T(8,128)S(1)}, u32[]{:S(2)}, u32[]{:S(2)}) collective-permute-start(f32[2,1,128,128]{3,2,1,0:T(8,128)S(1)} %shard_map.68.refs_0_), channel_id=1, source_target_pairs={{0,1},{1,0},{2,3},{3,2},{4,5},{5,4},{6,7},{7,6},{8,9},{9,8},{10,11... | collective-permute-start | bytes 393224 | tf_op jit(solution)/shard_map/ppermute | solution.py:247
  27.3 5.1 %collective-permute-start.12 = (f32[2,1,128,128]{3,2,1,0:T(8,128)S(1)}, f32[2,1,128,128]{3,2,1,0:T(8,128)S(1)}, u32[]{:S(2)}, u32[]{:S(2)}) collective-permute-start(f32[2,1,128,128]{3,2,1,0:T(8,128)S(1)} %shard_map.70), channel_id=1, source_target_pairs={{0,8},{4,12},{8,0},{12,4},{16,24},{20,28},{24,16},{28,20},{1,9},{5... | collective-permute-start | bytes 393224 | tf_op jit(solution)/shard_map/ppermute | solution.py:247
